TPU v7x, 32 devices: a whole 2x2x4 slice. The times are simulated.
32 devices in a mesh: groups: 2 (over x), lat: 16 (over z, y, core).
Axes of the slice: x: 2, y: 2, z: 4, core: 2. Of those that a mesh axis runs over, the one named last changes fastest.
Arguments:
- codes: bfloat16 [128, 64], P('groups'), parts along dimension 0, may hold values from 0.049804688 to 4
- indices: int32 [128, 64], P('groups'), parts along dimension 0, may hold values from 0 to 8191, as said below
- decoder: bfloat16 [8192, 8192], P('lat'), may hold values from -0.75 to 0.75
- targets: bfloat16 [128, 8192], P(('groups', 'lat')), parts along dimension 0, may hold values from -6 to 6
Outputs:
- error: bfloat16 [128, 8192], P(('groups', 'lat')), parts along dimension 0
- row_loss: float32 [128], P(('groups', 'lat')), parts along dimension 0
- code_grad: float32 [128, 64], P(('groups', 'lat')), parts along dimension 0
There are 2 independent parts, one for each index of `groups`. A program takes and returns all parts, laid end to end along the dimension named above; an argument that names none is the same for every part. Nothing has to cross between parts.
Inputs may be any that keep to these rules, and one draw needn't show every extreme that they name: `indices`: each row names 64 different latents; among the 4 token rows of one device of lat, at most 32 active latents lie in the 512 latents of any one device, and exactly 32 in those of some device.
All inputs are finite; a program needn't handle non-finite values.
Results may differ from a plain program's by a relative error of at most 0.0011.
Values may be sent and summed in bfloat16 or wider, within the bound.
No kernel may reach another device: no remote copies, remote signals or barrier semaphores. Data moves between devices by JAX's collectives and lax.ppermute only.
A program may use at most 128 MiB of HBM per device.

v0:
```python
import jax
import jax.numpy as jnp
from jax import lax
from jax.sharding import PartitionSpec as P


def local(codes, indices, decoder, targets):
    lat_dev = decoder.shape[0]
    width = decoder.shape[1]
    row_count = codes.shape[0]
    devices = lax.axis_size("lat")
    own_rows = row_count // devices
    offset_start = lax.axis_index("lat") * lat_dev
    row_start = lax.axis_index("lat") * own_rows
    local_ids = indices - offset_start
    inside = (local_ids >= 0) & (local_ids < lat_dev)
    clipped = jnp.clip(local_ids, 0, lat_dev - 1)
    row_numbers = jnp.broadcast_to(lax.iota(jnp.int32, row_count)[:, None], indices.shape)
    placed = jnp.where(inside, codes.astype(jnp.float32), 0.0)
    dense = (
        jnp.zeros((row_count, lat_dev), jnp.float32)
        .at[row_numbers, clipped]
        .add(placed)
        .astype(jnp.bfloat16)
    )
    partial_value = jnp.dot(dense, decoder, preferred_element_type=jnp.float32)
    mine = lax.dynamic_slice_in_dim(partial_value, row_start, own_rows, 0) - targets.astype(
        jnp.float32
    )
    partial_value = lax.dynamic_update_slice_in_dim(partial_value, mine, row_start, 0)
    diff_columns = lax.psum_scatter(partial_value, "lat", scatter_dimension=1, tiled=True)
    squares = jnp.sum(diff_columns * diff_columns, axis=1)
    row_loss = lax.psum_scatter(squares, "lat", scatter_dimension=0, tiled=True) / width
    error_columns = diff_columns.astype(jnp.bfloat16)
    piece = lax.all_gather(error_columns, "lat", axis=1, tiled=True)
    totals = lax.dot_general(
        piece, decoder, (((1,), (1,)), ((), ())), preferred_element_type=jnp.float32
    )
    kept = lax.dynamic_slice_in_dim(piece, row_start, own_rows, 0)
    picked = jnp.where(inside, jnp.take_along_axis(totals, clipped, axis=1), 0.0)
    code_grad = lax.psum_scatter(picked, "lat", scatter_dimension=0, tiled=True)
    return (kept, row_loss, code_grad)


def solution(mesh):
    in_specs = (P("groups", None), P("groups", None), P("lat", None), P(("groups", "lat"), None))
    out_specs = (P(("groups", "lat"), None), P(("groups", "lat")), P(("groups", "lat"), None))
    return jax.shard_map(local, mesh=mesh, in_specs=in_specs, out_specs=out_specs, check_vma=False)
```

profile of v0, /device:TPU:0, one launch (start us, length us, event | category | flops | bytes accessed | tf_op | source)
XLA Modules:
  0.0 258.0 jit_solution(17013316206327780871)
XLA Ops:
  7.2 0.0 reduce-scatter.2.cloned.1.call-start
  7.2 0.8 shift-left_or_fusion
  8.0 0.8 convert_select_fusion
  8.8 0.1 reshape.38
  8.9 0.7 and_reduce_fusion
  9.6 0.7 multiply_reduce_fusion.1
  10.4 0.1 reshape.36
  10.4 28.8 %scatter_custom_fusion = f32[32768]{0:T(1024)S(1)} fusion(s32[4096]{0:T(1024)S(1)} %reshape.36, f32[4096]{0:T(1024)S(1)} %reshape.38, f32[]{:T(128)} %constant.9.clone.1), kind=kCustom, calls=%fused_computation.6 | custom fusion | flops 4096 | bytes 131076
  39.2 0.1 reshape.29
  39.3 0.0 copy-start.2
  39.3 5.0 %fusion.4 = f32[64,8192]{1,0:T(8,128)S(1)} fusion(bf16[64,512]{1,0:T(8,128)(2,1)S(1)} %reshape.29, bf16[512,8192]{1,0:T(8,128)(2,1)} %param.6), kind=kOutput, calls=%fused_computation.19 | convolution fusion | flops 536870912 | bytes 10551296 | tf_op jit(solution)/shard_map/dot_general | solution.py:26
  44.3 0.0 copy-done.2
  44.3 0.0 copy-start.3
  44.3 0.1 subtract_dynamic-update-slice_fusion
  44.4 0.0 copy-start
  44.4 1.3 copy-done
  45.7 0.0 reduce-scatter.2.cloned.1.call-update
  45.8 0.0 all-gather.2.cloned.1.call-start
  45.8 64.4 %reduce-scatter.2.cloned.1.call-done = f32[64,512]{1,0:T(8,128)} async-done(((f32[64,8192]{1,0:T(8,128)}), f32[64,512]{1,0:T(8,128)}) %reduce-scatter.2.cloned.1.call-update) | async-done | bytes 131088 | tf_op jit(solution)/shard_map/reduce_scatter | solution.py:31
  110.2 1.7 multiply_reduce_fusion
  111.9 0.0 all-gather.2.cloned.1.call-update
  111.9 0.1 reshape.30
  112.0 0.0 copy-done.3
  112.0 0.6 dynamic-slice
  113.2 35.7 %all-gather.2.cloned.1.call-done = bf16[64,8192]{1,0:T(8,128)(2,1)} async-done(((bf16[64,512]{1,0:T(8,128)(2,1)}), bf16[64,8192]{1,0:T(8,128)(2,1)}) %all-gather.2.cloned.1.call-update) | async-done | bytes 1048592 | tf_op jit(solution)/shard_map/all_gather | solution.py:35
  148.9 6.4 %fusion.5 = f32[64,512]{1,0:T(8,128)S(1)} fusion(bf16[64,8192]{1,0:T(8,128)(2,1)} %all-gather.2.cloned.1.call-done, bf16[512,8192]{1,0:T(8,128)(2,1)} %param.6), kind=kOutput, calls=%fused_computation.20 | convolution fusion | flops 536870912 | bytes 9568256 | tf_op jit(solution)/shard_map/dot_general | solution.py:36
  155.3 0.0 copy-start.1
  155.3 32.8 %gather_fusion = f32[4096]{0:T(1024)S(1)} fusion(f32[64,512]{1,0:T(8,128)S(1)} %fusion.5, s32[4096]{0:T(1024)S(1)} %reshape.30), kind=kCustom, calls=%fused_computation | custom fusion | bytes 65536 | tf_op jit(solution)/shard_map/jit(take_along_axis)/gather | solution.py:40
  188.1 0.1 reshape.33
  188.2 0.0 copy-done.1
  188.2 60.2 %all-reduce.2 = (f32[64]{0:T(128)S(1)}, f32[64,64]{1,0:T(8,128)S(1)}) all-reduce(f32[64]{0:T(128)S(1)} %get-tuple-element.7, f32[64,64]{1,0:T(8,128)S(1)} %select_select_fusion), channel_id=3, replica_groups=mesh['groups'=2,'lat'=16] {'lat'}, use_global_device_ids=true, to_apply=%region_3.4.clone | all-reduce | flops 4160 | bytes 33280
  248.4 0.6 dynamic-slice_multiply_fusion
  249.0 0.6 constant_dynamic-slice_fusion.1
  249.6 1.6 constant_dynamic-slice_fusion
  (4 shorter events, 0.0 us)
Async XLA Ops:
  7.2 103.0 %reduce-scatter.2.cloned.1.call-start = ((), (), s32[]{:S(2)}) async-start(), calls=%async_computation.1 | async-start | bytes 2228224 | tf_op jit(solution)/shard_map/reduce_scatter | solution.py:31
  39.3 5.0 %copy-start.2 = (bf16[4,8192]{1,0:T(4,128)(2,1)S(1)}, bf16[4,8192]{1,0:T(4,128)(2,1)}, u32[]{:S(2)}) copy-start(bf16[4,8192]{1,0:T(4,128)(2,1)} %param.7) | copy-start | bytes 196612
  44.3 67.7 %copy-start.3 = (u32[32]{0:T(128)S(1)}, u32[32]{0:T(128)}, u32[]{:S(2)}) copy-start(u32[32]{0:T(128)} %constant.61) | copy-start | bytes 388
  44.4 1.4 copy-start
  45.8 103.2 %all-gather.2.cloned.1.call-start = ((), (), s32[]{:S(2)}) async-start(), calls=%async_computation.2 | async-start | bytes 1114112 | tf_op jit(solution)/shard_map/all_gather | solution.py:35
  155.3 32.9 %copy-start.1 = (s32[64,64]{1,0:T(8,128)S(1)}, s32[64,64]{1,0:T(8,128)}, u32[]{:S(2)}) copy-start(s32[64,64]{1,0:T(8,128)} %param.5) | copy-start | bytes 49156
Sparse Core Ops, SparseCore 0:
  45.9 64.2 reduce-scatter.1
  113.1 35.7 all-gather.1
where the time goes:
time: 258 us
  waiting for transfers between devices  100 us (39%)
  blocking collectives  60.2 us (23%)
  local copies, waits for them, and re-layouts  37.2 us (14%)
  other arithmetic  34.2 us (13%)
  between operations  14.8 us (6%)
  matrix products  11.4 us (4%)
    reduce_scatter x1, waiting for transfers between devices, local(): lax.psum_scatter(partial_value, 'lat', scatter_dimension=1, tiled=True)  64.4 us
    unnamed x1, blocking collectives  60.2 us
    all_gather x1, waiting for transfers between devices, local(): piece = lax.all_gather(error_columns, 'lat', axis=1, tiled=True)  35.7 us
    gather x2, local copies, waits for them, and re-layouts, local(): jnp.take_along_axis(totals, clipped, axis=1)  32.8 us
    unnamed x4, other arithmetic  30.2 us
    dot_general x1, matrix products, local(): lax.dot_general(piece, decoder, (((1,), (1,)), ((), ())), preferred_eleme...  6.37 us
  transfers between devices with their start and end apart: 2, of which 2 were waited for; matrix products, arithmetic and copies ran while one was open for 0% of the time, Pallas kernels for 0%

commit v1 on v0

v1 whole, which is shorter than its diff:
```python
import functools

import jax
import jax.numpy as jnp
from jax import lax
from jax.experimental import pallas as pl
from jax.experimental.pallas import tpu as pltpu
from jax.sharding import PartitionSpec as P

CHUNKS = 1
ROW_STEP = 16
VMEM = pl.BlockSpec(memory_space=pltpu.VMEM)
ANY = pl.BlockSpec(memory_space=pl.ANY)


def factors(n):
    c = 2 if n % 2 == 0 else 1
    m = n // c
    y = 1
    while 4 * y * y <= m and m % (2 * y) == 0:
        y *= 2
    return m // y, y, c


def place(n, index):
    _, y, c = factors(n)
    return index // (y * c), (index // c) % y, index % c


def shift(n, dz, dy, dc):
    fz, fy, fc = factors(n)
    pairs = []
    for i in range(n):
        z, y, c = place(n, i)
        to = (((z + dz) % fz) * fy + (y + dy) % fy) * fc + (c + dc) % fc
        pairs.append((i, to))
    return pairs


def cost(flops, size):
    return pl.CostEstimate(flops=flops, bytes_accessed=size, transcendentals=0)


def params():
    return pltpu.CompilerParams(vmem_limit_bytes=48 * 1024 * 1024)


def column_copy(decoder_ref, buf, sem, slot, col, width):
    return pltpu.make_async_copy(
        decoder_ref.at[:, pl.ds(pl.multiple_of(col, width), width)], buf.at[slot], sem.at[slot]
    )


def decode_kernel(n, own, chunk, chunks, dc, first, *refs):
    if first:
        ids_ref, codes_ref, decoder_ref, targets_ref, out_ref, dense_ref, buf, sem = refs
    else:
        dense_ref, decoder_ref, targets_ref, out_ref, buf, sem = refs
    fz, fy, fc = factors(n)
    me = lax.axis_index("lat")
    _, y, c = place(n, me)
    lat_dev = decoder_ref.shape[0]
    sub = buf.shape[2]
    cols = []
    for o in range(fy):
        block = ((c + dc) % fc) * fy + (y + o + 1) % fy
        cols.append((block * chunks + chunk) * sub)
    for o in range(fy):
        column_copy(decoder_ref, buf, sem, o, cols[o], sub).start()
    if first:
        rows, k_count = ids_ref.shape
        lanes = lax.broadcasted_iota(jnp.int32, (ROW_STEP, lat_dev), 1) + me * lat_dev

        def body(g, carry):
            at = pl.ds(pl.multiple_of(g * ROW_STEP, ROW_STEP), ROW_STEP)
            ids = ids_ref[at, :]
            codes = codes_ref[at, :].astype(jnp.float32)
            acc = jnp.zeros((ROW_STEP, lat_dev), jnp.float32)
            for k in range(k_count):
                acc = jnp.where(ids[:, k : k + 1] == lanes, codes[:, k : k + 1], acc)
            dense_ref[at, :] = acc.astype(jnp.bfloat16)
            return carry

        lax.fori_loop(0, rows // ROW_STEP, body, 0)
    rows = dense_ref.shape[0]
    row = lax.broadcasted_iota(jnp.int32, (rows, own), 0)
    want = lax.broadcasted_iota(jnp.int32, (rows, own), 1) + me * own
    mine = jnp.where(row == want, -1.0, 0.0).astype(jnp.bfloat16)
    for o in range(fy):
        column_copy(decoder_ref, buf, sem, o, cols[o], sub).wait()
        part = jnp.dot(dense_ref[...], buf[o], preferred_element_type=jnp.float32)
        tgt = targets_ref[:, pl.ds(pl.multiple_of(cols[o], sub), sub)]
        part += jnp.dot(mine, tgt, preferred_element_type=jnp.float32)
        out_ref[:, o * sub : (o + 1) * sub] = part


def decode(n, own, chunk, chunks, dc, sub, ids, codes, dense, decoder, targets):
    _, fy, _ = factors(n)
    lat_dev = decoder.shape[0]
    first = dense is None
    rows = ids.shape[0]
    out = jax.ShapeDtypeStruct((rows, fy * sub), jnp.float32)
    dense_shape = jax.ShapeDtypeStruct((rows, lat_dev), jnp.bfloat16)
    call = pl.pallas_call(
        functools.partial(decode_kernel, n, own, chunk, chunks, dc, first),
        out_shape=(out, dense_shape) if first else out,
        in_specs=[VMEM, VMEM, ANY, VMEM] if first else [VMEM, ANY, VMEM],
        out_specs=(VMEM, VMEM) if first else VMEM,
        scratch_shapes=[
            pltpu.VMEM((fy, lat_dev, sub), jnp.bfloat16),
            pltpu.SemaphoreType.DMA((fy,)),
        ],
        compiler_params=params(),
        cost_estimate=cost(2 * rows * lat_dev * fy * sub, (2 * lat_dev + 4 * rows) * fy * sub),
        name="decode",
    )
    if first:
        return call(ids, codes, decoder, targets)
    return call(dense, decoder, targets), dense


def grad_kernel(n, blocks, final, with_prev, *refs):
    refs = list(refs)
    errs = [refs.pop(0) for _ in blocks]
    decoder_ref = refs.pop(0)
    prev_ref = refs.pop(0) if with_prev else None
    if final:
        ids_ref, loss_ref, out_ref, buf, sem, totals_ref = refs
    else:
        totals_ref, buf, sem = refs
    fz, fy, fc = factors(n)
    me = lax.axis_index("lat")
    z, y, c = place(n, me)
    sub = buf.shape[2]
    cols = []
    for dc, dy, chunk, chunks in blocks:
        block = ((c + dc) % fc) * fy + (y + fy - dy) % fy
        cols.append((block * chunks + chunk) * sub)
    for i, col in enumerate(cols):
        column_copy(decoder_ref, buf, sem, i, col, sub).start()
    total = prev_ref[...] if with_prev else None
    for i, col in enumerate(cols):
        column_copy(decoder_ref, buf, sem, i, col, sub).wait()
        part = lax.dot_general(
            errs[i][...], buf[i], (((1,), (1,)), ((), ())), preferred_element_type=jnp.float32
        )
        total = part if total is None else total + part
    totals_ref[...] = total
    if final:
        rows, k_count = ids_ref.shape
        lat_dev = decoder_ref.shape[0]
        group = rows // fz
        own = out_ref.shape[1]
        lanes = lax.broadcasted_iota(jnp.int32, (ROW_STEP, lat_dev), 1) + me * lat_dev
        places = lax.broadcasted_iota(jnp.int32, (ROW_STEP, 128), 1)
        steps = group // ROW_STEP
        dests = ROW_STEP // own

        def body(g, carry):
            o, s = g // steps, g % steps
            z_of = (z + fz - o) % fz
            at = pl.multiple_of(z_of * group + s * ROW_STEP, ROW_STEP)
            ids = ids_ref[pl.ds(at, ROW_STEP), :]
            totals = totals_ref[pl.ds(pl.multiple_of(g * ROW_STEP, ROW_STEP), ROW_STEP), :]
            loss = loss_ref[pl.ds(pl.multiple_of(s * ROW_STEP, ROW_STEP), ROW_STEP), :]
            acc = jnp.where((places == k_count) & (o == 0), loss, 0.0)
            for k in range(k_count):
                hit = jnp.where(ids[:, k : k + 1] == lanes, totals, 0.0)
                acc = jnp.where(places == k, jnp.sum(hit, axis=1, keepdims=True), acc)
            for d in range(dests):
                out_ref[at // own + d] = acc[d * own : (d + 1) * own, :]
            return carry

        lax.fori_loop(0, rows // ROW_STEP, body, 0)


def grad(n, blocks, errs, decoder, prev, final=None):
    lat_dev = decoder.shape[0]
    rows, sub = errs[0].shape
    totals = jax.ShapeDtypeStruct((rows, lat_dev), jnp.float32)
    scratch = [
        pltpu.VMEM((len(errs), lat_dev, sub), jnp.bfloat16),
        pltpu.SemaphoreType.DMA((len(errs),)),
    ]
    args = list(errs) + [decoder]
    specs = [VMEM] * len(errs) + [ANY]
    if prev is not None:
        args.append(prev)
        specs.append(VMEM)
    out = totals
    if final is not None:
        args += list(final)
        specs += [VMEM] * len(final)
        out = jax.ShapeDtypeStruct((n, rows // n, 128), jnp.float32)
        scratch.append(pltpu.VMEM(totals.shape, totals.dtype))
    return pl.pallas_call(
        functools.partial(grad_kernel, n, tuple(blocks), final is not None, prev is not None),
        out_shape=out,
        in_specs=specs,
        out_specs=VMEM,
        scratch_shapes=scratch,
        compiler_params=params(),
        cost_estimate=cost(
            2 * rows * lat_dev * sub * len(errs), 2 * (lat_dev + rows) * sub * len(errs)
        ),
        name="grad",
    )(*args)


def own_kernel(n, blocks, own, *refs):
    errs, out_ref = refs[:-1], refs[-1]
    fz, fy, fc = factors(n)
    _, y, c = place(n, lax.axis_index("lat"))
    group, sub = errs[0].shape
    row = lax.broadcasted_iota(jnp.int32, (own, group), 0) + (y * fc + c) * own
    want = lax.broadcasted_iota(jnp.int32, (own, group), 1)
    mine = jnp.where(row == want, 1.0, 0.0).astype(jnp.bfloat16)
    for err, (dc, dy, chunk, chunks) in zip(errs, blocks):
        block = ((c + dc) % fc) * fy + (y + fy - dy) % fy
        col = pl.multiple_of((block * chunks + chunk) * sub, sub)
        rows = jnp.dot(mine, err[...], preferred_element_type=jnp.float32)
        out_ref[:, pl.ds(col, sub)] = rows.astype(jnp.bfloat16)


def own_rows(n, blocks, own, width, errs):
    return pl.pallas_call(
        functools.partial(own_kernel, n, tuple(blocks), own),
        out_shape=jax.ShapeDtypeStruct((own, width), jnp.bfloat16),
        in_specs=[VMEM] * len(errs),
        out_specs=VMEM,
        compiler_params=params(),
        name="own_rows",
    )(*errs)


def local(codes, indices, decoder, targets):
    width = decoder.shape[1]
    rows, k_count = codes.shape
    n = lax.axis_size("lat")
    own = rows // n
    fz, fy, fc = factors(n)
    group = rows // fz
    chunks = CHUNKS
    sub = width // (fc * fy * chunks)
    me = lax.axis_index("lat")
    z, _, _ = place(n, me)

    def send(x, dz=0, dy=0, dc=0):
        return lax.ppermute(x, "lat", shift(n, dz, dy, dc))

    dense = None
    far = {}
    for dc in range(1, fc):
        for p in range(chunks):
            part, dense = decode(n, own, p, chunks, dc, sub, indices, codes, dense, decoder, targets)
            far[dc, p] = send(part, dc=dc)
    kept = []
    for p in range(chunks):
        part, dense = decode(n, own, p, chunks, 0, sub, indices, codes, dense, decoder, targets)
        kept.append(part)

    diffs = []
    for p in range(chunks):
        summed = kept[p]
        for dc in range(1, fc):
            summed = summed + far[dc, p]
        mine = summed[:, (fy - 1) * sub :]
        got = [
            send(summed[:, o * sub : (o + 1) * sub], dy=o + 1) for o in range(fy - 1)
        ]
        for g in got:
            mine = mine + g
        diff = lax.dynamic_slice_in_dim(mine, z * group, group, 0)
        for o in range(1, fz):
            piece = lax.dynamic_slice_in_dim(mine, ((z + o) % fz) * group, group, 0)
            diff = diff + send(piece, dz=o)
        diffs.append(diff)

    loss = sum(jnp.sum(d * d, axis=1, keepdims=True) for d in diffs)

    near, near_blocks, other, other_blocks = [], [], [], []
    for p in range(chunks):
        err = diffs[p].astype(jnp.bfloat16)
        parts = [err] + [send(err, dz=o) for o in range(1, fz)]
        whole = jnp.concatenate(parts, axis=0)
        here = [whole] + [send(whole, dy=o) for o in range(1, fy)]
        for o, e in enumerate(here):
            near.append(e)
            near_blocks.append((0, o, p, chunks))
            for dc in range(1, fc):
                other.append(send(e, dc=dc))
                other_blocks.append((dc, o, p, chunks))

    totals = None
    for e, b in zip(near, near_blocks):
        totals = grad(n, [b], [e], decoder, totals)
    out = grad(n, other_blocks, other, decoder, totals, (indices, loss))
    error = own_rows(
        n, near_blocks + other_blocks, own, width, [e[:group] for e in near + other]
    )

    swapped = lax.all_to_all(out, "lat", 0, 0, tiled=True)
    back = jnp.sum(swapped, axis=0)
    return error, back[:, k_count] / width, back[:, :k_count]


def solution(mesh):
    in_specs = (P("groups", None), P("groups", None), P("lat", None), P(("groups", "lat"), None))
    out_specs = (P(("groups", "lat"), None), P(("groups", "lat")), P(("groups", "lat"), None))
    return jax.shard_map(local, mesh=mesh, in_specs=in_specs, out_specs=out_specs, check_vma=False)
```

time: 258 us -> 95.3 us (0.37)
  waiting for transfers between devices: 100 us -> 35.9 us
  blocking collectives: 60.2 us -> 0 us
  local copies, waits for them, and re-layouts: 37.2 us -> 2.49 us
  Pallas kernels: 0 us -> 34 us
  other arithmetic: 34.2 us -> 1.05 us
  starting transfers between devices: 0.08 us -> 20.7 us
  between operations: 14.8 us -> 0.79 us
  matrix products: 11.4 us -> 0 us
    reduce_scatter x1 -> x0, waiting for transfers between devices: 64.4 us -> none  [local(): lax.psum_scatter(partial_value, 'lat', scatter_dimension=1, tiled=True)]
    unnamed x1 -> x0, blocking collectives: 60.2 us -> none
    all_gather x1 -> x0, waiting for transfers between devices: 35.7 us -> none  [local(): piece = lax.all_gather(error_columns, 'lat', axis=1, tiled=True)]
    pallas_call x0 -> x6, Pallas kernels: none -> 34 us  [the longest x3 27.5 us: grad(): pl.pallas_call(functools.partial(grad_kernel, n, tuple(blocks), final is...]
    gather x2 -> x0, local copies, waits for them, and re-layouts: 32.8 us -> none  [local(): jnp.take_along_axis(totals, clipped, axis=1)]
    unnamed x4 -> x0, other arithmetic: 30.2 us -> none
    ppermute x0 -> x11, waiting for transfers between devices: none -> 30.1 us  [send(): return lax.ppermute(x, 'lat', shift(n, dz, dy, dc))]
    ppermute x0 -> x11, starting transfers between devices: none -> 16.3 us  [send(): return lax.ppermute(x, 'lat', shift(n, dz, dy, dc))]
  transfers between devices with their start and end apart: 2 -> 12, of which waited for: 2 -> 8; matrix products, arithmetic and copies ran while one was open for 0% -> 0% of each run, Pallas kernels for 0% -> 9%
where the time goes in v1:
time: 95.3 us; the launch traced here: 94.9 us
  waiting for transfers between devices  35.9 us (38%)
  Pallas kernels  34 us (36%)
  starting transfers between devices  20.7 us (22%)
  local copies, waits for them, and re-layouts  2.49 us (3%)
  other arithmetic  1.05 us (1%)
    ppermute x11, waiting for transfers between devices, send(): return lax.ppermute(x, 'lat', shift(n, dz, dy, dc))  30.1 us
    pallas_call x3, Pallas kernels, grad(): pl.pallas_call(functools.partial(grad_kernel, n, tuple(blocks), final is...  27.5 us
    ppermute x11, starting transfers between devices, send(): return lax.ppermute(x, 'lat', shift(n, dz, dy, dc))  16.3 us
    all_to_all x1, waiting for transfers between devices, local(): swapped = lax.all_to_all(out, 'lat', 0, 0, tiled=True)  5.74 us
    all_to_all x1, starting transfers between devices, local(): swapped = lax.all_to_all(out, 'lat', 0, 0, tiled=True)  4.43 us
    pallas_call x1, Pallas kernels, decode(): return call(ids, codes, decoder, targets)  2.84 us
    pallas_call x1, Pallas kernels, decode(): return (call(dense, decoder, targets), dense)  2.82 us
    unnamed x12, local copies, waits for them, and re-layouts  2.32 us
  transfers between devices with their start and end apart: 12, of which 8 were waited for; matrix products, arithmetic and copies ran while one was open for 0% of the time, Pallas kernels for 9%

profile of v1, /device:TPU:0, one launch (start us, length us, event | category | flops | bytes accessed | tf_op | source)
XLA Modules:
  0.0 94.9 jit_solution(646740435930017086)
XLA Ops:
  0.6 0.0 copy-start
  0.6 0.8 copy-done
  1.5 0.0 copy-start.2
  1.5 0.8 copy-done.2
  2.2 0.0 copy-start.4
  2.2 0.7 copy-done.4
  2.9 0.0 copy-start.1
  2.9 2.8 %decode.2 = (f32[64,4096]{1,0:T(8,128)S(1)}, bf16[64,512]{1,0:T(8,128)(2,1)S(1)}) custom-call(s32[64,64]{1,0:T(8,128)S(1)} %copy-done.2, bf16[64,64]{1,0:T(8,128)(2,1)S(1)} %copy-done.4, bf16[512,8192]{1,0:T(8,128)(2,1)} %refs_2_.5, bf16[4,8192]{1,0:T(4,128)(2,1)S(1)} %copy-done), custom_call_target="tpu_custom_call" | custom-call | flops 268435456 | bytes 5242880 | tf_op jit(solution)/shard_map/decode/pallas_call | solution.py:118
  5.8 0.5 collective-permute-start
  6.3 0.0 copy-done.1
  6.3 2.8 %decode.3 = f32[64,4096]{1,0:T(8,128)S(1)} custom-call(bf16[64,512]{1,0:T(8,128)(2,1)S(1)} %get-tuple-element.5.refs_0_, bf16[512,8192]{1,0:T(8,128)(2,1)} %refs_2_.5, bf16[4,8192]{1,0:T(4,128)(2,1)S(1)} %copy-done.1), custom_call_target="tpu_custom_call" | custom-call | flops 268435456 | bytes 5242880 | tf_op jit(solution)/shard_map/decode/pallas_call | solution.py:119
  9.1 0.0 collective-permute-done
  9.1 0.1 add.47
  9.3 2.6 %collective-permute-start.1 = (f32[64,2048]{1,0:T(8,128)S(1)}, f32[64,2048]{1,0:T(8,128)S(1)}, u32[]{:S(2)}, u32[]{:S(2)}) collective-permute-start(f32[64,2048]{1,0:T(8,128)S(1)} %slice.29), channel_id=1, source_target_pairs={{0,2},{1,3},{2,0},{3,1},{4,6},{5,7},{6,4},{7,5},{8,10},{9,11},{10,... | collective-permute-start | bytes 1572872 | tf_op jit(solution)/shard_map/ppermute | solution.py:249
  11.9 12.6 %collective-permute-done.1 = f32[64,2048]{1,0:T(8,128)S(1)} collective-permute-done((f32[64,2048]{1,0:T(8,128)S(1)}, f32[64,2048]{1,0:T(8,128)S(1)}, u32[]{:S(2)}, u32[]{:S(2)}) %collective-permute-start.1) | collective-permute-done | bytes 524320 | tf_op jit(solution)/shard_map/ppermute | solution.py:249
  24.5 0.1 slice_add_fusion
  24.6 1.9 %collective-permute-start.2 = (f32[16,2048]{1,0:T(8,128)S(1)}, f32[16,2048]{1,0:T(8,128)S(1)}, u32[]{:S(2)}, u32[]{:S(2)}) collective-permute-start(f32[16,2048]{1,0:T(8,128)S(1)} %get-tuple-element.9), channel_id=1, source_target_pairs={{0,4},{1,5},{2,6},{3,7},{4,8},{5,9},{6,10},{7,11},{8,12},{9,13},{1... | collective-permute-start | bytes 393224 | tf_op jit(solution)/shard_map/ppermute | solution.py:249
  26.4 2.6 %collective-permute-start.3 = (f32[16,2048]{1,0:T(8,128)S(1)}, f32[16,2048]{1,0:T(8,128)S(1)}, u32[]{:S(2)}, u32[]{:S(2)}) collective-permute-start(f32[16,2048]{1,0:T(8,128)S(1)} %get-tuple-element.11), channel_id=1, source_target_pairs={{0,8},{1,9},{2,10},{3,11},{4,12},{5,13},{6,14},{7,15},{8,0},{9,1},... | collective-permute-start | bytes 393224 | tf_op jit(solution)/shard_map/ppermute | solution.py:249
  29.0 1.3 %collective-permute-start.4 = (f32[16,2048]{1,0:T(8,128)S(1)}, f32[16,2048]{1,0:T(8,128)S(1)}, u32[]{:S(2)}, u32[]{:S(2)}) collective-permute-start(f32[16,2048]{1,0:T(8,128)S(1)} %get-tuple-element.10), channel_id=1, source_target_pairs={{0,12},{1,13},{2,14},{3,15},{4,0},{5,1},{6,2},{7,3},{8,4},{9,5},{1... | collective-permute-start | bytes 393224 | tf_op jit(solution)/shard_map/ppermute | solution.py:249
  30.4 2.5 %collective-permute-done.2 = f32[16,2048]{1,0:T(8,128)S(1)} collective-permute-done((f32[16,2048]{1,0:T(8,128)S(1)}, f32[16,2048]{1,0:T(8,128)S(1)}, u32[]{:S(2)}, u32[]{:S(2)}) %collective-permute-start.2) | collective-permute-done | bytes 131104 | tf_op jit(solution)/shard_map/ppermute | solution.py:249
  32.9 4.6 %collective-permute-done.3 = f32[16,2048]{1,0:T(8,128)S(1)} collective-permute-done((f32[16,2048]{1,0:T(8,128)S(1)}, f32[16,2048]{1,0:T(8,128)S(1)}, u32[]{:S(2)}, u32[]{:S(2)}) %collective-permute-start.3) | collective-permute-done | bytes 131104 | tf_op jit(solution)/shard_map/ppermute | solution.py:249
  37.5 0.0 collective-permute-done.4
  37.5 0.1 multiply_reduce_fusion
  37.7 3.3 %collective-permute-start.5 = (bf16[16,2048]{1,0:T(8,128)(2,1)S(1)}, bf16[16,2048]{1,0:T(8,128)(2,1)S(1)}, u32[]{:S(2)}, u32[]{:S(2)}) collective-permute-start(bf16[16,2048]{1,0:T(8,128)(2,1)S(1)} %get-tuple-element.8.refs_0_), channel_id=1, source_target_pairs={{0,4},{1,5},{2,6},{3,7},{4,8},{5,9},{6,10},{7,11},{8,12},{9,13},{1... | collective-permute-start | bytes 196616 | tf_op jit(solution)/shard_map/ppermute | solution.py:249
  41.0 1.6 %collective-permute-start.6 = (bf16[16,2048]{1,0:T(8,128)(2,1)S(1)}, bf16[16,2048]{1,0:T(8,128)(2,1)S(1)}, u32[]{:S(2)}, u32[]{:S(2)}) collective-permute-start(bf16[16,2048]{1,0:T(8,128)(2,1)S(1)} %get-tuple-element.8.refs_0_), channel_id=1, source_target_pairs={{0,8},{1,9},{2,10},{3,11},{4,12},{5,13},{6,14},{7,15},{8,0},{9,1},... | collective-permute-start | bytes 196616 | tf_op jit(solution)/shard_map/ppermute | solution.py:249
  42.6 0.8 collective-permute-start.7
  43.4 1.3 %collective-permute-done.5 = bf16[16,2048]{1,0:T(8,128)(2,1)S(1)} collective-permute-done((bf16[16,2048]{1,0:T(8,128)(2,1)S(1)}, bf16[16,2048]{1,0:T(8,128)(2,1)S(1)}, u32[]{:S(2)}, u32[]{:S(2)}) %collective-permute-start.5) | collective-permute-done | bytes 65568 | tf_op jit(solution)/shard_map/ppermute | solution.py:249
  44.7 2.5 %collective-permute-done.6 = bf16[16,2048]{1,0:T(8,128)(2,1)S(1)} collective-permute-done((bf16[16,2048]{1,0:T(8,128)(2,1)S(1)}, bf16[16,2048]{1,0:T(8,128)(2,1)S(1)}, u32[]{:S(2)}, u32[]{:S(2)}) %collective-permute-start.6) | collective-permute-done | bytes 65568 | tf_op jit(solution)/shard_map/ppermute | solution.py:249
  47.2 0.6 collective-permute-done.7
  47.9 1.6 %collective-permute-start.8 = (bf16[64,2048]{1,0:T(8,128)(2,1)S(1)}, bf16[64,2048]{1,0:T(8,128)(2,1)S(1)}, u32[]{:S(2)}, u32[]{:S(2)}) collective-permute-start(bf16[64,2048]{1,0:T(8,128)(2,1)S(1)} %pad_maximum_fusion.refs_0_), channel_id=1, source_target_pairs={{0,2},{1,3},{2,0},{3,1},{4,6},{5,7},{6,4},{7,5},{8,10},{9,11},{10,... | collective-permute-start | bytes 786440 | tf_op jit(solution)/shard_map/ppermute | solution.py:249
  49.4 0.0 collective-permute-start.9
  49.4 6.0 %collective-permute-done.8.refs_0_ = bf16[64,2048]{1,0:T(8,128)(2,1)S(1)} collective-permute-done((bf16[64,2048]{1,0:T(8,128)(2,1)S(1)}, bf16[64,2048]{1,0:T(8,128)(2,1)S(1)}, u32[]{:S(2)}, u32[]{:S(2)}) %collective-permute-start.8) | collective-permute-done | bytes 262176 | tf_op jit(solution)/shard_map/ppermute | solution.py:249
  55.4 0.0 collective-permute-start.10
  55.4 0.1 copy.7.refs_5_
  55.5 0.0 copy-start.3
  55.5 2.4 %grad.3.refs_2_ = f32[64,512]{1,0:T(8,128)S(1)} custom-call(bf16[64,2048]{1,0:T(8,128)(2,1)S(1)} %pad_maximum_fusion.refs_0_, bf16[512,8192]{1,0:T(8,128)(2,1)} %refs_2_.5), custom_call_target="tpu_custom_call" | custom-call | flops 134217728 | bytes 2359296 | tf_op jit(solution)/shard_map/grad/pallas_call | solution.py:196
  57.9 2.4 %grad.4.refs_3_ = f32[64,512]{1,0:T(8,128)S(1)} custom-call(bf16[64,2048]{1,0:T(8,128)(2,1)S(1)} %collective-permute-done.8.refs_0_, bf16[512,8192]{1,0:T(8,128)(2,1)} %refs_2_.5, f32[64,512]{1,0:T(8,128)S(1)} %grad.3.refs_2_), custom_call_target="tpu_custom_call" | custom-call | flops 134217728 | bytes 2359296 | tf_op jit(solution)/shard_map/grad/pallas_call | solution.py:196
  60.3 0.0 collective-permute-done.9.refs_0_
  60.3 0.0 collective-permute-done.10.refs_1_
  60.3 0.0 copy-done.3
  60.3 22.8 %grad.5 = f32[16,4,128]{2,1,0:T(4,128)} custom-call(bf16[64,2048]{1,0:T(8,128)(2,1)S(1)} %collective-permute-done.9.refs_0_, bf16[64,2048]{1,0:T(8,128)(2,1)S(1)} %collective-permute-done.10.refs_1_, bf16[512,8192]{1,0:T(8,128)(2,1)} %refs_2_.5, f32[64,512]{1,0:T(8,128)S(1)} %grad.4.refs_3_, s32[64,64]{1,0:T(8,128)S(1)} %copy-done.3, f32[16,1]{1,0:T(8,128)S(1)} %copy.7.refs_5_), custom_call_target="tpu_custom_call" | custom-call | flops 268435456 | bytes 4718592 | tf_op jit(solution)/shard_map/grad/pallas_call | solution.py:196
  83.1 4.4 %all-to-all-start = ((f32[16,4,128]{2,1,0:T(4,128)}), f32[16,4,128]{2,1,0:T(4,128)S(1)}, u32[]{:S(2)}, u32[]{:S(2)}) async-start(f32[16,4,128]{2,1,0:T(4,128)} %grad.5), calls=%async_computation | async-start | bytes 65536 | tf_op jit(solution)/shard_map/all_to_all | solution.py:302
  87.6 0.9 own_rows.1
  88.5 5.7 %all-to-all-done = f32[16,4,128]{2,1,0:T(4,128)S(1)} async-done(((f32[16,4,128]{2,1,0:T(4,128)}), f32[16,4,128]{2,1,0:T(4,128)S(1)}, u32[]{:S(2)}, u32[]{:S(2)}) %all-to-all-start) | async-done | bytes 32800 | tf_op jit(solution)/shard_map/all_to_all | solution.py:302
  94.2 0.0 copy-start.5
  94.2 0.7 multiply_reduce_fusion.1
  94.9 0.0 copy-done.5
  (7 shorter events, 0.1 us)
Async XLA Ops:
  0.6 0.8 copy-start
  1.5 0.8 copy-start.2
  2.2 0.7 copy-start.4
  2.9 3.4 %copy-start.1 = (bf16[4,8192]{1,0:T(4,128)(2,1)S(1)}, bf16[4,8192]{1,0:T(4,128)(2,1)}, u32[]{:S(2)}) copy-start(bf16[4,8192]{1,0:T(4,128)(2,1)} %refs_2_.4) | copy-start | bytes 196612
  5.8 3.3 %collective-permute-start = (f32[64,4096]{1,0:T(8,128)S(1)}, f32[64,4096]{1,0:T(8,128)S(1)}, u32[]{:S(2)}, u32[]{:S(2)}) collective-permute-start(f32[64,4096]{1,0:T(8,128)S(1)} %get-tuple-element.6), channel_id=1, source_target_pairs={{0,1},{1,0},{2,3},{3,2},{4,5},{5,4},{6,7},{7,6},{8,9},{9,8},{10,11... | collective-permute-start | bytes 3145736 | tf_op jit(solution)/shard_map/ppermute | solution.py:249
  9.3 15.2 %collective-permute-start.1 = (f32[64,2048]{1,0:T(8,128)S(1)}, f32[64,2048]{1,0:T(8,128)S(1)}, u32[]{:S(2)}, u32[]{:S(2)}) collective-permute-start(f32[64,2048]{1,0:T(8,128)S(1)} %slice.29), channel_id=1, source_target_pairs={{0,2},{1,3},{2,0},{3,1},{4,6},{5,7},{6,4},{7,5},{8,10},{9,11},{10,... | collective-permute-start | bytes 1572872 | tf_op jit(solution)/shard_map/ppermute | solution.py:249
  24.6 8.3 %collective-permute-start.2 = (f32[16,2048]{1,0:T(8,128)S(1)}, f32[16,2048]{1,0:T(8,128)S(1)}, u32[]{:S(2)}, u32[]{:S(2)}) collective-permute-start(f32[16,2048]{1,0:T(8,128)S(1)} %get-tuple-element.9), channel_id=1, source_target_pairs={{0,4},{1,5},{2,6},{3,7},{4,8},{5,9},{6,10},{7,11},{8,12},{9,13},{1... | collective-permute-start | bytes 393224 | tf_op jit(solution)/shard_map/ppermute | solution.py:249
  26.4 11.1 %collective-permute-start.3 = (f32[16,2048]{1,0:T(8,128)S(1)}, f32[16,2048]{1,0:T(8,128)S(1)}, u32[]{:S(2)}, u32[]{:S(2)}) collective-permute-start(f32[16,2048]{1,0:T(8,128)S(1)} %get-tuple-element.11), channel_id=1, source_target_pairs={{0,8},{1,9},{2,10},{3,11},{4,12},{5,13},{6,14},{7,15},{8,0},{9,1},... | collective-permute-start | bytes 393224 | tf_op jit(solution)/shard_map/ppermute | solution.py:249
  29.0 8.5 %collective-permute-start.4 = (f32[16,2048]{1,0:T(8,128)S(1)}, f32[16,2048]{1,0:T(8,128)S(1)}, u32[]{:S(2)}, u32[]{:S(2)}) collective-permute-start(f32[16,2048]{1,0:T(8,128)S(1)} %get-tuple-element.10), channel_id=1, source_target_pairs={{0,12},{1,13},{2,14},{3,15},{4,0},{5,1},{6,2},{7,3},{8,4},{9,5},{1... | collective-permute-start | bytes 393224 | tf_op jit(solution)/shard_map/ppermute | solution.py:249
  37.7 7.0 %collective-permute-start.5 = (bf16[16,2048]{1,0:T(8,128)(2,1)S(1)}, bf16[16,2048]{1,0:T(8,128)(2,1)S(1)}, u32[]{:S(2)}, u32[]{:S(2)}) collective-permute-start(bf16[16,2048]{1,0:T(8,128)(2,1)S(1)} %get-tuple-element.8.refs_0_), channel_id=1, source_target_pairs={{0,4},{1,5},{2,6},{3,7},{4,8},{5,9},{6,10},{7,11},{8,12},{9,13},{1... | collective-permute-start | bytes 196616 | tf_op jit(solution)/shard_map/ppermute | solution.py:249
  41.0 6.2 %collective-permute-start.6 = (bf16[16,2048]{1,0:T(8,128)(2,1)S(1)}, bf16[16,2048]{1,0:T(8,128)(2,1)S(1)}, u32[]{:S(2)}, u32[]{:S(2)}) collective-permute-start(bf16[16,2048]{1,0:T(8,128)(2,1)S(1)} %get-tuple-element.8.refs_0_), channel_id=1, source_target_pairs={{0,8},{1,9},{2,10},{3,11},{4,12},{5,13},{6,14},{7,15},{8,0},{9,1},... | collective-permute-start | bytes 196616 | tf_op jit(solution)/shard_map/ppermute | solution.py:249
  42.6 5.2 %collective-permute-start.7 = (bf16[16,2048]{1,0:T(8,128)(2,1)S(1)}, bf16[16,2048]{1,0:T(8,128)(2,1)S(1)}, u32[]{:S(2)}, u32[]{:S(2)}) collective-permute-start(bf16[16,2048]{1,0:T(8,128)(2,1)S(1)} %get-tuple-element.8.refs_0_), channel_id=1, source_target_pairs={{0,12},{1,13},{2,14},{3,15},{4,0},{5,1},{6,2},{7,3},{8,4},{9,5},{1... | collective-permute-start | bytes 196616 | tf_op jit(solution)/shard_map/ppermute | solution.py:249
  47.9 7.6 %collective-permute-start.8 = (bf16[64,2048]{1,0:T(8,128)(2,1)S(1)}, bf16[64,2048]{1,0:T(8,128)(2,1)S(1)}, u32[]{:S(2)}, u32[]{:S(2)}) collective-permute-start(bf16[64,2048]{1,0:T(8,128)(2,1)S(1)} %pad_maximum_fusion.refs_0_), channel_id=1, source_target_pairs={{0,2},{1,3},{2,0},{3,1},{4,6},{5,7},{6,4},{7,5},{8,10},{9,11},{10,... | collective-permute-start | bytes 786440 | tf_op jit(solution)/shard_map/ppermute | solution.py:249
  49.4 10.9 %collective-permute-start.9 = (bf16[64,2048]{1,0:T(8,128)(2,1)S(1)}, bf16[64,2048]{1,0:T(8,128)(2,1)S(1)}, u32[]{:S(2)}, u32[]{:S(2)}) collective-permute-start(bf16[64,2048]{1,0:T(8,128)(2,1)S(1)} %pad_maximum_fusion.refs_0_), channel_id=1, source_target_pairs={{0,1},{1,0},{2,3},{3,2},{4,5},{5,4},{6,7},{7,6},{8,9},{9,8},{10,11... | collective-permute-start | bytes 786440 | tf_op jit(solution)/shard_map/ppermute | solution.py:249
  55.4 4.9 %collective-permute-start.10 = (bf16[64,2048]{1,0:T(8,128)(2,1)S(1)}, bf16[64,2048]{1,0:T(8,128)(2,1)S(1)}, u32[]{:S(2)}, u32[]{:S(2)}) collective-permute-start(bf16[64,2048]{1,0:T(8,128)(2,1)S(1)} %collective-permute-done.8.refs_0_), channel_id=1, source_target_pairs={{0,1},{1,0},{2,3},{3,2},{4,5},{5,4},{6,7},{7,6},{8,9},{9,8},{10,11... | collective-permute-start | bytes 786440 | tf_op jit(solution)/shard_map/ppermute | solution.py:249
  55.5 4.8 %copy-start.3 = (s32[64,64]{1,0:T(8,128)S(1)}, s32[64,64]{1,0:T(8,128)}, u32[]{:S(2)}) copy-start(s32[64,64]{1,0:T(8,128)} %refs_4_.1) | copy-start | bytes 49156
  83.1 11.1 %all-to-all-start = ((f32[16,4,128]{2,1,0:T(4,128)}), f32[16,4,128]{2,1,0:T(4,128)S(1)}, u32[]{:S(2)}, u32[]{:S(2)}) async-start(f32[16,4,128]{2,1,0:T(4,128)} %grad.5), calls=%async_computation | async-start | bytes 65536 | tf_op jit(solution)/shard_map/all_to_all | solution.py:302
  94.2 0.7 copy-start.5

commit v2 on v1

v2 whole, which is shorter than its diff:
```python
import functools

import jax
import jax.numpy as jnp
from jax import lax
from jax.experimental import pallas as pl
from jax.experimental.pallas import tpu as pltpu
from jax.sharding import PartitionSpec as P

CHUNKS = 2
ROW_STEP = 16
LANES = 128
VMEM = pl.BlockSpec(memory_space=pltpu.VMEM)
HBM = pl.BlockSpec(memory_space=pltpu.HBM)


def factors(n):
    c = 2 if n % 2 == 0 else 1
    m = n // c
    y = 1
    while 4 * y * y <= m and m % (2 * y) == 0:
        y *= 2
    return m // y, y, c


def place(n, index):
    _, y, c = factors(n)
    return index // (y * c), (index // c) % y, index % c


def shift(n, dz, dy, dc):
    fz, fy, fc = factors(n)
    pairs = []
    for i in range(n):
        z, y, c = place(n, i)
        to = (((z + dz) % fz) * fy + (y + dy) % fy) * fc + (c + dc) % fc
        pairs.append((i, to))
    return pairs


def cost(flops, size):
    return pl.CostEstimate(flops=flops, bytes_accessed=size, transcendentals=0)


def params():
    return pltpu.CompilerParams(vmem_limit_bytes=24 * 1024 * 1024)


def column_copy(decoder_ref, buf, sem, slot, col, width):
    return pltpu.make_async_copy(
        decoder_ref.at[:, pl.ds(pl.multiple_of(col, width), width)], buf.at[slot], sem.at[slot]
    )


def decode_kernel(n, own, chunk, chunks, dc, first, *refs):
    if first:
        ids_hbm, codes_hbm, decoder_ref, targets_hbm = refs[:4]
        out_ref, buf, dense_ref, sem, ids_ref, codes_ref, targets_ref, small = refs[4:]
    else:
        dense_ref, decoder_ref, targets_ref, out_ref, buf, sem = refs
    fz, fy, fc = factors(n)
    me = lax.axis_index("lat")
    _, y, c = place(n, me)
    lat_dev = decoder_ref.shape[0]
    sub = buf.shape[2]
    cols = []
    for o in range(fy):
        block = ((c + dc) % fc) * fy + (y + o + 1) % fy
        cols.append((block * chunks + chunk) * sub)
    if first:
        pairs = ((ids_hbm, ids_ref), (codes_hbm, codes_ref), (targets_hbm, targets_ref))
        smalls = [pltpu.make_async_copy(a, b, small.at[i]) for i, (a, b) in enumerate(pairs)]
        for copy in smalls:
            copy.start()
    for o in range(fy):
        column_copy(decoder_ref, buf, sem, o, cols[o], sub).start()
    if first:
        for copy in smalls:
            copy.wait()
        rows, k_count = ids_ref.shape
        lanes = lax.broadcasted_iota(jnp.int32, (ROW_STEP, lat_dev), 1) + me * lat_dev

        def body(g, carry):
            at = pl.ds(pl.multiple_of(g * ROW_STEP, ROW_STEP), ROW_STEP)
            ids = ids_ref[at, :]
            codes = codes_ref[at, :].astype(jnp.float32)
            acc = jnp.zeros((ROW_STEP, lat_dev), jnp.float32)
            for k in range(k_count):
                acc = jnp.where(ids[:, k : k + 1] == lanes, codes[:, k : k + 1], acc)
            dense_ref[at, :] = acc.astype(jnp.bfloat16)
            return carry

        lax.fori_loop(0, rows // ROW_STEP, body, 0)
    rows = dense_ref.shape[0]
    row = lax.broadcasted_iota(jnp.int32, (rows, own), 0)
    want = lax.broadcasted_iota(jnp.int32, (rows, own), 1) + me * own
    mine = jnp.where(row == want, -1.0, 0.0).astype(jnp.bfloat16)
    for o in range(fy):
        column_copy(decoder_ref, buf, sem, o, cols[o], sub).wait()
        part = jnp.dot(dense_ref[...], buf[o], preferred_element_type=jnp.float32)
        tgt = targets_ref[:, pl.ds(pl.multiple_of(cols[o], sub), sub)]
        part += jnp.dot(mine, tgt, preferred_element_type=jnp.float32)
        out_ref[:, o * sub : (o + 1) * sub] = part


def decode(n, own, chunk, chunks, dc, sub, ids, codes, dense, decoder, targets):
    _, fy, _ = factors(n)
    lat_dev = decoder.shape[0]
    first = dense is None
    rows = ids.shape[0]
    out = [
        jax.ShapeDtypeStruct((rows, fy * sub), jnp.float32),
        jax.ShapeDtypeStruct((fy, lat_dev, sub), jnp.bfloat16),
    ]
    scratch = [pltpu.SemaphoreType.DMA((fy,))]
    if first:
        out.append(jax.ShapeDtypeStruct((rows, lat_dev), jnp.bfloat16))
        scratch += [pltpu.VMEM(x.shape, x.dtype) for x in (ids, codes, targets)]
        scratch.append(pltpu.SemaphoreType.DMA((3,)))
    got = pl.pallas_call(
        functools.partial(decode_kernel, n, own, chunk, chunks, dc, first),
        out_shape=out,
        in_specs=[HBM, HBM, HBM, HBM] if first else [VMEM, HBM, VMEM],
        out_specs=[VMEM] * len(out),
        scratch_shapes=scratch,
        compiler_params=params(),
        cost_estimate=cost(2 * rows * lat_dev * fy * sub, 4 * lat_dev * fy * sub),
        name="decode",
    )(*((ids, codes, decoder, targets) if first else (dense, decoder, targets)))
    return got[0], got[1], got[2] if first else dense


def grad_kernel(n, slots, final, with_prev, *refs):
    refs = list(refs)
    errs = [refs.pop(0) for _ in slots]
    bufs = [refs.pop(0) for _ in slots]
    prev_ref = refs.pop(0) if with_prev else None
    fz, fy, fc = factors(n)
    me = lax.axis_index("lat")
    z, _, _ = place(n, me)
    total = prev_ref[...] if with_prev else None
    for err, buf, slot in zip(errs, bufs, slots):
        part = lax.dot_general(
            err[...], buf[slot], (((1,), (1,)), ((), ())), preferred_element_type=jnp.float32
        )
        total = part if total is None else total + part
    if not final:
        refs[0][...] = total
        return
    ids_ref, loss_ref, out_ref, totals_ref = refs
    totals_ref[...] = total
    rows, k_count = ids_ref.shape
    lat_dev = total.shape[1]
    group = rows // fz
    steps = group // ROW_STEP
    places = lax.broadcasted_iota(jnp.int32, (ROW_STEP, LANES), 1)
    pad = jnp.zeros((ROW_STEP, LANES - k_count), jnp.int32)

    def body(g, carry):
        at = pl.ds(pl.multiple_of(g * ROW_STEP, ROW_STEP), ROW_STEP)
        ids = jnp.concatenate([ids_ref[at, :] - me * lat_dev, pad], axis=1)
        held = jnp.where(places < k_count, ids // LANES, -1)
        inside = ids % LANES
        loss = loss_ref[pl.ds(pl.multiple_of((g % steps) * ROW_STEP, ROW_STEP), ROW_STEP), :]
        acc = jnp.where((places == k_count) & (g // steps == z), loss, 0.0)
        for t in range(lat_dev // LANES):
            values = totals_ref[at, t * LANES : (t + 1) * LANES]
            found = jnp.take_along_axis(values, inside, axis=1, mode="promise_in_bounds")
            acc = jnp.where(held == t, found, acc)
        out_ref[at, :] = acc
        return carry

    lax.fori_loop(0, rows // ROW_STEP, body, 0)


def grad(n, errs, bufs, slots, prev, final=None):
    lat_dev = bufs[0].shape[1]
    rows, sub = errs[0].shape
    totals = jax.ShapeDtypeStruct((rows, lat_dev), jnp.float32)
    args = list(errs) + list(bufs)
    if prev is not None:
        args.append(prev)
    out, scratch = totals, []
    if final is not None:
        args += list(final)
        out = jax.ShapeDtypeStruct((rows, LANES), jnp.float32)
        scratch.append(pltpu.VMEM(totals.shape, totals.dtype))
    return pl.pallas_call(
        functools.partial(grad_kernel, n, tuple(slots), final is not None, prev is not None),
        out_shape=out,
        in_specs=[VMEM] * len(args),
        out_specs=VMEM,
        scratch_shapes=scratch,
        compiler_params=params(),
        cost_estimate=cost(2 * rows * lat_dev * sub * len(errs), 4 * lat_dev * sub * len(errs)),
        name="grad",
    )(*args)


def own_kernel(n, blocks, own, *refs):
    errs, out_ref = refs[:-1], refs[-1]
    fz, fy, fc = factors(n)
    _, y, c = place(n, lax.axis_index("lat"))
    group, sub = errs[0].shape
    row = lax.broadcasted_iota(jnp.int32, (own, group), 0) + (y * fc + c) * own
    want = lax.broadcasted_iota(jnp.int32, (own, group), 1)
    mine = jnp.where(row == want, 1.0, 0.0).astype(jnp.bfloat16)
    for err, (dc, dy, chunk, chunks) in zip(errs, blocks):
        block = ((c + dc) % fc) * fy + (y + fy - dy) % fy
        col = pl.multiple_of((block * chunks + chunk) * sub, sub)
        rows = jnp.dot(mine, err[...], preferred_element_type=jnp.float32)
        out_ref[:, pl.ds(col, sub)] = rows.astype(jnp.bfloat16)


def own_rows(n, blocks, own, width, errs):
    return pl.pallas_call(
        functools.partial(own_kernel, n, tuple(blocks), own),
        out_shape=jax.ShapeDtypeStruct((own, width), jnp.bfloat16),
        in_specs=[VMEM] * len(errs),
        out_specs=VMEM,
        compiler_params=params(),
        name="own_rows",
    )(*errs)


def local(codes, indices, decoder, targets):
    width = decoder.shape[1]
    rows, k_count = codes.shape
    n = lax.axis_size("lat")
    own = rows // n
    fz, fy, fc = factors(n)
    group = rows // fz
    chunks = CHUNKS
    sub = width // (fc * fy * chunks)
    z, _, _ = place(n, lax.axis_index("lat"))
    columns = [[at + i * fy * fc for i in range(fz)] for at in range(fy * fc)]

    def send(x, dy=0, dc=0):
        return lax.ppermute(x, "lat", shift(n, 0, dy, dc))

    def swap_z(x):
        return lax.all_to_all(x, "lat", 0, 0, axis_index_groups=columns, tiled=True)

    dense = None
    far, kept, bufs = {}, {}, {}
    for dc in list(range(1, fc)) + [0]:
        for p in range(chunks):
            part, bufs[dc, p], dense = decode(
                n, own, p, chunks, dc, sub, indices, codes, dense, decoder, targets
            )
            if dc:
                far[dc, p] = send(part, dc=dc)
            else:
                kept[p] = part

    diffs = []
    for p in range(chunks):
        summed = kept[p]
        for dc in range(1, fc):
            summed = summed + far[dc, p]
        mine = summed[:, (fy - 1) * sub :]
        got = [
            send(summed[:, o * sub : (o + 1) * sub], dy=o + 1) for o in range(fy - 1)
        ]
        for g in got:
            mine = mine + g
        diffs.append(jnp.sum(swap_z(mine).reshape(fz, group, sub), axis=0))

    loss = sum(jnp.sum(d * d, axis=1, keepdims=True) for d in diffs)

    near, near_at, other, other_at = [], [], [], []
    for p in range(chunks):
        err = diffs[p].astype(jnp.bfloat16)
        whole = swap_z(jnp.concatenate([err] * fz, axis=0))
        here = [whole] + [send(whole, dy=o) for o in range(1, fy)]
        for o, e in enumerate(here):
            near.append(e)
            near_at.append((0, o, p, chunks))
            for dc in range(1, fc):
                other.append(send(e, dc=dc))
                other_at.append((dc, o, p, chunks))

    def pieces(at):
        return [bufs[dc, p] for dc, _, p, _ in at], [(fy - 1 - dy) % fy for _, dy, _, _ in at]

    totals = None
    for e, at in zip(near, near_at):
        totals = grad(n, [e], *pieces([at]), totals)
    out = grad(n, other, *pieces(other_at), totals, (indices, loss))
    mine = [lax.dynamic_slice_in_dim(e, z * group, group, 0) for e in near + other]
    error = own_rows(n, near_at + other_at, own, width, mine)

    swapped = lax.all_to_all(out, "lat", 0, 0, tiled=True)
    back = jnp.sum(swapped.reshape(n, own, LANES), axis=0)
    return error, back[:, k_count] / width, back[:, :k_count]


def solution(mesh):
    in_specs = (P("groups", None), P("groups", None), P("lat", None), P(("groups", "lat"), None))
    out_specs = (P(("groups", "lat"), None), P(("groups", "lat")), P(("groups", "lat"), None))
    return jax.shard_map(local, mesh=mesh, in_specs=in_specs, out_specs=out_specs, check_vma=False)
```

time: 95.3 us -> 87.8 us (0.921)
  Pallas kernels: 34 us -> 11.1 us
  local copies, waits for them, and re-layouts: 2.49 us -> 11.4 us
  starting transfers between devices: 20.7 us -> 26.7 us
  waiting for transfers between devices: 35.9 us -> 32.9 us
  other arithmetic: 1.05 us -> 3.93 us
    ppermute x11 -> x10, waiting for transfers between devices: 30.1 us -> 5.59 us  [send(): return lax.ppermute(x, 'lat', shift(n, 0, dy, dc))]
    pallas_call x5 -> x9, Pallas kernels: 33.2 us -> 10.2 us  [the longest x4 6.08 us: decode(): pl.pallas_call(functools.partial(decode_kernel, n, own, chunk, chunks, dc...]
    all_to_all x0 -> x4, waiting for transfers between devices: none -> 21.6 us  [swap_z(): return lax.all_to_all(x, 'lat', 0, 0, axis_index_groups=columns, tiled=True)]
    all_to_all x0 -> x4, starting transfers between devices: none -> 15.5 us  [swap_z(): return lax.all_to_all(x, 'lat', 0, 0, axis_index_groups=columns, tiled=True)]
    ppermute x11 -> x10, starting transfers between devices: 16.3 us -> 7.32 us  [send(): return lax.ppermute(x, 'lat', shift(n, 0, dy, dc))]
    unnamed x12 -> x28, local copies, waits for them, and re-layouts: 2.32 us -> 11.2 us
    add x1 -> x2, other arithmetic: 0.06 us -> 1.48 us  [local(): mine = mine + g]
    concatenate x1 -> x2, other arithmetic: 0.02 us -> 1.33 us  [local(): whole = swap_z(jnp.concatenate([err] * fz, axis=0))]
  transfers between devices with their start and end apart: 12 -> 15, of which waited for: 8 -> 8; matrix products, arithmetic and copies ran while one was open for 0% -> 4% of each run, Pallas kernels for 9% -> 6%
where the time goes in v2:
time: 87.8 us; the launch traced here: 87 us
  waiting for transfers between devices  32.9 us (37%)
  starting transfers between devices  26.7 us (30%)
  local copies, waits for them, and re-layouts  11.4 us (13%)
  Pallas kernels  11.1 us (13%)
  other arithmetic  3.93 us (4%)
  between operations  0.91 us (1%)
    all_to_all x4, waiting for transfers between devices, swap_z(): return lax.all_to_all(x, 'lat', 0, 0, axis_index_groups=columns, tiled=True)  21.6 us
    all_to_all x4, starting transfers between devices, swap_z(): return lax.all_to_all(x, 'lat', 0, 0, axis_index_groups=columns, tiled=True)  15.5 us
    unnamed x28, local copies, waits for them, and re-layouts  11.2 us
    ppermute x10, starting transfers between devices, send(): return lax.ppermute(x, 'lat', shift(n, 0, dy, dc))  7.32 us
    pallas_call x4, Pallas kernels, decode(): pl.pallas_call(functools.partial(decode_kernel, n, own, chunk, chunks, dc...  6.08 us
    all_to_all x1, waiting for transfers between devices, local(): swapped = lax.all_to_all(out, 'lat', 0, 0, tiled=True)  5.74 us
    ppermute x10, waiting for transfers between devices, send(): return lax.ppermute(x, 'lat', shift(n, 0, dy, dc))  5.59 us
    pallas_call x5, Pallas kernels, grad(): pl.pallas_call(functools.partial(grad_kernel, n, tuple(slots), final is n...  4.16 us
  transfers between devices with their start and end apart: 15, of which 8 were waited for; matrix products, arithmetic and copies ran while one was open for 4% of the time, Pallas kernels for 6%

profile of v2, /device:TPU:0, one launch (start us, length us, event | category | flops | bytes accessed | tf_op | source)
XLA Modules:
  0.0 87.0 jit_solution(12290324785123616021)
XLA Ops:
  0.6 0.0 copy-start
  0.6 3.4 %copy-done = bf16[512,8192]{1,0:T(8,128)(2,1)S(1)} copy-done((bf16[512,8192]{1,0:T(8,128)(2,1)S(1)}, bf16[512,8192]{1,0:T(8,128)(2,1)}, u32[]{:S(2)}) %copy-start) | copy-done | bytes 8388632
  4.0 0.8 copy-done.8
  4.9 0.8 copy-done.10
  5.6 0.7 copy-done.12
  6.3 2.8 %decode.4 = (f32[64,2048]{1,0:T(8,128)S(1)}, bf16[2,512,1024]{2,1,0:T(8,128)(2,1)S(1)}, bf16[64,512]{1,0:T(8,128)(2,1)S(1)}) custom-call(s32[64,64]{1,0:T(8,128)S(1)} %copy-done.10, bf16[64,64]{1,0:T(8,128)(2,1)S(1)} %copy-done.12, bf16[512,8192]{1,0:T(8,128)(2,1)S(1)} %copy-done, bf16[4,8192]{1,0:T(4,128)(2,1)S(1)} %copy-done.8), custom_call_target="tpu_custom_call" | custom-call | flops 134217728 | bytes 4194304 | tf_op jit(solution)/shard_map/decode/pallas_call | solution.py:120
  9.1 0.0 copy-start.4
  9.1 1.3 %copy-done.4 = bf16[2,512,1024]{2,1,0:T(8,128)(2,1)} copy-done((bf16[2,512,1024]{2,1,0:T(8,128)(2,1)}, bf16[2,512,1024]{2,1,0:T(8,128)(2,1)S(1)}, u32[]{:S(2)}) %copy-start.4) | copy-done | bytes 2097176
  10.4 1.1 %decode.7 = (f32[64,2048]{1,0:T(8,128)S(1)}, bf16[2,512,1024]{2,1,0:T(8,128)(2,1)S(1)}) custom-call(bf16[64,512]{1,0:T(8,128)(2,1)S(1)} %get-tuple-element.12.refs_0_, bf16[512,8192]{1,0:T(8,128)(2,1)S(1)} %copy-done.1, bf16[4,8192]{1,0:T(4,128)(2,1)S(1)} %copy-done.9), custom_call_target="tpu_custom_call" | custom-call | flops 134217728 | bytes 4194304 | tf_op jit(solution)/shard_map/decode/pallas_call | solution.py:120
  11.6 0.0 copy-start.6
  11.6 0.5 collective-permute-start.3
  12.1 0.1 collective-permute-start
  12.2 1.1 %decode.6 = (f32[64,2048]{1,0:T(8,128)S(1)}, bf16[2,512,1024]{2,1,0:T(8,128)(2,1)S(1)}) custom-call(bf16[64,512]{1,0:T(8,128)(2,1)S(1)} %get-tuple-element.12.refs_0_, bf16[512,8192]{1,0:T(8,128)(2,1)S(1)} %copy-done.1, bf16[4,8192]{1,0:T(4,128)(2,1)S(1)} %copy-done.9), custom_call_target="tpu_custom_call" | custom-call | flops 134217728 | bytes 4194304 | tf_op jit(solution)/shard_map/decode/pallas_call | solution.py:120
  13.3 0.3 collective-permute-done.3
  13.6 0.1 add.31
  13.7 3.0 %collective-permute-start.4 = (f32[64,1024]{1,0:T(8,128)S(1)}, f32[64,1024]{1,0:T(8,128)S(1)}, u32[]{:S(2)}, u32[]{:S(2)}) collective-permute-start(f32[64,1024]{1,0:T(8,128)S(1)} %slice.27), channel_id=1, source_target_pairs={{0,2},{1,3},{2,0},{3,1},{4,6},{5,7},{6,4},{7,5},{8,10},{9,11},{10,... | collective-permute-start | bytes 786440 | tf_op jit(solution)/shard_map/ppermute | solution.py:239
  16.7 1.1 %decode.5 = (f32[64,2048]{1,0:T(8,128)S(1)}, bf16[2,512,1024]{2,1,0:T(8,128)(2,1)S(1)}) custom-call(bf16[64,512]{1,0:T(8,128)(2,1)S(1)} %get-tuple-element.12.refs_0_, bf16[512,8192]{1,0:T(8,128)(2,1)S(1)} %copy-done.1, bf16[4,8192]{1,0:T(4,128)(2,1)S(1)} %copy-done.9), custom_call_target="tpu_custom_call" | custom-call | flops 134217728 | bytes 4194304 | tf_op jit(solution)/shard_map/decode/pallas_call | solution.py:120
  17.8 1.3 %copy-done.2 = bf16[2,512,1024]{2,1,0:T(8,128)(2,1)} copy-done((bf16[2,512,1024]{2,1,0:T(8,128)(2,1)}, bf16[2,512,1024]{2,1,0:T(8,128)(2,1)S(1)}, u32[]{:S(2)}) %copy-start.2) | copy-done | bytes 2097176
  19.1 0.0 collective-permute-done
  19.1 0.1 add.28
  19.2 0.1 collective-permute-start.1
  19.3 4.4 %collective-permute-done.4 = f32[64,1024]{1,0:T(8,128)S(1)} collective-permute-done((f32[64,1024]{1,0:T(8,128)S(1)}, f32[64,1024]{1,0:T(8,128)S(1)}, u32[]{:S(2)}, u32[]{:S(2)}) %collective-permute-start.4) | collective-permute-done | bytes 262176 | tf_op jit(solution)/shard_map/ppermute | solution.py:239
  23.8 0.7 slice_add_fusion
  24.5 5.4 %all-to-all-start.2 = ((f32[4,16,1024]{2,1,0:T(8,128)}), f32[4,16,1024]{2,1,0:T(8,128)S(1)}, u32[]{:S(2)}, u32[]{:S(2)}) async-start(f32[4,16,1024]{2,1,0:T(8,128)} %bitcast.3), calls=%async_computation.2 | async-start | bytes 524288 | tf_op jit(solution)/shard_map/all_to_all | solution.py:242
  29.9 0.0 collective-permute-done.1
  29.9 0.8 slice_add_fusion.1
  30.6 6.3 %all-to-all-done.2 = f32[4,16,1024]{2,1,0:T(8,128)S(1)} async-done(((f32[4,16,1024]{2,1,0:T(8,128)}), f32[4,16,1024]{2,1,0:T(8,128)S(1)}, u32[]{:S(2)}, u32[]{:S(2)}) %all-to-all-start.2) | async-done | bytes 262176 | tf_op jit(solution)/shard_map/all_to_all | solution.py:242
  36.9 3.4 %all-to-all-start = ((f32[4,16,1024]{2,1,0:T(8,128)}), f32[4,16,1024]{2,1,0:T(8,128)S(1)}, u32[]{:S(2)}, u32[]{:S(2)}) async-start(f32[4,16,1024]{2,1,0:T(8,128)} %bitcast), calls=%async_computation | async-start | bytes 524288 | tf_op jit(solution)/shard_map/all_to_all | solution.py:242
  40.4 0.1 multiply_reduce_fusion
  40.5 0.7 pad_maximum_fusion.1
  41.2 5.9 %all-to-all-done = f32[4,16,1024]{2,1,0:T(8,128)S(1)} async-done(((f32[4,16,1024]{2,1,0:T(8,128)}), f32[4,16,1024]{2,1,0:T(8,128)S(1)}, u32[]{:S(2)}, u32[]{:S(2)}) %all-to-all-start) | async-done | bytes 262176 | tf_op jit(solution)/shard_map/all_to_all | solution.py:242
  47.1 3.4 %all-to-all-start.3 = ((bf16[4,16,1024]{2,1,0:T(8,128)(2,1)}), bf16[4,16,1024]{2,1,0:T(8,128)(2,1)S(1)}, u32[]{:S(2)}, u32[]{:S(2)}) async-start(bf16[4,16,1024]{2,1,0:T(8,128)(2,1)} %bitcast.4), calls=%async_computation.3 | async-start | bytes 262144 | tf_op jit(solution)/shard_map/all_to_all | solution.py:242
  50.5 0.1 multiply_reduce_fusion.1
  50.7 0.7 pad_maximum_fusion
  51.3 5.1 %all-to-all-done.3 = bf16[4,16,1024]{2,1,0:T(8,128)(2,1)S(1)} async-done(((bf16[4,16,1024]{2,1,0:T(8,128)(2,1)}), bf16[4,16,1024]{2,1,0:T(8,128)(2,1)S(1)}, u32[]{:S(2)}, u32[]{:S(2)}) %all-to-all-start.3) | async-done | bytes 131104 | tf_op jit(solution)/shard_map/all_to_all | solution.py:242
  56.4 3.3 %all-to-all-start.1 = ((bf16[4,16,1024]{2,1,0:T(8,128)(2,1)}), bf16[4,16,1024]{2,1,0:T(8,128)(2,1)S(1)}, u32[]{:S(2)}, u32[]{:S(2)}) async-start(bf16[4,16,1024]{2,1,0:T(8,128)(2,1)} %bitcast.1), calls=%async_computation.1 | async-start | bytes 262144 | tf_op jit(solution)/shard_map/all_to_all | solution.py:242
  59.8 0.1 copy.7.refs_10_
  59.9 1.5 %collective-permute-start.5 = (bf16[64,1024]{1,0:T(8,128)(2,1)S(1)}, bf16[64,1024]{1,0:T(8,128)(2,1)S(1)}, u32[]{:S(2)}, u32[]{:S(2)}) collective-permute-start(bf16[64,1024]{1,0:T(8,128)(2,1)S(1)} %bitcast.10), channel_id=1, source_target_pairs={{0,2},{1,3},{2,0},{3,1},{4,6},{5,7},{6,4},{7,5},{8,10},{9,11},{10,... | collective-permute-start | bytes 393224 | tf_op jit(solution)/shard_map/ppermute | solution.py:239
  61.4 0.0 collective-permute-start.8
  61.4 4.2 %all-to-all-done.1 = bf16[4,16,1024]{2,1,0:T(8,128)(2,1)S(1)} async-done(((bf16[4,16,1024]{2,1,0:T(8,128)(2,1)}), bf16[4,16,1024]{2,1,0:T(8,128)(2,1)S(1)}, u32[]{:S(2)}, u32[]{:S(2)}) %all-to-all-start.1) | async-done | bytes 131104 | tf_op jit(solution)/shard_map/all_to_all | solution.py:242
  65.7 1.5 %collective-permute-start.2 = (bf16[64,1024]{1,0:T(8,128)(2,1)S(1)}, bf16[64,1024]{1,0:T(8,128)(2,1)S(1)}, u32[]{:S(2)}, u32[]{:S(2)}) collective-permute-start(bf16[64,1024]{1,0:T(8,128)(2,1)S(1)} %bitcast.14), channel_id=1, source_target_pairs={{0,2},{1,3},{2,0},{3,1},{4,6},{5,7},{6,4},{7,5},{8,10},{9,11},{10,... | collective-permute-start | bytes 393224 | tf_op jit(solution)/shard_map/ppermute | solution.py:239
  67.2 0.0 collective-permute-start.6
  67.2 1.6 %copy-done.3 = bf16[2,512,1024]{2,1,0:T(8,128)(2,1)S(1)} copy-done((bf16[2,512,1024]{2,1,0:T(8,128)(2,1)S(1)}, bf16[2,512,1024]{2,1,0:T(8,128)(2,1)}, u32[]{:S(2)}) %copy-start.3) | copy-done | bytes 2097176
  68.8 0.4 grad.5.refs_2_
  69.2 0.0 collective-permute-done.5.refs_0_
  69.2 0.6 collective-permute-start.9
  69.8 0.8 collective-permute-done.2.refs_0_
  70.6 0.0 collective-permute-start.7
  70.6 0.0 collective-permute-done.8.refs_2_
  70.7 0.4 grad.6.refs_2_
  71.1 0.0 copy-start.11
  71.1 0.4 grad.7.refs_2_
  71.6 0.4 grad.8.refs_8_
  72.0 0.0 collective-permute-done.6.refs_0_
  72.0 0.0 collective-permute-done.9.refs_3_
  72.1 0.0 collective-permute-done.7.refs_1_
  72.1 0.6 copy-done.5
  72.7 0.6 copy-done.7
  73.3 2.4 %grad.9 = f32[64,128]{1,0:T(8,128)} custom-call(bf16[64,1024]{1,0:T(8,128)(2,1)S(1)} %collective-permute-done.6.refs_0_, bf16[64,1024]{1,0:T(8,128)(2,1)S(1)} %collective-permute-done.7.refs_1_, bf16[64,1024]{1,0:T(8,128)(2,1)S(1)} %collective-permute-done.8.refs_2_, bf16[64,1024]{1,0:T(8,128)(2,1)S(1)} %collective-permute-done.9.refs_3_, ...), custom_call_target="tpu_custom_call" | custom-call | flops 268435456 | bytes 8388608 | tf_op jit(solution)/shard_map/grad/pallas_call | solution.py:188
  75.7 3.9 %all-to-all-start.4 = ((f32[16,4,128]{2,1,0:T(4,128)}), f32[16,4,128]{2,1,0:T(4,128)S(1)}, u32[]{:S(2)}, u32[]{:S(2)}) async-start(f32[16,4,128]{2,1,0:T(4,128)} %bitcast.7), calls=%async_computation.4 | async-start | bytes 65536 | tf_op jit(solution)/shard_map/all_to_all | solution.py:293
  79.6 0.9 own_rows.1
  80.5 5.7 %all-to-all-done.4 = f32[16,4,128]{2,1,0:T(4,128)S(1)} async-done(((f32[16,4,128]{2,1,0:T(4,128)}), f32[16,4,128]{2,1,0:T(4,128)S(1)}, u32[]{:S(2)}, u32[]{:S(2)}) %all-to-all-start.4) | async-done | bytes 32800 | tf_op jit(solution)/shard_map/all_to_all | solution.py:293
  86.3 0.7 multiply_reduce_fusion.2
  87.0 0.0 copy-done.13
  (28 shorter events, 0.2 us)
Async XLA Ops:
  0.6 3.4 %copy-start = (bf16[512,8192]{1,0:T(8,128)(2,1)S(1)}, bf16[512,8192]{1,0:T(8,128)(2,1)}, u32[]{:S(2)}) copy-start(bf16[512,8192]{1,0:T(8,128)(2,1)} %refs_1_.7) | copy-start | bytes 25165828
  4.0 0.8 copy-start.8
  4.9 0.8 copy-start.10
  5.6 0.7 copy-start.12
  6.3 4.1 %copy-start.1 = (bf16[512,8192]{1,0:T(8,128)(2,1)S(1)}, bf16[512,8192]{1,0:T(8,128)(2,1)}, u32[]{:S(2)}) copy-start(bf16[512,8192]{1,0:T(8,128)(2,1)} %refs_1_.7) | copy-start | bytes 25165828
  6.3 4.1 %copy-start.9 = (bf16[4,8192]{1,0:T(4,128)(2,1)S(1)}, bf16[4,8192]{1,0:T(4,128)(2,1)}, u32[]{:S(2)}) copy-start(bf16[4,8192]{1,0:T(4,128)(2,1)} %refs_2_.7) | copy-start | bytes 196612
  9.1 1.3 %copy-start.4 = (bf16[2,512,1024]{2,1,0:T(8,128)(2,1)}, bf16[2,512,1024]{2,1,0:T(8,128)(2,1)S(1)}, u32[]{:S(2)}) copy-start(bf16[2,512,1024]{2,1,0:T(8,128)(2,1)S(1)} %get-tuple-element.17.refs_4_.refs_5_) | copy-start | bytes 6291460
  11.6 1.7 %copy-start.6 = (bf16[2,512,1024]{2,1,0:T(8,128)(2,1)}, bf16[2,512,1024]{2,1,0:T(8,128)(2,1)S(1)}, u32[]{:S(2)}) copy-start(bf16[2,512,1024]{2,1,0:T(8,128)(2,1)S(1)} %get-tuple-element.18.refs_6_.refs_7_) | copy-start | bytes 6291460
  11.6 2.1 %collective-permute-start.3 = (f32[64,2048]{1,0:T(8,128)S(1)}, f32[64,2048]{1,0:T(8,128)S(1)}, u32[]{:S(2)}, u32[]{:S(2)}) collective-permute-start(f32[64,2048]{1,0:T(8,128)S(1)} %get-tuple-element.16), channel_id=1, source_target_pairs={{0,1},{1,0},{2,3},{3,2},{4,5},{5,4},{6,7},{7,6},{8,9},{9,8},{10,11... | collective-permute-start | bytes 1572872 | tf_op jit(solution)/shard_map/ppermute | solution.py:239
  12.1 7.0 %collective-permute-start = (f32[64,2048]{1,0:T(8,128)S(1)}, f32[64,2048]{1,0:T(8,128)S(1)}, u32[]{:S(2)}, u32[]{:S(2)}) collective-permute-start(f32[64,2048]{1,0:T(8,128)S(1)} %get-tuple-element.14), channel_id=1, source_target_pairs={{0,1},{1,0},{2,3},{3,2},{4,5},{5,4},{6,7},{7,6},{8,9},{9,8},{10,11... | collective-permute-start | bytes 1572872 | tf_op jit(solution)/shard_map/ppermute | solution.py:239
  13.7 10.0 %collective-permute-start.4 = (f32[64,1024]{1,0:T(8,128)S(1)}, f32[64,1024]{1,0:T(8,128)S(1)}, u32[]{:S(2)}, u32[]{:S(2)}) collective-permute-start(f32[64,1024]{1,0:T(8,128)S(1)} %slice.27), channel_id=1, source_target_pairs={{0,2},{1,3},{2,0},{3,1},{4,6},{5,7},{6,4},{7,5},{8,10},{9,11},{10,... | collective-permute-start | bytes 786440 | tf_op jit(solution)/shard_map/ppermute | solution.py:239
  17.8 1.3 %copy-start.2 = (bf16[2,512,1024]{2,1,0:T(8,128)(2,1)}, bf16[2,512,1024]{2,1,0:T(8,128)(2,1)S(1)}, u32[]{:S(2)}) copy-start(bf16[2,512,1024]{2,1,0:T(8,128)(2,1)S(1)} %get-tuple-element.20.refs_1_) | copy-start | bytes 6291460
  19.2 10.7 %collective-permute-start.1 = (f32[64,1024]{1,0:T(8,128)S(1)}, f32[64,1024]{1,0:T(8,128)S(1)}, u32[]{:S(2)}, u32[]{:S(2)}) collective-permute-start(f32[64,1024]{1,0:T(8,128)S(1)} %slice.25), channel_id=1, source_target_pairs={{0,2},{1,3},{2,0},{3,1},{4,6},{5,7},{6,4},{7,5},{8,10},{9,11},{10,... | collective-permute-start | bytes 786440 | tf_op jit(solution)/shard_map/ppermute | solution.py:239
  24.5 12.4 %all-to-all-start.2 = ((f32[4,16,1024]{2,1,0:T(8,128)}), f32[4,16,1024]{2,1,0:T(8,128)S(1)}, u32[]{:S(2)}, u32[]{:S(2)}) async-start(f32[4,16,1024]{2,1,0:T(8,128)} %bitcast.3), calls=%async_computation.2 | async-start | bytes 524288 | tf_op jit(solution)/shard_map/all_to_all | solution.py:242
  36.9 10.2 %all-to-all-start = ((f32[4,16,1024]{2,1,0:T(8,128)}), f32[4,16,1024]{2,1,0:T(8,128)S(1)}, u32[]{:S(2)}, u32[]{:S(2)}) async-start(f32[4,16,1024]{2,1,0:T(8,128)} %bitcast), calls=%async_computation | async-start | bytes 524288 | tf_op jit(solution)/shard_map/all_to_all | solution.py:242
  47.1 9.4 %all-to-all-start.3 = ((bf16[4,16,1024]{2,1,0:T(8,128)(2,1)}), bf16[4,16,1024]{2,1,0:T(8,128)(2,1)S(1)}, u32[]{:S(2)}, u32[]{:S(2)}) async-start(bf16[4,16,1024]{2,1,0:T(8,128)(2,1)} %bitcast.4), calls=%async_computation.3 | async-start | bytes 262144 | tf_op jit(solution)/shard_map/all_to_all | solution.py:242
  56.4 9.2 %all-to-all-start.1 = ((bf16[4,16,1024]{2,1,0:T(8,128)(2,1)}), bf16[4,16,1024]{2,1,0:T(8,128)(2,1)S(1)}, u32[]{:S(2)}, u32[]{:S(2)}) async-start(bf16[4,16,1024]{2,1,0:T(8,128)(2,1)} %bitcast.1), calls=%async_computation.1 | async-start | bytes 262144 | tf_op jit(solution)/shard_map/all_to_all | solution.py:242
  59.9 9.4 %collective-permute-start.5 = (bf16[64,1024]{1,0:T(8,128)(2,1)S(1)}, bf16[64,1024]{1,0:T(8,128)(2,1)S(1)}, u32[]{:S(2)}, u32[]{:S(2)}) collective-permute-start(bf16[64,1024]{1,0:T(8,128)(2,1)S(1)} %bitcast.10), channel_id=1, source_target_pairs={{0,2},{1,3},{2,0},{3,1},{4,6},{5,7},{6,4},{7,5},{8,10},{9,11},{10,... | collective-permute-start | bytes 393224 | tf_op jit(solution)/shard_map/ppermute | solution.py:239
  61.4 9.2 %collective-permute-start.8 = (bf16[64,1024]{1,0:T(8,128)(2,1)S(1)}, bf16[64,1024]{1,0:T(8,128)(2,1)S(1)}, u32[]{:S(2)}, u32[]{:S(2)}) collective-permute-start(bf16[64,1024]{1,0:T(8,128)(2,1)S(1)} %bitcast.11), channel_id=1, source_target_pairs={{0,1},{1,0},{2,3},{3,2},{4,5},{5,4},{6,7},{7,6},{8,9},{9,8},{10,11... | collective-permute-start | bytes 393224 | tf_op jit(solution)/shard_map/ppermute | solution.py:239
  65.7 5.0 %collective-permute-start.2 = (bf16[64,1024]{1,0:T(8,128)(2,1)S(1)}, bf16[64,1024]{1,0:T(8,128)(2,1)S(1)}, u32[]{:S(2)}, u32[]{:S(2)}) collective-permute-start(bf16[64,1024]{1,0:T(8,128)(2,1)S(1)} %bitcast.14), channel_id=1, source_target_pairs={{0,2},{1,3},{2,0},{3,1},{4,6},{5,7},{6,4},{7,5},{8,10},{9,11},{10,... | collective-permute-start | bytes 393224 | tf_op jit(solution)/shard_map/ppermute | solution.py:239
  67.2 4.8 %collective-permute-start.6 = (bf16[64,1024]{1,0:T(8,128)(2,1)S(1)}, bf16[64,1024]{1,0:T(8,128)(2,1)S(1)}, u32[]{:S(2)}, u32[]{:S(2)}) collective-permute-start(bf16[64,1024]{1,0:T(8,128)(2,1)S(1)} %bitcast.15), channel_id=1, source_target_pairs={{0,1},{1,0},{2,3},{3,2},{4,5},{5,4},{6,7},{7,6},{8,9},{9,8},{10,11... | collective-permute-start | bytes 393224 | tf_op jit(solution)/shard_map/ppermute | solution.py:239
  67.2 1.6 %copy-start.3 = (bf16[2,512,1024]{2,1,0:T(8,128)(2,1)S(1)}, bf16[2,512,1024]{2,1,0:T(8,128)(2,1)}, u32[]{:S(2)}) copy-start(bf16[2,512,1024]{2,1,0:T(8,128)(2,1)} %copy-done.2) | copy-start | bytes 6291460
  69.2 2.8 %collective-permute-start.9 = (bf16[64,1024]{1,0:T(8,128)(2,1)S(1)}, bf16[64,1024]{1,0:T(8,128)(2,1)S(1)}, u32[]{:S(2)}, u32[]{:S(2)}) collective-permute-start(bf16[64,1024]{1,0:T(8,128)(2,1)S(1)} %collective-permute-done.5.refs_0_), channel_id=1, source_target_pairs={{0,1},{1,0},{2,3},{3,2},{4,5},{5,4},{6,7},{7,6},{8,9},{9,8},{10,11... | collective-permute-start | bytes 393224 | tf_op jit(solution)/shard_map/ppermute | solution.py:239
  70.6 1.4 %collective-permute-start.7 = (bf16[64,1024]{1,0:T(8,128)(2,1)S(1)}, bf16[64,1024]{1,0:T(8,128)(2,1)S(1)}, u32[]{:S(2)}, u32[]{:S(2)}) collective-permute-start(bf16[64,1024]{1,0:T(8,128)(2,1)S(1)} %collective-permute-done.2.refs_0_), channel_id=1, source_target_pairs={{0,1},{1,0},{2,3},{3,2},{4,5},{5,4},{6,7},{7,6},{8,9},{9,8},{10,11... | collective-permute-start | bytes 393224 | tf_op jit(solution)/shard_map/ppermute | solution.py:239
  71.1 1.6 %copy-start.5 = (bf16[2,512,1024]{2,1,0:T(8,128)(2,1)S(1)}, bf16[2,512,1024]{2,1,0:T(8,128)(2,1)}, u32[]{:S(2)}) copy-start(bf16[2,512,1024]{2,1,0:T(8,128)(2,1)} %copy-done.4) | copy-start | bytes 6291460
  71.1 2.2 %copy-start.7 = (bf16[2,512,1024]{2,1,0:T(8,128)(2,1)S(1)}, bf16[2,512,1024]{2,1,0:T(8,128)(2,1)}, u32[]{:S(2)}) copy-start(bf16[2,512,1024]{2,1,0:T(8,128)(2,1)} %copy-done.6) | copy-start | bytes 6291460
  71.1 2.2 %copy-start.11 = (s32[64,64]{1,0:T(8,128)S(1)}, s32[64,64]{1,0:T(8,128)}, u32[]{:S(2)}) copy-start(s32[64,64]{1,0:T(8,128)} %refs_9_.1) | copy-start | bytes 49156
  75.7 10.5 %all-to-all-start.4 = ((f32[16,4,128]{2,1,0:T(4,128)}), f32[16,4,128]{2,1,0:T(4,128)S(1)}, u32[]{:S(2)}, u32[]{:S(2)}) async-start(f32[16,4,128]{2,1,0:T(4,128)} %bitcast.7), calls=%async_computation.4 | async-start | bytes 65536 | tf_op jit(solution)/shard_map/all_to_all | solution.py:293
  86.3 0.7 copy-start.13

commit v3 on v2

--- a/solution.py
+++ b/solution.py
@@ -10,6 +10,7 @@
 CHUNKS = 2
 ROW_STEP = 16
 LANES = 128
+PIECE = 512
 VMEM = pl.BlockSpec(memory_space=pltpu.VMEM)
 HBM = pl.BlockSpec(memory_space=pltpu.HBM)
 
@@ -28,12 +29,16 @@
     return index // (y * c), (index // c) % y, index % c
 
 
+def partner(z, o, fz):
+    return z ^ o if fz & (fz - 1) == 0 else (o - z) % fz
+
+
 def shift(n, dz, dy, dc):
     fz, fy, fc = factors(n)
     pairs = []
     for i in range(n):
         z, y, c = place(n, i)
-        to = (((z + dz) % fz) * fy + (y + dy) % fy) * fc + (c + dc) % fc
+        to = (partner(z, dz, fz) * fy + (y + dy) % fy) * fc + (c + dc) % fc
         pairs.append((i, to))
     return pairs
 
@@ -46,9 +51,16 @@
     return pltpu.CompilerParams(vmem_limit_bytes=24 * 1024 * 1024)
 
 
-def column_copy(decoder_ref, buf, sem, slot, col, width):
+def in_hbm(x):
+    return pltpu.with_memory_space_constraint(x, pltpu.HBM)
+
+
+def column_copy(decoder_ref, buf, sem, slot, piece, col, width):
+    at = piece * width
     return pltpu.make_async_copy(
-        decoder_ref.at[:, pl.ds(pl.multiple_of(col, width), width)], buf.at[slot], sem.at[slot]
+        decoder_ref.at[:, pl.ds(pl.multiple_of(col + at, width), width)],
+        buf.at[slot, :, pl.ds(at, width)],
+        sem.at[slot, piece],
     )
 
 
@@ -72,8 +84,10 @@
         smalls = [pltpu.make_async_copy(a, b, small.at[i]) for i, (a, b) in enumerate(pairs)]
         for copy in smalls:
             copy.start()
+    width = min(sub, PIECE)
     for o in range(fy):
-        column_copy(decoder_ref, buf, sem, o, cols[o], sub).start()
+        for i in range(sub // width):
+            column_copy(decoder_ref, buf, sem, o, i, cols[o], width).start()
     if first:
         for copy in smalls:
             copy.wait()
@@ -96,11 +110,15 @@
     want = lax.broadcasted_iota(jnp.int32, (rows, own), 1) + me * own
     mine = jnp.where(row == want, -1.0, 0.0).astype(jnp.bfloat16)
     for o in range(fy):
-        column_copy(decoder_ref, buf, sem, o, cols[o], sub).wait()
-        part = jnp.dot(dense_ref[...], buf[o], preferred_element_type=jnp.float32)
-        tgt = targets_ref[:, pl.ds(pl.multiple_of(cols[o], sub), sub)]
-        part += jnp.dot(mine, tgt, preferred_element_type=jnp.float32)
-        out_ref[:, o * sub : (o + 1) * sub] = part
+        for i in range(sub // width):
+            column_copy(decoder_ref, buf, sem, o, i, cols[o], width).wait()
+            at = i * width
+            tgt = targets_ref[:, pl.ds(pl.multiple_of(cols[o] + at, width), width)]
+            part = jnp.dot(
+                dense_ref[...], buf[o, :, at : at + width], preferred_element_type=jnp.float32
+            )
+            part += jnp.dot(mine, tgt, preferred_element_type=jnp.float32)
+            out_ref[:, o * sub + at : o * sub + at + width] = part
 
 
 def decode(n, own, chunk, chunks, dc, sub, ids, codes, dense, decoder, targets):
@@ -109,14 +127,17 @@
     first = dense is None
     rows = ids.shape[0]
     out = [
-        jax.ShapeDtypeStruct((rows, fy * sub), jnp.float32),
-        jax.ShapeDtypeStruct((fy, lat_dev, sub), jnp.bfloat16),
+        pltpu.VMEM((rows, fy * sub), jnp.float32),
+        pltpu.VMEM((fy, lat_dev, sub), jnp.bfloat16),
     ]
-    scratch = [pltpu.SemaphoreType.DMA((fy,))]
-    if first:
-        out.append(jax.ShapeDtypeStruct((rows, lat_dev), jnp.bfloat16))
+    scratch = [pltpu.SemaphoreType.DMA((fy, sub // min(sub, PIECE)))]
+    if first:
+        out.append(pltpu.VMEM((rows, lat_dev), jnp.bfloat16))
         scratch += [pltpu.VMEM(x.shape, x.dtype) for x in (ids, codes, targets)]
         scratch.append(pltpu.SemaphoreType.DMA((3,)))
+    decoder = in_hbm(decoder)
+    if first:
+        ids, codes, targets = in_hbm(ids), in_hbm(codes), in_hbm(targets)
     got = pl.pallas_call(
         functools.partial(decode_kernel, n, own, chunk, chunks, dc, first),
         out_shape=out,
@@ -157,14 +178,16 @@
     pad = jnp.zeros((ROW_STEP, LANES - k_count), jnp.int32)
 
     def body(g, carry):
-        at = pl.ds(pl.multiple_of(g * ROW_STEP, ROW_STEP), ROW_STEP)
+        here = pl.ds(pl.multiple_of(g * ROW_STEP, ROW_STEP), ROW_STEP)
+        first = partner(z, g // steps, fz) * group + (g % steps) * ROW_STEP
+        at = pl.ds(pl.multiple_of(first, ROW_STEP), ROW_STEP)
         ids = jnp.concatenate([ids_ref[at, :] - me * lat_dev, pad], axis=1)
         held = jnp.where(places < k_count, ids // LANES, -1)
         inside = ids % LANES
         loss = loss_ref[pl.ds(pl.multiple_of((g % steps) * ROW_STEP, ROW_STEP), ROW_STEP), :]
-        acc = jnp.where((places == k_count) & (g // steps == z), loss, 0.0)
+        acc = jnp.where((places == k_count) & (g // steps == 0), loss, 0.0)
         for t in range(lat_dev // LANES):
-            values = totals_ref[at, t * LANES : (t + 1) * LANES]
+            values = totals_ref[here, t * LANES : (t + 1) * LANES]
             found = jnp.take_along_axis(values, inside, axis=1, mode="promise_in_bounds")
             acc = jnp.where(held == t, found, acc)
         out_ref[at, :] = acc
@@ -233,45 +256,45 @@
     chunks = CHUNKS
     sub = width // (fc * fy * chunks)
     z, _, _ = place(n, lax.axis_index("lat"))
-    columns = [[at + i * fy * fc for i in range(fz)] for at in range(fy * fc)]
-
-    def send(x, dy=0, dc=0):
-        return lax.ppermute(x, "lat", shift(n, 0, dy, dc))
-
-    def swap_z(x):
-        return lax.all_to_all(x, "lat", 0, 0, axis_index_groups=columns, tiled=True)
+    zs = [z] + [partner(z, o, fz) for o in range(1, fz)]
+
+    def send(x, dz=0, dy=0, dc=0):
+        return lax.ppermute(x, "lat", shift(n, dz, dy, dc))
+
+    def z_rows(x, o):
+        return lax.dynamic_slice_in_dim(x, zs[o] * group, group, 0)
 
     dense = None
-    far, kept, bufs = {}, {}, {}
-    for dc in list(range(1, fc)) + [0]:
-        for p in range(chunks):
-            part, bufs[dc, p], dense = decode(
+    bufs, summed = {}, []
+    for p in range(chunks):
+        parts = {}
+        for dc in list(range(1, fc)) + [0]:
+            parts[dc], bufs[dc, p], dense = decode(
                 n, own, p, chunks, dc, sub, indices, codes, dense, decoder, targets
             )
             if dc:
-                far[dc, p] = send(part, dc=dc)
-            else:
-                kept[p] = part
+                parts[dc] = send(parts[dc], dc=dc)
+        total = sum(parts[dc] for dc in range(1, fc)) + parts[0] if fc > 1 else parts[0]
+        mine = total[:, (fy - 1) * sub :]
+        go = [total[:, o * sub : (o + 1) * sub] for o in range(fy - 1)]
+        dense, go = lax.optimization_barrier((dense, go))
+        for o in range(fy - 1):
+            mine = mine + send(go[o], dy=o + 1)
+        summed.append(mine)
 
     diffs = []
-    for p in range(chunks):
-        summed = kept[p]
-        for dc in range(1, fc):
-            summed = summed + far[dc, p]
-        mine = summed[:, (fy - 1) * sub :]
-        got = [
-            send(summed[:, o * sub : (o + 1) * sub], dy=o + 1) for o in range(fy - 1)
-        ]
-        for g in got:
-            mine = mine + g
-        diffs.append(jnp.sum(swap_z(mine).reshape(fz, group, sub), axis=0))
+    for mine in summed:
+        diff = z_rows(mine, 0)
+        for o in range(1, fz):
+            diff = diff + send(z_rows(mine, o), dz=o)
+        diffs.append(diff)
 
     loss = sum(jnp.sum(d * d, axis=1, keepdims=True) for d in diffs)
 
     near, near_at, other, other_at = [], [], [], []
     for p in range(chunks):
         err = diffs[p].astype(jnp.bfloat16)
-        whole = swap_z(jnp.concatenate([err] * fz, axis=0))
+        whole = jnp.concatenate([err] + [send(err, dz=o) for o in range(1, fz)], axis=0)
         here = [whole] + [send(whole, dy=o) for o in range(1, fy)]
         for o, e in enumerate(here):
             near.append(e)
@@ -287,8 +310,7 @@
     for e, at in zip(near, near_at):
         totals = grad(n, [e], *pieces([at]), totals)
     out = grad(n, other, *pieces(other_at), totals, (indices, loss))
-    mine = [lax.dynamic_slice_in_dim(e, z * group, group, 0) for e in near + other]
-    error = own_rows(n, near_at + other_at, own, width, mine)
+    error = own_rows(n, near_at + other_at, own, width, [e[:group] for e in near + other])
 
     swapped = lax.all_to_all(out, "lat", 0, 0, tiled=True)
     back = jnp.sum(swapped.reshape(n, own, LANES), axis=0)

time: 87.8 us -> 71.5 us (0.81)
  waiting for transfers between devices: 32.9 us -> 16.4 us
  local copies, waits for them, and re-layouts: 11.4 us -> 6.43 us
  Pallas kernels: 11.1 us -> 15.1 us
  starting transfers between devices: 26.7 us -> 29.8 us
  other arithmetic: 3.93 us -> 2.64 us
    all_to_all x4 -> x0, waiting for transfers between devices: 21.6 us -> none  [swap_z(): return lax.all_to_all(x, 'lat', 0, 0, axis_index_groups=columns, tiled=True)]
    ppermute x10 -> x22, starting transfers between devices: 7.32 us -> 25.4 us  [send(): return lax.ppermute(x, 'lat', shift(n, dz, dy, dc))]
    all_to_all x4 -> x0, starting transfers between devices: 15.5 us -> none  [swap_z(): return lax.all_to_all(x, 'lat', 0, 0, axis_index_groups=columns, tiled=True)]
    unnamed x28 -> x18, local copies, waits for them, and re-layouts: 11.2 us -> 5.53 us
    ppermute x10 -> x22, waiting for transfers between devices: 5.59 us -> 10.7 us  [send(): return lax.ppermute(x, 'lat', shift(n, dz, dy, dc))]
    pallas_call x4, Pallas kernels: 6.08 us -> 10.1 us  [decode(): pl.pallas_call(functools.partial(decode_kernel, n, own, chunk, chunks, dc...]
    concatenate x2, other arithmetic: 1.33 us -> 0.02 us  [local(): jnp.concatenate([err] + [send(err, dz=o) for o in range(1, fz)], axis=0)]
  transfers between devices with their start and end apart: 15 -> 23, of which waited for: 8 -> 8; matrix products, arithmetic and copies ran while one was open for 4% -> 3% of each run, Pallas kernels for 6% -> 9%
where the time goes in v3:
time: 71.5 us; the launch traced here: 71.2 us
  starting transfers between devices  29.8 us (42%)
  waiting for transfers between devices  16.4 us (23%)
  Pallas kernels  15.1 us (21%)
  local copies, waits for them, and re-layouts  6.43 us (9%)
  other arithmetic  2.64 us (4%)
  between operations  0.89 us (1%)
    ppermute x22, starting transfers between devices, send(): return lax.ppermute(x, 'lat', shift(n, dz, dy, dc))  25.4 us
    ppermute x22, waiting for transfers between devices, send(): return lax.ppermute(x, 'lat', shift(n, dz, dy, dc))  10.7 us
    pallas_call x4, Pallas kernels, decode(): pl.pallas_call(functools.partial(decode_kernel, n, own, chunk, chunks, dc...  10.1 us
    all_to_all x1, waiting for transfers between devices, local(): swapped = lax.all_to_all(out, 'lat', 0, 0, tiled=True)  5.7 us
    unnamed x18, local copies, waits for them, and re-layouts  5.53 us
    all_to_all x1, starting transfers between devices, local(): swapped = lax.all_to_all(out, 'lat', 0, 0, tiled=True)  4.4 us
    pallas_call x5, Pallas kernels, grad(): pl.pallas_call(functools.partial(grad_kernel, n, tuple(slots), final is n...  4.15 us
    add x2, other arithmetic, local(): sum((parts[dc] for dc in range(1, fc))) + parts[0]  1.56 us
  transfers between devices with their start and end apart: 23, of which 8 were waited for; matrix products, arithmetic and copies ran while one was open for 3% of the time, Pallas kernels for 9%

profile of v3, /device:TPU:0, one launch (start us, length us, event | category | flops | bytes accessed | tf_op | source)
XLA Modules:
  0.0 71.2 jit_solution(8308894117862476211)
XLA Ops:
  0.6 4.0 %decode.4 = (f32[64,2048]{1,0:T(8,128)S(1)}, bf16[2,512,1024]{2,1,0:T(8,128)(2,1)S(1)}, bf16[64,512]{1,0:T(8,128)(2,1)S(1)}) custom-call(s32[64,64]{1,0:T(8,128)} %refs_9_.1, bf16[64,64]{1,0:T(8,128)(2,1)} %refs_1_.4, bf16[512,8192]{1,0:T(8,128)(2,1)} %refs_1_.7, bf16[4,8192]{1,0:T(4,128)(2,1)} %refs_2_.7), custom_call_target="tpu_custom_call" | custom-call | flops 134217728 | bytes 4194304 | tf_op jit(solution)/shard_map/decode/pallas_call | solution.py:141
  4.6 1.3 %copy-done.2 = bf16[2,512,1024]{2,1,0:T(8,128)(2,1)} copy-done((bf16[2,512,1024]{2,1,0:T(8,128)(2,1)}, bf16[2,512,1024]{2,1,0:T(8,128)(2,1)S(1)}, u32[]{:S(2)}) %copy-start.2) | copy-done | bytes 2097176
  6.0 0.4 collective-permute-start
  6.4 2.0 %decode.5 = (f32[64,2048]{1,0:T(8,128)S(1)}, bf16[2,512,1024]{2,1,0:T(8,128)(2,1)S(1)}) custom-call(bf16[64,512]{1,0:T(8,128)(2,1)S(1)} %get-tuple-element.19.refs_0_, bf16[512,8192]{1,0:T(8,128)(2,1)} %refs_1_.7, bf16[4,8192]{1,0:T(4,128)(2,1)S(1)} %copy-done.6), custom_call_target="tpu_custom_call" | custom-call | flops 134217728 | bytes 4194304 | tf_op jit(solution)/shard_map/decode/pallas_call | solution.py:141
  8.4 0.0 collective-permute-done
  8.4 0.1 add.52
  8.5 0.7 %slice.49 = f32[64,1024]{1,0:T(8,128)} slice(f32[64,2048]{1,0:T(8,128)S(1)} %add.52), slice={[0:64], [0:1024]} | slice | bytes 524288 | tf_op jit(solution)/shard_map/slice | solution.py:279
  9.2 2.0 %decode.6 = (f32[64,2048]{1,0:T(8,128)S(1)}, bf16[2,512,1024]{2,1,0:T(8,128)(2,1)S(1)}) custom-call(bf16[64,512]{1,0:T(8,128)(2,1)S(1)} %get-tuple-element.19.refs_0_, bf16[512,8192]{1,0:T(8,128)(2,1)} %refs_1_.7, bf16[4,8192]{1,0:T(4,128)(2,1)S(1)} %copy-done.6), custom_call_target="tpu_custom_call" | custom-call | flops 134217728 | bytes 4194304 | tf_op jit(solution)/shard_map/decode/pallas_call | solution.py:141
  11.3 1.3 %copy-done.4 = bf16[2,512,1024]{2,1,0:T(8,128)(2,1)} copy-done((bf16[2,512,1024]{2,1,0:T(8,128)(2,1)}, bf16[2,512,1024]{2,1,0:T(8,128)(2,1)S(1)}, u32[]{:S(2)}) %copy-start.4) | copy-done | bytes 2097176
  12.6 0.1 collective-permute-start.9
  12.7 2.9 %collective-permute-start.1 = (f32[64,1024]{1,0:T(8,128)}, f32[64,1024]{1,0:T(8,128)S(1)}, u32[]{:S(2)}, u32[]{:S(2)}) collective-permute-start(f32[64,1024]{1,0:T(8,128)} %slice.49), channel_id=1, source_target_pairs={{0,2},{1,3},{2,0},{3,1},{4,6},{5,7},{6,4},{7,5},{8,10},{9,11},{10,... | collective-permute-start | bytes 786440 | tf_op jit(solution)/shard_map/ppermute | solution.py:262
  15.6 2.0 %decode.7 = (f32[64,2048]{1,0:T(8,128)S(1)}, bf16[2,512,1024]{2,1,0:T(8,128)(2,1)S(1)}) custom-call(bf16[64,512]{1,0:T(8,128)(2,1)S(1)} %get-tuple-element.19.refs_0_, bf16[512,8192]{1,0:T(8,128)(2,1)} %refs_1_.7, bf16[4,8192]{1,0:T(4,128)(2,1)S(1)} %copy-done.6), custom_call_target="tpu_custom_call" | custom-call | flops 134217728 | bytes 4194304 | tf_op jit(solution)/shard_map/decode/pallas_call | solution.py:141
  17.6 0.0 collective-permute-done.9
  17.6 1.5 %add.61 = f32[64,2048]{1,0:T(8,128)S(1)} add(f32[64,2048]{1,0:T(8,128)} %collective-permute-done.9, f32[64,2048]{1,0:T(8,128)S(1)} %get-tuple-element.21) | non-fusion elementwise | flops 131072 | bytes 1572864 | tf_op jit(solution)/shard_map/add | solution.py:277
  19.2 0.1 collective-permute-start.10
  19.2 3.6 %collective-permute-done.1 = f32[64,1024]{1,0:T(8,128)S(1)} collective-permute-done((f32[64,1024]{1,0:T(8,128)}, f32[64,1024]{1,0:T(8,128)S(1)}, u32[]{:S(2)}, u32[]{:S(2)}) %collective-permute-start.1) | collective-permute-done | bytes 262176 | tf_op jit(solution)/shard_map/ppermute | solution.py:262
  22.9 2.2 %collective-permute-start.2 = (f32[16,1024]{1,0:T(8,128)S(1)}, f32[16,1024]{1,0:T(8,128)S(1)}, u32[]{:S(2)}, u32[]{:S(2)}) collective-permute-start(f32[16,1024]{1,0:T(8,128)S(1)} %get-tuple-element.34), channel_id=1, source_target_pairs={{0,4},{1,5},{2,6},{3,7},{4,0},{5,1},{6,2},{7,3},{8,12},{9,13},{10,... | collective-permute-start | bytes 196616 | tf_op jit(solution)/shard_map/ppermute | solution.py:262
  25.2 2.5 %collective-permute-start.4 = (f32[16,1024]{1,0:T(8,128)S(1)}, f32[16,1024]{1,0:T(8,128)S(1)}, u32[]{:S(2)}, u32[]{:S(2)}) collective-permute-start(f32[16,1024]{1,0:T(8,128)S(1)} %get-tuple-element.35), channel_id=1, source_target_pairs={{0,12},{1,13},{2,14},{3,15},{4,8},{5,9},{6,10},{7,11},{8,4},{9,5},... | collective-permute-start | bytes 196616 | tf_op jit(solution)/shard_map/ppermute | solution.py:262
  27.7 0.1 collective-permute-start.3
  27.8 0.1 collective-permute-done.10
  28.0 1.9 %collective-permute-start.11 = (f32[16,1024]{1,0:T(8,128)S(1)}, f32[16,1024]{1,0:T(8,128)S(1)}, u32[]{:S(2)}, u32[]{:S(2)}) collective-permute-start(f32[16,1024]{1,0:T(8,128)S(1)} %get-tuple-element.31), channel_id=1, source_target_pairs={{0,4},{1,5},{2,6},{3,7},{4,0},{5,1},{6,2},{7,3},{8,12},{9,13},{10,... | collective-permute-start | bytes 196616 | tf_op jit(solution)/shard_map/ppermute | solution.py:262
  29.9 2.5 %collective-permute-start.13 = (f32[16,1024]{1,0:T(8,128)S(1)}, f32[16,1024]{1,0:T(8,128)S(1)}, u32[]{:S(2)}, u32[]{:S(2)}) collective-permute-start(f32[16,1024]{1,0:T(8,128)S(1)} %get-tuple-element.32), channel_id=1, source_target_pairs={{0,12},{1,13},{2,14},{3,15},{4,8},{5,9},{6,10},{7,11},{8,4},{9,5},... | collective-permute-start | bytes 196616 | tf_op jit(solution)/shard_map/ppermute | solution.py:262
  32.4 0.0 collective-permute-done.2
  32.4 0.1 collective-permute-start.12
  32.5 0.0 collective-permute-done.4
  32.5 2.8 %collective-permute-done.3 = f32[16,1024]{1,0:T(8,128)S(1)} collective-permute-done((f32[16,1024]{1,0:T(8,128)S(1)}, f32[16,1024]{1,0:T(8,128)S(1)}, u32[]{:S(2)}, u32[]{:S(2)}) %collective-permute-start.3) | collective-permute-done | bytes 65568 | tf_op jit(solution)/shard_map/ppermute | solution.py:262
  35.3 0.1 multiply_reduce_fusion.1
  35.4 0.2 collective-permute-start.7
  35.6 0.4 collective-permute-start.6
  36.0 0.0 collective-permute-done.11
  36.0 3.9 %collective-permute-start.5 = (bf16[16,1024]{1,0:T(8,128)(2,1)S(1)}, bf16[16,1024]{1,0:T(8,128)(2,1)S(1)}, u32[]{:S(2)}, u32[]{:S(2)}) collective-permute-start(bf16[16,1024]{1,0:T(8,128)(2,1)S(1)} %get-tuple-element.30.refs_0_), channel_id=1, source_target_pairs={{0,4},{1,5},{2,6},{3,7},{4,0},{5,1},{6,2},{7,3},{8,12},{9,13},{10,... | collective-permute-start | bytes 98312 | tf_op jit(solution)/shard_map/ppermute | solution.py:262
  39.8 0.0 collective-permute-done.13
  39.8 0.7 collective-permute-done.12
  40.5 0.1 multiply_reduce_fusion
  40.6 2.6 %collective-permute-start.16 = (bf16[16,1024]{1,0:T(8,128)(2,1)S(1)}, bf16[16,1024]{1,0:T(8,128)(2,1)S(1)}, u32[]{:S(2)}, u32[]{:S(2)}) collective-permute-start(bf16[16,1024]{1,0:T(8,128)(2,1)S(1)} %get-tuple-element.28.refs_2_), channel_id=1, source_target_pairs={{0,12},{1,13},{2,14},{3,15},{4,8},{5,9},{6,10},{7,11},{8,4},{9,5},... | collective-permute-start | bytes 98312 | tf_op jit(solution)/shard_map/ppermute | solution.py:262
  43.2 0.0 collective-permute-start.15
  43.2 0.0 collective-permute-done.7
  43.2 1.9 %collective-permute-start.14 = (bf16[16,1024]{1,0:T(8,128)(2,1)S(1)}, bf16[16,1024]{1,0:T(8,128)(2,1)S(1)}, u32[]{:S(2)}, u32[]{:S(2)}) collective-permute-start(bf16[16,1024]{1,0:T(8,128)(2,1)S(1)} %get-tuple-element.28.refs_2_), channel_id=1, source_target_pairs={{0,4},{1,5},{2,6},{3,7},{4,0},{5,1},{6,2},{7,3},{8,12},{9,13},{10,... | collective-permute-start | bytes 98312 | tf_op jit(solution)/shard_map/ppermute | solution.py:262
  45.1 0.0 collective-permute-done.6
  45.1 0.0 collective-permute-done.5
  45.1 1.5 %collective-permute-start.8 = (bf16[64,1024]{1,0:T(8,128)(2,1)S(1)}, bf16[64,1024]{1,0:T(8,128)(2,1)S(1)}, u32[]{:S(2)}, u32[]{:S(2)}) collective-permute-start(bf16[64,1024]{1,0:T(8,128)(2,1)S(1)} %pad_maximum_fusion.refs_0_), channel_id=1, source_target_pairs={{0,2},{1,3},{2,0},{3,1},{4,6},{5,7},{6,4},{7,5},{8,10},{9,11},{10,... | collective-permute-start | bytes 393224 | tf_op jit(solution)/shard_map/ppermute | solution.py:262
  46.6 1.4 %collective-permute-done.15 = bf16[16,1024]{1,0:T(8,128)(2,1)S(1)} collective-permute-done((bf16[16,1024]{1,0:T(8,128)(2,1)S(1)}, bf16[16,1024]{1,0:T(8,128)(2,1)S(1)}, u32[]{:S(2)}, u32[]{:S(2)}) %collective-permute-start.15) | collective-permute-done | bytes 32800 | tf_op jit(solution)/shard_map/ppermute | solution.py:262
  48.0 0.0 collective-permute-done.14
  48.1 1.5 %collective-permute-start.17 = (bf16[64,1024]{1,0:T(8,128)(2,1)S(1)}, bf16[64,1024]{1,0:T(8,128)(2,1)S(1)}, u32[]{:S(2)}, u32[]{:S(2)}) collective-permute-start(bf16[64,1024]{1,0:T(8,128)(2,1)S(1)} %pad_maximum_fusion.1.refs_0_), channel_id=1, source_target_pairs={{0,2},{1,3},{2,0},{3,1},{4,6},{5,7},{6,4},{7,5},{8,10},{9,11},{10,... | collective-permute-start | bytes 393224 | tf_op jit(solution)/shard_map/ppermute | solution.py:262
  49.6 0.4 grad.5.refs_2_
  50.0 0.3 collective-permute-done.8.refs_0_
  50.3 0.3 collective-permute-start.19
  50.6 0.4 grad.6.refs_2_
  51.0 0.2 collective-permute-start.20
  51.3 1.8 %collective-permute-done.17.refs_0_ = bf16[64,1024]{1,0:T(8,128)(2,1)S(1)} collective-permute-done((bf16[64,1024]{1,0:T(8,128)(2,1)S(1)}, bf16[64,1024]{1,0:T(8,128)(2,1)S(1)}, u32[]{:S(2)}, u32[]{:S(2)}) %collective-permute-start.17) | collective-permute-done | bytes 131104 | tf_op jit(solution)/shard_map/ppermute | solution.py:262
  53.1 0.1 copy.7.refs_10_
  53.2 1.6 %copy-done.1 = bf16[2,512,1024]{2,1,0:T(8,128)(2,1)S(1)} copy-done((bf16[2,512,1024]{2,1,0:T(8,128)(2,1)S(1)}, bf16[2,512,1024]{2,1,0:T(8,128)(2,1)}, u32[]{:S(2)}) %copy-start.1) | copy-done | bytes 2097176
  54.8 0.4 grad.7.refs_2_
  55.2 0.4 grad.8.refs_8_
  55.7 0.0 collective-permute-done.18.refs_0_
  55.7 0.0 collective-permute-done.20.refs_2_
  55.7 0.0 collective-permute-done.21.refs_3_
  55.7 0.7 copy-done.3
  56.4 0.6 copy-done.5
  57.0 2.4 %grad.9 = f32[64,128]{1,0:T(8,128)} custom-call(bf16[64,1024]{1,0:T(8,128)(2,1)S(1)} %collective-permute-done.18.refs_0_, bf16[64,1024]{1,0:T(8,128)(2,1)S(1)} %collective-permute-done.19.refs_1_, bf16[64,1024]{1,0:T(8,128)(2,1)S(1)} %collective-permute-done.20.refs_2_, bf16[64,1024]{1,0:T(8,128)(2,1)S(1)} %collective-permute-done.21.refs_3_, ...), custom_call_target="tpu_custom_call" | custom-call | flops 268435456 | bytes 8388608 | tf_op jit(solution)/shard_map/grad/pallas_call | solution.py:211
  59.4 4.4 %all-to-all-start = ((f32[16,4,128]{2,1,0:T(4,128)}), f32[16,4,128]{2,1,0:T(4,128)S(1)}, u32[]{:S(2)}, u32[]{:S(2)}) async-start(f32[16,4,128]{2,1,0:T(4,128)} %bitcast.1), calls=%async_computation | async-start | bytes 65536 | tf_op jit(solution)/shard_map/all_to_all | solution.py:315
  63.9 0.9 %own_rows.1 = bf16[4,8192]{1,0:T(4,128)(2,1)} custom-call(bf16[16,1024]{1,0:T(8,128)(2,1)S(1)} %get-tuple-element.30.refs_0_, bf16[16,1024]{1,0:T(8,128)(2,1)S(1)} %slice.50.refs_1_, bf16[16,1024]{1,0:T(8,128)(2,1)S(1)} %get-tuple-element.28.refs_2_, bf16[16,1024]{1,0:T(8,128)(2,1)S(1)} %slice.53.refs_3_, bf16[16,1024]{1,0:T(8,128)(2,1)S(1)} %slice.54.refs_4_, ...), custom_call_target="tpu_custom_call" | custom-call | tf_op jit(solution)/shard_map/own_rows/pallas_call | solution.py:239
  64.7 5.7 %all-to-all-done = f32[16,4,128]{2,1,0:T(4,128)S(1)} async-done(((f32[16,4,128]{2,1,0:T(4,128)}), f32[16,4,128]{2,1,0:T(4,128)S(1)}, u32[]{:S(2)}, u32[]{:S(2)}) %all-to-all-start) | async-done | bytes 32800 | tf_op jit(solution)/shard_map/all_to_all | solution.py:315
  70.5 0.7 multiply_reduce_fusion.2
  (32 shorter events, 0.2 us)
Async XLA Ops:
  0.6 5.7 %copy-start.6 = (bf16[4,8192]{1,0:T(4,128)(2,1)S(1)}, bf16[4,8192]{1,0:T(4,128)(2,1)}, u32[]{:S(2)}) copy-start(bf16[4,8192]{1,0:T(4,128)(2,1)} %refs_2_.7) | copy-start | bytes 196612
  4.6 1.3 %copy-start.2 = (bf16[2,512,1024]{2,1,0:T(8,128)(2,1)}, bf16[2,512,1024]{2,1,0:T(8,128)(2,1)S(1)}, u32[]{:S(2)}) copy-start(bf16[2,512,1024]{2,1,0:T(8,128)(2,1)S(1)} %get-tuple-element.23.refs_4_.refs_5_) | copy-start | bytes 6291460
  6.0 2.5 %collective-permute-start = (f32[64,2048]{1,0:T(8,128)S(1)}, f32[64,2048]{1,0:T(8,128)S(1)}, u32[]{:S(2)}, u32[]{:S(2)}) collective-permute-start(f32[64,2048]{1,0:T(8,128)S(1)} %get-tuple-element.15), channel_id=1, source_target_pairs={{0,1},{1,0},{2,3},{3,2},{4,5},{5,4},{6,7},{7,6},{8,9},{9,8},{10,11... | collective-permute-start | bytes 1572872 | tf_op jit(solution)/shard_map/ppermute | solution.py:262
  11.3 1.3 %copy-start.4 = (bf16[2,512,1024]{2,1,0:T(8,128)(2,1)}, bf16[2,512,1024]{2,1,0:T(8,128)(2,1)S(1)}, u32[]{:S(2)}) copy-start(bf16[2,512,1024]{2,1,0:T(8,128)(2,1)S(1)} %get-tuple-element.24.refs_6_.refs_7_) | copy-start | bytes 6291460
  12.6 5.0 %collective-permute-start.9 = (f32[64,2048]{1,0:T(8,128)S(1)}, f32[64,2048]{1,0:T(8,128)}, u32[]{:S(2)}, u32[]{:S(2)}) collective-permute-start(f32[64,2048]{1,0:T(8,128)S(1)} %get-tuple-element.20), channel_id=1, source_target_pairs={{0,1},{1,0},{2,3},{3,2},{4,5},{5,4},{6,7},{7,6},{8,9},{9,8},{10,11... | collective-permute-start | bytes 1572872 | tf_op jit(solution)/shard_map/ppermute | solution.py:262
  12.7 10.2 %collective-permute-start.1 = (f32[64,1024]{1,0:T(8,128)}, f32[64,1024]{1,0:T(8,128)S(1)}, u32[]{:S(2)}, u32[]{:S(2)}) collective-permute-start(f32[64,1024]{1,0:T(8,128)} %slice.49), channel_id=1, source_target_pairs={{0,2},{1,3},{2,0},{3,1},{4,6},{5,7},{6,4},{7,5},{8,10},{9,11},{10,... | collective-permute-start | bytes 786440 | tf_op jit(solution)/shard_map/ppermute | solution.py:262
  17.6 10.3 %copy-start = (bf16[2,512,1024]{2,1,0:T(8,128)(2,1)}, bf16[2,512,1024]{2,1,0:T(8,128)(2,1)S(1)}, u32[]{:S(2)}) copy-start(bf16[2,512,1024]{2,1,0:T(8,128)(2,1)S(1)} %get-tuple-element.25.refs_1_) | copy-start | bytes 6291460
  19.2 8.7 %collective-permute-start.10 = (f32[64,1024]{1,0:T(8,128)S(1)}, f32[64,1024]{1,0:T(8,128)S(1)}, u32[]{:S(2)}, u32[]{:S(2)}) collective-permute-start(f32[64,1024]{1,0:T(8,128)S(1)} %slice.52), channel_id=1, source_target_pairs={{0,2},{1,3},{2,0},{3,1},{4,6},{5,7},{6,4},{7,5},{8,10},{9,11},{10,... | collective-permute-start | bytes 786440 | tf_op jit(solution)/shard_map/ppermute | solution.py:262
  22.9 9.4 %collective-permute-start.2 = (f32[16,1024]{1,0:T(8,128)S(1)}, f32[16,1024]{1,0:T(8,128)S(1)}, u32[]{:S(2)}, u32[]{:S(2)}) collective-permute-start(f32[16,1024]{1,0:T(8,128)S(1)} %get-tuple-element.34), channel_id=1, source_target_pairs={{0,4},{1,5},{2,6},{3,7},{4,0},{5,1},{6,2},{7,3},{8,12},{9,13},{10,... | collective-permute-start | bytes 196616 | tf_op jit(solution)/shard_map/ppermute | solution.py:262
  25.2 7.3 %collective-permute-start.4 = (f32[16,1024]{1,0:T(8,128)S(1)}, f32[16,1024]{1,0:T(8,128)S(1)}, u32[]{:S(2)}, u32[]{:S(2)}) collective-permute-start(f32[16,1024]{1,0:T(8,128)S(1)} %get-tuple-element.35), channel_id=1, source_target_pairs={{0,12},{1,13},{2,14},{3,15},{4,8},{5,9},{6,10},{7,11},{8,4},{9,5},... | collective-permute-start | bytes 196616 | tf_op jit(solution)/shard_map/ppermute | solution.py:262
  27.7 7.6 %collective-permute-start.3 = (f32[16,1024]{1,0:T(8,128)S(1)}, f32[16,1024]{1,0:T(8,128)S(1)}, u32[]{:S(2)}, u32[]{:S(2)}) collective-permute-start(f32[16,1024]{1,0:T(8,128)S(1)} %get-tuple-element.36), channel_id=1, source_target_pairs={{0,8},{1,9},{2,10},{3,11},{4,12},{5,13},{6,14},{7,15},{8,0},{9,1},... | collective-permute-start | bytes 196616 | tf_op jit(solution)/shard_map/ppermute | solution.py:262
  28.0 8.0 %collective-permute-start.11 = (f32[16,1024]{1,0:T(8,128)S(1)}, f32[16,1024]{1,0:T(8,128)S(1)}, u32[]{:S(2)}, u32[]{:S(2)}) collective-permute-start(f32[16,1024]{1,0:T(8,128)S(1)} %get-tuple-element.31), channel_id=1, source_target_pairs={{0,4},{1,5},{2,6},{3,7},{4,0},{5,1},{6,2},{7,3},{8,12},{9,13},{10,... | collective-permute-start | bytes 196616 | tf_op jit(solution)/shard_map/ppermute | solution.py:262
  29.9 10.0 %collective-permute-start.13 = (f32[16,1024]{1,0:T(8,128)S(1)}, f32[16,1024]{1,0:T(8,128)S(1)}, u32[]{:S(2)}, u32[]{:S(2)}) collective-permute-start(f32[16,1024]{1,0:T(8,128)S(1)} %get-tuple-element.32), channel_id=1, source_target_pairs={{0,12},{1,13},{2,14},{3,15},{4,8},{5,9},{6,10},{7,11},{8,4},{9,5},... | collective-permute-start | bytes 196616 | tf_op jit(solution)/shard_map/ppermute | solution.py:262
  32.4 8.1 %collective-permute-start.12 = (f32[16,1024]{1,0:T(8,128)S(1)}, f32[16,1024]{1,0:T(8,128)S(1)}, u32[]{:S(2)}, u32[]{:S(2)}) collective-permute-start(f32[16,1024]{1,0:T(8,128)S(1)} %get-tuple-element.33), channel_id=1, source_target_pairs={{0,8},{1,9},{2,10},{3,11},{4,12},{5,13},{6,14},{7,15},{8,0},{9,1},... | collective-permute-start | bytes 196616 | tf_op jit(solution)/shard_map/ppermute | solution.py:262
  35.4 7.8 %collective-permute-start.7 = (bf16[16,1024]{1,0:T(8,128)(2,1)S(1)}, bf16[16,1024]{1,0:T(8,128)(2,1)S(1)}, u32[]{:S(2)}, u32[]{:S(2)}) collective-permute-start(bf16[16,1024]{1,0:T(8,128)(2,1)S(1)} %get-tuple-element.30.refs_0_), channel_id=1, source_target_pairs={{0,12},{1,13},{2,14},{3,15},{4,8},{5,9},{6,10},{7,11},{8,4},{9,5},... | collective-permute-start | bytes 98312 | tf_op jit(solution)/shard_map/ppermute | solution.py:262
  35.6 9.5 %collective-permute-start.6 = (bf16[16,1024]{1,0:T(8,128)(2,1)S(1)}, bf16[16,1024]{1,0:T(8,128)(2,1)S(1)}, u32[]{:S(2)}, u32[]{:S(2)}) collective-permute-start(bf16[16,1024]{1,0:T(8,128)(2,1)S(1)} %get-tuple-element.30.refs_0_), channel_id=1, source_target_pairs={{0,8},{1,9},{2,10},{3,11},{4,12},{5,13},{6,14},{7,15},{8,0},{9,1},... | collective-permute-start | bytes 98312 | tf_op jit(solution)/shard_map/ppermute | solution.py:262
  36.0 9.1 %collective-permute-start.5 = (bf16[16,1024]{1,0:T(8,128)(2,1)S(1)}, bf16[16,1024]{1,0:T(8,128)(2,1)S(1)}, u32[]{:S(2)}, u32[]{:S(2)}) collective-permute-start(bf16[16,1024]{1,0:T(8,128)(2,1)S(1)} %get-tuple-element.30.refs_0_), channel_id=1, source_target_pairs={{0,4},{1,5},{2,6},{3,7},{4,0},{5,1},{6,2},{7,3},{8,12},{9,13},{10,... | collective-permute-start | bytes 98312 | tf_op jit(solution)/shard_map/ppermute | solution.py:262
  40.6 6.0 %collective-permute-start.16 = (bf16[16,1024]{1,0:T(8,128)(2,1)S(1)}, bf16[16,1024]{1,0:T(8,128)(2,1)S(1)}, u32[]{:S(2)}, u32[]{:S(2)}) collective-permute-start(bf16[16,1024]{1,0:T(8,128)(2,1)S(1)} %get-tuple-element.28.refs_2_), channel_id=1, source_target_pairs={{0,12},{1,13},{2,14},{3,15},{4,8},{5,9},{6,10},{7,11},{8,4},{9,5},... | collective-permute-start | bytes 98312 | tf_op jit(solution)/shard_map/ppermute | solution.py:262
  43.2 4.8 %collective-permute-start.15 = (bf16[16,1024]{1,0:T(8,128)(2,1)S(1)}, bf16[16,1024]{1,0:T(8,128)(2,1)S(1)}, u32[]{:S(2)}, u32[]{:S(2)}) collective-permute-start(bf16[16,1024]{1,0:T(8,128)(2,1)S(1)} %get-tuple-element.28.refs_2_), channel_id=1, source_target_pairs={{0,8},{1,9},{2,10},{3,11},{4,12},{5,13},{6,14},{7,15},{8,0},{9,1},... | collective-permute-start | bytes 98312 | tf_op jit(solution)/shard_map/ppermute | solution.py:262
  43.2 4.8 %collective-permute-start.14 = (bf16[16,1024]{1,0:T(8,128)(2,1)S(1)}, bf16[16,1024]{1,0:T(8,128)(2,1)S(1)}, u32[]{:S(2)}, u32[]{:S(2)}) collective-permute-start(bf16[16,1024]{1,0:T(8,128)(2,1)S(1)} %get-tuple-element.28.refs_2_), channel_id=1, source_target_pairs={{0,4},{1,5},{2,6},{3,7},{4,0},{5,1},{6,2},{7,3},{8,12},{9,13},{10,... | collective-permute-start | bytes 98312 | tf_op jit(solution)/shard_map/ppermute | solution.py:262
  45.1 5.2 %collective-permute-start.8 = (bf16[64,1024]{1,0:T(8,128)(2,1)S(1)}, bf16[64,1024]{1,0:T(8,128)(2,1)S(1)}, u32[]{:S(2)}, u32[]{:S(2)}) collective-permute-start(bf16[64,1024]{1,0:T(8,128)(2,1)S(1)} %pad_maximum_fusion.refs_0_), channel_id=1, source_target_pairs={{0,2},{1,3},{2,0},{3,1},{4,6},{5,7},{6,4},{7,5},{8,10},{9,11},{10,... | collective-permute-start | bytes 393224 | tf_op jit(solution)/shard_map/ppermute | solution.py:262
  48.1 5.0 %collective-permute-start.17 = (bf16[64,1024]{1,0:T(8,128)(2,1)S(1)}, bf16[64,1024]{1,0:T(8,128)(2,1)S(1)}, u32[]{:S(2)}, u32[]{:S(2)}) collective-permute-start(bf16[64,1024]{1,0:T(8,128)(2,1)S(1)} %pad_maximum_fusion.1.refs_0_), channel_id=1, source_target_pairs={{0,2},{1,3},{2,0},{3,1},{4,6},{5,7},{6,4},{7,5},{8,10},{9,11},{10,... | collective-permute-start | bytes 393224 | tf_op jit(solution)/shard_map/ppermute | solution.py:262
  49.6 6.1 %collective-permute-start.18 = (bf16[64,1024]{1,0:T(8,128)(2,1)S(1)}, bf16[64,1024]{1,0:T(8,128)(2,1)S(1)}, u32[]{:S(2)}, u32[]{:S(2)}) collective-permute-start(bf16[64,1024]{1,0:T(8,128)(2,1)S(1)} %pad_maximum_fusion.refs_0_), channel_id=1, source_target_pairs={{0,1},{1,0},{2,3},{3,2},{4,5},{5,4},{6,7},{7,6},{8,9},{9,8},{10,11... | collective-permute-start | bytes 393224 | tf_op jit(solution)/shard_map/ppermute | solution.py:262
  50.3 5.4 %collective-permute-start.19 = (bf16[64,1024]{1,0:T(8,128)(2,1)S(1)}, bf16[64,1024]{1,0:T(8,128)(2,1)S(1)}, u32[]{:S(2)}, u32[]{:S(2)}) collective-permute-start(bf16[64,1024]{1,0:T(8,128)(2,1)S(1)} %collective-permute-done.8.refs_0_), channel_id=1, source_target_pairs={{0,1},{1,0},{2,3},{3,2},{4,5},{5,4},{6,7},{7,6},{8,9},{9,8},{10,11... | collective-permute-start | bytes 393224 | tf_op jit(solution)/shard_map/ppermute | solution.py:262
  51.0 4.7 %collective-permute-start.20 = (bf16[64,1024]{1,0:T(8,128)(2,1)S(1)}, bf16[64,1024]{1,0:T(8,128)(2,1)S(1)}, u32[]{:S(2)}, u32[]{:S(2)}) collective-permute-start(bf16[64,1024]{1,0:T(8,128)(2,1)S(1)} %pad_maximum_fusion.1.refs_0_), channel_id=1, source_target_pairs={{0,1},{1,0},{2,3},{3,2},{4,5},{5,4},{6,7},{7,6},{8,9},{9,8},{10,11... | collective-permute-start | bytes 393224 | tf_op jit(solution)/shard_map/ppermute | solution.py:262
  53.1 2.6 %collective-permute-start.21 = (bf16[64,1024]{1,0:T(8,128)(2,1)S(1)}, bf16[64,1024]{1,0:T(8,128)(2,1)S(1)}, u32[]{:S(2)}, u32[]{:S(2)}) collective-permute-start(bf16[64,1024]{1,0:T(8,128)(2,1)S(1)} %collective-permute-done.17.refs_0_), channel_id=1, source_target_pairs={{0,1},{1,0},{2,3},{3,2},{4,5},{5,4},{6,7},{7,6},{8,9},{9,8},{10,11... | collective-permute-start | bytes 393224 | tf_op jit(solution)/shard_map/ppermute | solution.py:262
  53.2 1.6 %copy-start.1 = (bf16[2,512,1024]{2,1,0:T(8,128)(2,1)S(1)}, bf16[2,512,1024]{2,1,0:T(8,128)(2,1)}, u32[]{:S(2)}) copy-start(bf16[2,512,1024]{2,1,0:T(8,128)(2,1)} %copy-done) | copy-start | bytes 6291460
  54.8 1.6 %copy-start.3 = (bf16[2,512,1024]{2,1,0:T(8,128)(2,1)S(1)}, bf16[2,512,1024]{2,1,0:T(8,128)(2,1)}, u32[]{:S(2)}) copy-start(bf16[2,512,1024]{2,1,0:T(8,128)(2,1)} %copy-done.2) | copy-start | bytes 6291460
  54.8 2.2 %copy-start.5 = (bf16[2,512,1024]{2,1,0:T(8,128)(2,1)S(1)}, bf16[2,512,1024]{2,1,0:T(8,128)(2,1)}, u32[]{:S(2)}) copy-start(bf16[2,512,1024]{2,1,0:T(8,128)(2,1)} %copy-done.4) | copy-start | bytes 6291460
  54.8 2.2 %copy-start.7 = (s32[64,64]{1,0:T(8,128)S(1)}, s32[64,64]{1,0:T(8,128)}, u32[]{:S(2)}) copy-start(s32[64,64]{1,0:T(8,128)} %refs_9_.1) | copy-start | bytes 49156
  59.4 11.0 %all-to-all-start = ((f32[16,4,128]{2,1,0:T(4,128)}), f32[16,4,128]{2,1,0:T(4,128)S(1)}, u32[]{:S(2)}, u32[]{:S(2)}) async-start(f32[16,4,128]{2,1,0:T(4,128)} %bitcast.1), calls=%async_computation | async-start | bytes 65536 | tf_op jit(solution)/shard_map/all_to_all | solution.py:315
  70.5 0.7 copy-start.8

commit v4 on v0

v4 whole, which is shorter than its diff:
```python
import functools

import jax
import jax.numpy as jnp
from jax import lax
from jax.experimental import pallas as pl
from jax.experimental.pallas import tpu as pltpu
from jax.sharding import PartitionSpec as P

CHUNKS = 2
ROW_STEP = 16
LANES = 128
VMEM = pl.BlockSpec(memory_space=pltpu.VMEM)
HBM = pl.BlockSpec(memory_space=pltpu.HBM)
ANY = pl.BlockSpec(memory_space=pl.ANY)


def factors(n):
    assert n & (n - 1) == 0
    c = min(n, 2)
    m = n // c
    y = 1
    while 4 * y * y <= m:
        y *= 2
    return m // y, y, c


def place(n, index):
    _, y, c = factors(n)
    return index // (y * c), (index // c) % y, index % c


def bits(size):
    return [1 << i for i in range(size.bit_length() - 1)]


def z_order(fz):
    order = [0]
    for b in reversed(bits(fz)):
        order += [j | b for j in order]
    return order


def pairs(n, dz, dy, dc):
    _, fy, fc = factors(n)
    out = []
    for i in range(n):
        z, y, c = place(n, i)
        out.append((i, ((z ^ dz) * fy + (y ^ dy)) * fc + (c ^ dc)))
    return out


def cost(flops, size):
    return pl.CostEstimate(flops=flops, bytes_accessed=size, transcendentals=0)


def params():
    return pltpu.CompilerParams(vmem_limit_bytes=24 * 1024 * 1024)


def in_hbm(x):
    return pltpu.with_memory_space_constraint(x, pltpu.HBM)


def column(n, chunk, chunks, sub, dy, dc):
    _, fy, fc = factors(n)
    _, y, c = place(n, lax.axis_index("lat"))
    return pl.multiple_of((((c ^ dc) * fy + (y ^ dy)) * chunks + chunk) * sub, sub)


def partial_sums(n, own, cols, dense_ref, targets_ref, buf, out_ref):
    rows = dense_ref.shape[0]
    sub = buf.shape[2]
    row = lax.broadcasted_iota(jnp.int32, (rows, own), 0)
    want = lax.broadcasted_iota(jnp.int32, (rows, own), 1) + lax.axis_index("lat") * own
    mine = jnp.where(row == want, -1.0, 0.0).astype(jnp.bfloat16)
    for o, col in enumerate(cols):
        part = jnp.dot(dense_ref[...], buf[o], preferred_element_type=jnp.float32)
        part += jnp.dot(
            mine, targets_ref[:, pl.ds(col, sub)], preferred_element_type=jnp.float32
        )
        out_ref[:, o * sub : (o + 1) * sub] = part


def first_kernel(n, own, chunks, order, *refs):
    fz, fy, fc = factors(n)
    ids_hbm, codes_hbm, decoder_hbm, targets_hbm = refs[:4]
    out_ref, dense_ref, targets_ref = refs[4:7]
    kept = len(order) - 1
    bufs = refs[7 : 7 + kept]
    buf, ids_ref, codes_ref, small, sem = refs[7 + kept :]
    bufs = (buf,) + tuple(bufs)
    me = lax.axis_index("lat")
    lat_dev = decoder_hbm.shape[0]
    sub = buf.shape[2]
    smalls = [
        pltpu.make_async_copy(a, b, small.at[i])
        for i, (a, b) in enumerate(
            ((ids_hbm, ids_ref), (codes_hbm, codes_ref), (targets_hbm, targets_ref))
        )
    ]
    for copy in smalls:
        copy.start()
    cols = [[column(n, p, chunks, sub, o, dc) for o in range(fy)] for p, dc in order]
    loads = [
        [
            pltpu.make_async_copy(
                decoder_hbm.at[:, pl.ds(cols[i][o], sub)], bufs[i].at[o], sem.at[i, o]
            )
            for o in range(fy)
        ]
        for i in range(len(order))
    ]
    for group in loads:
        for copy in group:
            copy.start()
    for copy in smalls:
        copy.wait()
    rows, k_count = ids_ref.shape
    lanes = lax.broadcasted_iota(jnp.int32, (ROW_STEP, lat_dev), 1) + me * lat_dev

    def body(g, carry):
        at = pl.ds(pl.multiple_of(g * ROW_STEP, ROW_STEP), ROW_STEP)
        ids = ids_ref[at, :]
        codes = codes_ref[at, :].astype(jnp.float32)
        acc = jnp.zeros((ROW_STEP, lat_dev), jnp.float32)
        for k in range(k_count):
            acc = jnp.where(ids[:, k : k + 1] == lanes, codes[:, k : k + 1], acc)
        dense_ref[at, :] = acc.astype(jnp.bfloat16)
        return carry

    lax.fori_loop(0, rows // ROW_STEP, body, 0)
    for copy in loads[0]:
        copy.wait()
    partial_sums(n, own, cols[0], dense_ref, targets_ref, buf, out_ref)
    for group in loads[1:]:
        for copy in group:
            copy.wait()


def first_decode(n, chunks, order, sub, ids, codes, decoder, targets):
    _, fy, _ = factors(n)
    lat_dev = decoder.shape[0]
    rows = ids.shape[0]
    columns = (fy, lat_dev, sub)
    args = (ids, codes, decoder, targets)
    return pl.pallas_call(
        functools.partial(first_kernel, n, rows // n, chunks, order),
        out_shape=[
            pltpu.VMEM((rows, fy * sub), jnp.float32),
            pltpu.VMEM((rows, lat_dev), jnp.bfloat16),
            pltpu.VMEM(targets.shape, targets.dtype),
        ]
        + [pltpu.VMEM(columns, jnp.bfloat16)] * (len(order) - 1),
        in_specs=[HBM] * 4,
        out_specs=[VMEM] * (2 + len(order)),
        scratch_shapes=[
            pltpu.VMEM(columns, jnp.bfloat16),
            pltpu.VMEM(ids.shape, ids.dtype),
            pltpu.VMEM(codes.shape, codes.dtype),
            pltpu.SemaphoreType.DMA((3,)),
            pltpu.SemaphoreType.DMA((len(order), fy)),
        ],
        compiler_params=params(),
        cost_estimate=cost(2 * rows * lat_dev * fy * sub, decoder.size * 2),
        name="first_decode",
    )(*[in_hbm(x) for x in args])


def decode_kernel(n, own, chunk, chunks, dc, dense_ref, targets_ref, buf, _, out_ref):
    sub = buf.shape[2]
    cols = [column(n, chunk, chunks, sub, o, dc) for o in range(buf.shape[0])]
    partial_sums(n, own, cols, dense_ref, targets_ref, buf, out_ref)


def decode(n, chunk, chunks, dc, dense, targets, buf, after):
    rows, lat_dev = dense.shape
    fy, _, sub = buf.shape
    return pl.pallas_call(
        functools.partial(decode_kernel, n, rows // n, chunk, chunks, dc),
        out_shape=pltpu.VMEM((rows, fy * sub), jnp.float32),
        in_specs=[VMEM, VMEM, VMEM, ANY],
        out_specs=VMEM,
        compiler_params=params(),
        cost_estimate=cost(2 * rows * lat_dev * fy * sub, 3 * lat_dev * fy * sub),
        name="decode",
    )(dense, targets, buf, after)


def grad_kernel(n, at, final, with_prev, *refs):
    refs = list(refs)
    err_ref, decoder_ref = refs.pop(0), refs.pop(0)
    prev_ref = refs.pop(0) if with_prev else None
    sub = err_ref.shape[1]
    dc, dy, chunk, chunks = at
    col = column(n, chunk, chunks, sub, dy, dc)
    total = lax.dot_general(
        err_ref[...],
        decoder_ref[:, pl.ds(col, sub)],
        (((1,), (1,)), ((), ())),
        preferred_element_type=jnp.float32,
    )
    if with_prev:
        total += prev_ref[...]
    if not final:
        refs[0][...] = total
        return
    ids_ref, loss_ref, out_ref, totals_ref = refs
    totals_ref[...] = total
    rows, k_count = ids_ref.shape
    lat_dev = total.shape[1]
    own = out_ref.shape[1]
    fz, fy, fc = factors(n)
    me = lax.axis_index("lat")
    z, y, c = place(n, me)
    group = rows // fz
    places = lax.broadcasted_iota(jnp.int32, (ROW_STEP, LANES), 1)
    pad = jnp.zeros((ROW_STEP, LANES - k_count), jnp.int32)
    for q, j in enumerate(z_order(fz)):
        for s in range(0, group, ROW_STEP):
            rows_at = pl.ds(pl.multiple_of((z ^ j) * group + s, ROW_STEP), ROW_STEP)
            ids = jnp.concatenate([ids_ref[rows_at, :] - me * lat_dev, pad], axis=1)
            held = jnp.where(places < k_count, ids // LANES, -1)
            inside = ids % LANES
            acc = jnp.zeros((ROW_STEP, LANES), jnp.float32)
            if q == 0:
                acc = jnp.where(places == k_count, loss_ref[s : s + ROW_STEP, :], acc)
            for t in range(lat_dev // LANES):
                values = totals_ref[q * group + s : q * group + s + ROW_STEP, t * LANES : (t + 1) * LANES]
                found = jnp.take_along_axis(values, inside, axis=1, mode="promise_in_bounds")
                acc = jnp.where(held == t, found, acc)
            for d in range(ROW_STEP // own):
                to = s // own + d
                index = ((c ^ (to % fc)) * fy + (y ^ (to // fc))) * fz + q
                out_ref[index] = acc[d * own : (d + 1) * own, :]


def grad(n, at, err, decoder, prev, final=None):
    lat_dev = decoder.shape[0]
    rows, sub = err.shape
    args = [err, decoder]
    if prev is not None:
        args.append(prev)
    out, scratch = jax.ShapeDtypeStruct((rows, lat_dev), jnp.float32), []
    if final is not None:
        args += list(final)
        scratch.append(pltpu.VMEM(out.shape, out.dtype))
        out = jax.ShapeDtypeStruct((n, rows // n, LANES), jnp.float32)
    return pl.pallas_call(
        functools.partial(grad_kernel, n, at, final is not None, prev is not None),
        out_shape=out,
        in_specs=[VMEM] * len(args),
        out_specs=VMEM,
        scratch_shapes=scratch,
        compiler_params=params(),
        cost_estimate=cost(2 * rows * lat_dev * sub, 3 * lat_dev * sub),
        name="grad",
    )(*args)


def own_kernel(n, blocks, own, *refs):
    errs, out_ref = refs[:-1], refs[-1]
    _, fy, fc = factors(n)
    _, y, c = place(n, lax.axis_index("lat"))
    group, sub = errs[0].shape
    row = lax.broadcasted_iota(jnp.int32, (own, group), 0) + (y * fc + c) * own
    want = lax.broadcasted_iota(jnp.int32, (own, group), 1)
    mine = jnp.where(row == want, 1.0, 0.0).astype(jnp.bfloat16)
    for err, (dc, dy, chunk, chunks) in zip(errs, blocks):
        rows = jnp.dot(mine, err[...], preferred_element_type=jnp.float32)
        out_ref[:, pl.ds(column(n, chunk, chunks, sub, dy, dc), sub)] = rows.astype(jnp.bfloat16)


def own_rows(n, blocks, own, width, errs):
    return pl.pallas_call(
        functools.partial(own_kernel, n, tuple(blocks), own),
        out_shape=jax.ShapeDtypeStruct((own, width), jnp.bfloat16),
        in_specs=[VMEM] * len(errs),
        out_specs=VMEM,
        compiler_params=params(),
        name="own_rows",
    )(*errs)


def local(codes, indices, decoder, targets):
    width = decoder.shape[1]
    rows, k_count = codes.shape
    n = lax.axis_size("lat")
    own = rows // n
    fz, fy, fc = factors(n)
    group = rows // fz
    chunks = CHUNKS
    sub = width // (fc * fy * chunks)
    z, _, _ = place(n, lax.axis_index("lat"))

    def swap(x, dz=0, dy=0, dc=0):
        return lax.ppermute(x, "lat", pairs(n, dz, dy, dc))

    def join(xs, axis):
        return xs[0] if len(xs) == 1 else jnp.concatenate(xs, axis=axis)

    order = tuple((p, dc) for p in range(chunks) for dc in reversed(range(fc)))
    part, dense, tgt, *bufs = first_decode(
        n, chunks, order, sub, indices, codes, decoder, targets
    )
    summed, after = [], part
    for p in range(chunks):
        total = None
        for dc in reversed(range(fc)):
            i = order.index((p, dc))
            if i:
                part = decode(n, p, chunks, dc, dense, tgt, bufs[i - 1], after)
                after = part
            got = swap(part, dc=dc) if dc else part
            total = got if total is None else total + got
        blocks = [total[:, o * sub : (o + 1) * sub] for o in range(fy)]
        for b in reversed(bits(fy)):
            go = join(blocks[b:], 1)
            after = go
            got = swap(go, dy=b)
            blocks = [blocks[o] + got[:, o * sub : (o + 1) * sub] for o in range(b)]
        summed.append(blocks[0])

    diffs = []
    for mine in summed:
        blocks = {
            j: lax.dynamic_slice_in_dim(mine, (z ^ j) * group, group, 0) for j in range(fz)
        }
        for b in bits(fz):
            going = [j for j in blocks if j & b]
            got = swap(join([blocks[j] for j in going], 0), dz=b)
            blocks = {
                j ^ b: blocks[j ^ b] + got[i * group : (i + 1) * group]
                for i, j in enumerate(going)
            }
        diffs.append(blocks[0])

    loss = sum(jnp.sum(d * d, axis=1, keepdims=True) for d in diffs)

    pieces = []
    for p in range(chunks):
        whole = diffs[p].astype(jnp.bfloat16)
        for b in reversed(bits(fz)):
            whole = join([whole, swap(whole, dz=b)], 0)
        here = [whole]
        for b in bits(fy):
            here += [swap(e, dy=b) for e in here]
        for dc in range(fc):
            for dy, e in enumerate(here):
                pieces.append(((dc, dy, p, chunks), swap(e, dc=dc) if dc else e))

    totals = None
    for at, e in pieces[:-1]:
        totals = grad(n, at, e, decoder, totals)
    back = grad(n, *pieces[-1], decoder, totals, (indices, loss))
    error = own_rows(n, [at for at, _ in pieces], own, width, [e[:group] for _, e in pieces])

    steps = [dict(dc=b) for b in reversed(bits(fc))] + [dict(dy=b) for b in reversed(bits(fy))]
    for step in steps + [dict(dz=b) for b in bits(fz)]:
        half = back.shape[0] // 2
        back = back[:half] + swap(back[half:], **step)
    back = back[0]
    return error, back[:, k_count] / width, back[:, :k_count]


def solution(mesh):
    in_specs = (P("groups", None), P("groups", None), P("lat", None), P(("groups", "lat"), None))
    out_specs = (P(("groups", "lat"), None), P(("groups", "lat")), P(("groups", "lat"), None))
    return jax.shard_map(local, mesh=mesh, in_specs=in_specs, out_specs=out_specs, check_vma=False)
```

time: 258 us -> 79 us (0.31)
  waiting for transfers between devices: 100 us -> 25.3 us
  blocking collectives: 60.2 us -> 0 us
  other arithmetic: 34.2 us -> 1.22 us
  starting transfers between devices: 0.08 us -> 27.3 us
  local copies, waits for them, and re-layouts: 37.2 us -> 12.5 us
  between operations: 14.8 us -> 0.9 us
  Pallas kernels: 0 us -> 11.6 us
  matrix products: 11.4 us -> 0 us
    reduce_scatter x1 -> x0, waiting for transfers between devices: 64.4 us -> none  [local(): lax.psum_scatter(partial_value, 'lat', scatter_dimension=1, tiled=True)]
    unnamed x1 -> x0, blocking collectives: 60.2 us -> none
    all_gather x1 -> x0, waiting for transfers between devices: 35.7 us -> none  [local(): piece = lax.all_gather(error_columns, 'lat', axis=1, tiled=True)]
    gather x2 -> x0, local copies, waits for them, and re-layouts: 32.8 us -> none  [local(): jnp.take_along_axis(totals, clipped, axis=1)]
    unnamed x4 -> x1, other arithmetic: 30.2 us -> 0.01 us
    ppermute x0 -> x22, starting transfers between devices: none -> 27.3 us  [swap(): return lax.ppermute(x, 'lat', pairs(n, dz, dy, dc))]
    ppermute x0 -> x22, waiting for transfers between devices: none -> 25.3 us  [swap(): return lax.ppermute(x, 'lat', pairs(n, dz, dy, dc))]
    pallas_call x0 -> x13, Pallas kernels: none -> 11.6 us  [the longest x1 5.28 us: first_decode(): pl.pallas_call(functools.partial(first_kernel, n, rows // n, chunks, orde...]
  transfers between devices with their start and end apart: 2 -> 22, of which waited for: 2 -> 13; matrix products, arithmetic and copies ran while one was open for 0% -> 1% of each run, Pallas kernels for 0% -> 7%
where the time goes in v4:
time: 79 us; the launch traced here: 78.8 us
  starting transfers between devices  27.3 us (35%)
  waiting for transfers between devices  25.3 us (32%)
  local copies, waits for them, and re-layouts  12.5 us (16%)
  Pallas kernels  11.6 us (15%)
  other arithmetic  1.22 us (2%)
  between operations  0.9 us (1%)
    ppermute x22, starting transfers between devices, swap(): return lax.ppermute(x, 'lat', pairs(n, dz, dy, dc))  27.3 us
    ppermute x22, waiting for transfers between devices, swap(): return lax.ppermute(x, 'lat', pairs(n, dz, dy, dc))  25.3 us
    unnamed x16, local copies, waits for them, and re-layouts  12.3 us
    pallas_call x1, Pallas kernels, first_decode(): pl.pallas_call(functools.partial(first_kernel, n, rows // n, chunks, orde...  5.28 us
    pallas_call x8, Pallas kernels, grad(): pl.pallas_call(functools.partial(grad_kernel, n, at, final is not None, p...  3.75 us
    pallas_call x3, Pallas kernels, decode(): pl.pallas_call(functools.partial(decode_kernel, n, rows // n, chunk, chun...  1.73 us
  transfers between devices with their start and end apart: 22, of which 13 were waited for; matrix products, arithmetic and copies ran while one was open for 1% of the time, Pallas kernels for 7%

profile of v4, /device:TPU:0, one launch (start us, length us, event | category | flops | bytes accessed | tf_op | source)
XLA Modules:
  0.0 78.8 jit_solution(5119444376739093340)
XLA Ops:
  0.6 5.3 %first_decode.1 = (f32[64,2048]{1,0:T(8,128)S(1)}, bf16[64,512]{1,0:T(8,128)(2,1)S(1)}, bf16[4,8192]{1,0:T(4,128)(2,1)S(1)}, bf16[2,512,1024]{2,1,0:T(8,128)(2,1...) custom-call(s32[64,64]{1,0:T(8,128)} %refs_3_.3, bf16[64,64]{1,0:T(8,128)(2,1)} %refs_1_.9, ...), custom_call_target="tpu_custom_call" | custom-call | flops 134217728 | bytes 8388608 | tf_op jit(solution)/shard_map/first_decode/pallas_call | solution.py:147
  5.9 1.3 %copy-done.2 = bf16[2,512,1024]{2,1,0:T(8,128)(2,1)} copy-done((bf16[2,512,1024]{2,1,0:T(8,128)(2,1)}, bf16[2,512,1024]{2,1,0:T(8,128)(2,1)S(1)}, u32[]{:S(2)}) %copy-start.2) | copy-done | bytes 2097176
  7.3 0.5 collective-permute-start
  7.7 0.6 decode.3
  8.3 1.0 %collective-permute-done = f32[64,2048]{1,0:T(8,128)S(1)} collective-permute-done((f32[64,2048]{1,0:T(8,128)S(1)}, f32[64,2048]{1,0:T(8,128)S(1)}, u32[]{:S(2)}, u32[]{:S(2)}) %collective-permute-start) | collective-permute-done | bytes 524320 | tf_op jit(solution)/shard_map/ppermute | solution.py:297
  9.2 0.1 add.64
  9.3 3.0 %collective-permute-start.1 = (f32[64,1024]{1,0:T(8,128)S(1)}, f32[64,1024]{1,0:T(8,128)S(1)}, u32[]{:S(2)}, u32[]{:S(2)}) collective-permute-start(f32[64,1024]{1,0:T(8,128)S(1)} %slice.97._), channel_id=1, source_target_pairs={{0,2},{1,3},{2,0},{3,1},{4,6},{5,7},{6,4},{7,5},{8,10},{9,11},{10,... | collective-permute-start | bytes 786440 | tf_op jit(solution)/shard_map/ppermute | solution.py:297
  12.3 1.6 %copy-done.3 = bf16[2,512,1024]{2,1,0:T(8,128)(2,1)S(1)} copy-done((bf16[2,512,1024]{2,1,0:T(8,128)(2,1)S(1)}, bf16[2,512,1024]{2,1,0:T(8,128)(2,1)}, u32[]{:S(2)}) %copy-start.3) | copy-done | bytes 2097176
  13.9 0.6 decode.4._
  14.5 0.1 collective-permute-start.9
  14.5 4.4 %collective-permute-done.1 = f32[64,1024]{1,0:T(8,128)S(1)} collective-permute-done((f32[64,1024]{1,0:T(8,128)S(1)}, f32[64,1024]{1,0:T(8,128)S(1)}, u32[]{:S(2)}, u32[]{:S(2)}) %collective-permute-start.1) | collective-permute-done | bytes 262176 | tf_op jit(solution)/shard_map/ppermute | solution.py:297
  19.0 1.9 %collective-permute-start.2 = (f32[32,1024]{1,0:T(8,128)S(1)}, f32[32,1024]{1,0:T(8,128)S(1)}, u32[]{:S(2)}, u32[]{:S(2)}) collective-permute-start(f32[32,1024]{1,0:T(8,128)S(1)} %pad_maximum_fusion), channel_id=1, source_target_pairs={{0,4},{1,5},{2,6},{3,7},{4,0},{5,1},{6,2},{7,3},{8,12},{9,13},{10,... | collective-permute-start | bytes 393224 | tf_op jit(solution)/shard_map/ppermute | solution.py:297
  20.8 0.6 decode.5
  21.4 0.0 collective-permute-done.9
  21.4 0.1 add.73
  21.5 1.6 %collective-permute-start.10 = (f32[64,1024]{1,0:T(8,128)S(1)}, f32[64,1024]{1,0:T(8,128)S(1)}, u32[]{:S(2)}, u32[]{:S(2)}) collective-permute-start(f32[64,1024]{1,0:T(8,128)S(1)} %slice.104), channel_id=1, source_target_pairs={{0,2},{1,3},{2,0},{3,1},{4,6},{5,7},{6,4},{7,5},{8,10},{9,11},{10,... | collective-permute-start | bytes 786440 | tf_op jit(solution)/shard_map/ppermute | solution.py:297
  23.1 1.0 %collective-permute-done.2 = f32[32,1024]{1,0:T(8,128)S(1)} collective-permute-done((f32[32,1024]{1,0:T(8,128)S(1)}, f32[32,1024]{1,0:T(8,128)S(1)}, u32[]{:S(2)}, u32[]{:S(2)}) %collective-permute-start.2) | collective-permute-done | bytes 131104 | tf_op jit(solution)/shard_map/ppermute | solution.py:297
  24.1 2.8 %collective-permute-start.3 = (f32[16,1024]{1,0:T(8,128)S(1)}, f32[16,1024]{1,0:T(8,128)S(1)}, u32[]{:S(2)}, u32[]{:S(2)}) collective-permute-start(f32[16,1024]{1,0:T(8,128)S(1)} %slice_add_fusion.4), channel_id=1, source_target_pairs={{0,8},{1,9},{2,10},{3,11},{4,12},{5,13},{6,14},{7,15},{8,0},{9,1},... | collective-permute-start | bytes 196616 | tf_op jit(solution)/shard_map/ppermute | solution.py:297
  26.9 1.9 %collective-permute-done.10 = f32[64,1024]{1,0:T(8,128)S(1)} collective-permute-done((f32[64,1024]{1,0:T(8,128)S(1)}, f32[64,1024]{1,0:T(8,128)S(1)}, u32[]{:S(2)}, u32[]{:S(2)}) %collective-permute-start.10) | collective-permute-done | bytes 262176 | tf_op jit(solution)/shard_map/ppermute | solution.py:297
  28.9 0.6 collective-permute-start.11
  29.5 0.1 multiply_reduce_fusion.1
  29.6 3.2 %collective-permute-start.4 = (bf16[16,1024]{1,0:T(8,128)(2,1)S(1)}, bf16[16,1024]{1,0:T(8,128)(2,1)S(1)}, u32[]{:S(2)}, u32[]{:S(2)}) collective-permute-start(bf16[16,1024]{1,0:T(8,128)(2,1)S(1)} %get-tuple-element.18.refs_0_), channel_id=1, source_target_pairs={{0,8},{1,9},{2,10},{3,11},{4,12},{5,13},{6,14},{7,15},{8,0},{9,1},... | collective-permute-start | bytes 98312 | tf_op jit(solution)/shard_map/ppermute | solution.py:297
  32.9 1.0 %collective-permute-done.11 = f32[32,1024]{1,0:T(8,128)S(1)} collective-permute-done((f32[32,1024]{1,0:T(8,128)S(1)}, f32[32,1024]{1,0:T(8,128)S(1)}, u32[]{:S(2)}, u32[]{:S(2)}) %collective-permute-start.11) | collective-permute-done | bytes 131104 | tf_op jit(solution)/shard_map/ppermute | solution.py:297
  33.9 3.2 %collective-permute-start.12 = (f32[16,1024]{1,0:T(8,128)S(1)}, f32[16,1024]{1,0:T(8,128)S(1)}, u32[]{:S(2)}, u32[]{:S(2)}) collective-permute-start(f32[16,1024]{1,0:T(8,128)S(1)} %slice_add_fusion.2), channel_id=1, source_target_pairs={{0,8},{1,9},{2,10},{3,11},{4,12},{5,13},{6,14},{7,15},{8,0},{9,1},... | collective-permute-start | bytes 196616 | tf_op jit(solution)/shard_map/ppermute | solution.py:297
  37.2 0.0 collective-permute-done.4
  37.2 0.6 collective-permute-start.5
  37.8 2.5 %collective-permute-done.12 = f32[16,1024]{1,0:T(8,128)S(1)} collective-permute-done((f32[16,1024]{1,0:T(8,128)S(1)}, f32[16,1024]{1,0:T(8,128)S(1)}, u32[]{:S(2)}, u32[]{:S(2)}) %collective-permute-start.12) | collective-permute-done | bytes 65568 | tf_op jit(solution)/shard_map/ppermute | solution.py:297
  40.3 0.1 multiply_reduce_fusion
  40.4 2.5 %collective-permute-start.13 = (bf16[16,1024]{1,0:T(8,128)(2,1)S(1)}, bf16[16,1024]{1,0:T(8,128)(2,1)S(1)}, u32[]{:S(2)}, u32[]{:S(2)}) collective-permute-start(bf16[16,1024]{1,0:T(8,128)(2,1)S(1)} %get-tuple-element.16.refs_4_), channel_id=1, source_target_pairs={{0,8},{1,9},{2,10},{3,11},{4,12},{5,13},{6,14},{7,15},{8,0},{9,1},... | collective-permute-start | bytes 98312 | tf_op jit(solution)/shard_map/ppermute | solution.py:297
  42.9 0.0 collective-permute-done.5
  42.9 1.8 %collective-permute-start.6 = (bf16[64,1024]{1,0:T(8,128)(2,1)S(1)}, bf16[64,1024]{1,0:T(8,128)(2,1)S(1)}, u32[]{:S(2)}, u32[]{:S(2)}) collective-permute-start(bf16[64,1024]{1,0:T(8,128)(2,1)S(1)} %pad_maximum_fusion.1.refs_0_), channel_id=1, source_target_pairs={{0,2},{1,3},{2,0},{3,1},{4,6},{5,7},{6,4},{7,5},{8,10},{9,11},{10,... | collective-permute-start | bytes 393224 | tf_op jit(solution)/shard_map/ppermute | solution.py:297
  44.7 0.6 collective-permute-done.13
  45.3 0.0 collective-permute-start.14
  45.3 0.1 collective-permute-start.7
  45.4 2.6 %collective-permute-done.6.refs_0_ = bf16[64,1024]{1,0:T(8,128)(2,1)S(1)} collective-permute-done((bf16[64,1024]{1,0:T(8,128)(2,1)S(1)}, bf16[64,1024]{1,0:T(8,128)(2,1)S(1)}, u32[]{:S(2)}, u32[]{:S(2)}) %collective-permute-start.6) | collective-permute-done | bytes 131104 | tf_op jit(solution)/shard_map/ppermute | solution.py:297
  47.9 1.6 %collective-permute-done.14 = bf16[32,1024]{1,0:T(8,128)(2,1)S(1)} collective-permute-done((bf16[32,1024]{1,0:T(8,128)(2,1)S(1)}, bf16[32,1024]{1,0:T(8,128)(2,1)S(1)}, u32[]{:S(2)}, u32[]{:S(2)}) %collective-permute-start.14) | collective-permute-done | bytes 65568 | tf_op jit(solution)/shard_map/ppermute | solution.py:297
  49.6 1.6 %collective-permute-start.15 = (bf16[64,1024]{1,0:T(8,128)(2,1)S(1)}, bf16[64,1024]{1,0:T(8,128)(2,1)S(1)}, u32[]{:S(2)}, u32[]{:S(2)}) collective-permute-start(bf16[64,1024]{1,0:T(8,128)(2,1)S(1)} %pad_maximum_fusion.3.refs_0_), channel_id=1, source_target_pairs={{0,2},{1,3},{2,0},{3,1},{4,6},{5,7},{6,4},{7,5},{8,10},{9,11},{10,... | collective-permute-start | bytes 393224 | tf_op jit(solution)/shard_map/ppermute | solution.py:297
  51.1 3.4 %copy-done = bf16[512,8192]{1,0:T(8,128)(2,1)S(1)} copy-done((bf16[512,8192]{1,0:T(8,128)(2,1)S(1)}, bf16[512,8192]{1,0:T(8,128)(2,1)}, u32[]{:S(2)}) %copy-start) | copy-done | bytes 8388632
  54.5 0.4 grad.8.refs_2_
  55.0 0.5 grad.9.refs_2_
  55.4 0.0 collective-permute-done.7.refs_0_
  55.4 0.5 grad.10.refs_2_
  55.9 0.5 grad.11.refs_2_
  56.4 0.1 collective-permute-start.16
  56.5 0.5 collective-permute-start.17
  56.9 0.1 copy.8.refs_4_
  57.0 3.4 %copy-done.1 = bf16[512,8192]{1,0:T(8,128)(2,1)S(1)} copy-done((bf16[512,8192]{1,0:T(8,128)(2,1)S(1)}, bf16[512,8192]{1,0:T(8,128)(2,1)}, u32[]{:S(2)}) %copy-start.1) | copy-done | bytes 8388632
  60.4 0.4 grad.12.refs_2_
  60.9 0.0 slice-start
  60.9 0.5 grad.13.refs_2_
  61.3 0.0 copy-start.4
  61.4 0.5 grad.14.refs_2_
  61.8 1.2 %slice-done = s8[4194304]{0:T(1024)(128)(4,1)S(1)} async-done(((s8[8388608]{0:T(1024)(128)(4,1)}), s8[4194304]{0:T(1024)(128)(4,1)S(1)}, s32[]{:S(2)}) %slice-start) | async-done | bytes 4194328
  63.1 1.4 %slice-done.1 = s8[4194304]{0:T(1024)(128)(4,1)S(1)} async-done(((s8[8388608]{0:T(1024)(128)(4,1)}), s8[4194304]{0:T(1024)(128)(4,1)S(1)}, s32[]{:S(2)}) %slice-start.1) | async-done | bytes 4194328
  64.5 0.6 grad.15
  65.0 0.2 collective-permute-start.18
  65.2 1.1 %collective-permute-done.18 = f32[8,4,128]{2,1,0:T(4,128)S(1)} collective-permute-done((f32[8,4,128]{2,1,0:T(4,128)S(1)}, f32[8,4,128]{2,1,0:T(4,128)S(1)}, u32[]{:S(2)}, u32[]{:S(2)}) %collective-permute-start.18) | collective-permute-done | bytes 16416 | tf_op jit(solution)/shard_map/ppermute | solution.py:297
  66.3 0.6 collective-permute-start.19
  66.9 3.1 %collective-permute-done.19 = f32[4,4,128]{2,1,0:T(4,128)S(1)} collective-permute-done((f32[4,4,128]{2,1,0:T(4,128)S(1)}, f32[4,4,128]{2,1,0:T(4,128)S(1)}, u32[]{:S(2)}, u32[]{:S(2)}) %collective-permute-start.19) | collective-permute-done | bytes 8224 | tf_op jit(solution)/shard_map/ppermute | solution.py:297
  70.0 3.6 %collective-permute-done.20 = f32[2,4,128]{2,1,0:T(4,128)S(1)} collective-permute-done((f32[2,4,128]{2,1,0:T(4,128)S(1)}, f32[2,4,128]{2,1,0:T(4,128)S(1)}, u32[]{:S(2)}, u32[]{:S(2)}) %collective-permute-start.20) | collective-permute-done | bytes 4128 | tf_op jit(solution)/shard_map/ppermute | solution.py:297
  73.6 2.6 %collective-permute-start.21 = (f32[1,4,128]{2,1,0:T(4,128)S(1)}, f32[1,4,128]{2,1,0:T(4,128)S(1)}, u32[]{:S(2)}, u32[]{:S(2)}) collective-permute-start(f32[1,4,128]{2,1,0:T(4,128)S(1)} %slice.117), channel_id=1, source_target_pairs={{0,8},{1,9},{2,10},{3,11},{4,12},{5,13},{6,14},{7,15},{8,0},{9,1},... | collective-permute-start | bytes 6152 | tf_op jit(solution)/shard_map/ppermute | solution.py:297
  76.3 0.8 %own_rows.1 = bf16[4,8192]{1,0:T(4,128)(2,1)} custom-call(bf16[16,1024]{1,0:T(8,128)(2,1)S(1)} %get-tuple-element.18.refs_0_, bf16[16,1024]{1,0:T(8,128)(2,1)S(1)} %slice.100.refs_1_, bf16[16,1024]{1,0:T(8,128)(2,1)S(1)} %slice.101.refs_2_, bf16[16,1024]{1,0:T(8,128)(2,1)S(1)} %slice.102.refs_3_, bf16[16,1024]{1,0:T(8,128)(2,1)S(1)} %get-tuple-element.16.refs_4_, ...), custom_call_target="tpu_custom_call" | custom-call | tf_op jit(solution)/shard_map/own_rows/pallas_call | solution.py:275
  77.2 1.0 %collective-permute-done.21 = f32[1,4,128]{2,1,0:T(4,128)S(1)} collective-permute-done((f32[1,4,128]{2,1,0:T(4,128)S(1)}, f32[1,4,128]{2,1,0:T(4,128)S(1)}, u32[]{:S(2)}, u32[]{:S(2)}) %collective-permute-start.21) | collective-permute-done | bytes 2080 | tf_op jit(solution)/shard_map/ppermute | solution.py:297
  78.1 0.7 multiply_reduce_fusion.2
  (45 shorter events, 0.3 us)
Async XLA Ops:
  5.9 1.3 %copy-start.2 = (bf16[2,512,1024]{2,1,0:T(8,128)(2,1)}, bf16[2,512,1024]{2,1,0:T(8,128)(2,1)S(1)}, u32[]{:S(2)}) copy-start(bf16[2,512,1024]{2,1,0:T(8,128)(2,1)S(1)} %get-tuple-element.13.buf) | copy-start | bytes 6291460
  7.3 2.0 %collective-permute-start = (f32[64,2048]{1,0:T(8,128)S(1)}, f32[64,2048]{1,0:T(8,128)S(1)}, u32[]{:S(2)}, u32[]{:S(2)}) collective-permute-start(f32[64,2048]{1,0:T(8,128)S(1)} %get-tuple-element.9._), channel_id=1, source_target_pairs={{0,1},{1,0},{2,3},{3,2},{4,5},{5,4},{6,7},{7,6},{8,9},{9,8},{10,11... | collective-permute-start | bytes 1572872 | tf_op jit(solution)/shard_map/ppermute | solution.py:297
  9.3 9.6 %collective-permute-start.1 = (f32[64,1024]{1,0:T(8,128)S(1)}, f32[64,1024]{1,0:T(8,128)S(1)}, u32[]{:S(2)}, u32[]{:S(2)}) collective-permute-start(f32[64,1024]{1,0:T(8,128)S(1)} %slice.97._), channel_id=1, source_target_pairs={{0,2},{1,3},{2,0},{3,1},{4,6},{5,7},{6,4},{7,5},{8,10},{9,11},{10,... | collective-permute-start | bytes 786440 | tf_op jit(solution)/shard_map/ppermute | solution.py:297
  12.3 1.6 %copy-start.3 = (bf16[2,512,1024]{2,1,0:T(8,128)(2,1)S(1)}, bf16[2,512,1024]{2,1,0:T(8,128)(2,1)}, u32[]{:S(2)}) copy-start(bf16[2,512,1024]{2,1,0:T(8,128)(2,1)} %copy-done.2) | copy-start | bytes 6291460
  14.5 7.0 %collective-permute-start.9 = (f32[64,2048]{1,0:T(8,128)S(1)}, f32[64,2048]{1,0:T(8,128)S(1)}, u32[]{:S(2)}, u32[]{:S(2)}) collective-permute-start(f32[64,2048]{1,0:T(8,128)S(1)} %decode.4._), channel_id=1, source_target_pairs={{0,1},{1,0},{2,3},{3,2},{4,5},{5,4},{6,7},{7,6},{8,9},{9,8},{10,11... | collective-permute-start | bytes 1572872 | tf_op jit(solution)/shard_map/ppermute | solution.py:297
  19.0 5.1 %collective-permute-start.2 = (f32[32,1024]{1,0:T(8,128)S(1)}, f32[32,1024]{1,0:T(8,128)S(1)}, u32[]{:S(2)}, u32[]{:S(2)}) collective-permute-start(f32[32,1024]{1,0:T(8,128)S(1)} %pad_maximum_fusion), channel_id=1, source_target_pairs={{0,4},{1,5},{2,6},{3,7},{4,0},{5,1},{6,2},{7,3},{8,12},{9,13},{10,... | collective-permute-start | bytes 393224 | tf_op jit(solution)/shard_map/ppermute | solution.py:297
  21.5 7.3 %collective-permute-start.10 = (f32[64,1024]{1,0:T(8,128)S(1)}, f32[64,1024]{1,0:T(8,128)S(1)}, u32[]{:S(2)}, u32[]{:S(2)}) collective-permute-start(f32[64,1024]{1,0:T(8,128)S(1)} %slice.104), channel_id=1, source_target_pairs={{0,2},{1,3},{2,0},{3,1},{4,6},{5,7},{6,4},{7,5},{8,10},{9,11},{10,... | collective-permute-start | bytes 786440 | tf_op jit(solution)/shard_map/ppermute | solution.py:297
  24.1 5.4 %collective-permute-start.3 = (f32[16,1024]{1,0:T(8,128)S(1)}, f32[16,1024]{1,0:T(8,128)S(1)}, u32[]{:S(2)}, u32[]{:S(2)}) collective-permute-start(f32[16,1024]{1,0:T(8,128)S(1)} %slice_add_fusion.4), channel_id=1, source_target_pairs={{0,8},{1,9},{2,10},{3,11},{4,12},{5,13},{6,14},{7,15},{8,0},{9,1},... | collective-permute-start | bytes 196616 | tf_op jit(solution)/shard_map/ppermute | solution.py:297
  28.9 5.0 %collective-permute-start.11 = (f32[32,1024]{1,0:T(8,128)S(1)}, f32[32,1024]{1,0:T(8,128)S(1)}, u32[]{:S(2)}, u32[]{:S(2)}) collective-permute-start(f32[32,1024]{1,0:T(8,128)S(1)} %pad_maximum_fusion.2), channel_id=1, source_target_pairs={{0,4},{1,5},{2,6},{3,7},{4,0},{5,1},{6,2},{7,3},{8,12},{9,13},{10,... | collective-permute-start | bytes 393224 | tf_op jit(solution)/shard_map/ppermute | solution.py:297
  29.6 7.5 %collective-permute-start.4 = (bf16[16,1024]{1,0:T(8,128)(2,1)S(1)}, bf16[16,1024]{1,0:T(8,128)(2,1)S(1)}, u32[]{:S(2)}, u32[]{:S(2)}) collective-permute-start(bf16[16,1024]{1,0:T(8,128)(2,1)S(1)} %get-tuple-element.18.refs_0_), channel_id=1, source_target_pairs={{0,8},{1,9},{2,10},{3,11},{4,12},{5,13},{6,14},{7,15},{8,0},{9,1},... | collective-permute-start | bytes 98312 | tf_op jit(solution)/shard_map/ppermute | solution.py:297
  33.9 6.3 %collective-permute-start.12 = (f32[16,1024]{1,0:T(8,128)S(1)}, f32[16,1024]{1,0:T(8,128)S(1)}, u32[]{:S(2)}, u32[]{:S(2)}) collective-permute-start(f32[16,1024]{1,0:T(8,128)S(1)} %slice_add_fusion.2), channel_id=1, source_target_pairs={{0,8},{1,9},{2,10},{3,11},{4,12},{5,13},{6,14},{7,15},{8,0},{9,1},... | collective-permute-start | bytes 196616 | tf_op jit(solution)/shard_map/ppermute | solution.py:297
  37.2 5.7 %collective-permute-start.5 = (bf16[32,1024]{1,0:T(8,128)(2,1)S(1)}, bf16[32,1024]{1,0:T(8,128)(2,1)S(1)}, u32[]{:S(2)}, u32[]{:S(2)}) collective-permute-start(bf16[32,1024]{1,0:T(8,128)(2,1)S(1)} %pad_maximum_fusion.4), channel_id=1, source_target_pairs={{0,4},{1,5},{2,6},{3,7},{4,0},{5,1},{6,2},{7,3},{8,12},{9,13},{10,... | collective-permute-start | bytes 196616 | tf_op jit(solution)/shard_map/ppermute | solution.py:297
  40.4 4.9 %collective-permute-start.13 = (bf16[16,1024]{1,0:T(8,128)(2,1)S(1)}, bf16[16,1024]{1,0:T(8,128)(2,1)S(1)}, u32[]{:S(2)}, u32[]{:S(2)}) collective-permute-start(bf16[16,1024]{1,0:T(8,128)(2,1)S(1)} %get-tuple-element.16.refs_4_), channel_id=1, source_target_pairs={{0,8},{1,9},{2,10},{3,11},{4,12},{5,13},{6,14},{7,15},{8,0},{9,1},... | collective-permute-start | bytes 98312 | tf_op jit(solution)/shard_map/ppermute | solution.py:297
  42.9 5.0 %collective-permute-start.6 = (bf16[64,1024]{1,0:T(8,128)(2,1)S(1)}, bf16[64,1024]{1,0:T(8,128)(2,1)S(1)}, u32[]{:S(2)}, u32[]{:S(2)}) collective-permute-start(bf16[64,1024]{1,0:T(8,128)(2,1)S(1)} %pad_maximum_fusion.1.refs_0_), channel_id=1, source_target_pairs={{0,2},{1,3},{2,0},{3,1},{4,6},{5,7},{6,4},{7,5},{8,10},{9,11},{10,... | collective-permute-start | bytes 393224 | tf_op jit(solution)/shard_map/ppermute | solution.py:297
  45.3 4.3 %collective-permute-start.14 = (bf16[32,1024]{1,0:T(8,128)(2,1)S(1)}, bf16[32,1024]{1,0:T(8,128)(2,1)S(1)}, u32[]{:S(2)}, u32[]{:S(2)}) collective-permute-start(bf16[32,1024]{1,0:T(8,128)(2,1)S(1)} %pad_maximum_fusion.5), channel_id=1, source_target_pairs={{0,4},{1,5},{2,6},{3,7},{4,0},{5,1},{6,2},{7,3},{8,12},{9,13},{10,... | collective-permute-start | bytes 196616 | tf_op jit(solution)/shard_map/ppermute | solution.py:297
  45.3 10.1 %collective-permute-start.7 = (bf16[64,1024]{1,0:T(8,128)(2,1)S(1)}, bf16[64,1024]{1,0:T(8,128)(2,1)S(1)}, u32[]{:S(2)}, u32[]{:S(2)}) collective-permute-start(bf16[64,1024]{1,0:T(8,128)(2,1)S(1)} %pad_maximum_fusion.1.refs_0_), channel_id=1, source_target_pairs={{0,1},{1,0},{2,3},{3,2},{4,5},{5,4},{6,7},{7,6},{8,9},{9,8},{10,11... | collective-permute-start | bytes 393224 | tf_op jit(solution)/shard_map/ppermute | solution.py:297
  47.9 8.0 %collective-permute-start.8 = (bf16[64,1024]{1,0:T(8,128)(2,1)S(1)}, bf16[64,1024]{1,0:T(8,128)(2,1)S(1)}, u32[]{:S(2)}, u32[]{:S(2)}) collective-permute-start(bf16[64,1024]{1,0:T(8,128)(2,1)S(1)} %collective-permute-done.6.refs_0_), channel_id=1, source_target_pairs={{0,1},{1,0},{2,3},{3,2},{4,5},{5,4},{6,7},{7,6},{8,9},{9,8},{10,11... | collective-permute-start | bytes 393224 | tf_op jit(solution)/shard_map/ppermute | solution.py:297
  49.6 6.9 %collective-permute-start.15 = (bf16[64,1024]{1,0:T(8,128)(2,1)S(1)}, bf16[64,1024]{1,0:T(8,128)(2,1)S(1)}, u32[]{:S(2)}, u32[]{:S(2)}) collective-permute-start(bf16[64,1024]{1,0:T(8,128)(2,1)S(1)} %pad_maximum_fusion.3.refs_0_), channel_id=1, source_target_pairs={{0,2},{1,3},{2,0},{3,1},{4,6},{5,7},{6,4},{7,5},{8,10},{9,11},{10,... | collective-permute-start | bytes 393224 | tf_op jit(solution)/shard_map/ppermute | solution.py:297
  51.1 3.4 %copy-start = (bf16[512,8192]{1,0:T(8,128)(2,1)S(1)}, bf16[512,8192]{1,0:T(8,128)(2,1)}, u32[]{:S(2)}) copy-start(bf16[512,8192]{1,0:T(8,128)(2,1)} %refs_1_.17) | copy-start | bytes 25165828
  56.4 5.0 %collective-permute-start.16 = (bf16[64,1024]{1,0:T(8,128)(2,1)S(1)}, bf16[64,1024]{1,0:T(8,128)(2,1)S(1)}, u32[]{:S(2)}, u32[]{:S(2)}) collective-permute-start(bf16[64,1024]{1,0:T(8,128)(2,1)S(1)} %pad_maximum_fusion.3.refs_0_), channel_id=1, source_target_pairs={{0,1},{1,0},{2,3},{3,2},{4,5},{5,4},{6,7},{7,6},{8,9},{9,8},{10,11... | collective-permute-start | bytes 393224 | tf_op jit(solution)/shard_map/ppermute | solution.py:297
  56.5 5.4 %collective-permute-start.17 = (bf16[64,1024]{1,0:T(8,128)(2,1)S(1)}, bf16[64,1024]{1,0:T(8,128)(2,1)S(1)}, u32[]{:S(2)}, u32[]{:S(2)}) collective-permute-start(bf16[64,1024]{1,0:T(8,128)(2,1)S(1)} %collective-permute-done.15.refs_0_), channel_id=1, source_target_pairs={{0,1},{1,0},{2,3},{3,2},{4,5},{5,4},{6,7},{7,6},{8,9},{9,8},{10,11... | collective-permute-start | bytes 393224 | tf_op jit(solution)/shard_map/ppermute | solution.py:297
  57.0 3.4 %copy-start.1 = (bf16[512,8192]{1,0:T(8,128)(2,1)S(1)}, bf16[512,8192]{1,0:T(8,128)(2,1)}, u32[]{:S(2)}) copy-start(bf16[512,8192]{1,0:T(8,128)(2,1)} %refs_1_.17) | copy-start | bytes 25165828
  60.9 2.2 %slice-start = ((s8[8388608]{0:T(1024)(128)(4,1)}), s8[4194304]{0:T(1024)(128)(4,1)S(1)}, s32[]{:S(2)}) async-start(s8[8388608]{0:T(1024)(128)(4,1)} %bitcast.5), calls=%async_computation | async-start | bytes 8388608
  61.3 3.1 %slice-start.1 = ((s8[8388608]{0:T(1024)(128)(4,1)}), s8[4194304]{0:T(1024)(128)(4,1)S(1)}, s32[]{:S(2)}) async-start(s8[8388608]{0:T(1024)(128)(4,1)} %bitcast.5), calls=%async_computation.1 | async-start | bytes 8388608
  61.3 3.1 %copy-start.4 = (s32[64,64]{1,0:T(8,128)S(1)}, s32[64,64]{1,0:T(8,128)}, u32[]{:S(2)}) copy-start(s32[64,64]{1,0:T(8,128)} %refs_3_.3) | copy-start | bytes 49156
  65.0 1.2 %collective-permute-start.18 = (f32[8,4,128]{2,1,0:T(4,128)S(1)}, f32[8,4,128]{2,1,0:T(4,128)S(1)}, u32[]{:S(2)}, u32[]{:S(2)}) collective-permute-start(f32[8,4,128]{2,1,0:T(4,128)S(1)} %slice.111), channel_id=1, source_target_pairs={{0,1},{1,0},{2,3},{3,2},{4,5},{5,4},{6,7},{7,6},{8,9},{9,8},{10,11... | collective-permute-start | bytes 49160 | tf_op jit(solution)/shard_map/ppermute | solution.py:297
  66.3 3.7 %collective-permute-start.19 = (f32[4,4,128]{2,1,0:T(4,128)S(1)}, f32[4,4,128]{2,1,0:T(4,128)S(1)}, u32[]{:S(2)}, u32[]{:S(2)}) collective-permute-start(f32[4,4,128]{2,1,0:T(4,128)S(1)} %slice.113), channel_id=1, source_target_pairs={{0,2},{1,3},{2,0},{3,1},{4,6},{5,7},{6,4},{7,5},{8,10},{9,11},{10,... | collective-permute-start | bytes 24584 | tf_op jit(solution)/shard_map/ppermute | solution.py:297
  70.0 3.6 %collective-permute-start.20 = (f32[2,4,128]{2,1,0:T(4,128)S(1)}, f32[2,4,128]{2,1,0:T(4,128)S(1)}, u32[]{:S(2)}, u32[]{:S(2)}) collective-permute-start(f32[2,4,128]{2,1,0:T(4,128)S(1)} %slice.115), channel_id=1, source_target_pairs={{0,4},{1,5},{2,6},{3,7},{4,0},{5,1},{6,2},{7,3},{8,12},{9,13},{10,... | collective-permute-start | bytes 12296 | tf_op jit(solution)/shard_map/ppermute | solution.py:297
  73.6 4.5 %collective-permute-start.21 = (f32[1,4,128]{2,1,0:T(4,128)S(1)}, f32[1,4,128]{2,1,0:T(4,128)S(1)}, u32[]{:S(2)}, u32[]{:S(2)}) collective-permute-start(f32[1,4,128]{2,1,0:T(4,128)S(1)} %slice.117), channel_id=1, source_target_pairs={{0,8},{1,9},{2,10},{3,11},{4,12},{5,13},{6,14},{7,15},{8,0},{9,1},... | collective-permute-start | bytes 6152 | tf_op jit(solution)/shard_map/ppermute | solution.py:297
  78.1 0.7 copy-start.5

commit v5 on v2

v5 whole, which is shorter than its diff:
```python
import functools

import jax
import jax.numpy as jnp
from jax import lax
from jax.experimental import pallas as pl
from jax.experimental.pallas import tpu as pltpu
from jax.sharding import PartitionSpec as P

CHUNKS = 2
ROW_STEP = 16
LANES = 128
VMEM = pl.BlockSpec(memory_space=pltpu.VMEM)
HBM = pl.BlockSpec(memory_space=pltpu.HBM)
ANY = pl.BlockSpec(memory_space=pl.ANY)


def factors(n):
    assert n & (n - 1) == 0
    c = min(n, 2)
    m = n // c
    y = 1
    while 4 * y * y <= m:
        y *= 2
    return m // y, y, c


def place(n, index):
    _, y, c = factors(n)
    return index // (y * c), (index // c) % y, index % c


def bits(size):
    return [1 << i for i in range(size.bit_length() - 1)]


def pairs(n, dz, dy, dc):
    _, fy, fc = factors(n)
    out = []
    for i in range(n):
        z, y, c = place(n, i)
        out.append((i, ((z ^ dz) * fy + (y ^ dy)) * fc + (c ^ dc)))
    return out


def cost(flops, size):
    return pl.CostEstimate(flops=flops, bytes_accessed=size, transcendentals=0)


def params():
    return pltpu.CompilerParams(vmem_limit_bytes=24 * 1024 * 1024)


def in_hbm(x):
    return pltpu.with_memory_space_constraint(x, pltpu.HBM)


def column(n, chunk, chunks, sub, dy, dc):
    _, fy, fc = factors(n)
    _, y, c = place(n, lax.axis_index("lat"))
    return pl.multiple_of((((c ^ dc) * fy + (y ^ dy)) * chunks + chunk) * sub, sub)


def hold(x, *after):
    return pl.pallas_call(
        lambda *refs: None,
        out_shape=jax.ShapeDtypeStruct(x.shape, x.dtype),
        in_specs=[ANY] * (1 + len(after)),
        out_specs=ANY,
        input_output_aliases={0: 0},
        name="hold",
    )(x, *after)


def load(decoder_hbm, col, buf, sem):
    return pltpu.make_async_copy(decoder_hbm.at[:, pl.ds(col, buf.shape[1])], buf, sem)


def decode_kernel(n, own, chunk, chunks, first, *refs):
    fz, fy, fc = factors(n)
    me = lax.axis_index("lat")
    if first:
        ids_hbm, codes_hbm, decoder_hbm, targets_hbm = refs[:4]
        outs, dense_ref = refs[4 : 4 + fc], refs[4 + fc]
        buf, sem, targets_ref, small, ids_ref, codes_ref = refs[5 + fc :]
        pairs_in = ((ids_hbm, ids_ref), (codes_hbm, codes_ref), (targets_hbm, targets_ref))
    else:
        dense_ref, decoder_hbm, targets_hbm, _ = refs[:4]
        outs = refs[4 : 4 + fc]
        buf, sem, targets_ref, small = refs[4 + fc :]
        pairs_in = ((targets_hbm, targets_ref),)
    sub = buf.shape[3]
    smalls = [pltpu.make_async_copy(a, b, small.at[i]) for i, (a, b) in enumerate(pairs_in)]
    for copy in smalls:
        copy.start()
    blocks = [(dc, o) for dc in reversed(range(fc)) for o in reversed(range(fy))]
    cols = {at: column(n, chunk, chunks, sub, at[1], at[0]) for at in blocks}
    loads = {at: load(decoder_hbm, cols[at], buf.at[at], sem.at[at]) for at in blocks}
    for at in blocks:
        loads[at].start()
    for copy in smalls:
        copy.wait()
    if first:
        rows, k_count = ids_ref.shape
        lat_dev = decoder_hbm.shape[0]
        lanes = lax.broadcasted_iota(jnp.int32, (ROW_STEP, lat_dev), 1) + me * lat_dev

        def body(g, carry):
            at = pl.ds(pl.multiple_of(g * ROW_STEP, ROW_STEP), ROW_STEP)
            ids = ids_ref[at, :]
            codes = codes_ref[at, :].astype(jnp.float32)
            acc = jnp.zeros((ROW_STEP, lat_dev), jnp.float32)
            for k in range(k_count):
                acc = jnp.where(ids[:, k : k + 1] == lanes, codes[:, k : k + 1], acc)
            dense_ref[at, :] = acc.astype(jnp.bfloat16)
            return carry

        lax.fori_loop(0, rows // ROW_STEP, body, 0)
    rows = dense_ref.shape[0]
    row = lax.broadcasted_iota(jnp.int32, (rows, own), 0)
    want = lax.broadcasted_iota(jnp.int32, (rows, own), 1) + me * own
    mine = jnp.where(row == want, -1.0, 0.0).astype(jnp.bfloat16)
    for dc, o in blocks:
        loads[dc, o].wait()
        part = jnp.dot(dense_ref[...], buf[dc, o], preferred_element_type=jnp.float32)
        part += jnp.dot(
            mine, targets_ref[:, pl.ds(cols[dc, o], sub)], preferred_element_type=jnp.float32
        )
        outs[dc][:, o * sub : (o + 1) * sub] = part


def decode(n, chunk, chunks, sub, ids, codes, dense, decoder, targets, after):
    _, fy, fc = factors(n)
    rows, lat_dev = ids.shape[0], decoder.shape[0]
    first = dense is None
    out = [pltpu.VMEM((rows, fy * sub), jnp.float32)] * fc
    scratch = [
        pltpu.VMEM((fc, fy, lat_dev, sub), jnp.bfloat16),
        pltpu.SemaphoreType.DMA((fc, fy)),
        pltpu.VMEM(targets.shape, targets.dtype),
        pltpu.SemaphoreType.DMA((3,)),
    ]
    if first:
        out.append(pltpu.VMEM((rows, lat_dev), jnp.bfloat16))
        scratch += [pltpu.VMEM(x.shape, x.dtype) for x in (ids, codes)]
        args, specs = [in_hbm(x) for x in (ids, codes, decoder, targets)], [HBM] * 4
    else:
        args = [dense, in_hbm(decoder), in_hbm(targets), after]
        specs = [VMEM, HBM, HBM, ANY]
    got = pl.pallas_call(
        functools.partial(decode_kernel, n, rows // n, chunk, chunks, first),
        out_shape=out,
        in_specs=specs,
        out_specs=[VMEM] * len(out),
        scratch_shapes=scratch,
        compiler_params=params(),
        cost_estimate=cost(2 * rows * lat_dev * fc * fy * sub, 4 * lat_dev * fc * fy * sub),
        name="decode",
    )(*args)
    return got[:fc], got[fc] if first else dense


def grad_kernel(n, blocks, after, final, with_prev, *refs):
    refs = list(refs)
    errs = [refs.pop(0) for _ in blocks]
    decoder_ref = refs.pop(0)
    prev_ref = refs.pop(0) if with_prev else None
    sub = errs[0].shape[1]
    total = prev_ref[...] if with_prev else None
    loads = []
    if not final:
        out_ref = refs.pop(0)
        next_ref = refs.pop(0) if after else None
        buf, sem = refs
        for i, (dc, dy, chunk, chunks) in enumerate(blocks):
            col = column(n, chunk, chunks, sub, dy, dc)
            loads.append(load(decoder_ref, col, buf.at[i], sem.at[i]))
        if after:
            dc, dy, chunk, chunks = after
            col = column(n, chunk, chunks, sub, dy, dc)
            loads.append(load(decoder_ref, col, next_ref, sem.at[len(blocks)]))
        for copy in loads:
            copy.start()
    for i, err in enumerate(errs):
        if not final:
            loads[i].wait()
        part = lax.dot_general(
            err[...],
            decoder_ref[...] if final else buf[i],
            (((1,), (1,)), ((), ())),
            preferred_element_type=jnp.float32,
        )
        total = part if total is None else total + part
    if not final:
        out_ref[...] = total
        if after:
            loads[-1].wait()
        return
    ids_ref, loss_ref, out_ref, totals_ref = refs
    totals_ref[...] = total
    rows, k_count = ids_ref.shape
    lat_dev = total.shape[1]
    own = out_ref.shape[1]
    fz, _, _ = factors(n)
    me = lax.axis_index("lat")
    z, _, _ = place(n, me)
    group = rows // fz
    places = lax.broadcasted_iota(jnp.int32, (ROW_STEP, LANES), 1)
    pad = jnp.zeros((ROW_STEP, LANES - k_count), jnp.int32)
    for j in range(fz):
        for s in range(0, group, ROW_STEP):
            first = (z ^ j) * group + s
            rows_at = pl.ds(pl.multiple_of(first, ROW_STEP), ROW_STEP)
            ids = jnp.concatenate([ids_ref[rows_at, :] - me * lat_dev, pad], axis=1)
            held = jnp.where(places < k_count, ids // LANES, -1)
            inside = ids % LANES
            acc = jnp.zeros((ROW_STEP, LANES), jnp.float32)
            if j == 0:
                acc = jnp.where(places == k_count, loss_ref[s : s + ROW_STEP, :], acc)
            here = slice(j * group + s, j * group + s + ROW_STEP)
            for t in range(lat_dev // LANES):
                values = totals_ref[here, t * LANES : (t + 1) * LANES]
                found = jnp.take_along_axis(values, inside, axis=1, mode="promise_in_bounds")
                acc = jnp.where(held == t, found, acc)
            for d in range(ROW_STEP // own):
                out_ref[first // own + d] = acc[d * own : (d + 1) * own, :]


def grad(n, blocks, errs, decoder, prev, after=None, final=None):
    rows, sub = errs[0].shape
    lat_dev = decoder.shape[0]
    count = len(errs)
    args = list(errs) + [decoder if final is not None else in_hbm(decoder)]
    specs = [VMEM] * count + [HBM if final is None else VMEM]
    if prev is not None:
        args.append(prev)
        specs.append(VMEM)
    totals = pltpu.VMEM((rows, lat_dev), jnp.float32)
    if final is None:
        out = [totals] + ([pltpu.VMEM((lat_dev, sub), jnp.bfloat16)] if after else [])
        scratch = [
            pltpu.VMEM((count, lat_dev, sub), jnp.bfloat16),
            pltpu.SemaphoreType.DMA((count + 1,)),
        ]
    else:
        args += list(final)
        specs += [VMEM] * len(final)
        out = [jax.ShapeDtypeStruct((n, rows // n, LANES), jnp.float32)]
        scratch = [totals]
    return pl.pallas_call(
        functools.partial(grad_kernel, n, tuple(blocks), after, final is not None, prev is not None),
        out_shape=out,
        in_specs=specs,
        out_specs=[VMEM] * len(out),
        scratch_shapes=scratch,
        compiler_params=params(),
        cost_estimate=cost(2 * rows * lat_dev * sub * count, 4 * lat_dev * sub * count),
        name="grad",
    )(*args)


def own_kernel(n, blocks, own, *refs):
    errs, out_ref = refs[:-1], refs[-1]
    _, fy, fc = factors(n)
    _, y, c = place(n, lax.axis_index("lat"))
    group, sub = errs[0].shape
    row = lax.broadcasted_iota(jnp.int32, (own, group), 0) + (y * fc + c) * own
    want = lax.broadcasted_iota(jnp.int32, (own, group), 1)
    mine = jnp.where(row == want, 1.0, 0.0).astype(jnp.bfloat16)
    for err, (dc, dy, chunk, chunks) in zip(errs, blocks):
        rows = jnp.dot(mine, err[...], preferred_element_type=jnp.float32)
        out_ref[:, pl.ds(column(n, chunk, chunks, sub, dy, dc), sub)] = rows.astype(jnp.bfloat16)


def own_rows(n, blocks, own, width, errs):
    return pl.pallas_call(
        functools.partial(own_kernel, n, tuple(blocks), own),
        out_shape=jax.ShapeDtypeStruct((own, width), jnp.bfloat16),
        in_specs=[VMEM] * len(errs),
        out_specs=VMEM,
        compiler_params=params(),
        name="own_rows",
    )(*errs)


def local(codes, indices, decoder, targets):
    width = decoder.shape[1]
    rows, k_count = codes.shape
    n = lax.axis_size("lat")
    own = rows // n
    fz, fy, fc = factors(n)
    group = rows // fz
    chunks = CHUNKS
    sub = width // (fc * fy * chunks)
    z, _, _ = place(n, lax.axis_index("lat"))

    def swap(x, dz=0, dy=0, dc=0):
        return lax.ppermute(x, "lat", pairs(n, dz, dy, dc))

    def join(xs, axis):
        return xs[0] if len(xs) == 1 else jnp.concatenate(xs, axis=axis)

    dense, after, summed = None, None, []
    for p in range(chunks):
        parts, dense = decode(
            n, p, chunks, sub, indices, codes, dense, decoder, targets, after
        )
        total = parts[0]
        for dc in range(1, fc):
            total = total + swap(parts[dc], dc=dc)
        blocks = [total[:, o * sub : (o + 1) * sub] for o in range(fy)]
        for b in reversed(bits(fy)):
            after = join(blocks[b:], 1)
            got = swap(after, dy=b)
            blocks = [blocks[o] + got[:, o * sub : (o + 1) * sub] for o in range(b)]
        summed.append(blocks[0])

    diffs = []
    for mine in summed:
        blocks = [
            lax.dynamic_slice_in_dim(mine, (z ^ j) * group, group, 0) for j in range(fz)
        ]
        diff = blocks[0]
        for j in range(1, fz):
            diff = diff + swap(blocks[j], dz=j)
        diffs.append(diff)

    loss = sum(jnp.sum(d * d, axis=1, keepdims=True) for d in diffs)

    pieces, totals = [], None

    def add(some, after=None):
        return grad(n, [at for at, _ in some], [e for _, e in some], decoder, totals, after)

    done = 0
    for p in range(chunks):
        err = diffs[p].astype(jnp.bfloat16)
        here = [join([err] + [swap(err, dz=j) for j in range(1, fz)], 0)]
        pieces.append(((0, 0, p, chunks), here[0]))
        for b in bits(fy):
            last = p == chunks - 1 and 2 * b >= fy
            if last:
                (totals,) = add(pieces[done:])
                done = len(pieces)
            got = [swap(e, dy=b) for e in here]
            if last:
                got = [hold(e, totals) for e in got]
            pieces += [((0, b | i, p, chunks), e) for i, e in enumerate(got)]
            here += got
        for dc in range(1, fc):
            pieces += [((dc, i, p, chunks), swap(e, dc=dc)) for i, e in enumerate(here)]
    totals, columns = add(pieces[done:-1], pieces[-1][0])
    at, e = pieces[-1]
    (back,) = grad(n, [at], [e], columns, totals, None, (indices, loss))
    error = own_rows(n, [at for at, _ in pieces], own, width, [e[:group] for _, e in pieces])

    back = jnp.sum(lax.all_to_all(back, "lat", 0, 0, tiled=True), axis=0)
    return error, back[:, k_count] / width, back[:, :k_count]


def solution(mesh):
    in_specs = (P("groups", None), P("groups", None), P("lat", None), P(("groups", "lat"), None))
    out_specs = (P(("groups", "lat"), None), P(("groups", "lat")), P(("groups", "lat"), None))
    return jax.shard_map(local, mesh=mesh, in_specs=in_specs, out_specs=out_specs, check_vma=False)
```

time: 87.8 us -> 70.2 us (0.80)
  waiting for transfers between devices: 32.9 us -> 20.1 us
  local copies, waits for them, and re-layouts: 11.4 us -> 4.06 us
  starting transfers between devices: 26.7 us -> 29.7 us
  Pallas kernels: 11.1 us -> 14 us
  other arithmetic: 3.93 us -> 1.21 us
    all_to_all x5 -> x1, waiting for transfers between devices: 27.3 us -> 4.93 us  [local(): back = jnp.sum(lax.all_to_all(back, 'lat', 0, 0, tiled=True), axis=0)]
    ppermute x10 -> x22, starting transfers between devices: 7.32 us -> 26.2 us  [swap(): return lax.ppermute(x, 'lat', pairs(n, dz, dy, dc))]
    all_to_all x5 -> x1, starting transfers between devices: 19.4 us -> 3.5 us  [local(): back = jnp.sum(lax.all_to_all(back, 'lat', 0, 0, tiled=True), axis=0)]
    ppermute x10 -> x22, waiting for transfers between devices: 5.59 us -> 15.2 us  [swap(): return lax.ppermute(x, 'lat', pairs(n, dz, dy, dc))]
    unnamed x28 -> x12, local copies, waits for them, and re-layouts: 11.2 us -> 3.1 us
    pallas_call x9 -> x6, Pallas kernels: 10.2 us -> 13.1 us  [the longest x3 6.57 us: grad(): pl.pallas_call(functools.partial(grad_kernel, n, tuple(blocks), after, fi...]
    add x4, other arithmetic: 1.6 us -> 0.2 us  [the longest x2 0.14 us: local(): total = total + swap(parts[dc], dc=dc)]
    concatenate x2, other arithmetic: 1.33 us -> 0.02 us  [join(): return xs[0] if len(xs) == 1 else jnp.concatenate(xs, axis=axis)]
  transfers between devices with their start and end apart: 15 -> 23, of which waited for: 8 -> 10; matrix products, arithmetic and copies ran while one was open for 4% -> 2% of each run, Pallas kernels for 6% -> 13%
where the time goes in v5:
time: 70.2 us; the launch traced here: 69.9 us
  starting transfers between devices  29.7 us (42%)
  waiting for transfers between devices  20.1 us (29%)
  Pallas kernels  14 us (20%)
  local copies, waits for them, and re-layouts  4.06 us (6%)
  other arithmetic  1.21 us (2%)
  between operations  0.86 us (1%)
    ppermute x22, starting transfers between devices, swap(): return lax.ppermute(x, 'lat', pairs(n, dz, dy, dc))  26.2 us
    ppermute x22, waiting for transfers between devices, swap(): return lax.ppermute(x, 'lat', pairs(n, dz, dy, dc))  15.2 us
    pallas_call x3, Pallas kernels, grad(): pl.pallas_call(functools.partial(grad_kernel, n, tuple(blocks), after, fi...  6.57 us
    pallas_call x2, Pallas kernels, decode(): pl.pallas_call(functools.partial(decode_kernel, n, rows // n, chunk, chun...  6.55 us
    all_to_all x1, waiting for transfers between devices, local(): back = jnp.sum(lax.all_to_all(back, 'lat', 0, 0, tiled=True), axis=0)  4.93 us
    all_to_all x1, starting transfers between devices, local(): back = jnp.sum(lax.all_to_all(back, 'lat', 0, 0, tiled=True), axis=0)  3.5 us
    unnamed x12, local copies, waits for them, and re-layouts  3.1 us
  transfers between devices with their start and end apart: 23, of which 10 were waited for; matrix products, arithmetic and copies ran while one was open for 2% of the time, Pallas kernels for 13%

profile of v5, /device:TPU:0, one launch (start us, length us, event | category | flops | bytes accessed | tf_op | source)
XLA Modules:
  0.0 69.9 jit_solution(10288715850422767362)
XLA Ops:
  0.6 3.8 %decode.2 = (f32[64,2048]{1,0:T(8,128)S(1)}, f32[64,2048]{1,0:T(8,128)S(1)}, bf16[64,512]{1,0:T(8,128)(2,1)S(1)}) custom-call(s32[64,64]{1,0:T(8,128)} %refs_3_.3, bf16[64,64]{1,0:T(8,128)(2,1)} %refs_1_.2, bf16[512,8192]{1,0:T(8,128)(2,1)} %refs_2_.5, bf16[4,8192]{1,0:T(4,128)(2,1)} %refs_2_.4), custom_call_target="tpu_custom_call" | custom-call | flops 268435456 | bytes 8388608 | tf_op jit(solution)/shard_map/decode/pallas_call | solution.py:150
  4.5 0.5 collective-permute-start
  5.0 1.5 %collective-permute-done = f32[64,2048]{1,0:T(8,128)S(1)} collective-permute-done((f32[64,2048]{1,0:T(8,128)S(1)}, f32[64,2048]{1,0:T(8,128)S(1)}, u32[]{:S(2)}, u32[]{:S(2)}) %collective-permute-start) | collective-permute-done | bytes 524320 | tf_op jit(solution)/shard_map/ppermute | solution.py:298
  6.5 0.1 add.52
  6.6 2.9 %collective-permute-start.1 = (f32[64,1024]{1,0:T(8,128)S(1)}, f32[64,1024]{1,0:T(8,128)S(1)}, u32[]{:S(2)}, u32[]{:S(2)}) collective-permute-start(f32[64,1024]{1,0:T(8,128)S(1)} %slice.49.refs_3_), channel_id=1, source_target_pairs={{0,2},{1,3},{2,0},{3,1},{4,6},{5,7},{6,4},{7,5},{8,10},{9,11},{10,... | collective-permute-start | bytes 786440 | tf_op jit(solution)/shard_map/ppermute | solution.py:298
  9.6 2.7 %decode.3 = (f32[64,2048]{1,0:T(8,128)S(1)}, f32[64,2048]{1,0:T(8,128)S(1)}) custom-call(bf16[64,512]{1,0:T(8,128)(2,1)S(1)} %get-tuple-element.12.refs_0_, bf16[512,8192]{1,0:T(8,128)(2,1)} %refs_2_.5, bf16[4,8192]{1,0:T(4,128)(2,1)} %refs_2_.4, f32[64,1024]{1,0:T(8,128)S(1)} %slice.49.refs_3_), custom_call_target="tpu_custom_call" | custom-call | flops 268435456 | bytes 8388608 | tf_op jit(solution)/shard_map/decode/pallas_call | solution.py:150
  12.3 0.1 collective-permute-start.11
  12.4 3.8 %collective-permute-done.1 = f32[64,1024]{1,0:T(8,128)S(1)} collective-permute-done((f32[64,1024]{1,0:T(8,128)S(1)}, f32[64,1024]{1,0:T(8,128)S(1)}, u32[]{:S(2)}, u32[]{:S(2)}) %collective-permute-start.1) | collective-permute-done | bytes 262176 | tf_op jit(solution)/shard_map/ppermute | solution.py:298
  16.3 1.9 %collective-permute-start.2 = (f32[16,1024]{1,0:T(8,128)S(1)}, f32[16,1024]{1,0:T(8,128)S(1)}, u32[]{:S(2)}, u32[]{:S(2)}) collective-permute-start(f32[16,1024]{1,0:T(8,128)S(1)} %get-tuple-element.24), channel_id=1, source_target_pairs={{0,4},{1,5},{2,6},{3,7},{4,0},{5,1},{6,2},{7,3},{8,12},{9,13},{10,... | collective-permute-start | bytes 196616 | tf_op jit(solution)/shard_map/ppermute | solution.py:298
  18.1 2.5 %collective-permute-start.4 = (f32[16,1024]{1,0:T(8,128)S(1)}, f32[16,1024]{1,0:T(8,128)S(1)}, u32[]{:S(2)}, u32[]{:S(2)}) collective-permute-start(f32[16,1024]{1,0:T(8,128)S(1)} %get-tuple-element.25), channel_id=1, source_target_pairs={{0,12},{1,13},{2,14},{3,15},{4,8},{5,9},{6,10},{7,11},{8,4},{9,5},... | collective-permute-start | bytes 196616 | tf_op jit(solution)/shard_map/ppermute | solution.py:298
  20.6 0.1 collective-permute-start.3
  20.7 0.0 collective-permute-done.11
  20.7 0.1 add.61
  20.8 1.6 %collective-permute-start.12 = (f32[64,1024]{1,0:T(8,128)S(1)}, f32[64,1024]{1,0:T(8,128)S(1)}, u32[]{:S(2)}, u32[]{:S(2)}) collective-permute-start(f32[64,1024]{1,0:T(8,128)S(1)} %slice.54), channel_id=1, source_target_pairs={{0,2},{1,3},{2,0},{3,1},{4,6},{5,7},{6,4},{7,5},{8,10},{9,11},{10,... | collective-permute-start | bytes 786440 | tf_op jit(solution)/shard_map/ppermute | solution.py:298
  22.4 0.0 collective-permute-done.2
  22.4 2.0 %collective-permute-done.4 = f32[16,1024]{1,0:T(8,128)S(1)} collective-permute-done((f32[16,1024]{1,0:T(8,128)S(1)}, f32[16,1024]{1,0:T(8,128)S(1)}, u32[]{:S(2)}, u32[]{:S(2)}) %collective-permute-start.4) | collective-permute-done | bytes 65568 | tf_op jit(solution)/shard_map/ppermute | solution.py:298
  24.5 2.1 %collective-permute-done.3 = f32[16,1024]{1,0:T(8,128)S(1)} collective-permute-done((f32[16,1024]{1,0:T(8,128)S(1)}, f32[16,1024]{1,0:T(8,128)S(1)}, u32[]{:S(2)}, u32[]{:S(2)}) %collective-permute-start.3) | collective-permute-done | bytes 65568 | tf_op jit(solution)/shard_map/ppermute | solution.py:298
  26.6 0.1 multiply_reduce_fusion.1
  26.7 2.8 %collective-permute-start.7 = (bf16[16,1024]{1,0:T(8,128)(2,1)S(1)}, bf16[16,1024]{1,0:T(8,128)(2,1)S(1)}, u32[]{:S(2)}, u32[]{:S(2)}) collective-permute-start(bf16[16,1024]{1,0:T(8,128)(2,1)S(1)} %get-tuple-element.20.refs_0_), channel_id=1, source_target_pairs={{0,12},{1,13},{2,14},{3,15},{4,8},{5,9},{6,10},{7,11},{8,4},{9,5},... | collective-permute-start | bytes 98312 | tf_op jit(solution)/shard_map/ppermute | solution.py:298
  29.5 0.0 collective-permute-start.6
  29.5 1.7 %collective-permute-start.5 = (bf16[16,1024]{1,0:T(8,128)(2,1)S(1)}, bf16[16,1024]{1,0:T(8,128)(2,1)S(1)}, u32[]{:S(2)}, u32[]{:S(2)}) collective-permute-start(bf16[16,1024]{1,0:T(8,128)(2,1)S(1)} %get-tuple-element.20.refs_0_), channel_id=1, source_target_pairs={{0,4},{1,5},{2,6},{3,7},{4,0},{5,1},{6,2},{7,3},{8,12},{9,13},{10,... | collective-permute-start | bytes 98312 | tf_op jit(solution)/shard_map/ppermute | solution.py:298
  31.1 0.0 collective-permute-done.12
  31.2 0.4 collective-permute-start.13
  31.6 2.4 %collective-permute-start.15 = (f32[16,1024]{1,0:T(8,128)S(1)}, f32[16,1024]{1,0:T(8,128)S(1)}, u32[]{:S(2)}, u32[]{:S(2)}) collective-permute-start(f32[16,1024]{1,0:T(8,128)S(1)} %get-tuple-element.22), channel_id=1, source_target_pairs={{0,12},{1,13},{2,14},{3,15},{4,8},{5,9},{6,10},{7,11},{8,4},{9,5},... | collective-permute-start | bytes 196616 | tf_op jit(solution)/shard_map/ppermute | solution.py:298
  34.1 0.0 collective-permute-done.7
  34.1 0.7 collective-permute-start.14
  34.8 0.2 collective-permute-done.6
  34.9 0.0 collective-permute-done.5
  34.9 1.6 %collective-permute-start.8 = (bf16[64,1024]{1,0:T(8,128)(2,1)S(1)}, bf16[64,1024]{1,0:T(8,128)(2,1)S(1)}, u32[]{:S(2)}, u32[]{:S(2)}) collective-permute-start(bf16[64,1024]{1,0:T(8,128)(2,1)S(1)} %pad_maximum_fusion.refs_0_), channel_id=1, source_target_pairs={{0,2},{1,3},{2,0},{3,1},{4,6},{5,7},{6,4},{7,5},{8,10},{9,11},{10,... | collective-permute-start | bytes 393224 | tf_op jit(solution)/shard_map/ppermute | solution.py:298
  36.5 0.0 collective-permute-done.13
  36.5 1.3 %collective-permute-done.15 = f32[16,1024]{1,0:T(8,128)S(1)} collective-permute-done((f32[16,1024]{1,0:T(8,128)S(1)}, f32[16,1024]{1,0:T(8,128)S(1)}, u32[]{:S(2)}, u32[]{:S(2)}) %collective-permute-start.15) | collective-permute-done | bytes 65568 | tf_op jit(solution)/shard_map/ppermute | solution.py:298
  37.8 2.3 %collective-permute-done.14 = f32[16,1024]{1,0:T(8,128)S(1)} collective-permute-done((f32[16,1024]{1,0:T(8,128)S(1)}, f32[16,1024]{1,0:T(8,128)S(1)}, u32[]{:S(2)}, u32[]{:S(2)}) %collective-permute-start.14) | collective-permute-done | bytes 65568 | tf_op jit(solution)/shard_map/ppermute | solution.py:298
  40.1 0.1 multiply_reduce_fusion
  40.2 2.1 %collective-permute-start.18 = (bf16[16,1024]{1,0:T(8,128)(2,1)S(1)}, bf16[16,1024]{1,0:T(8,128)(2,1)S(1)}, u32[]{:S(2)}, u32[]{:S(2)}) collective-permute-start(bf16[16,1024]{1,0:T(8,128)(2,1)S(1)} %get-tuple-element.18.refs_4_), channel_id=1, source_target_pairs={{0,12},{1,13},{2,14},{3,15},{4,8},{5,9},{6,10},{7,11},{8,4},{9,5},... | collective-permute-start | bytes 98312 | tf_op jit(solution)/shard_map/ppermute | solution.py:298
  42.4 0.0 collective-permute-start.17
  42.4 2.3 %collective-permute-start.16 = (bf16[16,1024]{1,0:T(8,128)(2,1)S(1)}, bf16[16,1024]{1,0:T(8,128)(2,1)S(1)}, u32[]{:S(2)}, u32[]{:S(2)}) collective-permute-start(bf16[16,1024]{1,0:T(8,128)(2,1)S(1)} %get-tuple-element.18.refs_4_), channel_id=1, source_target_pairs={{0,4},{1,5},{2,6},{3,7},{4,0},{5,1},{6,2},{7,3},{8,12},{9,13},{10,... | collective-permute-start | bytes 98312 | tf_op jit(solution)/shard_map/ppermute | solution.py:298
  44.7 0.0 collective-permute-start.9
  44.7 0.0 collective-permute-done.8.refs_1_
  44.7 0.5 collective-permute-start.10
  45.2 0.8 %collective-permute-done.18 = bf16[16,1024]{1,0:T(8,128)(2,1)S(1)} collective-permute-done((bf16[16,1024]{1,0:T(8,128)(2,1)S(1)}, bf16[16,1024]{1,0:T(8,128)(2,1)S(1)}, u32[]{:S(2)}, u32[]{:S(2)}) %collective-permute-start.18) | collective-permute-done | bytes 32800 | tf_op jit(solution)/shard_map/ppermute | solution.py:298
  46.0 1.2 %collective-permute-done.17 = bf16[16,1024]{1,0:T(8,128)(2,1)S(1)} collective-permute-done((bf16[16,1024]{1,0:T(8,128)(2,1)S(1)}, bf16[16,1024]{1,0:T(8,128)(2,1)S(1)}, u32[]{:S(2)}, u32[]{:S(2)}) %collective-permute-start.17) | collective-permute-done | bytes 32800 | tf_op jit(solution)/shard_map/ppermute | solution.py:298
  47.2 0.0 collective-permute-done.16
  47.2 0.0 copy-start.4
  47.2 1.6 %collective-permute-start.19 = (bf16[64,1024]{1,0:T(8,128)(2,1)S(1)}, bf16[64,1024]{1,0:T(8,128)(2,1)S(1)}, u32[]{:S(2)}, u32[]{:S(2)}) collective-permute-start(bf16[64,1024]{1,0:T(8,128)(2,1)S(1)} %pad_maximum_fusion.1.refs_4_), channel_id=1, source_target_pairs={{0,2},{1,3},{2,0},{3,1},{4,6},{5,7},{6,4},{7,5},{8,10},{9,11},{10,... | collective-permute-start | bytes 393224 | tf_op jit(solution)/shard_map/ppermute | solution.py:298
  48.8 0.0 collective-permute-start.20
  48.8 0.0 collective-permute-done.9.refs_2_
  48.8 0.0 collective-permute-done.10.refs_3_
  48.8 3.4 %grad.3.refs_1_.refs_3_ = f32[64,512]{1,0:T(8,128)S(1)} custom-call(bf16[64,1024]{1,0:T(8,128)(2,1)S(1)} %pad_maximum_fusion.refs_0_, bf16[64,1024]{1,0:T(8,128)(2,1)S(1)} %collective-permute-done.8.refs_1_, bf16[64,1024]{1,0:T(8,128)(2,1)S(1)} %collective-permute-done.9.refs_2_, bf16[64,1024]{1,0:T(8,128)(2,1)S(1)} %collective-permute-done.10.refs_3_, ...), custom_call_target="tpu_custom_call" | custom-call | flops 335544320 | bytes 10485760 | tf_op jit(solution)/shard_map/grad/pallas_call | solution.py:250
  52.2 0.6 copy-done
  52.8 0.0 collective-permute-done.19.refs_0_
  52.8 0.7 copy-done.2
  53.5 0.5 collective-permute-start.21
  54.0 0.1 copy.8.refs_4_
  54.1 0.0 collective-permute-done.20.refs_1_
  54.1 0.9 %copy-done.1 = f32[64,512]{1,0:T(8,128)S(1)} copy-done((f32[64,512]{1,0:T(8,128)S(1)}, f32[64,512]{1,0:T(8,128)}, u32[]{:S(2)}) %copy-start.1) | copy-done | bytes 131096
  55.0 0.9 %copy-done.3 = bf16[64,1024]{1,0:T(8,128)(2,1)S(1)} copy-done((bf16[64,1024]{1,0:T(8,128)(2,1)S(1)}, bf16[64,1024]{1,0:T(8,128)(2,1)}, u32[]{:S(2)}) %copy-start.3) | copy-done | bytes 131096
  55.9 2.0 %grad.4 = (f32[64,512]{1,0:T(8,128)S(1)}, bf16[512,1024]{1,0:T(8,128)(2,1)S(1)}) custom-call(bf16[64,1024]{1,0:T(8,128)(2,1)S(1)} %copy-done.3, bf16[64,1024]{1,0:T(8,128)(2,1)S(1)} %collective-permute-done.20.refs_1_, bf16[512,8192]{1,0:T(8,128)(2,1)} %refs_2_.5, f32[64,512]{1,0:T(8,128)S(1)} %copy-done.1), custom_call_target="tpu_custom_call" | custom-call | flops 134217728 | bytes 4194304 | tf_op jit(solution)/shard_map/grad/pallas_call | solution.py:250
  57.9 0.0 collective-permute-done.21.refs_0_
  57.9 1.2 %grad.5 = f32[16,4,128]{2,1,0:T(4,128)} custom-call(bf16[64,1024]{1,0:T(8,128)(2,1)S(1)} %collective-permute-done.21.refs_0_, bf16[512,1024]{1,0:T(8,128)(2,1)S(1)} %get-tuple-element.15.refs_1_, f32[64,512]{1,0:T(8,128)S(1)} %get-tuple-element.16.refs_2_, s32[64,64]{1,0:T(8,128)S(1)} %copy-done.4, f32[16,1]{1,0:T(8,128)S(1)} %copy.8.refs_4_), custom_call_target="tpu_custom_call" | custom-call | flops 67108864 | bytes 2097152 | tf_op jit(solution)/shard_map/grad/pallas_call | solution.py:250
  59.1 3.5 %all-to-all-start = ((f32[16,4,128]{2,1,0:T(4,128)}), f32[16,4,128]{2,1,0:T(4,128)S(1)}, u32[]{:S(2)}, u32[]{:S(2)}) async-start(f32[16,4,128]{2,1,0:T(4,128)} %grad.5), calls=%async_computation | async-start | bytes 65536 | tf_op jit(solution)/shard_map/all_to_all | solution.py:357
  62.6 0.8 %slice.55.refs_5_ = bf16[16,1024]{1,0:T(8,128)(2,1)S(1)} slice(bf16[64,1024]{1,0:T(8,128)(2,1)} %hold.1.refs_0_), slice={[0:16], [0:1024]} | slice | bytes 65536 | tf_op jit(solution)/shard_map/slice | solution.py:355
  63.4 0.9 %own_rows.1 = bf16[4,8192]{1,0:T(4,128)(2,1)} custom-call(bf16[16,1024]{1,0:T(8,128)(2,1)S(1)} %get-tuple-element.20.refs_0_, bf16[16,1024]{1,0:T(8,128)(2,1)S(1)} %slice.50.refs_1_, bf16[16,1024]{1,0:T(8,128)(2,1)S(1)} %slice.51.refs_2_, bf16[16,1024]{1,0:T(8,128)(2,1)S(1)} %slice.52.refs_3_, bf16[16,1024]{1,0:T(8,128)(2,1)S(1)} %get-tuple-element.18.refs_4_, ...), custom_call_target="tpu_custom_call" | custom-call | tf_op jit(solution)/shard_map/own_rows/pallas_call | solution.py:276
  64.3 4.9 %all-to-all-done = f32[16,4,128]{2,1,0:T(4,128)S(1)} async-done(((f32[16,4,128]{2,1,0:T(4,128)}), f32[16,4,128]{2,1,0:T(4,128)S(1)}, u32[]{:S(2)}, u32[]{:S(2)}) %all-to-all-start) | async-done | bytes 32800 | tf_op jit(solution)/shard_map/all_to_all | solution.py:357
  69.2 0.7 multiply_reduce_fusion.2
  (23 shorter events, 0.2 us)
Async XLA Ops:
  4.5 2.1 %collective-permute-start = (f32[64,2048]{1,0:T(8,128)S(1)}, f32[64,2048]{1,0:T(8,128)S(1)}, u32[]{:S(2)}, u32[]{:S(2)}) collective-permute-start(f32[64,2048]{1,0:T(8,128)S(1)} %get-tuple-element.11), channel_id=1, source_target_pairs={{0,1},{1,0},{2,3},{3,2},{4,5},{5,4},{6,7},{7,6},{8,9},{9,8},{10,11... | collective-permute-start | bytes 1572872 | tf_op jit(solution)/shard_map/ppermute | solution.py:298
  6.6 9.6 %collective-permute-start.1 = (f32[64,1024]{1,0:T(8,128)S(1)}, f32[64,1024]{1,0:T(8,128)S(1)}, u32[]{:S(2)}, u32[]{:S(2)}) collective-permute-start(f32[64,1024]{1,0:T(8,128)S(1)} %slice.49.refs_3_), channel_id=1, source_target_pairs={{0,2},{1,3},{2,0},{3,1},{4,6},{5,7},{6,4},{7,5},{8,10},{9,11},{10,... | collective-permute-start | bytes 786440 | tf_op jit(solution)/shard_map/ppermute | solution.py:298
  12.3 8.4 %collective-permute-start.11 = (f32[64,2048]{1,0:T(8,128)S(1)}, f32[64,2048]{1,0:T(8,128)S(1)}, u32[]{:S(2)}, u32[]{:S(2)}) collective-permute-start(f32[64,2048]{1,0:T(8,128)S(1)} %get-tuple-element.14), channel_id=1, source_target_pairs={{0,1},{1,0},{2,3},{3,2},{4,5},{5,4},{6,7},{7,6},{8,9},{9,8},{10,11... | collective-permute-start | bytes 1572872 | tf_op jit(solution)/shard_map/ppermute | solution.py:298
  16.3 6.1 %collective-permute-start.2 = (f32[16,1024]{1,0:T(8,128)S(1)}, f32[16,1024]{1,0:T(8,128)S(1)}, u32[]{:S(2)}, u32[]{:S(2)}) collective-permute-start(f32[16,1024]{1,0:T(8,128)S(1)} %get-tuple-element.24), channel_id=1, source_target_pairs={{0,4},{1,5},{2,6},{3,7},{4,0},{5,1},{6,2},{7,3},{8,12},{9,13},{10,... | collective-permute-start | bytes 196616 | tf_op jit(solution)/shard_map/ppermute | solution.py:298
  18.1 6.3 %collective-permute-start.4 = (f32[16,1024]{1,0:T(8,128)S(1)}, f32[16,1024]{1,0:T(8,128)S(1)}, u32[]{:S(2)}, u32[]{:S(2)}) collective-permute-start(f32[16,1024]{1,0:T(8,128)S(1)} %get-tuple-element.25), channel_id=1, source_target_pairs={{0,12},{1,13},{2,14},{3,15},{4,8},{5,9},{6,10},{7,11},{8,4},{9,5},... | collective-permute-start | bytes 196616 | tf_op jit(solution)/shard_map/ppermute | solution.py:298
  20.6 5.9 %collective-permute-start.3 = (f32[16,1024]{1,0:T(8,128)S(1)}, f32[16,1024]{1,0:T(8,128)S(1)}, u32[]{:S(2)}, u32[]{:S(2)}) collective-permute-start(f32[16,1024]{1,0:T(8,128)S(1)} %get-tuple-element.26), channel_id=1, source_target_pairs={{0,8},{1,9},{2,10},{3,11},{4,12},{5,13},{6,14},{7,15},{8,0},{9,1},... | collective-permute-start | bytes 196616 | tf_op jit(solution)/shard_map/ppermute | solution.py:298
  20.8 10.3 %collective-permute-start.12 = (f32[64,1024]{1,0:T(8,128)S(1)}, f32[64,1024]{1,0:T(8,128)S(1)}, u32[]{:S(2)}, u32[]{:S(2)}) collective-permute-start(f32[64,1024]{1,0:T(8,128)S(1)} %slice.54), channel_id=1, source_target_pairs={{0,2},{1,3},{2,0},{3,1},{4,6},{5,7},{6,4},{7,5},{8,10},{9,11},{10,... | collective-permute-start | bytes 786440 | tf_op jit(solution)/shard_map/ppermute | solution.py:298
  26.7 7.4 %collective-permute-start.7 = (bf16[16,1024]{1,0:T(8,128)(2,1)S(1)}, bf16[16,1024]{1,0:T(8,128)(2,1)S(1)}, u32[]{:S(2)}, u32[]{:S(2)}) collective-permute-start(bf16[16,1024]{1,0:T(8,128)(2,1)S(1)} %get-tuple-element.20.refs_0_), channel_id=1, source_target_pairs={{0,12},{1,13},{2,14},{3,15},{4,8},{5,9},{6,10},{7,11},{8,4},{9,5},... | collective-permute-start | bytes 98312 | tf_op jit(solution)/shard_map/ppermute | solution.py:298
  29.5 5.4 %collective-permute-start.6 = (bf16[16,1024]{1,0:T(8,128)(2,1)S(1)}, bf16[16,1024]{1,0:T(8,128)(2,1)S(1)}, u32[]{:S(2)}, u32[]{:S(2)}) collective-permute-start(bf16[16,1024]{1,0:T(8,128)(2,1)S(1)} %get-tuple-element.20.refs_0_), channel_id=1, source_target_pairs={{0,8},{1,9},{2,10},{3,11},{4,12},{5,13},{6,14},{7,15},{8,0},{9,1},... | collective-permute-start | bytes 98312 | tf_op jit(solution)/shard_map/ppermute | solution.py:298
  29.5 5.4 %collective-permute-start.5 = (bf16[16,1024]{1,0:T(8,128)(2,1)S(1)}, bf16[16,1024]{1,0:T(8,128)(2,1)S(1)}, u32[]{:S(2)}, u32[]{:S(2)}) collective-permute-start(bf16[16,1024]{1,0:T(8,128)(2,1)S(1)} %get-tuple-element.20.refs_0_), channel_id=1, source_target_pairs={{0,4},{1,5},{2,6},{3,7},{4,0},{5,1},{6,2},{7,3},{8,12},{9,13},{10,... | collective-permute-start | bytes 98312 | tf_op jit(solution)/shard_map/ppermute | solution.py:298
  31.2 5.3 %collective-permute-start.13 = (f32[16,1024]{1,0:T(8,128)S(1)}, f32[16,1024]{1,0:T(8,128)S(1)}, u32[]{:S(2)}, u32[]{:S(2)}) collective-permute-start(f32[16,1024]{1,0:T(8,128)S(1)} %get-tuple-element.21), channel_id=1, source_target_pairs={{0,4},{1,5},{2,6},{3,7},{4,0},{5,1},{6,2},{7,3},{8,12},{9,13},{10,... | collective-permute-start | bytes 196616 | tf_op jit(solution)/shard_map/ppermute | solution.py:298
  31.6 6.2 %collective-permute-start.15 = (f32[16,1024]{1,0:T(8,128)S(1)}, f32[16,1024]{1,0:T(8,128)S(1)}, u32[]{:S(2)}, u32[]{:S(2)}) collective-permute-start(f32[16,1024]{1,0:T(8,128)S(1)} %get-tuple-element.22), channel_id=1, source_target_pairs={{0,12},{1,13},{2,14},{3,15},{4,8},{5,9},{6,10},{7,11},{8,4},{9,5},... | collective-permute-start | bytes 196616 | tf_op jit(solution)/shard_map/ppermute | solution.py:298
  34.1 6.0 %collective-permute-start.14 = (f32[16,1024]{1,0:T(8,128)S(1)}, f32[16,1024]{1,0:T(8,128)S(1)}, u32[]{:S(2)}, u32[]{:S(2)}) collective-permute-start(f32[16,1024]{1,0:T(8,128)S(1)} %get-tuple-element.23), channel_id=1, source_target_pairs={{0,8},{1,9},{2,10},{3,11},{4,12},{5,13},{6,14},{7,15},{8,0},{9,1},... | collective-permute-start | bytes 196616 | tf_op jit(solution)/shard_map/ppermute | solution.py:298
  34.9 9.8 %collective-permute-start.8 = (bf16[64,1024]{1,0:T(8,128)(2,1)S(1)}, bf16[64,1024]{1,0:T(8,128)(2,1)S(1)}, u32[]{:S(2)}, u32[]{:S(2)}) collective-permute-start(bf16[64,1024]{1,0:T(8,128)(2,1)S(1)} %pad_maximum_fusion.refs_0_), channel_id=1, source_target_pairs={{0,2},{1,3},{2,0},{3,1},{4,6},{5,7},{6,4},{7,5},{8,10},{9,11},{10,... | collective-permute-start | bytes 393224 | tf_op jit(solution)/shard_map/ppermute | solution.py:298
  40.2 5.8 %collective-permute-start.18 = (bf16[16,1024]{1,0:T(8,128)(2,1)S(1)}, bf16[16,1024]{1,0:T(8,128)(2,1)S(1)}, u32[]{:S(2)}, u32[]{:S(2)}) collective-permute-start(bf16[16,1024]{1,0:T(8,128)(2,1)S(1)} %get-tuple-element.18.refs_4_), channel_id=1, source_target_pairs={{0,12},{1,13},{2,14},{3,15},{4,8},{5,9},{6,10},{7,11},{8,4},{9,5},... | collective-permute-start | bytes 98312 | tf_op jit(solution)/shard_map/ppermute | solution.py:298
  42.4 4.8 %collective-permute-start.17 = (bf16[16,1024]{1,0:T(8,128)(2,1)S(1)}, bf16[16,1024]{1,0:T(8,128)(2,1)S(1)}, u32[]{:S(2)}, u32[]{:S(2)}) collective-permute-start(bf16[16,1024]{1,0:T(8,128)(2,1)S(1)} %get-tuple-element.18.refs_4_), channel_id=1, source_target_pairs={{0,8},{1,9},{2,10},{3,11},{4,12},{5,13},{6,14},{7,15},{8,0},{9,1},... | collective-permute-start | bytes 98312 | tf_op jit(solution)/shard_map/ppermute | solution.py:298
  42.4 4.8 %collective-permute-start.16 = (bf16[16,1024]{1,0:T(8,128)(2,1)S(1)}, bf16[16,1024]{1,0:T(8,128)(2,1)S(1)}, u32[]{:S(2)}, u32[]{:S(2)}) collective-permute-start(bf16[16,1024]{1,0:T(8,128)(2,1)S(1)} %get-tuple-element.18.refs_4_), channel_id=1, source_target_pairs={{0,4},{1,5},{2,6},{3,7},{4,0},{5,1},{6,2},{7,3},{8,12},{9,13},{10,... | collective-permute-start | bytes 98312 | tf_op jit(solution)/shard_map/ppermute | solution.py:298
  44.7 4.1 %collective-permute-start.9 = (bf16[64,1024]{1,0:T(8,128)(2,1)S(1)}, bf16[64,1024]{1,0:T(8,128)(2,1)S(1)}, u32[]{:S(2)}, u32[]{:S(2)}) collective-permute-start(bf16[64,1024]{1,0:T(8,128)(2,1)S(1)} %pad_maximum_fusion.refs_0_), channel_id=1, source_target_pairs={{0,1},{1,0},{2,3},{3,2},{4,5},{5,4},{6,7},{7,6},{8,9},{9,8},{10,11... | collective-permute-start | bytes 393224 | tf_op jit(solution)/shard_map/ppermute | solution.py:298
  44.7 4.1 %collective-permute-start.10 = (bf16[64,1024]{1,0:T(8,128)(2,1)S(1)}, bf16[64,1024]{1,0:T(8,128)(2,1)S(1)}, u32[]{:S(2)}, u32[]{:S(2)}) collective-permute-start(bf16[64,1024]{1,0:T(8,128)(2,1)S(1)} %collective-permute-done.8.refs_1_), channel_id=1, source_target_pairs={{0,1},{1,0},{2,3},{3,2},{4,5},{5,4},{6,7},{7,6},{8,9},{9,8},{10,11... | collective-permute-start | bytes 393224 | tf_op jit(solution)/shard_map/ppermute | solution.py:298
  47.2 10.7 %copy-start.4 = (s32[64,64]{1,0:T(8,128)S(1)}, s32[64,64]{1,0:T(8,128)}, u32[]{:S(2)}) copy-start(s32[64,64]{1,0:T(8,128)} %refs_3_.3) | copy-start | bytes 49156
  47.2 5.6 %collective-permute-start.19 = (bf16[64,1024]{1,0:T(8,128)(2,1)S(1)}, bf16[64,1024]{1,0:T(8,128)(2,1)S(1)}, u32[]{:S(2)}, u32[]{:S(2)}) collective-permute-start(bf16[64,1024]{1,0:T(8,128)(2,1)S(1)} %pad_maximum_fusion.1.refs_4_), channel_id=1, source_target_pairs={{0,2},{1,3},{2,0},{3,1},{4,6},{5,7},{6,4},{7,5},{8,10},{9,11},{10,... | collective-permute-start | bytes 393224 | tf_op jit(solution)/shard_map/ppermute | solution.py:298
  48.8 5.3 %collective-permute-start.20 = (bf16[64,1024]{1,0:T(8,128)(2,1)S(1)}, bf16[64,1024]{1,0:T(8,128)(2,1)S(1)}, u32[]{:S(2)}, u32[]{:S(2)}) collective-permute-start(bf16[64,1024]{1,0:T(8,128)(2,1)S(1)} %pad_maximum_fusion.1.refs_4_), channel_id=1, source_target_pairs={{0,1},{1,0},{2,3},{3,2},{4,5},{5,4},{6,7},{7,6},{8,9},{9,8},{10,11... | collective-permute-start | bytes 393224 | tf_op jit(solution)/shard_map/ppermute | solution.py:298
  52.2 0.6 copy-start
  52.8 0.7 copy-start.2
  53.5 4.4 %collective-permute-start.21 = (bf16[64,1024]{1,0:T(8,128)(2,1)}, bf16[64,1024]{1,0:T(8,128)(2,1)S(1)}, u32[]{:S(2)}, u32[]{:S(2)}) collective-permute-start(bf16[64,1024]{1,0:T(8,128)(2,1)} %hold.1.refs_0_), channel_id=1, source_target_pairs={{0,1},{1,0},{2,3},{3,2},{4,5},{5,4},{6,7},{7,6},{8,9},{9,8},{10,11... | collective-permute-start | bytes 393224 | tf_op jit(solution)/shard_map/ppermute | solution.py:298
  54.1 0.9 %copy-start.1 = (f32[64,512]{1,0:T(8,128)S(1)}, f32[64,512]{1,0:T(8,128)}, u32[]{:S(2)}) copy-start(f32[64,512]{1,0:T(8,128)} %copy-done) | copy-start | bytes 393220
  55.0 0.9 %copy-start.3 = (bf16[64,1024]{1,0:T(8,128)(2,1)S(1)}, bf16[64,1024]{1,0:T(8,128)(2,1)}, u32[]{:S(2)}) copy-start(bf16[64,1024]{1,0:T(8,128)(2,1)} %hold.1.refs_0_) | copy-start | bytes 393220
  59.1 10.1 %all-to-all-start = ((f32[16,4,128]{2,1,0:T(4,128)}), f32[16,4,128]{2,1,0:T(4,128)S(1)}, u32[]{:S(2)}, u32[]{:S(2)}) async-start(f32[16,4,128]{2,1,0:T(4,128)} %grad.5), calls=%async_computation | async-start | bytes 65536 | tf_op jit(solution)/shard_map/all_to_all | solution.py:357
  69.2 0.7 %copy-start.5 = (f32[4,128]{1,0:T(4,128)}, f32[4,128]{1,0:T(4,128)S(1)}, u32[]{:S(2)}) copy-start(f32[4,128]{1,0:T(4,128)S(1)} %reduce_sum.29) | copy-start | bytes 6148

commit v6 on v5

--- a/solution.py
+++ b/solution.py
@@ -12,7 +12,6 @@
 LANES = 128
 VMEM = pl.BlockSpec(memory_space=pltpu.VMEM)
 HBM = pl.BlockSpec(memory_space=pltpu.HBM)
-ANY = pl.BlockSpec(memory_space=pl.ANY)
 
 
 def factors(n):
@@ -55,6 +54,10 @@
     return pltpu.with_memory_space_constraint(x, pltpu.HBM)
 
 
+def in_vmem(x):
+    return pltpu.with_memory_space_constraint(x, pltpu.VMEM)
+
+
 def column(n, chunk, chunks, sub, dy, dc):
     _, fy, fc = factors(n)
     _, y, c = place(n, lax.axis_index("lat"))
@@ -65,44 +68,41 @@
     return pl.pallas_call(
         lambda *refs: None,
         out_shape=jax.ShapeDtypeStruct(x.shape, x.dtype),
-        in_specs=[ANY] * (1 + len(after)),
-        out_specs=ANY,
+        in_specs=[VMEM] * (1 + len(after)),
+        out_specs=VMEM,
         input_output_aliases={0: 0},
+        compiler_params=params(),
         name="hold",
-    )(x, *after)
+    )(*[in_vmem(a) for a in (x, *after)])
 
 
 def load(decoder_hbm, col, buf, sem):
     return pltpu.make_async_copy(decoder_hbm.at[:, pl.ds(col, buf.shape[1])], buf, sem)
 
 
-def decode_kernel(n, own, chunk, chunks, first, *refs):
+def decode_kernel(n, own, chunks, parts, first, *refs):
     fz, fy, fc = factors(n)
     me = lax.axis_index("lat")
     if first:
-        ids_hbm, codes_hbm, decoder_hbm, targets_hbm = refs[:4]
-        outs, dense_ref = refs[4 : 4 + fc], refs[4 + fc]
-        buf, sem, targets_ref, small, ids_ref, codes_ref = refs[5 + fc :]
-        pairs_in = ((ids_hbm, ids_ref), (codes_hbm, codes_ref), (targets_hbm, targets_ref))
+        ids_hbm, codes_hbm, decoder_hbm, targets_hbm, out_ref, dense_ref = refs[:6]
+        buf, sem, targets_ref, small, ids_ref, codes_ref = refs[6:]
+        smalls_in = [(ids_hbm, ids_ref), (codes_hbm, codes_ref), (targets_hbm, targets_ref)]
     else:
-        dense_ref, decoder_hbm, targets_hbm, _ = refs[:4]
-        outs = refs[4 : 4 + fc]
-        buf, sem, targets_ref, small = refs[4 + fc :]
-        pairs_in = ((targets_hbm, targets_ref),)
-    sub = buf.shape[3]
-    smalls = [pltpu.make_async_copy(a, b, small.at[i]) for i, (a, b) in enumerate(pairs_in)]
+        dense_ref, decoder_hbm, targets_hbm = refs[:3]
+        out_ref, buf, sem, targets_ref, small = refs[-5:]
+        smalls_in = [(targets_hbm, targets_ref)]
+    smalls = [pltpu.make_async_copy(a, b, small.at[i]) for i, (a, b) in enumerate(smalls_in)]
     for copy in smalls:
         copy.start()
-    blocks = [(dc, o) for dc in reversed(range(fc)) for o in reversed(range(fy))]
-    cols = {at: column(n, chunk, chunks, sub, at[1], at[0]) for at in blocks}
-    loads = {at: load(decoder_hbm, cols[at], buf.at[at], sem.at[at]) for at in blocks}
-    for at in blocks:
-        loads[at].start()
+    lat_dev, sub = buf.shape[1:]
+    cols = [column(n, p, chunks, sub, o, dc) for p, dc in parts for o in range(fy)]
+    loads = [load(decoder_hbm, col, buf.at[i], sem.at[i]) for i, col in enumerate(cols)]
+    for copy in loads:
+        copy.start()
     for copy in smalls:
         copy.wait()
     if first:
         rows, k_count = ids_ref.shape
-        lat_dev = decoder_hbm.shape[0]
         lanes = lax.broadcasted_iota(jnp.int32, (ROW_STEP, lat_dev), 1) + me * lat_dev
 
         def body(g, carry):
@@ -120,50 +120,55 @@
     row = lax.broadcasted_iota(jnp.int32, (rows, own), 0)
     want = lax.broadcasted_iota(jnp.int32, (rows, own), 1) + me * own
     mine = jnp.where(row == want, -1.0, 0.0).astype(jnp.bfloat16)
-    for dc, o in blocks:
-        loads[dc, o].wait()
-        part = jnp.dot(dense_ref[...], buf[dc, o], preferred_element_type=jnp.float32)
+    for i, col in enumerate(cols):
+        loads[i].wait()
+        part = jnp.dot(dense_ref[...], buf[i], preferred_element_type=jnp.float32)
         part += jnp.dot(
-            mine, targets_ref[:, pl.ds(cols[dc, o], sub)], preferred_element_type=jnp.float32
+            mine, targets_ref[:, pl.ds(col, sub)], preferred_element_type=jnp.float32
         )
-        outs[dc][:, o * sub : (o + 1) * sub] = part
-
-
-def decode(n, chunk, chunks, sub, ids, codes, dense, decoder, targets, after):
-    _, fy, fc = factors(n)
-    rows, lat_dev = ids.shape[0], decoder.shape[0]
-    first = dense is None
-    out = [pltpu.VMEM((rows, fy * sub), jnp.float32)] * fc
+        out_ref[:, i * sub : (i + 1) * sub] = part
+
+
+def decode(n, chunks, sub, parts, decoder, targets, start=None, dense=None, after=None):
+    _, fy, _ = factors(n)
+    first = start is not None
+    rows = start[0].shape[0] if first else dense.shape[0]
+    lat_dev = decoder.shape[0]
+    count = len(parts) * fy
+    out = [pltpu.VMEM((rows, count * sub), jnp.float32)]
     scratch = [
-        pltpu.VMEM((fc, fy, lat_dev, sub), jnp.bfloat16),
-        pltpu.SemaphoreType.DMA((fc, fy)),
+        pltpu.VMEM((count, lat_dev, sub), jnp.bfloat16),
+        pltpu.SemaphoreType.DMA((count,)),
         pltpu.VMEM(targets.shape, targets.dtype),
         pltpu.SemaphoreType.DMA((3,)),
     ]
     if first:
+        args = [in_hbm(x) for x in (*start, decoder, targets)]
+        specs = [HBM] * 4
         out.append(pltpu.VMEM((rows, lat_dev), jnp.bfloat16))
-        scratch += [pltpu.VMEM(x.shape, x.dtype) for x in (ids, codes)]
-        args, specs = [in_hbm(x) for x in (ids, codes, decoder, targets)], [HBM] * 4
+        scratch += [pltpu.VMEM(x.shape, x.dtype) for x in start]
     else:
-        args = [dense, in_hbm(decoder), in_hbm(targets), after]
-        specs = [VMEM, HBM, HBM, ANY]
-    got = pl.pallas_call(
-        functools.partial(decode_kernel, n, rows // n, chunk, chunks, first),
+        args, specs = [dense, in_hbm(decoder), in_hbm(targets)], [VMEM, HBM, HBM]
+        if after is not None:
+            args.append(in_vmem(after))
+            specs.append(VMEM)
+    return pl.pallas_call(
+        functools.partial(decode_kernel, n, rows // n, chunks, parts, first),
         out_shape=out,
         in_specs=specs,
         out_specs=[VMEM] * len(out),
         scratch_shapes=scratch,
         compiler_params=params(),
-        cost_estimate=cost(2 * rows * lat_dev * fc * fy * sub, 4 * lat_dev * fc * fy * sub),
+        cost_estimate=cost(2 * rows * lat_dev * count * sub, 4 * lat_dev * count * sub),
         name="decode",
     )(*args)
-    return got[:fc], got[fc] if first else dense
-
-
-def grad_kernel(n, blocks, after, final, with_prev, *refs):
+
+
+def grad_kernel(n, blocks, after, final, with_prev, loaded, *refs):
     refs = list(refs)
     errs = [refs.pop(0) for _ in blocks]
-    decoder_ref = refs.pop(0)
+    decoder_ref = None if final else refs.pop(0)
+    loaded_ref = refs.pop(0) if loaded else None
     prev_ref = refs.pop(0) if with_prev else None
     sub = errs[0].shape[1]
     total = prev_ref[...] if with_prev else None
@@ -173,6 +178,8 @@
         next_ref = refs.pop(0) if after else None
         buf, sem = refs
         for i, (dc, dy, chunk, chunks) in enumerate(blocks):
+            if loaded and i == 0:
+                continue
             col = column(n, chunk, chunks, sub, dy, dc)
             loads.append(load(decoder_ref, col, buf.at[i], sem.at[i]))
         if after:
@@ -182,11 +189,12 @@
         for copy in loads:
             copy.start()
     for i, err in enumerate(errs):
-        if not final:
-            loads[i].wait()
+        here = loaded and i == 0
+        if not here:
+            loads[i - loaded].wait()
         part = lax.dot_general(
             err[...],
-            decoder_ref[...] if final else buf[i],
+            loaded_ref[...] if here else buf[i],
             (((1,), (1,)), ((), ())),
             preferred_element_type=jnp.float32,
         )
@@ -226,15 +234,18 @@
                 out_ref[first // own + d] = acc[d * own : (d + 1) * own, :]
 
 
-def grad(n, blocks, errs, decoder, prev, after=None, final=None):
+def grad(n, blocks, errs, decoder, prev, columns=None, after=None, final=None):
     rows, sub = errs[0].shape
     lat_dev = decoder.shape[0]
     count = len(errs)
-    args = list(errs) + [decoder if final is not None else in_hbm(decoder)]
-    specs = [VMEM] * count + [HBM if final is None else VMEM]
-    if prev is not None:
-        args.append(prev)
-        specs.append(VMEM)
+    args, specs = list(errs), [VMEM] * count
+    if final is None:
+        args.append(in_hbm(decoder))
+        specs.append(HBM)
+    for x in (columns, prev):
+        if x is not None:
+            args.append(in_vmem(x))
+            specs.append(VMEM)
     totals = pltpu.VMEM((rows, lat_dev), jnp.float32)
     if final is None:
         out = [totals] + ([pltpu.VMEM((lat_dev, sub), jnp.bfloat16)] if after else [])
@@ -248,7 +259,9 @@
         out = [jax.ShapeDtypeStruct((n, rows // n, LANES), jnp.float32)]
         scratch = [totals]
     return pl.pallas_call(
-        functools.partial(grad_kernel, n, tuple(blocks), after, final is not None, prev is not None),
+        functools.partial(
+            grad_kernel, n, tuple(blocks), after, final is not None, prev is not None, columns is not None
+        ),
         out_shape=out,
         in_specs=specs,
         out_specs=[VMEM] * len(out),
@@ -300,58 +313,74 @@
     def join(xs, axis):
         return xs[0] if len(xs) == 1 else jnp.concatenate(xs, axis=axis)
 
-    dense, after, summed = None, None, []
+    wide = fy * sub
+    others = tuple((p, dc) for dc in range(1, fc) for p in range(chunks))
+    part, dense = decode(n, chunks, sub, others, decoder, targets, (indices, codes))
+    came = swap(part, dc=1)
+    summed, leaving, after = [], [], None
     for p in range(chunks):
-        parts, dense = decode(
-            n, p, chunks, sub, indices, codes, dense, decoder, targets, after
-        )
-        total = parts[0]
-        for dc in range(1, fc):
-            total = total + swap(parts[dc], dc=dc)
+        (part,) = decode(n, chunks, sub, ((p, 0),), decoder, targets, dense=dense, after=after)
+        total = part + came[:, p * wide : (p + 1) * wide]
         blocks = [total[:, o * sub : (o + 1) * sub] for o in range(fy)]
+        got = None
         for b in reversed(bits(fy)):
+            if got is not None:
+                blocks = [blocks[o] + got[:, o * sub : (o + 1) * sub] for o in range(2 * b)]
             after = join(blocks[b:], 1)
             got = swap(after, dy=b)
-            blocks = [blocks[o] + got[:, o * sub : (o + 1) * sub] for o in range(b)]
-        summed.append(blocks[0])
-
-    diffs = []
-    for mine in summed:
+        leaving.append(after)
+        summed.append((blocks[0], got))
+
+    sums, moved = [], []
+    for p, (x, y) in enumerate(summed):
+        x = x + (hold(y, leaving[p + 1]) if p + 1 < chunks else y)
         blocks = [
-            lax.dynamic_slice_in_dim(mine, (z ^ j) * group, group, 0) for j in range(fz)
+            lax.dynamic_slice_in_dim(x, (z ^ j) * group, group, 0) for j in range(fz)
         ]
-        diff = blocks[0]
-        for j in range(1, fz):
-            diff = diff + swap(blocks[j], dz=j)
-        diffs.append(diff)
-
-    loss = sum(jnp.sum(d * d, axis=1, keepdims=True) for d in diffs)
-
-    pieces, totals = [], None
-
-    def add(some, after=None):
-        return grad(n, [at for at, _ in some], [e for _, e in some], decoder, totals, after)
-
-    done = 0
+        sums.append(blocks[0])
+        moved.append([swap(e, dz=j) for j, e in enumerate(blocks) if j])
+    errs, gathered, loss = [], [], 0.0
     for p in range(chunks):
-        err = diffs[p].astype(jnp.bfloat16)
-        here = [join([err] + [swap(err, dz=j) for j in range(1, fz)], 0)]
-        pieces.append(((0, 0, p, chunks), here[0]))
+        if p + 1 < chunks:
+            moved[p][-1] = hold(moved[p][-1], sums[p + 1])
+        if p:
+            moved[p][0] = hold(moved[p][0], errs[p - 1])
+        diff = sum(moved[p], sums[p])
+        loss = loss + jnp.sum(diff * diff, axis=1, keepdims=True)
+        errs.append(diff.astype(jnp.bfloat16))
+        gathered.append([swap(errs[p], dz=j) for j in range(1, fz)])
+
+    pieces, columns, totals, wholes = [], None, None, []
+    for p in range(chunks):
+        if p + 1 < chunks:
+            gathered[p][-1] = hold(gathered[p][-1], errs[p + 1])
+        if p:
+            gathered[p][0] = hold(gathered[p][0], wholes[p - 1])
+        wholes.append(join([errs[p]] + gathered[p], 0))
+    first = [((0, 0, p, chunks), e) for p, e in enumerate(wholes)]
+    done = None
+    for p in range(chunks):
+        here = [wholes[p]]
         for b in bits(fy):
-            last = p == chunks - 1 and 2 * b >= fy
-            if last:
-                (totals,) = add(pieces[done:])
+            got = [swap(e, dy=b) for e in here]
+            if p == chunks - 1 and 2 * b >= fy:
+                (totals,) = grad(n, [at for at, _ in first], [e for _, e in first], decoder, None)
+                if pieces:
+                    totals, columns = grad(
+                        n, [at for at, _ in pieces], [e for _, e in pieces], decoder, totals, None, (0, b, p, chunks)
+                    )
                 done = len(pieces)
-            got = [swap(e, dy=b) for e in here]
-            if last:
-                got = [hold(e, totals) for e in got]
+                got = [hold(got[0], totals)] + got[1:]
             pieces += [((0, b | i, p, chunks), e) for i, e in enumerate(got)]
             here += got
         for dc in range(1, fc):
             pieces += [((dc, i, p, chunks), swap(e, dc=dc)) for i, e in enumerate(here)]
-    totals, columns = add(pieces[done:-1], pieces[-1][0])
-    at, e = pieces[-1]
-    (back,) = grad(n, [at], [e], columns, totals, None, (indices, loss))
+    some, last = pieces[done:-1], pieces[-1]
+    totals, columns = grad(
+        n, [at for at, _ in some], [e for _, e in some], decoder, totals, columns, last[0]
+    )
+    (back,) = grad(n, [last[0]], [last[1]], decoder, totals, columns, None, (indices, loss))
+    pieces = first + pieces
     error = own_rows(n, [at for at, _ in pieces], own, width, [e[:group] for _, e in pieces])
 
     back = jnp.sum(lax.all_to_all(back, "lat", 0, 0, tiled=True), axis=0)

time: 70.2 us -> 66.4 us (0.946)
  local copies, waits for them, and re-layouts: 4.06 us -> 0.21 us
  Pallas kernels: 14 us -> 16.3 us
  starting transfers between devices: 29.7 us -> 28 us
    unnamed x12 -> x4, local copies, waits for them, and re-layouts: 3.1 us -> 0.01 us
    ppermute x22 -> x21, starting transfers between devices: 26.2 us -> 24 us  [swap(): return lax.ppermute(x, 'lat', pairs(n, dz, dy, dc))]
    ppermute x22 -> x21, waiting for transfers between devices: 15.2 us -> 13.9 us  [swap(): return lax.ppermute(x, 'lat', pairs(n, dz, dy, dc))]
    pallas_call x2 -> x3, Pallas kernels: 6.55 us -> 7.84 us  [decode(): pl.pallas_call(functools.partial(decode_kernel, n, rows // n, chunks, par...]
    pallas_call x3 -> x4, Pallas kernels: 6.57 us -> 7.63 us  [grad(): pl.pallas_call(functools.partial(grad_kernel, n, tuple(blocks), after, fi...]
    all_to_all x1, waiting for transfers between devices: 4.93 us -> 5.7 us  [local(): back = jnp.sum(lax.all_to_all(back, 'lat', 0, 0, tiled=True), axis=0)]
    slice x6, local copies, waits for them, and re-layouts: 0.78 us -> 0.03 us  [local(): e[:group]]
  transfers between devices with their start and end apart: 23 -> 22, of which waited for: 10 -> 11; matrix products, arithmetic and copies ran while one was open for 2% -> 1% of each run, Pallas kernels for 13% -> 17%
where the time goes in v6:
time: 66.4 us; the launch traced here: 66.1 us
  starting transfers between devices  28 us (42%)
  waiting for transfers between devices  19.6 us (30%)
  Pallas kernels  16.3 us (25%)
  other arithmetic  1.18 us (2%)
  between operations  0.87 us (1%)
    ppermute x21, starting transfers between devices, swap(): return lax.ppermute(x, 'lat', pairs(n, dz, dy, dc))  24 us
    ppermute x21, waiting for transfers between devices, swap(): return lax.ppermute(x, 'lat', pairs(n, dz, dy, dc))  13.9 us
    pallas_call x3, Pallas kernels, decode(): pl.pallas_call(functools.partial(decode_kernel, n, rows // n, chunks, par...  7.84 us
    pallas_call x4, Pallas kernels, grad(): pl.pallas_call(functools.partial(grad_kernel, n, tuple(blocks), after, fi...  7.63 us
    all_to_all x1, waiting for transfers between devices, local(): back = jnp.sum(lax.all_to_all(back, 'lat', 0, 0, tiled=True), axis=0)  5.7 us
    all_to_all x1, starting transfers between devices, local(): back = jnp.sum(lax.all_to_all(back, 'lat', 0, 0, tiled=True), axis=0)  3.95 us
  transfers between devices with their start and end apart: 22, of which 11 were waited for; matrix products, arithmetic and copies ran while one was open for 1% of the time, Pallas kernels for 17%

profile of v6, /device:TPU:0, one launch (start us, length us, event | category | flops | bytes accessed | tf_op | source)
XLA Modules:
  0.0 66.1 jit_solution(3917127703385494146)
XLA Ops:
  0.6 3.8 %decode.3 = (f32[64,4096]{1,0:T(8,128)S(1)}, bf16[64,512]{1,0:T(8,128)(2,1)S(1)}) custom-call(s32[64,64]{1,0:T(8,128)} %refs_3_.5, bf16[64,64]{1,0:T(8,128)(2,1)} %refs_1_.3, bf16[512,8192]{1,0:T(8,128)(2,1)} %refs_2_.9, bf16[4,8192]{1,0:T(4,128)(2,1)} %refs_2_.7), custom_call_target="tpu_custom_call" | custom-call | flops 268435456 | bytes 8388608 | tf_op jit(solution)/shard_map/decode/pallas_call | solution.py:155
  4.5 0.5 collective-permute-start
  5.0 2.0 %decode.4 = f32[64,2048]{1,0:T(8,128)S(1)} custom-call(bf16[64,512]{1,0:T(8,128)(2,1)S(1)} %get-tuple-element.9.refs_0_, bf16[512,8192]{1,0:T(8,128)(2,1)} %refs_2_.9, bf16[4,8192]{1,0:T(4,128)(2,1)} %refs_2_.7), custom_call_target="tpu_custom_call" | custom-call | flops 134217728 | bytes 4194304 | tf_op jit(solution)/shard_map/decode/pallas_call | solution.py:155
  7.0 0.3 collective-permute-done
  7.3 0.1 slice_add_fusion.1
  7.4 2.9 %collective-permute-start.1 = (f32[64,1024]{1,0:T(8,128)S(1)}, f32[64,1024]{1,0:T(8,128)S(1)}, u32[]{:S(2)}, u32[]{:S(2)}) collective-permute-start(f32[64,1024]{1,0:T(8,128)S(1)} %slice.58.refs_3_), channel_id=1, source_target_pairs={{0,2},{1,3},{2,0},{3,1},{4,6},{5,7},{6,4},{7,5},{8,10},{9,11},{10,... | collective-permute-start | bytes 786440 | tf_op jit(solution)/shard_map/ppermute | solution.py:311
  10.3 2.0 %decode.5 = f32[64,2048]{1,0:T(8,128)S(1)} custom-call(bf16[64,512]{1,0:T(8,128)(2,1)S(1)} %get-tuple-element.9.refs_0_, bf16[512,8192]{1,0:T(8,128)(2,1)} %refs_2_.9, bf16[4,8192]{1,0:T(4,128)(2,1)} %refs_2_.7, f32[64,1024]{1,0:T(8,128)S(1)} %slice.58.refs_3_), custom_call_target="tpu_custom_call" | custom-call | flops 134217728 | bytes 4194304 | tf_op jit(solution)/shard_map/decode/pallas_call | solution.py:155
  12.3 0.1 slice_add_fusion
  12.4 0.1 collective-permute-start.5
  12.5 4.9 %collective-permute-done.1.refs_0_ = f32[64,1024]{1,0:T(8,128)S(1)} collective-permute-done((f32[64,1024]{1,0:T(8,128)S(1)}, f32[64,1024]{1,0:T(8,128)S(1)}, u32[]{:S(2)}, u32[]{:S(2)}) %collective-permute-start.1) | collective-permute-done | bytes 262176 | tf_op jit(solution)/shard_map/ppermute | solution.py:311
  17.5 4.2 %collective-permute-start.4 = (f32[16,1024]{1,0:T(8,128)S(1)}, f32[16,1024]{1,0:T(8,128)S(1)}, u32[]{:S(2)}, u32[]{:S(2)}) collective-permute-start(f32[16,1024]{1,0:T(8,128)S(1)} %get-tuple-element.24), channel_id=1, source_target_pairs={{0,12},{1,13},{2,14},{3,15},{4,8},{5,9},{6,10},{7,11},{8,4},{9,5},... | collective-permute-start | bytes 196616 | tf_op jit(solution)/shard_map/ppermute | solution.py:311
  21.7 0.0 collective-permute-start.3
  21.7 0.6 collective-permute-start.2
  22.3 0.2 collective-permute-done.5
  22.6 3.9 %collective-permute-start.8 = (f32[16,1024]{1,0:T(8,128)S(1)}, f32[16,1024]{1,0:T(8,128)S(1)}, u32[]{:S(2)}, u32[]{:S(2)}) collective-permute-start(f32[16,1024]{1,0:T(8,128)S(1)} %get-tuple-element.20), channel_id=1, source_target_pairs={{0,12},{1,13},{2,14},{3,15},{4,8},{5,9},{6,10},{7,11},{8,4},{9,5},... | collective-permute-start | bytes 196616 | tf_op jit(solution)/shard_map/ppermute | solution.py:311
  26.5 0.0 collective-permute-start.7
  26.5 0.0 collective-permute-done.4.refs_0_
  26.5 0.6 collective-permute-start.6
  27.1 1.0 %collective-permute-done.3 = f32[16,1024]{1,0:T(8,128)S(1)} collective-permute-done((f32[16,1024]{1,0:T(8,128)S(1)}, f32[16,1024]{1,0:T(8,128)S(1)}, u32[]{:S(2)}, u32[]{:S(2)}) %collective-permute-start.3) | collective-permute-done | bytes 65568 | tf_op jit(solution)/shard_map/ppermute | solution.py:311
  28.1 0.0 collective-permute-done.2
  28.1 0.1 multiply_reduce_fusion.1
  28.2 2.9 %collective-permute-start.11 = (bf16[16,1024]{1,0:T(8,128)(2,1)S(1)}, bf16[16,1024]{1,0:T(8,128)(2,1)S(1)}, u32[]{:S(2)}, u32[]{:S(2)}) collective-permute-start(bf16[16,1024]{1,0:T(8,128)(2,1)S(1)} %get-tuple-element.18.refs_1_.refs_0_), channel_id=1, source_target_pairs={{0,12},{1,13},{2,14},{3,15},{4,8},{5,9},{6,10},{7,11},{8,4},{9,5},... | collective-permute-start | bytes 98312 | tf_op jit(solution)/shard_map/ppermute | solution.py:311
  31.1 0.0 collective-permute-start.10
  31.1 0.0 collective-permute-done.6.refs_0_
  31.1 2.0 %collective-permute-start.9 = (bf16[16,1024]{1,0:T(8,128)(2,1)S(1)}, bf16[16,1024]{1,0:T(8,128)(2,1)S(1)}, u32[]{:S(2)}, u32[]{:S(2)}) collective-permute-start(bf16[16,1024]{1,0:T(8,128)(2,1)S(1)} %get-tuple-element.18.refs_1_.refs_0_), channel_id=1, source_target_pairs={{0,4},{1,5},{2,6},{3,7},{4,0},{5,1},{6,2},{7,3},{8,12},{9,13},{10,... | collective-permute-start | bytes 98312 | tf_op jit(solution)/shard_map/ppermute | solution.py:311
  33.1 0.0 collective-permute-done.8
  33.1 0.3 collective-permute-done.7
  33.4 0.1 multiply_reduce_fusion
  33.5 0.6 collective-permute-done.11.refs_0_
  34.1 1.8 %collective-permute-done.10 = bf16[16,1024]{1,0:T(8,128)(2,1)S(1)} collective-permute-done((bf16[16,1024]{1,0:T(8,128)(2,1)S(1)}, bf16[16,1024]{1,0:T(8,128)(2,1)S(1)}, u32[]{:S(2)}, u32[]{:S(2)}) %collective-permute-start.10) | collective-permute-done | bytes 32800 | tf_op jit(solution)/shard_map/ppermute | solution.py:311
  35.9 0.0 collective-permute-done.9
  35.9 1.6 %collective-permute-start.12 = (bf16[64,1024]{1,0:T(8,128)(2,1)S(1)}, bf16[64,1024]{1,0:T(8,128)(2,1)S(1)}, u32[]{:S(2)}, u32[]{:S(2)}) collective-permute-start(bf16[64,1024]{1,0:T(8,128)(2,1)S(1)} %pad_maximum_fusion.refs_1_.refs_0_), channel_id=1, source_target_pairs={{0,2},{1,3},{2,0},{3,1},{4,6},{5,7},{6,4},{7,5},{8,10},{9,11},{10,... | collective-permute-start | bytes 393224 | tf_op jit(solution)/shard_map/ppermute | solution.py:311
  37.5 1.1 %collective-permute-start.15 = (bf16[16,1024]{1,0:T(8,128)(2,1)S(1)}, bf16[16,1024]{1,0:T(8,128)(2,1)S(1)}, u32[]{:S(2)}, u32[]{:S(2)}) collective-permute-start(bf16[16,1024]{1,0:T(8,128)(2,1)S(1)} %get-tuple-element.16.refs_1_), channel_id=1, source_target_pairs={{0,4},{1,5},{2,6},{3,7},{4,0},{5,1},{6,2},{7,3},{8,12},{9,13},{10,... | collective-permute-start | bytes 98312 | tf_op jit(solution)/shard_map/ppermute | solution.py:311
  38.6 2.4 %collective-permute-start.17 = (bf16[16,1024]{1,0:T(8,128)(2,1)S(1)}, bf16[16,1024]{1,0:T(8,128)(2,1)S(1)}, u32[]{:S(2)}, u32[]{:S(2)}) collective-permute-start(bf16[16,1024]{1,0:T(8,128)(2,1)S(1)} %get-tuple-element.16.refs_1_), channel_id=1, source_target_pairs={{0,12},{1,13},{2,14},{3,15},{4,8},{5,9},{6,10},{7,11},{8,4},{9,5},... | collective-permute-start | bytes 98312 | tf_op jit(solution)/shard_map/ppermute | solution.py:311
  41.0 0.0 collective-permute-start.16
  41.0 0.0 collective-permute-start.13
  41.0 0.8 %collective-permute-done.15.refs_0_ = bf16[16,1024]{1,0:T(8,128)(2,1)S(1)} collective-permute-done((bf16[16,1024]{1,0:T(8,128)(2,1)S(1)}, bf16[16,1024]{1,0:T(8,128)(2,1)S(1)}, u32[]{:S(2)}, u32[]{:S(2)}) %collective-permute-start.15) | collective-permute-done | bytes 32800 | tf_op jit(solution)/shard_map/ppermute | solution.py:311
  41.8 0.0 collective-permute-done.12.refs_0_
  41.8 0.0 collective-permute-start.14
  41.8 2.5 %collective-permute-done.17 = bf16[16,1024]{1,0:T(8,128)(2,1)S(1)} collective-permute-done((bf16[16,1024]{1,0:T(8,128)(2,1)S(1)}, bf16[16,1024]{1,0:T(8,128)(2,1)S(1)}, u32[]{:S(2)}, u32[]{:S(2)}) %collective-permute-start.17) | collective-permute-done | bytes 32800 | tf_op jit(solution)/shard_map/ppermute | solution.py:311
  44.3 1.5 %collective-permute-done.16 = bf16[16,1024]{1,0:T(8,128)(2,1)S(1)} collective-permute-done((bf16[16,1024]{1,0:T(8,128)(2,1)S(1)}, bf16[16,1024]{1,0:T(8,128)(2,1)S(1)}, u32[]{:S(2)}, u32[]{:S(2)}) %collective-permute-start.16) | collective-permute-done | bytes 32800 | tf_op jit(solution)/shard_map/ppermute | solution.py:311
  45.8 0.6 collective-permute-start.18
  46.4 0.0 collective-permute-start.19
  46.4 2.3 %grad.4.refs_4_ = f32[64,512]{1,0:T(8,128)S(1)} custom-call(bf16[64,1024]{1,0:T(8,128)(2,1)S(1)} %pad_maximum_fusion.refs_1_.refs_0_, bf16[64,1024]{1,0:T(8,128)(2,1)S(1)} %pad_maximum_fusion.1.refs_1_, bf16[512,8192]{1,0:T(8,128)(2,1)} %refs_2_.9), custom_call_target="tpu_custom_call" | custom-call | flops 134217728 | bytes 4194304 | tf_op jit(solution)/shard_map/grad/pallas_call | solution.py:261
  48.7 0.0 copy-start
  48.7 0.0 collective-permute-done.13.refs_1_
  48.8 0.0 collective-permute-done.14.refs_2_
  48.8 2.4 %grad.5 = (f32[64,512]{1,0:T(8,128)S(1)}, bf16[512,1024]{1,0:T(8,128)(2,1)S(1)}) custom-call(bf16[64,1024]{1,0:T(8,128)(2,1)S(1)} %collective-permute-done.12.refs_0_, bf16[64,1024]{1,0:T(8,128)(2,1)S(1)} %collective-permute-done.13.refs_1_, bf16[64,1024]{1,0:T(8,128)(2,1)S(1)} %collective-permute-done.14.refs_2_, bf16[512,8192]{1,0:T(8,128)(2,1)} %refs_2_.9, ...), custom_call_target="tpu_custom_call" | custom-call | flops 201326592 | bytes 6291456 | tf_op jit(solution)/shard_map/grad/pallas_call | solution.py:261
  51.2 0.0 collective-permute-done.18.refs_0_
  51.2 0.6 collective-permute-start.20
  51.8 0.1 copy.13.refs_4_
  51.8 0.0 collective-permute-done.19.refs_1_
  51.9 1.7 %grad.6 = (f32[64,512]{1,0:T(8,128)S(1)}, bf16[512,1024]{1,0:T(8,128)(2,1)S(1)}) custom-call(bf16[64,1024]{1,0:T(8,128)(2,1)S(1)} %hold.11.refs_0_, bf16[64,1024]{1,0:T(8,128)(2,1)S(1)} %collective-permute-done.19.refs_1_, bf16[512,8192]{1,0:T(8,128)(2,1)} %refs_2_.9, bf16[512,1024]{1,0:T(8,128)(2,1)S(1)} %get-tuple-element.12.refs_3_, ...), custom_call_target="tpu_custom_call" | custom-call | flops 134217728 | bytes 4194304 | tf_op jit(solution)/shard_map/grad/pallas_call | solution.py:261
  53.6 0.0 collective-permute-done.20.refs_0_
  53.6 0.0 copy-done
  53.6 1.2 %grad.7 = f32[16,4,128]{2,1,0:T(4,128)} custom-call(bf16[64,1024]{1,0:T(8,128)(2,1)S(1)} %collective-permute-done.20.refs_0_, bf16[512,1024]{1,0:T(8,128)(2,1)S(1)} %get-tuple-element.13.refs_1_, f32[64,512]{1,0:T(8,128)S(1)} %get-tuple-element.14.refs_2_, s32[64,64]{1,0:T(8,128)S(1)} %copy-done, f32[16,1]{1,0:T(8,128)S(1)} %copy.13.refs_4_), custom_call_target="tpu_custom_call" | custom-call | flops 67108864 | bytes 2097152 | tf_op jit(solution)/shard_map/grad/pallas_call | solution.py:261
  54.8 4.0 %all-to-all-start = ((f32[16,4,128]{2,1,0:T(4,128)}), f32[16,4,128]{2,1,0:T(4,128)S(1)}, u32[]{:S(2)}, u32[]{:S(2)}) async-start(f32[16,4,128]{2,1,0:T(4,128)} %grad.7), calls=%async_computation | async-start | bytes 65536 | tf_op jit(solution)/shard_map/all_to_all | solution.py:386
  58.8 0.9 %own_rows.1 = bf16[4,8192]{1,0:T(4,128)(2,1)} custom-call(bf16[16,1024]{1,0:T(8,128)(2,1)S(1)} %get-tuple-element.18.refs_1_.refs_0_, bf16[16,1024]{1,0:T(8,128)(2,1)S(1)} %get-tuple-element.16.refs_1_, bf16[16,1024]{1,0:T(8,128)(2,1)S(1)} %slice.62.refs_2_, bf16[16,1024]{1,0:T(8,128)(2,1)S(1)} %slice.63.refs_3_, bf16[16,1024]{1,0:T(8,128)(2,1)S(1)} %slice.64.refs_4_, ...), custom_call_target="tpu_custom_call" | custom-call | tf_op jit(solution)/shard_map/own_rows/pallas_call | solution.py:289
  59.7 5.7 %all-to-all-done = f32[16,4,128]{2,1,0:T(4,128)S(1)} async-done(((f32[16,4,128]{2,1,0:T(4,128)}), f32[16,4,128]{2,1,0:T(4,128)S(1)}, u32[]{:S(2)}, u32[]{:S(2)}) %all-to-all-start) | async-done | bytes 32800 | tf_op jit(solution)/shard_map/all_to_all | solution.py:386
  65.4 0.0 copy-start.1
  65.4 0.7 %multiply_reduce_fusion.2 = f32[4]{0:T(128)} fusion(f32[4,128]{1,0:T(4,128)S(1)} %reduce_sum.29), kind=kLoop, calls=%fused_computation.10 | loop fusion | flops 4 | bytes 32 | tf_op jit(solution)/shard_map/div | solution.py:387
  66.1 0.0 copy-done.1
  (22 shorter events, 0.2 us)
Async XLA Ops:
  4.5 2.8 %collective-permute-start = (f32[64,4096]{1,0:T(8,128)S(1)}, f32[64,4096]{1,0:T(8,128)S(1)}, u32[]{:S(2)}, u32[]{:S(2)}) collective-permute-start(f32[64,4096]{1,0:T(8,128)S(1)} %get-tuple-element.10), channel_id=1, source_target_pairs={{0,1},{1,0},{2,3},{3,2},{4,5},{5,4},{6,7},{7,6},{8,9},{9,8},{10,11... | collective-permute-start | bytes 3145736 | tf_op jit(solution)/shard_map/ppermute | solution.py:311
  7.4 10.0 %collective-permute-start.1 = (f32[64,1024]{1,0:T(8,128)S(1)}, f32[64,1024]{1,0:T(8,128)S(1)}, u32[]{:S(2)}, u32[]{:S(2)}) collective-permute-start(f32[64,1024]{1,0:T(8,128)S(1)} %slice.58.refs_3_), channel_id=1, source_target_pairs={{0,2},{1,3},{2,0},{3,1},{4,6},{5,7},{6,4},{7,5},{8,10},{9,11},{10,... | collective-permute-start | bytes 786440 | tf_op jit(solution)/shard_map/ppermute | solution.py:311
  12.4 10.1 %collective-permute-start.5 = (f32[64,1024]{1,0:T(8,128)S(1)}, f32[64,1024]{1,0:T(8,128)S(1)}, u32[]{:S(2)}, u32[]{:S(2)}) collective-permute-start(f32[64,1024]{1,0:T(8,128)S(1)} %slice.60.refs_1_), channel_id=1, source_target_pairs={{0,2},{1,3},{2,0},{3,1},{4,6},{5,7},{6,4},{7,5},{8,10},{9,11},{10,... | collective-permute-start | bytes 786440 | tf_op jit(solution)/shard_map/ppermute | solution.py:311
  17.5 9.0 %collective-permute-start.4 = (f32[16,1024]{1,0:T(8,128)S(1)}, f32[16,1024]{1,0:T(8,128)S(1)}, u32[]{:S(2)}, u32[]{:S(2)}) collective-permute-start(f32[16,1024]{1,0:T(8,128)S(1)} %get-tuple-element.24), channel_id=1, source_target_pairs={{0,12},{1,13},{2,14},{3,15},{4,8},{5,9},{6,10},{7,11},{8,4},{9,5},... | collective-permute-start | bytes 196616 | tf_op jit(solution)/shard_map/ppermute | solution.py:311
  21.7 6.4 %collective-permute-start.3 = (f32[16,1024]{1,0:T(8,128)S(1)}, f32[16,1024]{1,0:T(8,128)S(1)}, u32[]{:S(2)}, u32[]{:S(2)}) collective-permute-start(f32[16,1024]{1,0:T(8,128)S(1)} %get-tuple-element.25), channel_id=1, source_target_pairs={{0,8},{1,9},{2,10},{3,11},{4,12},{5,13},{6,14},{7,15},{8,0},{9,1},... | collective-permute-start | bytes 196616 | tf_op jit(solution)/shard_map/ppermute | solution.py:311
  21.7 6.4 %collective-permute-start.2 = (f32[16,1024]{1,0:T(8,128)S(1)}, f32[16,1024]{1,0:T(8,128)S(1)}, u32[]{:S(2)}, u32[]{:S(2)}) collective-permute-start(f32[16,1024]{1,0:T(8,128)S(1)} %get-tuple-element.23), channel_id=1, source_target_pairs={{0,4},{1,5},{2,6},{3,7},{4,0},{5,1},{6,2},{7,3},{8,12},{9,13},{10,... | collective-permute-start | bytes 196616 | tf_op jit(solution)/shard_map/ppermute | solution.py:311
  22.6 10.5 %collective-permute-start.8 = (f32[16,1024]{1,0:T(8,128)S(1)}, f32[16,1024]{1,0:T(8,128)S(1)}, u32[]{:S(2)}, u32[]{:S(2)}) collective-permute-start(f32[16,1024]{1,0:T(8,128)S(1)} %get-tuple-element.20), channel_id=1, source_target_pairs={{0,12},{1,13},{2,14},{3,15},{4,8},{5,9},{6,10},{7,11},{8,4},{9,5},... | collective-permute-start | bytes 196616 | tf_op jit(solution)/shard_map/ppermute | solution.py:311
  26.5 6.9 %collective-permute-start.7 = (f32[16,1024]{1,0:T(8,128)S(1)}, f32[16,1024]{1,0:T(8,128)S(1)}, u32[]{:S(2)}, u32[]{:S(2)}) collective-permute-start(f32[16,1024]{1,0:T(8,128)S(1)} %get-tuple-element.21), channel_id=1, source_target_pairs={{0,8},{1,9},{2,10},{3,11},{4,12},{5,13},{6,14},{7,15},{8,0},{9,1},... | collective-permute-start | bytes 196616 | tf_op jit(solution)/shard_map/ppermute | solution.py:311
  26.5 4.6 %collective-permute-start.6 = (f32[16,1024]{1,0:T(8,128)S(1)}, f32[16,1024]{1,0:T(8,128)S(1)}, u32[]{:S(2)}, u32[]{:S(2)}) collective-permute-start(f32[16,1024]{1,0:T(8,128)S(1)} %get-tuple-element.19), channel_id=1, source_target_pairs={{0,4},{1,5},{2,6},{3,7},{4,0},{5,1},{6,2},{7,3},{8,12},{9,13},{10,... | collective-permute-start | bytes 196616 | tf_op jit(solution)/shard_map/ppermute | solution.py:311
  28.2 5.9 %collective-permute-start.11 = (bf16[16,1024]{1,0:T(8,128)(2,1)S(1)}, bf16[16,1024]{1,0:T(8,128)(2,1)S(1)}, u32[]{:S(2)}, u32[]{:S(2)}) collective-permute-start(bf16[16,1024]{1,0:T(8,128)(2,1)S(1)} %get-tuple-element.18.refs_1_.refs_0_), channel_id=1, source_target_pairs={{0,12},{1,13},{2,14},{3,15},{4,8},{5,9},{6,10},{7,11},{8,4},{9,5},... | collective-permute-start | bytes 98312 | tf_op jit(solution)/shard_map/ppermute | solution.py:311
  31.1 4.8 %collective-permute-start.10 = (bf16[16,1024]{1,0:T(8,128)(2,1)S(1)}, bf16[16,1024]{1,0:T(8,128)(2,1)S(1)}, u32[]{:S(2)}, u32[]{:S(2)}) collective-permute-start(bf16[16,1024]{1,0:T(8,128)(2,1)S(1)} %get-tuple-element.18.refs_1_.refs_0_), channel_id=1, source_target_pairs={{0,8},{1,9},{2,10},{3,11},{4,12},{5,13},{6,14},{7,15},{8,0},{9,1},... | collective-permute-start | bytes 98312 | tf_op jit(solution)/shard_map/ppermute | solution.py:311
  31.1 4.8 %collective-permute-start.9 = (bf16[16,1024]{1,0:T(8,128)(2,1)S(1)}, bf16[16,1024]{1,0:T(8,128)(2,1)S(1)}, u32[]{:S(2)}, u32[]{:S(2)}) collective-permute-start(bf16[16,1024]{1,0:T(8,128)(2,1)S(1)} %get-tuple-element.18.refs_1_.refs_0_), channel_id=1, source_target_pairs={{0,4},{1,5},{2,6},{3,7},{4,0},{5,1},{6,2},{7,3},{8,12},{9,13},{10,... | collective-permute-start | bytes 98312 | tf_op jit(solution)/shard_map/ppermute | solution.py:311
  35.9 5.9 %collective-permute-start.12 = (bf16[64,1024]{1,0:T(8,128)(2,1)S(1)}, bf16[64,1024]{1,0:T(8,128)(2,1)S(1)}, u32[]{:S(2)}, u32[]{:S(2)}) collective-permute-start(bf16[64,1024]{1,0:T(8,128)(2,1)S(1)} %pad_maximum_fusion.refs_1_.refs_0_), channel_id=1, source_target_pairs={{0,2},{1,3},{2,0},{3,1},{4,6},{5,7},{6,4},{7,5},{8,10},{9,11},{10,... | collective-permute-start | bytes 393224 | tf_op jit(solution)/shard_map/ppermute | solution.py:311
  37.5 4.3 %collective-permute-start.15 = (bf16[16,1024]{1,0:T(8,128)(2,1)S(1)}, bf16[16,1024]{1,0:T(8,128)(2,1)S(1)}, u32[]{:S(2)}, u32[]{:S(2)}) collective-permute-start(bf16[16,1024]{1,0:T(8,128)(2,1)S(1)} %get-tuple-element.16.refs_1_), channel_id=1, source_target_pairs={{0,4},{1,5},{2,6},{3,7},{4,0},{5,1},{6,2},{7,3},{8,12},{9,13},{10,... | collective-permute-start | bytes 98312 | tf_op jit(solution)/shard_map/ppermute | solution.py:311
  38.6 5.7 %collective-permute-start.17 = (bf16[16,1024]{1,0:T(8,128)(2,1)S(1)}, bf16[16,1024]{1,0:T(8,128)(2,1)S(1)}, u32[]{:S(2)}, u32[]{:S(2)}) collective-permute-start(bf16[16,1024]{1,0:T(8,128)(2,1)S(1)} %get-tuple-element.16.refs_1_), channel_id=1, source_target_pairs={{0,12},{1,13},{2,14},{3,15},{4,8},{5,9},{6,10},{7,11},{8,4},{9,5},... | collective-permute-start | bytes 98312 | tf_op jit(solution)/shard_map/ppermute | solution.py:311
  41.0 4.8 %collective-permute-start.16 = (bf16[16,1024]{1,0:T(8,128)(2,1)S(1)}, bf16[16,1024]{1,0:T(8,128)(2,1)S(1)}, u32[]{:S(2)}, u32[]{:S(2)}) collective-permute-start(bf16[16,1024]{1,0:T(8,128)(2,1)S(1)} %get-tuple-element.16.refs_1_), channel_id=1, source_target_pairs={{0,8},{1,9},{2,10},{3,11},{4,12},{5,13},{6,14},{7,15},{8,0},{9,1},... | collective-permute-start | bytes 98312 | tf_op jit(solution)/shard_map/ppermute | solution.py:311
  41.0 7.7 %collective-permute-start.13 = (bf16[64,1024]{1,0:T(8,128)(2,1)S(1)}, bf16[64,1024]{1,0:T(8,128)(2,1)S(1)}, u32[]{:S(2)}, u32[]{:S(2)}) collective-permute-start(bf16[64,1024]{1,0:T(8,128)(2,1)S(1)} %pad_maximum_fusion.refs_1_.refs_0_), channel_id=1, source_target_pairs={{0,1},{1,0},{2,3},{3,2},{4,5},{5,4},{6,7},{7,6},{8,9},{9,8},{10,11... | collective-permute-start | bytes 393224 | tf_op jit(solution)/shard_map/ppermute | solution.py:311
  41.8 7.0 %collective-permute-start.14 = (bf16[64,1024]{1,0:T(8,128)(2,1)S(1)}, bf16[64,1024]{1,0:T(8,128)(2,1)S(1)}, u32[]{:S(2)}, u32[]{:S(2)}) collective-permute-start(bf16[64,1024]{1,0:T(8,128)(2,1)S(1)} %collective-permute-done.12.refs_0_), channel_id=1, source_target_pairs={{0,1},{1,0},{2,3},{3,2},{4,5},{5,4},{6,7},{7,6},{8,9},{9,8},{10,11... | collective-permute-start | bytes 393224 | tf_op jit(solution)/shard_map/ppermute | solution.py:311
  45.8 5.3 %collective-permute-start.18 = (bf16[64,1024]{1,0:T(8,128)(2,1)S(1)}, bf16[64,1024]{1,0:T(8,128)(2,1)S(1)}, u32[]{:S(2)}, u32[]{:S(2)}) collective-permute-start(bf16[64,1024]{1,0:T(8,128)(2,1)S(1)} %pad_maximum_fusion.1.refs_1_), channel_id=1, source_target_pairs={{0,2},{1,3},{2,0},{3,1},{4,6},{5,7},{6,4},{7,5},{8,10},{9,11},{10,... | collective-permute-start | bytes 393224 | tf_op jit(solution)/shard_map/ppermute | solution.py:311
  46.4 5.5 %collective-permute-start.19 = (bf16[64,1024]{1,0:T(8,128)(2,1)S(1)}, bf16[64,1024]{1,0:T(8,128)(2,1)S(1)}, u32[]{:S(2)}, u32[]{:S(2)}) collective-permute-start(bf16[64,1024]{1,0:T(8,128)(2,1)S(1)} %pad_maximum_fusion.1.refs_1_), channel_id=1, source_target_pairs={{0,1},{1,0},{2,3},{3,2},{4,5},{5,4},{6,7},{7,6},{8,9},{9,8},{10,11... | collective-permute-start | bytes 393224 | tf_op jit(solution)/shard_map/ppermute | solution.py:311
  48.7 4.9 %copy-start = (s32[64,64]{1,0:T(8,128)S(1)}, s32[64,64]{1,0:T(8,128)}, u32[]{:S(2)}) copy-start(s32[64,64]{1,0:T(8,128)} %refs_3_.5) | copy-start | bytes 49156
  51.2 2.4 %collective-permute-start.20 = (bf16[64,1024]{1,0:T(8,128)(2,1)S(1)}, bf16[64,1024]{1,0:T(8,128)(2,1)S(1)}, u32[]{:S(2)}, u32[]{:S(2)}) collective-permute-start(bf16[64,1024]{1,0:T(8,128)(2,1)S(1)} %hold.11.refs_0_), channel_id=1, source_target_pairs={{0,1},{1,0},{2,3},{3,2},{4,5},{5,4},{6,7},{7,6},{8,9},{9,8},{10,11... | collective-permute-start | bytes 393224 | tf_op jit(solution)/shard_map/ppermute | solution.py:311
  54.8 10.6 %all-to-all-start = ((f32[16,4,128]{2,1,0:T(4,128)}), f32[16,4,128]{2,1,0:T(4,128)S(1)}, u32[]{:S(2)}, u32[]{:S(2)}) async-start(f32[16,4,128]{2,1,0:T(4,128)} %grad.7), calls=%async_computation | async-start | bytes 65536 | tf_op jit(solution)/shard_map/all_to_all | solution.py:386
  65.4 0.7 %copy-start.1 = (f32[4,128]{1,0:T(4,128)}, f32[4,128]{1,0:T(4,128)S(1)}, u32[]{:S(2)}) copy-start(f32[4,128]{1,0:T(4,128)S(1)} %reduce_sum.29) | copy-start | bytes 6148

commit v7 on v6

--- a/solution.py
+++ b/solution.py
@@ -10,13 +10,15 @@
 CHUNKS = 2
 ROW_STEP = 16
 LANES = 128
+SUBLANES = 8
+FETCHES = 8
 VMEM = pl.BlockSpec(memory_space=pltpu.VMEM)
 HBM = pl.BlockSpec(memory_space=pltpu.HBM)
 
 
 def factors(n):
-    assert n & (n - 1) == 0
-    c = min(n, 2)
+    assert n > 1 and n & (n - 1) == 0
+    c = 2
     m = n // c
     y = 1
     while 4 * y * y <= m:
@@ -116,17 +118,16 @@
             return carry
 
         lax.fori_loop(0, rows // ROW_STEP, body, 0)
-    rows = dense_ref.shape[0]
-    row = lax.broadcasted_iota(jnp.int32, (rows, own), 0)
-    want = lax.broadcasted_iota(jnp.int32, (rows, own), 1) + me * own
-    mine = jnp.where(row == want, -1.0, 0.0).astype(jnp.bfloat16)
+    per = SUBLANES // own
+    tile = pl.ds(pl.multiple_of(me // per * SUBLANES, SUBLANES), SUBLANES)
+    mine = lax.broadcasted_iota(jnp.int32, (SUBLANES, sub), 0) // own == me % per
     for i, col in enumerate(cols):
         loads[i].wait()
-        part = jnp.dot(dense_ref[...], buf[i], preferred_element_type=jnp.float32)
-        part += jnp.dot(
-            mine, targets_ref[:, pl.ds(col, sub)], preferred_element_type=jnp.float32
-        )
-        out_ref[:, i * sub : (i + 1) * sub] = part
+        here = slice(i * sub, (i + 1) * sub)
+        out_ref[:, here] = jnp.dot(dense_ref[...], buf[i], preferred_element_type=jnp.float32)
+        target = targets_ref[:, pl.ds(col, sub)].astype(jnp.float32)
+        target = jnp.concatenate([target] * per, axis=0)
+        out_ref[tile, here] -= jnp.where(mine, target, 0.0)
 
 
 def decode(n, chunks, sub, parts, decoder, targets, start=None, dense=None, after=None):
@@ -164,45 +165,49 @@
     )(*args)
 
 
-def grad_kernel(n, blocks, after, final, with_prev, loaded, *refs):
+def fetch_kernel(decoder_hbm, _, out_ref, sem):
+    step = out_ref.shape[0] // FETCHES
+    parts = [pl.ds(i * step, step) for i in range(FETCHES)]
+    copies = [
+        pltpu.make_async_copy(decoder_hbm.at[at], out_ref.at[at], sem.at[i])
+        for i, at in enumerate(parts)
+    ]
+    for copy in copies:
+        copy.start()
+    for copy in copies:
+        copy.wait()
+
+
+def fetch(decoder, after):
+    return pl.pallas_call(
+        fetch_kernel,
+        out_shape=pltpu.VMEM(decoder.shape, decoder.dtype),
+        in_specs=[HBM, VMEM],
+        out_specs=VMEM,
+        scratch_shapes=[pltpu.SemaphoreType.DMA((FETCHES,))],
+        compiler_params=params(),
+        cost_estimate=cost(0, decoder.size * 2),
+        name="fetch",
+    )(in_hbm(decoder), in_vmem(after))
+
+
+def grad_kernel(n, places, counts, final, with_prev, *refs):
     refs = list(refs)
-    errs = [refs.pop(0) for _ in blocks]
-    decoder_ref = None if final else refs.pop(0)
-    loaded_ref = refs.pop(0) if loaded else None
-    prev_ref = refs.pop(0) if with_prev else None
-    sub = errs[0].shape[1]
-    total = prev_ref[...] if with_prev else None
-    loads = []
-    if not final:
-        out_ref = refs.pop(0)
-        next_ref = refs.pop(0) if after else None
-        buf, sem = refs
-        for i, (dc, dy, chunk, chunks) in enumerate(blocks):
-            if loaded and i == 0:
-                continue
-            col = column(n, chunk, chunks, sub, dy, dc)
-            loads.append(load(decoder_ref, col, buf.at[i], sem.at[i]))
-        if after:
-            dc, dy, chunk, chunks = after
-            col = column(n, chunk, chunks, sub, dy, dc)
-            loads.append(load(decoder_ref, col, next_ref, sem.at[len(blocks)]))
-        for copy in loads:
-            copy.start()
-    for i, err in enumerate(errs):
-        here = loaded and i == 0
-        if not here:
-            loads[i - loaded].wait()
+    errs = [[refs.pop(0) for _ in range(count)] for count in counts]
+    decoder_ref = refs.pop(0)
+    total = refs.pop(0)[...] if with_prev else None
+    for parts, (dc, dy) in zip(errs, places):
+        err = parts[0][...] if len(parts) == 1 else jnp.concatenate([e[...] for e in parts], axis=0)
+        width = err.shape[1]
         part = lax.dot_general(
-            err[...],
-            loaded_ref[...] if here else buf[i],
+            err,
+            decoder_ref[:, pl.ds(column(n, 0, 1, width, dy, dc), width)],
             (((1,), (1,)), ((), ())),
             preferred_element_type=jnp.float32,
         )
         total = part if total is None else total + part
     if not final:
-        out_ref[...] = total
-        if after:
-            loads[-1].wait()
+        refs[0][...] = total
         return
     ids_ref, loss_ref, out_ref, totals_ref = refs
     totals_ref[...] = total
@@ -234,40 +239,25 @@
                 out_ref[first // own + d] = acc[d * own : (d + 1) * own, :]
 
 
-def grad(n, blocks, errs, decoder, prev, columns=None, after=None, final=None):
-    rows, sub = errs[0].shape
+def grad(n, rows, pieces, decoder, prev, final=None):
     lat_dev = decoder.shape[0]
-    count = len(errs)
-    args, specs = list(errs), [VMEM] * count
-    if final is None:
-        args.append(in_hbm(decoder))
-        specs.append(HBM)
-    for x in (columns, prev):
-        if x is not None:
-            args.append(in_vmem(x))
-            specs.append(VMEM)
+    places = tuple(at for at, _ in pieces)
+    counts = tuple(len(e) for _, e in pieces)
+    args = [x for _, e in pieces for x in e] + [in_vmem(decoder)]
+    if prev is not None:
+        args.append(in_vmem(prev))
+    if final is not None:
+        args += list(final)
     totals = pltpu.VMEM((rows, lat_dev), jnp.float32)
-    if final is None:
-        out = [totals] + ([pltpu.VMEM((lat_dev, sub), jnp.bfloat16)] if after else [])
-        scratch = [
-            pltpu.VMEM((count, lat_dev, sub), jnp.bfloat16),
-            pltpu.SemaphoreType.DMA((count + 1,)),
-        ]
-    else:
-        args += list(final)
-        specs += [VMEM] * len(final)
-        out = [jax.ShapeDtypeStruct((n, rows // n, LANES), jnp.float32)]
-        scratch = [totals]
-    return pl.pallas_call(
-        functools.partial(
-            grad_kernel, n, tuple(blocks), after, final is not None, prev is not None, columns is not None
-        ),
-        out_shape=out,
-        in_specs=specs,
-        out_specs=[VMEM] * len(out),
-        scratch_shapes=scratch,
-        compiler_params=params(),
-        cost_estimate=cost(2 * rows * lat_dev * sub * count, 4 * lat_dev * sub * count),
+    size = pieces[0][1][0].shape[1] * len(pieces)
+    return pl.pallas_call(
+        functools.partial(grad_kernel, n, places, counts, final is not None, prev is not None),
+        out_shape=totals if final is None else jax.ShapeDtypeStruct((n, rows // n, LANES), jnp.float32),
+        in_specs=[VMEM] * len(args),
+        out_specs=VMEM,
+        scratch_shapes=[] if final is None else [totals],
+        compiler_params=params(),
+        cost_estimate=cost(2 * rows * lat_dev * size, 4 * lat_dev * size),
         name="grad",
     )(*args)
 
@@ -280,9 +270,9 @@
     row = lax.broadcasted_iota(jnp.int32, (own, group), 0) + (y * fc + c) * own
     want = lax.broadcasted_iota(jnp.int32, (own, group), 1)
     mine = jnp.where(row == want, 1.0, 0.0).astype(jnp.bfloat16)
-    for err, (dc, dy, chunk, chunks) in zip(errs, blocks):
+    for err, (dc, dy) in zip(errs, blocks):
         rows = jnp.dot(mine, err[...], preferred_element_type=jnp.float32)
-        out_ref[:, pl.ds(column(n, chunk, chunks, sub, dy, dc), sub)] = rows.astype(jnp.bfloat16)
+        out_ref[:, pl.ds(column(n, 0, 1, sub, dy, dc), sub)] = rows.astype(jnp.bfloat16)
 
 
 def own_rows(n, blocks, own, width, errs):
@@ -331,15 +321,16 @@
         leaving.append(after)
         summed.append((blocks[0], got))
 
+    fetched = fetch(decoder, leaving[-1])
     sums, moved = [], []
     for p, (x, y) in enumerate(summed):
-        x = x + (hold(y, leaving[p + 1]) if p + 1 < chunks else y)
+        x = x + (hold(y, fetched) if p == 0 else y)
         blocks = [
             lax.dynamic_slice_in_dim(x, (z ^ j) * group, group, 0) for j in range(fz)
         ]
         sums.append(blocks[0])
         moved.append([swap(e, dz=j) for j, e in enumerate(blocks) if j])
-    errs, gathered, loss = [], [], 0.0
+    errs, loss = [], 0.0
     for p in range(chunks):
         if p + 1 < chunks:
             moved[p][-1] = hold(moved[p][-1], sums[p + 1])
@@ -348,40 +339,29 @@
         diff = sum(moved[p], sums[p])
         loss = loss + jnp.sum(diff * diff, axis=1, keepdims=True)
         errs.append(diff.astype(jnp.bfloat16))
-        gathered.append([swap(errs[p], dz=j) for j in range(1, fz)])
-
-    pieces, columns, totals, wholes = [], None, None, []
-    for p in range(chunks):
-        if p + 1 < chunks:
-            gathered[p][-1] = hold(gathered[p][-1], errs[p + 1])
-        if p:
-            gathered[p][0] = hold(gathered[p][0], wholes[p - 1])
-        wholes.append(join([errs[p]] + gathered[p], 0))
-    first = [((0, 0, p, chunks), e) for p, e in enumerate(wholes)]
-    done = None
-    for p in range(chunks):
-        here = [wholes[p]]
-        for b in bits(fy):
-            got = [swap(e, dy=b) for e in here]
-            if p == chunks - 1 and 2 * b >= fy:
-                (totals,) = grad(n, [at for at, _ in first], [e for _, e in first], decoder, None)
-                if pieces:
-                    totals, columns = grad(
-                        n, [at for at, _ in pieces], [e for _, e in pieces], decoder, totals, None, (0, b, p, chunks)
-                    )
-                done = len(pieces)
-                got = [hold(got[0], totals)] + got[1:]
-            pieces += [((0, b | i, p, chunks), e) for i, e in enumerate(got)]
-            here += got
-        for dc in range(1, fc):
-            pieces += [((dc, i, p, chunks), swap(e, dc=dc)) for i, e in enumerate(here)]
-    some, last = pieces[done:-1], pieces[-1]
-    totals, columns = grad(
-        n, [at for at, _ in some], [e for _, e in some], decoder, totals, columns, last[0]
-    )
-    (back,) = grad(n, [last[0]], [last[1]], decoder, totals, columns, None, (indices, loss))
-    pieces = first + pieces
-    error = own_rows(n, [at for at, _ in pieces], own, width, [e[:group] for _, e in pieces])
+
+    err = join(errs, 1)
+    come = [err] + [swap(err, dz=j) for j in range(1, fz)]
+    half = fz // 2
+    near = [((0, 0), [join(come[:half], 0), join(come[half:], 0)])]
+    for b in bits(fy):
+        last = [((0, b | at[1]), [swap(e, dy=b) for e in parts]) for at, parts in near]
+        near += last
+    near = near[: -len(last)]
+
+    def to_core(pieces):
+        sent = swap(join([e for _, parts in pieces for e in parts], 0), dc=1)
+        return [((1, at[1]), [sent[i * rows : (i + 1) * rows]]) for i, (at, _) in enumerate(pieces)]
+
+    far = to_core(near)
+    totals = grad(n, rows, near, fetched, None)
+    totals = grad(n, rows, far, fetched, totals)
+    last[-1][1][0] = hold(last[-1][1][0], totals)
+    far_last = to_core(last)
+    totals = grad(n, rows, last, fetched, totals)
+    back = grad(n, rows, far_last, fetched, totals, (indices, loss))
+    pieces = near + far + last + far_last
+    error = own_rows(n, [at for at, _ in pieces], own, width, [e[0][:group] for _, e in pieces])
 
     back = jnp.sum(lax.all_to_all(back, "lat", 0, 0, tiled=True), axis=0)
     return error, back[:, k_count] / width, back[:, :k_count]

time: 66.4 us -> 69.2 us (1.042)
  local copies, waits for them, and re-layouts: 0.21 us -> 6.21 us
  starting transfers between devices: 28 us -> 24 us
  waiting for transfers between devices: 19.6 us -> 21 us
  Pallas kernels: 16.3 us -> 15.6 us
    unnamed x4 -> x11, local copies, waits for them, and re-layouts: 0.01 us -> 6 us
    ppermute x21 -> x16, starting transfers between devices: 24 us -> 19.7 us  [swap(): return lax.ppermute(x, 'lat', pairs(n, dz, dy, dc))]
    ppermute x21 -> x16, waiting for transfers between devices: 13.9 us -> 15.2 us  [swap(): return lax.ppermute(x, 'lat', pairs(n, dz, dy, dc))]
    pallas_call x4 -> x5, Pallas kernels: 7.63 us -> 7.25 us  [the longest x4 3.77 us: grad(): pl.pallas_call(functools.partial(grad_kernel, n, places, counts, final is...]
  transfers between devices with their start and end apart: 22 -> 17, of which waited for: 11 -> 10; matrix products, arithmetic and copies ran while one was open for 1% -> 1% of each run, Pallas kernels for 17% -> 15%
where the time goes in v7:
time: 69.2 us; the launch traced here: 68.9 us
  starting transfers between devices  24 us (35%)
  waiting for transfers between devices  21 us (30%)
  Pallas kernels  15.6 us (23%)
  local copies, waits for them, and re-layouts  6.21 us (9%)
  other arithmetic  1.21 us (2%)
  between operations  0.89 us (1%)
    ppermute x16, starting transfers between devices, swap(): return lax.ppermute(x, 'lat', pairs(n, dz, dy, dc))  19.7 us
    ppermute x16, waiting for transfers between devices, swap(): return lax.ppermute(x, 'lat', pairs(n, dz, dy, dc))  15.2 us
    pallas_call x3, Pallas kernels, decode(): pl.pallas_call(functools.partial(decode_kernel, n, rows // n, chunks, par...  7.51 us
    unnamed x11, local copies, waits for them, and re-layouts  6 us
    all_to_all x1, waiting for transfers between devices, local(): back = jnp.sum(lax.all_to_all(back, 'lat', 0, 0, tiled=True), axis=0)  5.74 us
    all_to_all x1, starting transfers between devices, local(): back = jnp.sum(lax.all_to_all(back, 'lat', 0, 0, tiled=True), axis=0)  4.37 us
    pallas_call x4, Pallas kernels, grad(): pl.pallas_call(functools.partial(grad_kernel, n, places, counts, final is...  3.77 us
    pallas_call x1, Pallas kernels, fetch(): pl.pallas_call(fetch_kernel, out_shape=pltpu.VMEM(decoder.shape, decoder....  3.47 us
  transfers between devices with their start and end apart: 17, of which 10 were waited for; matrix products, arithmetic and copies ran while one was open for 1% of the time, Pallas kernels for 15%

profile of v7, /device:TPU:0, one launch (start us, length us, event | category | flops | bytes accessed | tf_op | source)
XLA Modules:
  0.0 68.9 jit_solution(2007858930706351123)
XLA Ops:
  0.6 3.7 %decode.3 = (f32[64,4096]{1,0:T(8,128)S(1)}, bf16[64,512]{1,0:T(8,128)(2,1)S(1)}) custom-call(s32[64,64]{1,0:T(8,128)} %refs_3_.3, bf16[64,64]{1,0:T(8,128)(2,1)} %refs_1_.3, bf16[512,8192]{1,0:T(8,128)(2,1)} %decoder_hbm.1, bf16[4,8192]{1,0:T(4,128)(2,1)} %refs_2_.5), custom_call_target="tpu_custom_call" | custom-call | flops 268435456 | bytes 8388608 | tf_op jit(solution)/shard_map/decode/pallas_call | solution.py:156
  4.3 0.5 collective-permute-start
  4.8 1.9 %decode.4 = f32[64,2048]{1,0:T(8,128)S(1)} custom-call(bf16[64,512]{1,0:T(8,128)(2,1)S(1)} %get-tuple-element.5.refs_0_, bf16[512,8192]{1,0:T(8,128)(2,1)} %decoder_hbm.1, bf16[4,8192]{1,0:T(4,128)(2,1)} %refs_2_.5), custom_call_target="tpu_custom_call" | custom-call | flops 134217728 | bytes 4194304 | tf_op jit(solution)/shard_map/decode/pallas_call | solution.py:156
  6.7 0.4 collective-permute-done
  7.1 0.1 slice_add_fusion.1
  7.2 3.0 %collective-permute-start.1 = (f32[64,1024]{1,0:T(8,128)S(1)}, f32[64,1024]{1,0:T(8,128)S(1)}, u32[]{:S(2)}, u32[]{:S(2)}) collective-permute-start(f32[64,1024]{1,0:T(8,128)S(1)} %slice.46.refs_3_), channel_id=1, source_target_pairs={{0,2},{1,3},{2,0},{3,1},{4,6},{5,7},{6,4},{7,5},{8,10},{9,11},{10,... | collective-permute-start | bytes 786440 | tf_op jit(solution)/shard_map/ppermute | solution.py:301
  10.1 1.9 %decode.5 = f32[64,2048]{1,0:T(8,128)S(1)} custom-call(bf16[64,512]{1,0:T(8,128)(2,1)S(1)} %get-tuple-element.5.refs_0_, bf16[512,8192]{1,0:T(8,128)(2,1)} %decoder_hbm.1, bf16[4,8192]{1,0:T(4,128)(2,1)} %refs_2_.5, f32[64,1024]{1,0:T(8,128)S(1)} %slice.46.refs_3_), custom_call_target="tpu_custom_call" | custom-call | flops 134217728 | bytes 4194304 | tf_op jit(solution)/shard_map/decode/pallas_call | solution.py:156
  12.1 0.1 slice_add_fusion
  12.2 0.1 collective-permute-start.5
  12.2 3.5 %fetch.1.refs_1_.refs_2_ = bf16[512,8192]{1,0:T(8,128)(2,1)S(1)} custom-call(bf16[512,8192]{1,0:T(8,128)(2,1)} %decoder_hbm.1, f32[64,1024]{1,0:T(8,128)S(1)} %slice.48._), custom_call_target="tpu_custom_call" | custom-call | bytes 8388608 | tf_op jit(solution)/shard_map/fetch/pallas_call | solution.py:182
  15.7 0.0 copy-start
  15.7 1.5 %collective-permute-done.1.refs_0_ = f32[64,1024]{1,0:T(8,128)S(1)} collective-permute-done((f32[64,1024]{1,0:T(8,128)S(1)}, f32[64,1024]{1,0:T(8,128)S(1)}, u32[]{:S(2)}, u32[]{:S(2)}) %collective-permute-start.1) | collective-permute-done | bytes 262176 | tf_op jit(solution)/shard_map/ppermute | solution.py:301
  17.3 2.2 %collective-permute-start.2 = (f32[16,1024]{1,0:T(8,128)S(1)}, f32[16,1024]{1,0:T(8,128)S(1)}, u32[]{:S(2)}, u32[]{:S(2)}) collective-permute-start(f32[16,1024]{1,0:T(8,128)S(1)} %get-tuple-element.11), channel_id=1, source_target_pairs={{0,4},{1,5},{2,6},{3,7},{4,0},{5,1},{6,2},{7,3},{8,12},{9,13},{10,... | collective-permute-start | bytes 196616 | tf_op jit(solution)/shard_map/ppermute | solution.py:301
  19.5 2.5 %collective-permute-start.4 = (f32[16,1024]{1,0:T(8,128)S(1)}, f32[16,1024]{1,0:T(8,128)S(1)}, u32[]{:S(2)}, u32[]{:S(2)}) collective-permute-start(f32[16,1024]{1,0:T(8,128)S(1)} %get-tuple-element.12), channel_id=1, source_target_pairs={{0,12},{1,13},{2,14},{3,15},{4,8},{5,9},{6,10},{7,11},{8,4},{9,5},... | collective-permute-start | bytes 196616 | tf_op jit(solution)/shard_map/ppermute | solution.py:301
  22.0 0.1 collective-permute-start.3
  22.1 0.3 collective-permute-done.5
  22.4 1.9 %collective-permute-start.6 = (f32[16,1024]{1,0:T(8,128)S(1)}, f32[16,1024]{1,0:T(8,128)S(1)}, u32[]{:S(2)}, u32[]{:S(2)}) collective-permute-start(f32[16,1024]{1,0:T(8,128)S(1)} %get-tuple-element.14), channel_id=1, source_target_pairs={{0,4},{1,5},{2,6},{3,7},{4,0},{5,1},{6,2},{7,3},{8,12},{9,13},{10,... | collective-permute-start | bytes 196616 | tf_op jit(solution)/shard_map/ppermute | solution.py:301
  24.3 2.5 %collective-permute-start.8 = (f32[16,1024]{1,0:T(8,128)S(1)}, f32[16,1024]{1,0:T(8,128)S(1)}, u32[]{:S(2)}, u32[]{:S(2)}) collective-permute-start(f32[16,1024]{1,0:T(8,128)S(1)} %get-tuple-element.15), channel_id=1, source_target_pairs={{0,12},{1,13},{2,14},{3,15},{4,8},{5,9},{6,10},{7,11},{8,4},{9,5},... | collective-permute-start | bytes 196616 | tf_op jit(solution)/shard_map/ppermute | solution.py:301
  26.8 0.0 collective-permute-done.4.refs_0_
  26.8 0.1 collective-permute-start.7
  26.9 0.0 collective-permute-done.2
  26.9 2.1 %collective-permute-done.3 = f32[16,1024]{1,0:T(8,128)S(1)} collective-permute-done((f32[16,1024]{1,0:T(8,128)S(1)}, f32[16,1024]{1,0:T(8,128)S(1)}, u32[]{:S(2)}, u32[]{:S(2)}) %collective-permute-start.3) | collective-permute-done | bytes 65568 | tf_op jit(solution)/shard_map/ppermute | solution.py:301
  29.0 0.1 multiply_reduce_fusion.1
  29.1 0.0 collective-permute-done.6.refs_0_
  29.1 1.7 %collective-permute-done.8 = f32[16,1024]{1,0:T(8,128)S(1)} collective-permute-done((f32[16,1024]{1,0:T(8,128)S(1)}, f32[16,1024]{1,0:T(8,128)S(1)}, u32[]{:S(2)}, u32[]{:S(2)}) %collective-permute-start.8) | collective-permute-done | bytes 65568 | tf_op jit(solution)/shard_map/ppermute | solution.py:301
  30.8 2.6 %collective-permute-done.7 = f32[16,1024]{1,0:T(8,128)S(1)} collective-permute-done((f32[16,1024]{1,0:T(8,128)S(1)}, f32[16,1024]{1,0:T(8,128)S(1)}, u32[]{:S(2)}, u32[]{:S(2)}) %collective-permute-start.7) | collective-permute-done | bytes 65568 | tf_op jit(solution)/shard_map/ppermute | solution.py:301
  33.4 0.1 multiply_reduce_fusion
  33.6 0.1 collective-permute-start.9
  33.7 1.8 %collective-permute-start.11 = (bf16[16,2048]{1,0:T(8,128)(2,1)S(1)}, bf16[16,2048]{1,0:T(8,128)(2,1)S(1)}, u32[]{:S(2)}, u32[]{:S(2)}) collective-permute-start(bf16[16,2048]{1,0:T(8,128)(2,1)S(1)} %pad_maximum_fusion.3.refs_0_), channel_id=1, source_target_pairs={{0,12},{1,13},{2,14},{3,15},{4,8},{5,9},{6,10},{7,11},{8,4},{9,5},... | collective-permute-start | bytes 196616 | tf_op jit(solution)/shard_map/ppermute | solution.py:301
  35.4 1.7 %collective-permute-start.10 = (bf16[16,2048]{1,0:T(8,128)(2,1)S(1)}, bf16[16,2048]{1,0:T(8,128)(2,1)S(1)}, u32[]{:S(2)}, u32[]{:S(2)}) collective-permute-start(bf16[16,2048]{1,0:T(8,128)(2,1)S(1)} %pad_maximum_fusion.3.refs_0_), channel_id=1, source_target_pairs={{0,8},{1,9},{2,10},{3,11},{4,12},{5,13},{6,14},{7,15},{8,0},{9,1},... | collective-permute-start | bytes 196616 | tf_op jit(solution)/shard_map/ppermute | solution.py:301
  37.1 1.6 %collective-permute-done.9 = bf16[16,2048]{1,0:T(8,128)(2,1)S(1)} collective-permute-done((bf16[16,2048]{1,0:T(8,128)(2,1)S(1)}, bf16[16,2048]{1,0:T(8,128)(2,1)S(1)}, u32[]{:S(2)}, u32[]{:S(2)}) %collective-permute-start.9) | collective-permute-done | bytes 65568 | tf_op jit(solution)/shard_map/ppermute | solution.py:301
  38.7 1.6 %collective-permute-start.13 = (bf16[32,2048]{1,0:T(8,128)(2,1)S(1)}, bf16[32,2048]{1,0:T(8,128)(2,1)S(1)}, u32[]{:S(2)}, u32[]{:S(2)}) collective-permute-start(bf16[32,2048]{1,0:T(8,128)(2,1)S(1)} %pad_maximum_fusion.2.refs_0_), channel_id=1, source_target_pairs={{0,2},{1,3},{2,0},{3,1},{4,6},{5,7},{6,4},{7,5},{8,10},{9,11},{10,... | collective-permute-start | bytes 393224 | tf_op jit(solution)/shard_map/ppermute | solution.py:301
  40.3 0.0 collective-permute-done.11
  40.3 2.4 %collective-permute-done.10 = bf16[16,2048]{1,0:T(8,128)(2,1)S(1)} collective-permute-done((bf16[16,2048]{1,0:T(8,128)(2,1)S(1)}, bf16[16,2048]{1,0:T(8,128)(2,1)S(1)}, u32[]{:S(2)}, u32[]{:S(2)}) %collective-permute-start.10) | collective-permute-done | bytes 65568 | tf_op jit(solution)/shard_map/ppermute | solution.py:301
  42.7 0.1 collective-permute-start.12
  42.8 1.6 %collective-permute-start.14 = (bf16[32,2048]{1,0:T(8,128)(2,1)S(1)}, bf16[32,2048]{1,0:T(8,128)(2,1)S(1)}, u32[]{:S(2)}, u32[]{:S(2)}) collective-permute-start(bf16[32,2048]{1,0:T(8,128)(2,1)S(1)} %constant_dynamic-update-slice_fusion.refs_1_), channel_id=1, source_target_pairs={{0,2},{1,3},{2,0},{3,1},{4,6},{5,7},{6,4},{7,5},{8,10},{9,11},{10,... | collective-permute-start | bytes 393224 | tf_op jit(solution)/shard_map/ppermute | solution.py:301
  44.4 0.8 %grad.4.refs_2_ = f32[64,512]{1,0:T(8,128)S(1)} custom-call(bf16[32,2048]{1,0:T(8,128)(2,1)S(1)} %pad_maximum_fusion.2.refs_0_, bf16[32,2048]{1,0:T(8,128)(2,1)S(1)} %constant_dynamic-update-slice_fusion.refs_1_, bf16[512,8192]{1,0:T(8,128)(2,1)S(1)} %fetch.1.refs_1_.refs_2_), custom_call_target="tpu_custom_call" | custom-call | flops 134217728 | bytes 4194304 | tf_op jit(solution)/shard_map/grad/pallas_call | solution.py:253
  45.1 0.0 copy-start.3
  45.2 0.0 collective-permute-done.12.refs_0_
  45.2 0.0 copy-done
  45.2 0.8 %grad.5.refs_1_.refs_3_ = f32[64,512]{1,0:T(8,128)S(1)} custom-call(bf16[64,2048]{1,0:T(8,128)(2,1)S(1)} %collective-permute-done.12.refs_0_, bf16[512,8192]{1,0:T(8,128)(2,1)S(1)} %fetch.1.refs_1_.refs_2_, f32[64,512]{1,0:T(8,128)S(1)} %grad.4.refs_2_), custom_call_target="tpu_custom_call" | custom-call | flops 134217728 | bytes 4194304 | tf_op jit(solution)/shard_map/grad/pallas_call | solution.py:253
  46.0 0.0 collective-permute-done.13.refs_0_
  46.0 2.8 %collective-permute-done.14.refs_1_ = bf16[32,2048]{1,0:T(8,128)(2,1)S(1)} collective-permute-done((bf16[32,2048]{1,0:T(8,128)(2,1)S(1)}, bf16[32,2048]{1,0:T(8,128)(2,1)S(1)}, u32[]{:S(2)}, u32[]{:S(2)}) %collective-permute-start.14) | collective-permute-done | bytes 131104 | tf_op jit(solution)/shard_map/ppermute | solution.py:301
  48.8 0.1 collective-permute-start.15
  48.9 0.1 copy.11.refs_4_
  48.9 0.0 copy-start.1
  48.9 3.4 %copy-done.1 = bf16[512,8192]{1,0:T(8,128)(2,1)S(1)} copy-done((bf16[512,8192]{1,0:T(8,128)(2,1)S(1)}, bf16[512,8192]{1,0:T(8,128)(2,1)}, u32[]{:S(2)}) %copy-start.1) | copy-done | bytes 8388632
  52.3 0.0 copy-start.2
  52.3 0.8 %grad.6.refs_2_ = f32[64,512]{1,0:T(8,128)S(1)} custom-call(bf16[32,2048]{1,0:T(8,128)(2,1)S(1)} %hold.7.refs_0_, bf16[32,2048]{1,0:T(8,128)(2,1)S(1)} %collective-permute-done.14.refs_1_, bf16[512,8192]{1,0:T(8,128)(2,1)S(1)} %copy-done.1, f32[64,512]{1,0:T(8,128)S(1)} %grad.5.refs_1_.refs_3_), custom_call_target="tpu_custom_call" | custom-call | flops 134217728 | bytes 4194304 | tf_op jit(solution)/shard_map/grad/pallas_call | solution.py:253
  53.1 0.0 collective-permute-done.15.refs_0_
  53.1 0.0 copy-done.3
  53.1 2.6 %copy-done.2 = bf16[512,8192]{1,0:T(8,128)(2,1)S(1)} copy-done((bf16[512,8192]{1,0:T(8,128)(2,1)S(1)}, bf16[512,8192]{1,0:T(8,128)(2,1)}, u32[]{:S(2)}) %copy-start.2) | copy-done | bytes 8388632
  55.7 1.5 %grad.7 = f32[16,4,128]{2,1,0:T(4,128)} custom-call(bf16[64,2048]{1,0:T(8,128)(2,1)S(1)} %collective-permute-done.15.refs_0_, bf16[512,8192]{1,0:T(8,128)(2,1)S(1)} %copy-done.2, f32[64,512]{1,0:T(8,128)S(1)} %grad.6.refs_2_, s32[64,64]{1,0:T(8,128)S(1)} %copy-done.3, f32[16,1]{1,0:T(8,128)S(1)} %copy.11.refs_4_), custom_call_target="tpu_custom_call" | custom-call | flops 134217728 | bytes 4194304 | tf_op jit(solution)/shard_map/grad/pallas_call | solution.py:253
  57.2 4.4 %all-to-all-start = ((f32[16,4,128]{2,1,0:T(4,128)}), f32[16,4,128]{2,1,0:T(4,128)S(1)}, u32[]{:S(2)}, u32[]{:S(2)}) async-start(f32[16,4,128]{2,1,0:T(4,128)} %grad.7), calls=%async_computation | async-start | bytes 65536 | tf_op jit(solution)/shard_map/all_to_all | solution.py:366
  61.6 0.8 %own_rows.1 = bf16[4,8192]{1,0:T(4,128)(2,1)} custom-call(bf16[16,2048]{1,0:T(8,128)(2,1)S(1)} %pad_maximum_fusion.3.refs_0_, bf16[16,2048]{1,0:T(8,128)(2,1)S(1)} %slice.50.refs_1_, bf16[16,2048]{1,0:T(8,128)(2,1)S(1)} %slice.51.refs_2_, bf16[16,2048]{1,0:T(8,128)(2,1)S(1)} %slice.52.refs_3_), custom_call_target="tpu_custom_call" | custom-call | tf_op jit(solution)/shard_map/own_rows/pallas_call | solution.py:279
  62.5 5.7 %all-to-all-done = f32[16,4,128]{2,1,0:T(4,128)S(1)} async-done(((f32[16,4,128]{2,1,0:T(4,128)}), f32[16,4,128]{2,1,0:T(4,128)S(1)}, u32[]{:S(2)}, u32[]{:S(2)}) %all-to-all-start) | async-done | bytes 32800 | tf_op jit(solution)/shard_map/all_to_all | solution.py:366
  68.2 0.0 copy-start.4
  68.2 0.7 %multiply_reduce_fusion.2 = f32[4]{0:T(128)} fusion(f32[4,128]{1,0:T(4,128)S(1)} %reduce_sum.29), kind=kLoop, calls=%fused_computation.14 | loop fusion | flops 4 | bytes 32 | tf_op jit(solution)/shard_map/div | solution.py:367
  68.9 0.0 copy-done.4
  (21 shorter events, 0.3 us)
Async XLA Ops:
  4.3 2.8 %collective-permute-start = (f32[64,4096]{1,0:T(8,128)S(1)}, f32[64,4096]{1,0:T(8,128)S(1)}, u32[]{:S(2)}, u32[]{:S(2)}) collective-permute-start(f32[64,4096]{1,0:T(8,128)S(1)} %get-tuple-element.6), channel_id=1, source_target_pairs={{0,1},{1,0},{2,3},{3,2},{4,5},{5,4},{6,7},{7,6},{8,9},{9,8},{10,11... | collective-permute-start | bytes 3145736 | tf_op jit(solution)/shard_map/ppermute | solution.py:301
  7.2 10.0 %collective-permute-start.1 = (f32[64,1024]{1,0:T(8,128)S(1)}, f32[64,1024]{1,0:T(8,128)S(1)}, u32[]{:S(2)}, u32[]{:S(2)}) collective-permute-start(f32[64,1024]{1,0:T(8,128)S(1)} %slice.46.refs_3_), channel_id=1, source_target_pairs={{0,2},{1,3},{2,0},{3,1},{4,6},{5,7},{6,4},{7,5},{8,10},{9,11},{10,... | collective-permute-start | bytes 786440 | tf_op jit(solution)/shard_map/ppermute | solution.py:301
  12.2 10.2 %collective-permute-start.5 = (f32[64,1024]{1,0:T(8,128)S(1)}, f32[64,1024]{1,0:T(8,128)S(1)}, u32[]{:S(2)}, u32[]{:S(2)}) collective-permute-start(f32[64,1024]{1,0:T(8,128)S(1)} %slice.48._), channel_id=1, source_target_pairs={{0,2},{1,3},{2,0},{3,1},{4,6},{5,7},{6,4},{7,5},{8,10},{9,11},{10,... | collective-permute-start | bytes 786440 | tf_op jit(solution)/shard_map/ppermute | solution.py:301
  15.7 29.4 %copy-start = (bf16[512,8192]{1,0:T(8,128)(2,1)}, bf16[512,8192]{1,0:T(8,128)(2,1)S(1)}, u32[]{:S(2)}) copy-start(bf16[512,8192]{1,0:T(8,128)(2,1)S(1)} %fetch.1.refs_1_.refs_2_) | copy-start | bytes 25165828
  17.3 9.6 %collective-permute-start.2 = (f32[16,1024]{1,0:T(8,128)S(1)}, f32[16,1024]{1,0:T(8,128)S(1)}, u32[]{:S(2)}, u32[]{:S(2)}) collective-permute-start(f32[16,1024]{1,0:T(8,128)S(1)} %get-tuple-element.11), channel_id=1, source_target_pairs={{0,4},{1,5},{2,6},{3,7},{4,0},{5,1},{6,2},{7,3},{8,12},{9,13},{10,... | collective-permute-start | bytes 196616 | tf_op jit(solution)/shard_map/ppermute | solution.py:301
  19.5 7.3 %collective-permute-start.4 = (f32[16,1024]{1,0:T(8,128)S(1)}, f32[16,1024]{1,0:T(8,128)S(1)}, u32[]{:S(2)}, u32[]{:S(2)}) collective-permute-start(f32[16,1024]{1,0:T(8,128)S(1)} %get-tuple-element.12), channel_id=1, source_target_pairs={{0,12},{1,13},{2,14},{3,15},{4,8},{5,9},{6,10},{7,11},{8,4},{9,5},... | collective-permute-start | bytes 196616 | tf_op jit(solution)/shard_map/ppermute | solution.py:301
  22.0 7.0 %collective-permute-start.3 = (f32[16,1024]{1,0:T(8,128)S(1)}, f32[16,1024]{1,0:T(8,128)S(1)}, u32[]{:S(2)}, u32[]{:S(2)}) collective-permute-start(f32[16,1024]{1,0:T(8,128)S(1)} %get-tuple-element.13), channel_id=1, source_target_pairs={{0,8},{1,9},{2,10},{3,11},{4,12},{5,13},{6,14},{7,15},{8,0},{9,1},... | collective-permute-start | bytes 196616 | tf_op jit(solution)/shard_map/ppermute | solution.py:301
  22.4 6.7 %collective-permute-start.6 = (f32[16,1024]{1,0:T(8,128)S(1)}, f32[16,1024]{1,0:T(8,128)S(1)}, u32[]{:S(2)}, u32[]{:S(2)}) collective-permute-start(f32[16,1024]{1,0:T(8,128)S(1)} %get-tuple-element.14), channel_id=1, source_target_pairs={{0,4},{1,5},{2,6},{3,7},{4,0},{5,1},{6,2},{7,3},{8,12},{9,13},{10,... | collective-permute-start | bytes 196616 | tf_op jit(solution)/shard_map/ppermute | solution.py:301
  24.3 6.5 %collective-permute-start.8 = (f32[16,1024]{1,0:T(8,128)S(1)}, f32[16,1024]{1,0:T(8,128)S(1)}, u32[]{:S(2)}, u32[]{:S(2)}) collective-permute-start(f32[16,1024]{1,0:T(8,128)S(1)} %get-tuple-element.15), channel_id=1, source_target_pairs={{0,12},{1,13},{2,14},{3,15},{4,8},{5,9},{6,10},{7,11},{8,4},{9,5},... | collective-permute-start | bytes 196616 | tf_op jit(solution)/shard_map/ppermute | solution.py:301
  26.8 6.7 %collective-permute-start.7 = (f32[16,1024]{1,0:T(8,128)S(1)}, f32[16,1024]{1,0:T(8,128)S(1)}, u32[]{:S(2)}, u32[]{:S(2)}) collective-permute-start(f32[16,1024]{1,0:T(8,128)S(1)} %get-tuple-element.16), channel_id=1, source_target_pairs={{0,8},{1,9},{2,10},{3,11},{4,12},{5,13},{6,14},{7,15},{8,0},{9,1},... | collective-permute-start | bytes 196616 | tf_op jit(solution)/shard_map/ppermute | solution.py:301
  33.6 5.1 %collective-permute-start.9 = (bf16[16,2048]{1,0:T(8,128)(2,1)S(1)}, bf16[16,2048]{1,0:T(8,128)(2,1)S(1)}, u32[]{:S(2)}, u32[]{:S(2)}) collective-permute-start(bf16[16,2048]{1,0:T(8,128)(2,1)S(1)} %pad_maximum_fusion.3.refs_0_), channel_id=1, source_target_pairs={{0,4},{1,5},{2,6},{3,7},{4,0},{5,1},{6,2},{7,3},{8,12},{9,13},{10,... | collective-permute-start | bytes 196616 | tf_op jit(solution)/shard_map/ppermute | solution.py:301
  33.7 6.6 %collective-permute-start.11 = (bf16[16,2048]{1,0:T(8,128)(2,1)S(1)}, bf16[16,2048]{1,0:T(8,128)(2,1)S(1)}, u32[]{:S(2)}, u32[]{:S(2)}) collective-permute-start(bf16[16,2048]{1,0:T(8,128)(2,1)S(1)} %pad_maximum_fusion.3.refs_0_), channel_id=1, source_target_pairs={{0,12},{1,13},{2,14},{3,15},{4,8},{5,9},{6,10},{7,11},{8,4},{9,5},... | collective-permute-start | bytes 196616 | tf_op jit(solution)/shard_map/ppermute | solution.py:301
  35.4 7.2 %collective-permute-start.10 = (bf16[16,2048]{1,0:T(8,128)(2,1)S(1)}, bf16[16,2048]{1,0:T(8,128)(2,1)S(1)}, u32[]{:S(2)}, u32[]{:S(2)}) collective-permute-start(bf16[16,2048]{1,0:T(8,128)(2,1)S(1)} %pad_maximum_fusion.3.refs_0_), channel_id=1, source_target_pairs={{0,8},{1,9},{2,10},{3,11},{4,12},{5,13},{6,14},{7,15},{8,0},{9,1},... | collective-permute-start | bytes 196616 | tf_op jit(solution)/shard_map/ppermute | solution.py:301
  38.7 7.2 %collective-permute-start.13 = (bf16[32,2048]{1,0:T(8,128)(2,1)S(1)}, bf16[32,2048]{1,0:T(8,128)(2,1)S(1)}, u32[]{:S(2)}, u32[]{:S(2)}) collective-permute-start(bf16[32,2048]{1,0:T(8,128)(2,1)S(1)} %pad_maximum_fusion.2.refs_0_), channel_id=1, source_target_pairs={{0,2},{1,3},{2,0},{3,1},{4,6},{5,7},{6,4},{7,5},{8,10},{9,11},{10,... | collective-permute-start | bytes 393224 | tf_op jit(solution)/shard_map/ppermute | solution.py:301
  42.7 2.5 %collective-permute-start.12 = (bf16[64,2048]{1,0:T(8,128)(2,1)S(1)}, bf16[64,2048]{1,0:T(8,128)(2,1)S(1)}, u32[]{:S(2)}, u32[]{:S(2)}) collective-permute-start(bf16[64,2048]{1,0:T(8,128)(2,1)S(1)} %pad_maximum_fusion), channel_id=1, source_target_pairs={{0,1},{1,0},{2,3},{3,2},{4,5},{5,4},{6,7},{7,6},{8,9},{9,8},{10,11... | collective-permute-start | bytes 786440 | tf_op jit(solution)/shard_map/ppermute | solution.py:301
  42.8 5.9 %collective-permute-start.14 = (bf16[32,2048]{1,0:T(8,128)(2,1)S(1)}, bf16[32,2048]{1,0:T(8,128)(2,1)S(1)}, u32[]{:S(2)}, u32[]{:S(2)}) collective-permute-start(bf16[32,2048]{1,0:T(8,128)(2,1)S(1)} %constant_dynamic-update-slice_fusion.refs_1_), channel_id=1, source_target_pairs={{0,2},{1,3},{2,0},{3,1},{4,6},{5,7},{6,4},{7,5},{8,10},{9,11},{10,... | collective-permute-start | bytes 393224 | tf_op jit(solution)/shard_map/ppermute | solution.py:301
  45.1 8.0 %copy-start.3 = (s32[64,64]{1,0:T(8,128)S(1)}, s32[64,64]{1,0:T(8,128)}, u32[]{:S(2)}) copy-start(s32[64,64]{1,0:T(8,128)} %refs_3_.3) | copy-start | bytes 49156
  48.8 4.3 %collective-permute-start.15 = (bf16[64,2048]{1,0:T(8,128)(2,1)S(1)}, bf16[64,2048]{1,0:T(8,128)(2,1)S(1)}, u32[]{:S(2)}, u32[]{:S(2)}) collective-permute-start(bf16[64,2048]{1,0:T(8,128)(2,1)S(1)} %pad_maximum_fusion.1), channel_id=1, source_target_pairs={{0,1},{1,0},{2,3},{3,2},{4,5},{5,4},{6,7},{7,6},{8,9},{9,8},{10,11... | collective-permute-start | bytes 786440 | tf_op jit(solution)/shard_map/ppermute | solution.py:301
  48.9 3.4 %copy-start.1 = (bf16[512,8192]{1,0:T(8,128)(2,1)S(1)}, bf16[512,8192]{1,0:T(8,128)(2,1)}, u32[]{:S(2)}) copy-start(bf16[512,8192]{1,0:T(8,128)(2,1)} %copy-done) | copy-start | bytes 25165828
  52.3 3.4 %copy-start.2 = (bf16[512,8192]{1,0:T(8,128)(2,1)S(1)}, bf16[512,8192]{1,0:T(8,128)(2,1)}, u32[]{:S(2)}) copy-start(bf16[512,8192]{1,0:T(8,128)(2,1)} %copy-done) | copy-start | bytes 25165828
  57.2 11.0 %all-to-all-start = ((f32[16,4,128]{2,1,0:T(4,128)}), f32[16,4,128]{2,1,0:T(4,128)S(1)}, u32[]{:S(2)}, u32[]{:S(2)}) async-start(f32[16,4,128]{2,1,0:T(4,128)} %grad.7), calls=%async_computation | async-start | bytes 65536 | tf_op jit(solution)/shard_map/all_to_all | solution.py:366
  68.2 0.7 %copy-start.4 = (f32[4,128]{1,0:T(4,128)}, f32[4,128]{1,0:T(4,128)S(1)}, u32[]{:S(2)}) copy-start(f32[4,128]{1,0:T(4,128)S(1)} %reduce_sum.29) | copy-start | bytes 6148

commit v8 on v7

--- a/solution.py
+++ b/solution.py
@@ -11,7 +11,7 @@
 ROW_STEP = 16
 LANES = 128
 SUBLANES = 8
-FETCHES = 8
+FETCHES = 4
 VMEM = pl.BlockSpec(memory_space=pltpu.VMEM)
 HBM = pl.BlockSpec(memory_space=pltpu.HBM)
 
@@ -33,6 +33,10 @@
 
 def bits(size):
     return [1 << i for i in range(size.bit_length() - 1)]
+
+
+def z_order(fz):
+    return ([fz - 1] if fz > 1 else []) + list(range(1, fz - 1))
 
 
 def pairs(n, dz, dy, dc):
@@ -82,29 +86,44 @@
     return pltpu.make_async_copy(decoder_hbm.at[:, pl.ds(col, buf.shape[1])], buf, sem)
 
 
-def decode_kernel(n, own, chunks, parts, first, *refs):
+def decode_kernel(n, own, chunks, parts, first, loaded, keep, *refs):
     fz, fy, fc = factors(n)
     me = lax.axis_index("lat")
+    refs = list(refs)
     if first:
-        ids_hbm, codes_hbm, decoder_hbm, targets_hbm, out_ref, dense_ref = refs[:6]
-        buf, sem, targets_ref, small, ids_ref, codes_ref = refs[6:]
-        smalls_in = [(ids_hbm, ids_ref), (codes_hbm, codes_ref), (targets_hbm, targets_ref)]
+        ids_hbm, codes_hbm = refs.pop(0), refs.pop(0)
     else:
-        dense_ref, decoder_hbm, targets_hbm = refs[:3]
-        out_ref, buf, sem, targets_ref, small = refs[-5:]
-        smalls_in = [(targets_hbm, targets_ref)]
+        dense_ref = refs.pop(0)
+    decoder_ref, targets_hbm = refs.pop(0), refs.pop(0)
+    if not first and not loaded:
+        refs.pop(0)
+    outs = [refs.pop(0) for _ in parts]
+    if first:
+        dense_ref, kept_ref = refs.pop(0), refs.pop(0)
+    targets_ref, small = refs.pop(0), refs.pop(0)
+    smalls_in = [(targets_hbm, targets_ref)]
+    if first:
+        smalls_in = [(ids_hbm, refs[0]), (codes_hbm, refs[1])] + smalls_in
+        ids_ref, codes_ref = refs.pop(0), refs.pop(0)
     smalls = [pltpu.make_async_copy(a, b, small.at[i]) for i, (a, b) in enumerate(smalls_in)]
     for copy in smalls:
         copy.start()
-    lat_dev, sub = buf.shape[1:]
+    rows, lat_dev = dense_ref.shape
+    sub = outs[0].shape[1] // fy
     cols = [column(n, p, chunks, sub, o, dc) for p, dc in parts for o in range(fy)]
-    loads = [load(decoder_hbm, col, buf.at[i], sem.at[i]) for i, col in enumerate(cols)]
-    for copy in loads:
+    loads, later, buf = [], [], decoder_ref
+    if not loaded:
+        buf, sem = refs
+        loads = [load(decoder_ref, col, buf.at[i], sem.at[i]) for i, col in enumerate(cols)]
+        for i, (p, dc, o) in enumerate((p, dc, o) for p, dc in keep for o in range(fy)):
+            col = column(n, p, chunks, sub, o, dc)
+            later.append(load(decoder_ref, col, kept_ref.at[i], sem.at[len(cols) + i]))
+    for copy in loads + later:
         copy.start()
     for copy in smalls:
         copy.wait()
     if first:
-        rows, k_count = ids_ref.shape
+        k_count = ids_ref.shape[1]
         lanes = lax.broadcasted_iota(jnp.int32, (ROW_STEP, lat_dev), 1) + me * lat_dev
 
         def body(g, carry):
@@ -122,39 +141,46 @@
     tile = pl.ds(pl.multiple_of(me // per * SUBLANES, SUBLANES), SUBLANES)
     mine = lax.broadcasted_iota(jnp.int32, (SUBLANES, sub), 0) // own == me % per
     for i, col in enumerate(cols):
-        loads[i].wait()
-        here = slice(i * sub, (i + 1) * sub)
+        if loads:
+            loads[i].wait()
+        out_ref = outs[i // fy]
+        here = slice(i % fy * sub, (i % fy + 1) * sub)
         out_ref[:, here] = jnp.dot(dense_ref[...], buf[i], preferred_element_type=jnp.float32)
         target = targets_ref[:, pl.ds(col, sub)].astype(jnp.float32)
         target = jnp.concatenate([target] * per, axis=0)
         out_ref[tile, here] -= jnp.where(mine, target, 0.0)
-
-
-def decode(n, chunks, sub, parts, decoder, targets, start=None, dense=None, after=None):
+    for copy in later:
+        copy.wait()
+
+
+def decode(n, chunks, sub, parts, decoder, targets, start=None, keep=(), dense=None, after=None):
     _, fy, _ = factors(n)
-    first = start is not None
+    first, loaded = start is not None, decoder.ndim == 3
     rows = start[0].shape[0] if first else dense.shape[0]
-    lat_dev = decoder.shape[0]
+    lat_dev = decoder.shape[-2]
     count = len(parts) * fy
-    out = [pltpu.VMEM((rows, count * sub), jnp.float32)]
-    scratch = [
-        pltpu.VMEM((count, lat_dev, sub), jnp.bfloat16),
-        pltpu.SemaphoreType.DMA((count,)),
-        pltpu.VMEM(targets.shape, targets.dtype),
-        pltpu.SemaphoreType.DMA((3,)),
-    ]
+    out = [pltpu.VMEM((rows, fy * sub), jnp.float32)] * len(parts)
+    scratch = [pltpu.VMEM(targets.shape, targets.dtype), pltpu.SemaphoreType.DMA((3,))]
     if first:
         args = [in_hbm(x) for x in (*start, decoder, targets)]
         specs = [HBM] * 4
-        out.append(pltpu.VMEM((rows, lat_dev), jnp.bfloat16))
+        out += [
+            pltpu.VMEM((rows, lat_dev), jnp.bfloat16),
+            pltpu.VMEM((len(keep) * fy, lat_dev, sub), jnp.bfloat16),
+        ]
         scratch += [pltpu.VMEM(x.shape, x.dtype) for x in start]
+    elif loaded:
+        args, specs = [dense, in_vmem(decoder), in_hbm(targets)], [VMEM, VMEM, HBM]
     else:
-        args, specs = [dense, in_hbm(decoder), in_hbm(targets)], [VMEM, HBM, HBM]
-        if after is not None:
-            args.append(in_vmem(after))
-            specs.append(VMEM)
+        args = [dense, in_hbm(decoder), in_hbm(targets), in_vmem(after)]
+        specs = [VMEM, HBM, HBM, VMEM]
+    if not loaded:
+        scratch += [
+            pltpu.VMEM((count, lat_dev, sub), jnp.bfloat16),
+            pltpu.SemaphoreType.DMA((count + len(keep) * fy,)),
+        ]
     return pl.pallas_call(
-        functools.partial(decode_kernel, n, rows // n, chunks, parts, first),
+        functools.partial(decode_kernel, n, rows // n, chunks, parts, first, loaded, keep),
         out_shape=out,
         in_specs=specs,
         out_specs=[VMEM] * len(out),
@@ -165,43 +191,49 @@
     )(*args)
 
 
-def fetch_kernel(decoder_hbm, _, out_ref, sem):
-    step = out_ref.shape[0] // FETCHES
-    parts = [pl.ds(i * step, step) for i in range(FETCHES)]
-    copies = [
-        pltpu.make_async_copy(decoder_hbm.at[at], out_ref.at[at], sem.at[i])
-        for i, at in enumerate(parts)
-    ]
+def fetch_kernel(n, dys, decoder_hbm, _, out_ref, sem):
+    _, lat_dev, width = out_ref.shape
+    step = lat_dev // FETCHES
+    copies = []
+    for slot, (dc, dy) in enumerate((dc, dy) for dc in range(2) for dy in dys):
+        col = column(n, 0, 1, width, dy, dc)
+        for i in range(FETCHES):
+            at = pl.ds(i * step, step)
+            copies.append(
+                pltpu.make_async_copy(
+                    decoder_hbm.at[at, pl.ds(col, width)], out_ref.at[slot, at], sem.at[slot, i]
+                )
+            )
     for copy in copies:
         copy.start()
     for copy in copies:
         copy.wait()
 
 
-def fetch(decoder, after):
+def fetch(n, width, dys, decoder, after):
+    count = 2 * len(dys)
     return pl.pallas_call(
-        fetch_kernel,
-        out_shape=pltpu.VMEM(decoder.shape, decoder.dtype),
+        functools.partial(fetch_kernel, n, dys),
+        out_shape=pltpu.VMEM((count, decoder.shape[0], width), decoder.dtype),
         in_specs=[HBM, VMEM],
         out_specs=VMEM,
-        scratch_shapes=[pltpu.SemaphoreType.DMA((FETCHES,))],
+        scratch_shapes=[pltpu.SemaphoreType.DMA((count, FETCHES))],
         compiler_params=params(),
-        cost_estimate=cost(0, decoder.size * 2),
+        cost_estimate=cost(0, decoder.shape[0] * count * width * 2),
         name="fetch",
     )(in_hbm(decoder), in_vmem(after))
 
 
-def grad_kernel(n, places, counts, final, with_prev, *refs):
+def grad_kernel(n, slots, counts, final, with_prev, *refs):
     refs = list(refs)
     errs = [[refs.pop(0) for _ in range(count)] for count in counts]
     decoder_ref = refs.pop(0)
     total = refs.pop(0)[...] if with_prev else None
-    for parts, (dc, dy) in zip(errs, places):
+    for parts, slot in zip(errs, slots):
         err = parts[0][...] if len(parts) == 1 else jnp.concatenate([e[...] for e in parts], axis=0)
-        width = err.shape[1]
         part = lax.dot_general(
             err,
-            decoder_ref[:, pl.ds(column(n, 0, 1, width, dy, dc), width)],
+            decoder_ref[slot],
             (((1,), (1,)), ((), ())),
             preferred_element_type=jnp.float32,
         )
@@ -220,7 +252,7 @@
     group = rows // fz
     places = lax.broadcasted_iota(jnp.int32, (ROW_STEP, LANES), 1)
     pad = jnp.zeros((ROW_STEP, LANES - k_count), jnp.int32)
-    for j in range(fz):
+    for q, j in enumerate([0] + z_order(fz)):
         for s in range(0, group, ROW_STEP):
             first = (z ^ j) * group + s
             rows_at = pl.ds(pl.multiple_of(first, ROW_STEP), ROW_STEP)
@@ -228,9 +260,9 @@
             held = jnp.where(places < k_count, ids // LANES, -1)
             inside = ids % LANES
             acc = jnp.zeros((ROW_STEP, LANES), jnp.float32)
-            if j == 0:
+            if q == 0:
                 acc = jnp.where(places == k_count, loss_ref[s : s + ROW_STEP, :], acc)
-            here = slice(j * group + s, j * group + s + ROW_STEP)
+            here = slice(q * group + s, q * group + s + ROW_STEP)
             for t in range(lat_dev // LANES):
                 values = totals_ref[here, t * LANES : (t + 1) * LANES]
                 found = jnp.take_along_axis(values, inside, axis=1, mode="promise_in_bounds")
@@ -240,8 +272,8 @@
 
 
 def grad(n, rows, pieces, decoder, prev, final=None):
-    lat_dev = decoder.shape[0]
-    places = tuple(at for at, _ in pieces)
+    count, lat_dev, _ = decoder.shape
+    slots = tuple(dc * (count // 2) + dy % (count // 2) for (dc, dy), _ in pieces)
     counts = tuple(len(e) for _, e in pieces)
     args = [x for _, e in pieces for x in e] + [in_vmem(decoder)]
     if prev is not None:
@@ -251,7 +283,7 @@
     totals = pltpu.VMEM((rows, lat_dev), jnp.float32)
     size = pieces[0][1][0].shape[1] * len(pieces)
     return pl.pallas_call(
-        functools.partial(grad_kernel, n, places, counts, final is not None, prev is not None),
+        functools.partial(grad_kernel, n, slots, counts, final is not None, prev is not None),
         out_shape=totals if final is None else jax.ShapeDtypeStruct((n, rows // n, LANES), jnp.float32),
         in_specs=[VMEM] * len(args),
         out_specs=VMEM,
@@ -303,14 +335,24 @@
     def join(xs, axis):
         return xs[0] if len(xs) == 1 else jnp.concatenate(xs, axis=axis)
 
-    wide = fy * sub
-    others = tuple((p, dc) for dc in range(1, fc) for p in range(chunks))
-    part, dense = decode(n, chunks, sub, others, decoder, targets, (indices, codes))
-    came = swap(part, dc=1)
+    def in_order(xs, after=None):
+        for i, x in enumerate(xs):
+            if after is not None:
+                xs[i] = hold(x, after)
+            after = xs[i]
+        return xs
+
+    others = tuple((p, 1) for p in range(chunks))
+    *parts, dense, columns = decode(
+        n, chunks, sub, others, decoder, targets, (indices, codes), ((0, 0),)
+    )
+    came = [swap(part, dc=1) for part in parts]
     summed, leaving, after = [], [], None
     for p in range(chunks):
-        (part,) = decode(n, chunks, sub, ((p, 0),), decoder, targets, dense=dense, after=after)
-        total = part + came[:, p * wide : (p + 1) * wide]
+        (part,) = decode(
+            n, chunks, sub, ((p, 0),), decoder if p else columns, targets, dense=dense, after=after
+        )
+        total = part + came[p]
         blocks = [total[:, o * sub : (o + 1) * sub] for o in range(fy)]
         got = None
         for b in reversed(bits(fy)):
@@ -321,31 +363,39 @@
         leaving.append(after)
         summed.append((blocks[0], got))
 
-    fetched = fetch(decoder, leaving[-1])
+    wide = chunks * sub
+    half = fy // 2
+    near_columns = fetch(n, wide, tuple(range(half)), decoder, leaving[-1])
     sums, moved = [], []
     for p, (x, y) in enumerate(summed):
-        x = x + (hold(y, fetched) if p == 0 else y)
-        blocks = [
-            lax.dynamic_slice_in_dim(x, (z ^ j) * group, group, 0) for j in range(fz)
-        ]
-        sums.append(blocks[0])
-        moved.append([swap(e, dz=j) for j, e in enumerate(blocks) if j])
-    errs, loss = [], 0.0
+        x = x + (hold(y, near_columns) if p == 0 else y)
+        sums.append(lax.dynamic_slice_in_dim(x, z * group, group, 0))
+        moved.append(
+            [
+                swap(lax.dynamic_slice_in_dim(x, (z ^ j) * group, group, 0), dz=j)
+                for j in z_order(fz)
+            ]
+        )
+    errs, loss, after = [], 0.0, sums[-1]
     for p in range(chunks):
-        if p + 1 < chunks:
-            moved[p][-1] = hold(moved[p][-1], sums[p + 1])
-        if p:
-            moved[p][0] = hold(moved[p][0], errs[p - 1])
-        diff = sum(moved[p], sums[p])
+        diff = sum(in_order(moved[p], after), sums[p])
         loss = loss + jnp.sum(diff * diff, axis=1, keepdims=True)
         errs.append(diff.astype(jnp.bfloat16))
+        after = errs[p]
 
     err = join(errs, 1)
-    come = [err] + [swap(err, dz=j) for j in range(1, fz)]
-    half = fz // 2
-    near = [((0, 0), [join(come[:half], 0), join(come[half:], 0)])]
+    come = [swap(err, dz=j) for j in z_order(fz)]
+    far_columns = fetch(n, wide, tuple(range(half, fy)), decoder, err)
+    own_part = swap(err, dy=1)
+    come = in_order(come[:-1], far_columns) + come[-1:]
+    own_part = hold(own_part, come[-2])
+    come[-1] = hold(come[-1], own_part)
+    near = [((0, 0), [err, join(come[:-1], 0), come[-1]])]
     for b in bits(fy):
-        last = [((0, b | at[1]), [swap(e, dy=b) for e in parts]) for at, parts in near]
+        last = [
+            ((0, b | at[1]), in_order([own_part if e is err else swap(e, dy=b) for e in parts]))
+            for at, parts in near
+        ]
         near += last
     near = near[: -len(last)]
 
@@ -354,12 +404,12 @@
         return [((1, at[1]), [sent[i * rows : (i + 1) * rows]]) for i, (at, _) in enumerate(pieces)]
 
     far = to_core(near)
-    totals = grad(n, rows, near, fetched, None)
-    totals = grad(n, rows, far, fetched, totals)
-    last[-1][1][0] = hold(last[-1][1][0], totals)
+    totals = grad(n, rows, near, near_columns, None)
+    totals = grad(n, rows, far, near_columns, totals)
+    last[-1][1][-1] = hold(last[-1][1][-1], totals)
     far_last = to_core(last)
-    totals = grad(n, rows, last, fetched, totals)
-    back = grad(n, rows, far_last, fetched, totals, (indices, loss))
+    totals = grad(n, rows, last, far_columns, totals)
+    back = grad(n, rows, far_last, far_columns, totals, (indices, loss))
     pieces = near + far + last + far_last
     error = own_rows(n, [at for at, _ in pieces], own, width, [e[0][:group] for _, e in pieces])
 

time: 69.2 us -> 70.5 us (1.019)
  local copies, waits for them, and re-layouts: 6.21 us -> 3.8 us
  Pallas kernels: 15.6 us -> 17.6 us
  starting transfers between devices: 24 us -> 25.1 us
    unnamed x11 -> x10, local copies, waits for them, and re-layouts: 6 us -> 3.61 us
    ppermute x16 -> x18, starting transfers between devices: 19.7 us -> 21.4 us  [swap(): return lax.ppermute(x, 'lat', pairs(n, dz, dy, dc))]
    pallas_call x3, Pallas kernels: 7.51 us -> 8.55 us  [decode(): pl.pallas_call(functools.partial(decode_kernel, n, rows // n, chunks, par...]
    pallas_call x5 -> x6, Pallas kernels: 7.25 us -> 8.2 us  [the longest x2 4.44 us: fetch(): pl.pallas_call(functools.partial(fetch_kernel, n, dys), out_shape=pltpu.V...]
    ppermute x16 -> x18, waiting for transfers between devices: 15.2 us -> 15.7 us  [swap(): return lax.ppermute(x, 'lat', pairs(n, dz, dy, dc))]
  transfers between devices with their start and end apart: 17 -> 19, of which waited for: 10 -> 9; matrix products, arithmetic and copies ran while one was open for 1% -> 1% of each run, Pallas kernels for 15% -> 14%
where the time goes in v8:
time: 70.5 us; the launch traced here: 70.2 us
  starting transfers between devices  25.1 us (36%)
  waiting for transfers between devices  21.5 us (30%)
  Pallas kernels  17.6 us (25%)
  local copies, waits for them, and re-layouts  3.8 us (5%)
  other arithmetic  1.22 us (2%)
  between operations  0.92 us (1%)
    ppermute x18, starting transfers between devices, swap(): return lax.ppermute(x, 'lat', pairs(n, dz, dy, dc))  21.4 us
    ppermute x18, waiting for transfers between devices, swap(): return lax.ppermute(x, 'lat', pairs(n, dz, dy, dc))  15.7 us
    pallas_call x3, Pallas kernels, decode(): pl.pallas_call(functools.partial(decode_kernel, n, rows // n, chunks, par...  8.55 us
    all_to_all x1, waiting for transfers between devices, local(): back = jnp.sum(lax.all_to_all(back, 'lat', 0, 0, tiled=True), axis=0)  5.76 us
    pallas_call x2, Pallas kernels, fetch(): pl.pallas_call(functools.partial(fetch_kernel, n, dys), out_shape=pltpu.V...  4.44 us
    pallas_call x4, Pallas kernels, grad(): pl.pallas_call(functools.partial(grad_kernel, n, slots, counts, final is...  3.76 us
    all_to_all x1, starting transfers between devices, local(): back = jnp.sum(lax.all_to_all(back, 'lat', 0, 0, tiled=True), axis=0)  3.69 us
    unnamed x10, local copies, waits for them, and re-layouts  3.61 us
  transfers between devices with their start and end apart: 19, of which 9 were waited for; matrix products, arithmetic and copies ran while one was open for 1% of the time, Pallas kernels for 14%

profile of v8, /device:TPU:0, one launch (start us, length us, event | category | flops | bytes accessed | tf_op | source)
XLA Modules:
  0.0 70.2 jit_solution(14486971269595585696)
XLA Ops:
  0.6 5.3 %decode.3 = (f32[64,2048]{1,0:T(8,128)S(1)}, f32[64,2048]{1,0:T(8,128)S(1)}, bf16[64,512]{1,0:T(8,128)(2,1)S(1)}, bf16[2,512,1024]{2,1,0:T(8,128)(2,1)S(1)}) custom-call(s32[64,64]{1,0:T(8,128)} %refs_3_.3, bf16[64,64]{1,0:T(8,128)(2,1)} %refs_1_.2, bf16[512,8192]{1,0:T(8,128)(2,1)} %decoder_hbm.3, bf16[4,8192]{1,0:T(4,128)(2,1)} %refs_2_.5), custom_call_target="tpu_custom_call" | custom-call | flops 268435456 | bytes 8388608 | tf_op jit(solution)/shard_map/decode/pallas_call | solution.py:182
  5.9 0.5 collective-permute-start
  6.4 0.1 collective-permute-start.2
  6.5 1.3 %decode.4 = f32[64,2048]{1,0:T(8,128)S(1)} custom-call(bf16[64,512]{1,0:T(8,128)(2,1)S(1)} %get-tuple-element.7.refs_0_, bf16[2,512,1024]{2,1,0:T(8,128)(2,1)S(1)} %get-tuple-element.8.refs_1_, bf16[4,8192]{1,0:T(4,128)(2,1)} %refs_2_.5), custom_call_target="tpu_custom_call" | custom-call | flops 134217728 | bytes 4194304 | tf_op jit(solution)/shard_map/decode/pallas_call | solution.py:182
  7.9 0.1 collective-permute-done
  8.0 0.1 add.52
  8.1 3.0 %collective-permute-start.1 = (f32[64,1024]{1,0:T(8,128)S(1)}, f32[64,1024]{1,0:T(8,128)S(1)}, u32[]{:S(2)}, u32[]{:S(2)}) collective-permute-start(f32[64,1024]{1,0:T(8,128)S(1)} %slice.33.refs_3_), channel_id=1, source_target_pairs={{0,2},{1,3},{2,0},{3,1},{4,6},{5,7},{6,4},{7,5},{8,10},{9,11},{10,... | collective-permute-start | bytes 786440 | tf_op jit(solution)/shard_map/ppermute | solution.py:333
  11.0 1.9 %decode.5 = f32[64,2048]{1,0:T(8,128)S(1)} custom-call(bf16[64,512]{1,0:T(8,128)(2,1)S(1)} %get-tuple-element.7.refs_0_, bf16[512,8192]{1,0:T(8,128)(2,1)} %decoder_hbm.3, bf16[4,8192]{1,0:T(4,128)(2,1)} %refs_2_.5, f32[64,1024]{1,0:T(8,128)S(1)} %slice.33.refs_3_), custom_call_target="tpu_custom_call" | custom-call | flops 134217728 | bytes 4194304 | tf_op jit(solution)/shard_map/decode/pallas_call | solution.py:182
  12.9 0.0 collective-permute-done.2
  13.0 0.1 add.53
  13.0 0.1 collective-permute-start.4
  13.2 2.2 %fetch.2.refs_1_.refs_3_ = bf16[2,512,2048]{2,1,0:T(8,128)(2,1)S(1)} custom-call(bf16[512,8192]{1,0:T(8,128)(2,1)} %decoder_hbm.3, f32[64,1024]{1,0:T(8,128)S(1)} %slice.34._), custom_call_target="tpu_custom_call" | custom-call | bytes 4194304 | tf_op jit(solution)/shard_map/fetch/pallas_call | solution.py:215
  15.4 2.7 %collective-permute-done.1.refs_0_ = f32[64,1024]{1,0:T(8,128)S(1)} collective-permute-done((f32[64,1024]{1,0:T(8,128)S(1)}, f32[64,1024]{1,0:T(8,128)S(1)}, u32[]{:S(2)}, u32[]{:S(2)}) %collective-permute-start.1) | collective-permute-done | bytes 262176 | tf_op jit(solution)/shard_map/ppermute | solution.py:333
  18.2 3.2 %collective-permute-start.6 = (f32[16,1024]{1,0:T(8,128)S(1)}, f32[16,1024]{1,0:T(8,128)S(1)}, u32[]{:S(2)}, u32[]{:S(2)}) collective-permute-start(f32[16,1024]{1,0:T(8,128)S(1)} %get-tuple-element.20), channel_id=1, source_target_pairs={{0,8},{1,9},{2,10},{3,11},{4,12},{5,13},{6,14},{7,15},{8,0},{9,1},... | collective-permute-start | bytes 196616 | tf_op jit(solution)/shard_map/ppermute | solution.py:333
  21.4 1.6 %collective-permute-start.5 = (f32[16,1024]{1,0:T(8,128)S(1)}, f32[16,1024]{1,0:T(8,128)S(1)}, u32[]{:S(2)}, u32[]{:S(2)}) collective-permute-start(f32[16,1024]{1,0:T(8,128)S(1)} %get-tuple-element.21), channel_id=1, source_target_pairs={{0,4},{1,5},{2,6},{3,7},{4,0},{5,1},{6,2},{7,3},{8,12},{9,13},{10,... | collective-permute-start | bytes 196616 | tf_op jit(solution)/shard_map/ppermute | solution.py:333
  22.9 0.0 collective-permute-start.3
  22.9 0.3 collective-permute-done.4
  23.3 2.9 %collective-permute-start.9 = (f32[16,1024]{1,0:T(8,128)S(1)}, f32[16,1024]{1,0:T(8,128)S(1)}, u32[]{:S(2)}, u32[]{:S(2)}) collective-permute-start(f32[16,1024]{1,0:T(8,128)S(1)} %get-tuple-element.16), channel_id=1, source_target_pairs={{0,8},{1,9},{2,10},{3,11},{4,12},{5,13},{6,14},{7,15},{8,0},{9,1},... | collective-permute-start | bytes 196616 | tf_op jit(solution)/shard_map/ppermute | solution.py:333
  26.2 1.6 %collective-permute-start.8 = (f32[16,1024]{1,0:T(8,128)S(1)}, f32[16,1024]{1,0:T(8,128)S(1)}, u32[]{:S(2)}, u32[]{:S(2)}) collective-permute-start(f32[16,1024]{1,0:T(8,128)S(1)} %get-tuple-element.17), channel_id=1, source_target_pairs={{0,4},{1,5},{2,6},{3,7},{4,0},{5,1},{6,2},{7,3},{8,12},{9,13},{10,... | collective-permute-start | bytes 196616 | tf_op jit(solution)/shard_map/ppermute | solution.py:333
  27.8 1.8 %collective-permute-done.3.refs_0_ = f32[16,1024]{1,0:T(8,128)S(1)} collective-permute-done((f32[16,1024]{1,0:T(8,128)S(1)}, f32[16,1024]{1,0:T(8,128)S(1)}, u32[]{:S(2)}, u32[]{:S(2)}) %collective-permute-start.3) | collective-permute-done | bytes 65568 | tf_op jit(solution)/shard_map/ppermute | solution.py:333
  29.6 0.3 collective-permute-start.7
  29.9 0.0 collective-permute-done.5.refs_0_
  29.9 0.0 collective-permute-done.6.refs_0_
  29.9 0.1 multiply_reduce_fusion.1
  30.0 5.7 %collective-permute-done.7.refs_0_ = f32[16,1024]{1,0:T(8,128)S(1)} collective-permute-done((f32[16,1024]{1,0:T(8,128)S(1)}, f32[16,1024]{1,0:T(8,128)S(1)}, u32[]{:S(2)}, u32[]{:S(2)}) %collective-permute-start.7) | collective-permute-done | bytes 65568 | tf_op jit(solution)/shard_map/ppermute | solution.py:333
  35.7 0.0 collective-permute-done.8.refs_0_
  35.7 0.0 collective-permute-done.9.refs_0_
  35.7 0.1 multiply_reduce_fusion
  35.9 0.3 collective-permute-start.10
  36.2 0.0 collective-permute-start.11
  36.2 1.5 %collective-permute-start.13 = (bf16[16,2048]{1,0:T(8,128)(2,1)S(1)}, bf16[16,2048]{1,0:T(8,128)(2,1)S(1)}, u32[]{:S(2)}, u32[]{:S(2)}) collective-permute-start(bf16[16,2048]{1,0:T(8,128)(2,1)S(1)} %pad_maximum_fusion.3._.refs_0_), channel_id=1, source_target_pairs={{0,2},{1,3},{2,0},{3,1},{4,6},{5,7},{6,4},{7,5},{8,10},{9,11},{10,... | collective-permute-start | bytes 196616 | tf_op jit(solution)/shard_map/ppermute | solution.py:333
  37.7 4.2 %collective-permute-start.12 = (bf16[16,2048]{1,0:T(8,128)(2,1)S(1)}, bf16[16,2048]{1,0:T(8,128)(2,1)S(1)}, u32[]{:S(2)}, u32[]{:S(2)}) collective-permute-start(bf16[16,2048]{1,0:T(8,128)(2,1)S(1)} %pad_maximum_fusion.3._.refs_0_), channel_id=1, source_target_pairs={{0,8},{1,9},{2,10},{3,11},{4,12},{5,13},{6,14},{7,15},{8,0},{9,1},... | collective-permute-start | bytes 196616 | tf_op jit(solution)/shard_map/ppermute | solution.py:333
  41.9 2.2 %fetch.3.refs_1_.refs_3_ = bf16[2,512,2048]{2,1,0:T(8,128)(2,1)S(1)} custom-call(bf16[512,8192]{1,0:T(8,128)(2,1)} %decoder_hbm.3, bf16[16,2048]{1,0:T(8,128)(2,1)S(1)} %pad_maximum_fusion.3._.refs_0_), custom_call_target="tpu_custom_call" | custom-call | bytes 4194304 | tf_op jit(solution)/shard_map/fetch/pallas_call | solution.py:215
  44.1 0.0 copy-start
  44.1 0.0 collective-permute-done.10.refs_0_
  44.1 0.0 collective-permute-done.11.refs_0_
  44.1 0.0 collective-permute-done.13.refs_0_
  44.2 0.6 collective-permute-done.12.refs_0_
  44.8 0.1 collective-permute-start.14
  44.9 0.6 collective-permute-start.15
  45.5 1.5 %collective-permute-start.16 = (bf16[16,2048]{1,0:T(8,128)(2,1)S(1)}, bf16[16,2048]{1,0:T(8,128)(2,1)S(1)}, u32[]{:S(2)}, u32[]{:S(2)}) collective-permute-start(bf16[16,2048]{1,0:T(8,128)(2,1)S(1)} %hold.24.refs_2_), channel_id=1, source_target_pairs={{0,2},{1,3},{2,0},{3,1},{4,6},{5,7},{6,4},{7,5},{8,10},{9,11},{10,... | collective-permute-start | bytes 196616 | tf_op jit(solution)/shard_map/ppermute | solution.py:333
  47.0 0.8 %grad.4.refs_2_ = f32[64,512]{1,0:T(8,128)S(1)} custom-call(bf16[16,2048]{1,0:T(8,128)(2,1)S(1)} %pad_maximum_fusion.3._.refs_0_, bf16[32,2048]{1,0:T(8,128)(2,1)S(1)} %pad_maximum_fusion.2.refs_1_, bf16[16,2048]{1,0:T(8,128)(2,1)S(1)} %hold.24.refs_2_, bf16[2,512,2048]{2,1,0:T(8,128)(2,1)S(1)} %fetch.2.refs_1_.refs_3_), custom_call_target="tpu_custom_call" | custom-call | flops 134217728 | bytes 4194304 | tf_op jit(solution)/shard_map/grad/pallas_call | solution.py:285
  47.8 0.0 copy-done
  47.8 3.5 %collective-permute-done.15.refs_0_ = bf16[32,2048]{1,0:T(8,128)(2,1)S(1)} collective-permute-done((bf16[32,2048]{1,0:T(8,128)(2,1)S(1)}, bf16[32,2048]{1,0:T(8,128)(2,1)S(1)}, u32[]{:S(2)}, u32[]{:S(2)}) %collective-permute-start.15) | collective-permute-done | bytes 131104 | tf_op jit(solution)/shard_map/ppermute | solution.py:333
  51.3 1.0 %collective-permute-done.16.refs_0_ = bf16[16,2048]{1,0:T(8,128)(2,1)S(1)} collective-permute-done((bf16[16,2048]{1,0:T(8,128)(2,1)S(1)}, bf16[16,2048]{1,0:T(8,128)(2,1)S(1)}, u32[]{:S(2)}, u32[]{:S(2)}) %collective-permute-start.16) | collective-permute-done | bytes 65568 | tf_op jit(solution)/shard_map/ppermute | solution.py:333
  52.3 0.0 copy-start.3
  52.3 0.0 collective-permute-done.14.refs_0_
  52.3 0.8 %grad.5.refs_1_.refs_4_ = f32[64,512]{1,0:T(8,128)S(1)} custom-call(bf16[64,2048]{1,0:T(8,128)(2,1)S(1)} %collective-permute-done.14.refs_0_, bf16[2,512,2048]{2,1,0:T(8,128)(2,1)S(1)} %fetch.2.refs_1_.refs_3_, f32[64,512]{1,0:T(8,128)S(1)} %grad.4.refs_2_), custom_call_target="tpu_custom_call" | custom-call | flops 134217728 | bytes 4194304 | tf_op jit(solution)/shard_map/grad/pallas_call | solution.py:285
  53.1 0.1 collective-permute-start.17
  53.2 0.1 copy.21.refs_4_
  53.3 0.0 copy-start.1
  53.3 2.2 %copy-done.1 = bf16[2,512,2048]{2,1,0:T(8,128)(2,1)S(1)} copy-done((bf16[2,512,2048]{2,1,0:T(8,128)(2,1)S(1)}, bf16[2,512,2048]{2,1,0:T(8,128)(2,1)}, u32[]{:S(2)}) %copy-start.1) | copy-done | bytes 4194328
  55.4 0.0 copy-start.2
  55.4 0.8 %grad.6.refs_2_ = f32[64,512]{1,0:T(8,128)S(1)} custom-call(bf16[16,2048]{1,0:T(8,128)(2,1)S(1)} %hold.23.refs_1_.refs_2_.refs_0_, bf16[32,2048]{1,0:T(8,128)(2,1)S(1)} %hold.25.refs_1_, bf16[16,2048]{1,0:T(8,128)(2,1)S(1)} %hold.27.refs_2_, bf16[2,512,2048]{2,1,0:T(8,128)(2,1)S(1)} %copy-done.1, f32[64,512]{1,0:T(8,128)S(1)} %grad.5.refs_1_.refs_4_), custom_call_target="tpu_custom_call" | custom-call | flops 134217728 | bytes 4194304 | tf_op jit(solution)/shard_map/grad/pallas_call | solution.py:285
  56.2 0.0 collective-permute-done.17.refs_0_
  56.2 0.0 copy-done.3
  56.2 1.4 %copy-done.2 = bf16[2,512,2048]{2,1,0:T(8,128)(2,1)S(1)} copy-done((bf16[2,512,2048]{2,1,0:T(8,128)(2,1)S(1)}, bf16[2,512,2048]{2,1,0:T(8,128)(2,1)}, u32[]{:S(2)}) %copy-start.2) | copy-done | bytes 4194328
  57.6 1.5 %grad.7 = f32[16,4,128]{2,1,0:T(4,128)} custom-call(bf16[64,2048]{1,0:T(8,128)(2,1)S(1)} %collective-permute-done.17.refs_0_, bf16[2,512,2048]{2,1,0:T(8,128)(2,1)S(1)} %copy-done.2, f32[64,512]{1,0:T(8,128)S(1)} %grad.6.refs_2_, s32[64,64]{1,0:T(8,128)S(1)} %copy-done.3, f32[16,1]{1,0:T(8,128)S(1)} %copy.21.refs_4_), custom_call_target="tpu_custom_call" | custom-call | flops 134217728 | bytes 4194304 | tf_op jit(solution)/shard_map/grad/pallas_call | solution.py:285
  59.1 3.7 %all-to-all-start = ((f32[16,4,128]{2,1,0:T(4,128)}), f32[16,4,128]{2,1,0:T(4,128)S(1)}, u32[]{:S(2)}, u32[]{:S(2)}) async-start(f32[16,4,128]{2,1,0:T(4,128)} %grad.7), calls=%async_computation | async-start | bytes 65536 | tf_op jit(solution)/shard_map/all_to_all | solution.py:416
  62.9 0.8 %own_rows.1 = bf16[4,8192]{1,0:T(4,128)(2,1)} custom-call(bf16[16,2048]{1,0:T(8,128)(2,1)S(1)} %pad_maximum_fusion.3._.refs_0_, bf16[16,2048]{1,0:T(8,128)(2,1)S(1)} %slice.36.refs_1_, bf16[16,2048]{1,0:T(8,128)(2,1)S(1)} %hold.23.refs_1_.refs_2_.refs_0_, bf16[16,2048]{1,0:T(8,128)(2,1)S(1)} %slice.37.refs_3_), custom_call_target="tpu_custom_call" | custom-call | tf_op jit(solution)/shard_map/own_rows/pallas_call | solution.py:311
  63.7 5.8 %all-to-all-done = f32[16,4,128]{2,1,0:T(4,128)S(1)} async-done(((f32[16,4,128]{2,1,0:T(4,128)}), f32[16,4,128]{2,1,0:T(4,128)S(1)}, u32[]{:S(2)}, u32[]{:S(2)}) %all-to-all-start) | async-done | bytes 32800 | tf_op jit(solution)/shard_map/all_to_all | solution.py:416
  69.5 0.0 copy-start.4
  69.5 0.7 multiply_reduce_fusion.2
  70.2 0.0 copy-done.4
  (28 shorter events, 0.3 us)
Async XLA Ops:
  5.9 2.1 %collective-permute-start = (f32[64,2048]{1,0:T(8,128)S(1)}, f32[64,2048]{1,0:T(8,128)S(1)}, u32[]{:S(2)}, u32[]{:S(2)}) collective-permute-start(f32[64,2048]{1,0:T(8,128)S(1)} %get-tuple-element.9), channel_id=1, source_target_pairs={{0,1},{1,0},{2,3},{3,2},{4,5},{5,4},{6,7},{7,6},{8,9},{9,8},{10,11... | collective-permute-start | bytes 1572872 | tf_op jit(solution)/shard_map/ppermute | solution.py:333
  6.4 6.5 %collective-permute-start.2 = (f32[64,2048]{1,0:T(8,128)S(1)}, f32[64,2048]{1,0:T(8,128)S(1)}, u32[]{:S(2)}, u32[]{:S(2)}) collective-permute-start(f32[64,2048]{1,0:T(8,128)S(1)} %get-tuple-element.10), channel_id=1, source_target_pairs={{0,1},{1,0},{2,3},{3,2},{4,5},{5,4},{6,7},{7,6},{8,9},{9,8},{10,11... | collective-permute-start | bytes 1572872 | tf_op jit(solution)/shard_map/ppermute | solution.py:333
  8.1 10.0 %collective-permute-start.1 = (f32[64,1024]{1,0:T(8,128)S(1)}, f32[64,1024]{1,0:T(8,128)S(1)}, u32[]{:S(2)}, u32[]{:S(2)}) collective-permute-start(f32[64,1024]{1,0:T(8,128)S(1)} %slice.33.refs_3_), channel_id=1, source_target_pairs={{0,2},{1,3},{2,0},{3,1},{4,6},{5,7},{6,4},{7,5},{8,10},{9,11},{10,... | collective-permute-start | bytes 786440 | tf_op jit(solution)/shard_map/ppermute | solution.py:333
  13.0 10.2 %collective-permute-start.4 = (f32[64,1024]{1,0:T(8,128)S(1)}, f32[64,1024]{1,0:T(8,128)S(1)}, u32[]{:S(2)}, u32[]{:S(2)}) collective-permute-start(f32[64,1024]{1,0:T(8,128)S(1)} %slice.34._), channel_id=1, source_target_pairs={{0,2},{1,3},{2,0},{3,1},{4,6},{5,7},{6,4},{7,5},{8,10},{9,11},{10,... | collective-permute-start | bytes 786440 | tf_op jit(solution)/shard_map/ppermute | solution.py:333
  18.2 11.7 %collective-permute-start.6 = (f32[16,1024]{1,0:T(8,128)S(1)}, f32[16,1024]{1,0:T(8,128)S(1)}, u32[]{:S(2)}, u32[]{:S(2)}) collective-permute-start(f32[16,1024]{1,0:T(8,128)S(1)} %get-tuple-element.20), channel_id=1, source_target_pairs={{0,8},{1,9},{2,10},{3,11},{4,12},{5,13},{6,14},{7,15},{8,0},{9,1},... | collective-permute-start | bytes 196616 | tf_op jit(solution)/shard_map/ppermute | solution.py:333
  21.4 8.5 %collective-permute-start.5 = (f32[16,1024]{1,0:T(8,128)S(1)}, f32[16,1024]{1,0:T(8,128)S(1)}, u32[]{:S(2)}, u32[]{:S(2)}) collective-permute-start(f32[16,1024]{1,0:T(8,128)S(1)} %get-tuple-element.21), channel_id=1, source_target_pairs={{0,4},{1,5},{2,6},{3,7},{4,0},{5,1},{6,2},{7,3},{8,12},{9,13},{10,... | collective-permute-start | bytes 196616 | tf_op jit(solution)/shard_map/ppermute | solution.py:333
  22.9 6.6 %collective-permute-start.3 = (f32[16,1024]{1,0:T(8,128)S(1)}, f32[16,1024]{1,0:T(8,128)S(1)}, u32[]{:S(2)}, u32[]{:S(2)}) collective-permute-start(f32[16,1024]{1,0:T(8,128)S(1)} %get-tuple-element.19), channel_id=1, source_target_pairs={{0,12},{1,13},{2,14},{3,15},{4,8},{5,9},{6,10},{7,11},{8,4},{9,5},... | collective-permute-start | bytes 196616 | tf_op jit(solution)/shard_map/ppermute | solution.py:333
  23.3 12.4 %collective-permute-start.9 = (f32[16,1024]{1,0:T(8,128)S(1)}, f32[16,1024]{1,0:T(8,128)S(1)}, u32[]{:S(2)}, u32[]{:S(2)}) collective-permute-start(f32[16,1024]{1,0:T(8,128)S(1)} %get-tuple-element.16), channel_id=1, source_target_pairs={{0,8},{1,9},{2,10},{3,11},{4,12},{5,13},{6,14},{7,15},{8,0},{9,1},... | collective-permute-start | bytes 196616 | tf_op jit(solution)/shard_map/ppermute | solution.py:333
  26.2 9.6 %collective-permute-start.8 = (f32[16,1024]{1,0:T(8,128)S(1)}, f32[16,1024]{1,0:T(8,128)S(1)}, u32[]{:S(2)}, u32[]{:S(2)}) collective-permute-start(f32[16,1024]{1,0:T(8,128)S(1)} %get-tuple-element.17), channel_id=1, source_target_pairs={{0,4},{1,5},{2,6},{3,7},{4,0},{5,1},{6,2},{7,3},{8,12},{9,13},{10,... | collective-permute-start | bytes 196616 | tf_op jit(solution)/shard_map/ppermute | solution.py:333
  29.6 6.2 %collective-permute-start.7 = (f32[16,1024]{1,0:T(8,128)S(1)}, f32[16,1024]{1,0:T(8,128)S(1)}, u32[]{:S(2)}, u32[]{:S(2)}) collective-permute-start(f32[16,1024]{1,0:T(8,128)S(1)} %get-tuple-element.18), channel_id=1, source_target_pairs={{0,12},{1,13},{2,14},{3,15},{4,8},{5,9},{6,10},{7,11},{8,4},{9,5},... | collective-permute-start | bytes 196616 | tf_op jit(solution)/shard_map/ppermute | solution.py:333
  35.9 8.2 %collective-permute-start.10 = (bf16[16,2048]{1,0:T(8,128)(2,1)S(1)}, bf16[16,2048]{1,0:T(8,128)(2,1)S(1)}, u32[]{:S(2)}, u32[]{:S(2)}) collective-permute-start(bf16[16,2048]{1,0:T(8,128)(2,1)S(1)} %pad_maximum_fusion.3._.refs_0_), channel_id=1, source_target_pairs={{0,12},{1,13},{2,14},{3,15},{4,8},{5,9},{6,10},{7,11},{8,4},{9,5},... | collective-permute-start | bytes 196616 | tf_op jit(solution)/shard_map/ppermute | solution.py:333
  36.2 8.0 %collective-permute-start.11 = (bf16[16,2048]{1,0:T(8,128)(2,1)S(1)}, bf16[16,2048]{1,0:T(8,128)(2,1)S(1)}, u32[]{:S(2)}, u32[]{:S(2)}) collective-permute-start(bf16[16,2048]{1,0:T(8,128)(2,1)S(1)} %pad_maximum_fusion.3._.refs_0_), channel_id=1, source_target_pairs={{0,4},{1,5},{2,6},{3,7},{4,0},{5,1},{6,2},{7,3},{8,12},{9,13},{10,... | collective-permute-start | bytes 196616 | tf_op jit(solution)/shard_map/ppermute | solution.py:333
  36.2 8.0 %collective-permute-start.13 = (bf16[16,2048]{1,0:T(8,128)(2,1)S(1)}, bf16[16,2048]{1,0:T(8,128)(2,1)S(1)}, u32[]{:S(2)}, u32[]{:S(2)}) collective-permute-start(bf16[16,2048]{1,0:T(8,128)(2,1)S(1)} %pad_maximum_fusion.3._.refs_0_), channel_id=1, source_target_pairs={{0,2},{1,3},{2,0},{3,1},{4,6},{5,7},{6,4},{7,5},{8,10},{9,11},{10,... | collective-permute-start | bytes 196616 | tf_op jit(solution)/shard_map/ppermute | solution.py:333
  37.7 7.1 %collective-permute-start.12 = (bf16[16,2048]{1,0:T(8,128)(2,1)S(1)}, bf16[16,2048]{1,0:T(8,128)(2,1)S(1)}, u32[]{:S(2)}, u32[]{:S(2)}) collective-permute-start(bf16[16,2048]{1,0:T(8,128)(2,1)S(1)} %pad_maximum_fusion.3._.refs_0_), channel_id=1, source_target_pairs={{0,8},{1,9},{2,10},{3,11},{4,12},{5,13},{6,14},{7,15},{8,0},{9,1},... | collective-permute-start | bytes 196616 | tf_op jit(solution)/shard_map/ppermute | solution.py:333
  44.1 3.7 %copy-start = (bf16[2,512,2048]{2,1,0:T(8,128)(2,1)}, bf16[2,512,2048]{2,1,0:T(8,128)(2,1)S(1)}, u32[]{:S(2)}) copy-start(bf16[2,512,2048]{2,1,0:T(8,128)(2,1)S(1)} %fetch.3.refs_1_.refs_3_) | copy-start | bytes 12582916
  44.8 7.5 %collective-permute-start.14 = (bf16[64,2048]{1,0:T(8,128)(2,1)S(1)}, bf16[64,2048]{1,0:T(8,128)(2,1)S(1)}, u32[]{:S(2)}, u32[]{:S(2)}) collective-permute-start(bf16[64,2048]{1,0:T(8,128)(2,1)S(1)} %pad_maximum_fusion), channel_id=1, source_target_pairs={{0,1},{1,0},{2,3},{3,2},{4,5},{5,4},{6,7},{7,6},{8,9},{9,8},{10,11... | collective-permute-start | bytes 786440 | tf_op jit(solution)/shard_map/ppermute | solution.py:333
  44.9 6.4 %collective-permute-start.15 = (bf16[32,2048]{1,0:T(8,128)(2,1)S(1)}, bf16[32,2048]{1,0:T(8,128)(2,1)S(1)}, u32[]{:S(2)}, u32[]{:S(2)}) collective-permute-start(bf16[32,2048]{1,0:T(8,128)(2,1)S(1)} %pad_maximum_fusion.2.refs_1_), channel_id=1, source_target_pairs={{0,2},{1,3},{2,0},{3,1},{4,6},{5,7},{6,4},{7,5},{8,10},{9,11},{10,... | collective-permute-start | bytes 393224 | tf_op jit(solution)/shard_map/ppermute | solution.py:333
  45.5 6.8 %collective-permute-start.16 = (bf16[16,2048]{1,0:T(8,128)(2,1)S(1)}, bf16[16,2048]{1,0:T(8,128)(2,1)S(1)}, u32[]{:S(2)}, u32[]{:S(2)}) collective-permute-start(bf16[16,2048]{1,0:T(8,128)(2,1)S(1)} %hold.24.refs_2_), channel_id=1, source_target_pairs={{0,2},{1,3},{2,0},{3,1},{4,6},{5,7},{6,4},{7,5},{8,10},{9,11},{10,... | collective-permute-start | bytes 196616 | tf_op jit(solution)/shard_map/ppermute | solution.py:333
  52.3 3.9 %copy-start.3 = (s32[64,64]{1,0:T(8,128)S(1)}, s32[64,64]{1,0:T(8,128)}, u32[]{:S(2)}) copy-start(s32[64,64]{1,0:T(8,128)} %refs_3_.3) | copy-start | bytes 49156
  53.1 3.1 %collective-permute-start.17 = (bf16[64,2048]{1,0:T(8,128)(2,1)S(1)}, bf16[64,2048]{1,0:T(8,128)(2,1)S(1)}, u32[]{:S(2)}, u32[]{:S(2)}) collective-permute-start(bf16[64,2048]{1,0:T(8,128)(2,1)S(1)} %pad_maximum_fusion.1), channel_id=1, source_target_pairs={{0,1},{1,0},{2,3},{3,2},{4,5},{5,4},{6,7},{7,6},{8,9},{9,8},{10,11... | collective-permute-start | bytes 786440 | tf_op jit(solution)/shard_map/ppermute | solution.py:333
  53.3 2.2 %copy-start.1 = (bf16[2,512,2048]{2,1,0:T(8,128)(2,1)S(1)}, bf16[2,512,2048]{2,1,0:T(8,128)(2,1)}, u32[]{:S(2)}) copy-start(bf16[2,512,2048]{2,1,0:T(8,128)(2,1)} %copy-done) | copy-start | bytes 12582916
  55.4 2.2 %copy-start.2 = (bf16[2,512,2048]{2,1,0:T(8,128)(2,1)S(1)}, bf16[2,512,2048]{2,1,0:T(8,128)(2,1)}, u32[]{:S(2)}) copy-start(bf16[2,512,2048]{2,1,0:T(8,128)(2,1)} %copy-done) | copy-start | bytes 12582916
  59.1 10.3 %all-to-all-start = ((f32[16,4,128]{2,1,0:T(4,128)}), f32[16,4,128]{2,1,0:T(4,128)S(1)}, u32[]{:S(2)}, u32[]{:S(2)}) async-start(f32[16,4,128]{2,1,0:T(4,128)} %grad.7), calls=%async_computation | async-start | bytes 65536 | tf_op jit(solution)/shard_map/all_to_all | solution.py:416
  69.5 0.7 copy-start.4

commit v9 on v8

--- a/solution.py
+++ b/solution.py
@@ -11,7 +11,7 @@
 ROW_STEP = 16
 LANES = 128
 SUBLANES = 8
-FETCHES = 4
+LOADS = 8
 VMEM = pl.BlockSpec(memory_space=pltpu.VMEM)
 HBM = pl.BlockSpec(memory_space=pltpu.HBM)
 
@@ -82,11 +82,20 @@
     )(*[in_vmem(a) for a in (x, *after)])
 
 
-def load(decoder_hbm, col, buf, sem):
-    return pltpu.make_async_copy(decoder_hbm.at[:, pl.ds(col, buf.shape[1])], buf, sem)
-
-
-def decode_kernel(n, own, chunks, parts, first, loaded, keep, *refs):
+def loads_of(decoder_hbm, col, buf, sem):
+    count = sem.shape[0]
+    step = buf.shape[0] // count
+    return [
+        pltpu.make_async_copy(
+            decoder_hbm.at[pl.ds(i * step, step), pl.ds(col, buf.shape[1])],
+            buf.at[pl.ds(i * step, step)],
+            sem.at[i],
+        )
+        for i in range(count)
+    ]
+
+
+def decode_kernel(n, own, chunks, parts, first, *refs):
     fz, fy, fc = factors(n)
     me = lax.axis_index("lat")
     refs = list(refs)
@@ -94,32 +103,32 @@
         ids_hbm, codes_hbm = refs.pop(0), refs.pop(0)
     else:
         dense_ref = refs.pop(0)
-    decoder_ref, targets_hbm = refs.pop(0), refs.pop(0)
-    if not first and not loaded:
+    decoder_hbm, targets_hbm = refs.pop(0), refs.pop(0)
+    if len(refs) > 4 + len(parts) and not first:
         refs.pop(0)
     outs = [refs.pop(0) for _ in parts]
     if first:
-        dense_ref, kept_ref = refs.pop(0), refs.pop(0)
-    targets_ref, small = refs.pop(0), refs.pop(0)
+        dense_ref = refs.pop(0)
+    buf, sem, targets_ref, small = refs[:4]
     smalls_in = [(targets_hbm, targets_ref)]
     if first:
-        smalls_in = [(ids_hbm, refs[0]), (codes_hbm, refs[1])] + smalls_in
-        ids_ref, codes_ref = refs.pop(0), refs.pop(0)
+        ids_ref, codes_ref = refs[4:]
+        smalls_in = [(ids_hbm, ids_ref), (codes_hbm, codes_ref)] + smalls_in
     smalls = [pltpu.make_async_copy(a, b, small.at[i]) for i, (a, b) in enumerate(smalls_in)]
     for copy in smalls:
         copy.start()
     rows, lat_dev = dense_ref.shape
     sub = outs[0].shape[1] // fy
     cols = [column(n, p, chunks, sub, o, dc) for p, dc in parts for o in range(fy)]
-    loads, later, buf = [], [], decoder_ref
-    if not loaded:
-        buf, sem = refs
-        loads = [load(decoder_ref, col, buf.at[i], sem.at[i]) for i, col in enumerate(cols)]
-        for i, (p, dc, o) in enumerate((p, dc, o) for p, dc in keep for o in range(fy)):
-            col = column(n, p, chunks, sub, o, dc)
-            later.append(load(decoder_ref, col, kept_ref.at[i], sem.at[len(cols) + i]))
-    for copy in loads + later:
-        copy.start()
+    if first:
+        _, _, c = place(n, me)
+        slab = pl.multiple_of((c ^ 1) * buf.shape[2], buf.shape[2])
+        loads = [loads_of(decoder_hbm, slab, buf.at[0], sem.at[0])]
+    else:
+        loads = [loads_of(decoder_hbm, col, buf.at[i], sem.at[i]) for i, col in enumerate(cols)]
+    for copies in loads:
+        for copy in copies:
+            copy.start()
     for copy in smalls:
         copy.wait()
     if first:
@@ -137,50 +146,52 @@
             return carry
 
         lax.fori_loop(0, rows // ROW_STEP, body, 0)
+        for copy in loads[0]:
+            copy.wait()
     per = SUBLANES // own
     tile = pl.ds(pl.multiple_of(me // per * SUBLANES, SUBLANES), SUBLANES)
     mine = lax.broadcasted_iota(jnp.int32, (SUBLANES, sub), 0) // own == me % per
     for i, col in enumerate(cols):
-        if loads:
-            loads[i].wait()
+        if first:
+            columns = buf[0, :, pl.ds(pl.multiple_of(col - slab, sub), sub)]
+        else:
+            for copy in loads[i]:
+                copy.wait()
+            columns = buf[i]
         out_ref = outs[i // fy]
         here = slice(i % fy * sub, (i % fy + 1) * sub)
-        out_ref[:, here] = jnp.dot(dense_ref[...], buf[i], preferred_element_type=jnp.float32)
+        out_ref[:, here] = jnp.dot(dense_ref[...], columns, preferred_element_type=jnp.float32)
         target = targets_ref[:, pl.ds(col, sub)].astype(jnp.float32)
         target = jnp.concatenate([target] * per, axis=0)
         out_ref[tile, here] -= jnp.where(mine, target, 0.0)
-    for copy in later:
-        copy.wait()
-
-
-def decode(n, chunks, sub, parts, decoder, targets, start=None, keep=(), dense=None, after=None):
+
+
+def decode(n, chunks, sub, parts, decoder, targets, start=None, dense=None, after=None):
     _, fy, _ = factors(n)
-    first, loaded = start is not None, decoder.ndim == 3
+    first = start is not None
     rows = start[0].shape[0] if first else dense.shape[0]
-    lat_dev = decoder.shape[-2]
+    lat_dev = decoder.shape[0]
+    out = [pltpu.VMEM((rows, fy * sub), jnp.float32)] * len(parts)
     count = len(parts) * fy
-    out = [pltpu.VMEM((rows, fy * sub), jnp.float32)] * len(parts)
-    scratch = [pltpu.VMEM(targets.shape, targets.dtype), pltpu.SemaphoreType.DMA((3,))]
+    blocks = (1, lat_dev, count * sub) if first else (count, lat_dev, sub)
+    scratch = [
+        pltpu.VMEM(blocks, jnp.bfloat16),
+        pltpu.SemaphoreType.DMA((blocks[0], LOADS if first else 2)),
+        pltpu.VMEM(targets.shape, targets.dtype),
+        pltpu.SemaphoreType.DMA((3,)),
+    ]
     if first:
         args = [in_hbm(x) for x in (*start, decoder, targets)]
         specs = [HBM] * 4
-        out += [
-            pltpu.VMEM((rows, lat_dev), jnp.bfloat16),
-            pltpu.VMEM((len(keep) * fy, lat_dev, sub), jnp.bfloat16),
-        ]
+        out.append(pltpu.VMEM((rows, lat_dev), jnp.bfloat16))
         scratch += [pltpu.VMEM(x.shape, x.dtype) for x in start]
-    elif loaded:
-        args, specs = [dense, in_vmem(decoder), in_hbm(targets)], [VMEM, VMEM, HBM]
     else:
-        args = [dense, in_hbm(decoder), in_hbm(targets), in_vmem(after)]
-        specs = [VMEM, HBM, HBM, VMEM]
-    if not loaded:
-        scratch += [
-            pltpu.VMEM((count, lat_dev, sub), jnp.bfloat16),
-            pltpu.SemaphoreType.DMA((count + len(keep) * fy,)),
-        ]
+        args, specs = [dense, in_hbm(decoder), in_hbm(targets)], [VMEM, HBM, HBM]
+        if after is not None:
+            args.append(in_vmem(after))
+            specs.append(VMEM)
     return pl.pallas_call(
-        functools.partial(decode_kernel, n, rows // n, chunks, parts, first, loaded, keep),
+        functools.partial(decode_kernel, n, rows // n, chunks, parts, first),
         out_shape=out,
         in_specs=specs,
         out_specs=[VMEM] * len(out),
@@ -191,55 +202,41 @@
     )(*args)
 
 
-def fetch_kernel(n, dys, decoder_hbm, _, out_ref, sem):
-    _, lat_dev, width = out_ref.shape
-    step = lat_dev // FETCHES
-    copies = []
-    for slot, (dc, dy) in enumerate((dc, dy) for dc in range(2) for dy in dys):
-        col = column(n, 0, 1, width, dy, dc)
-        for i in range(FETCHES):
-            at = pl.ds(i * step, step)
-            copies.append(
-                pltpu.make_async_copy(
-                    decoder_hbm.at[at, pl.ds(col, width)], out_ref.at[slot, at], sem.at[slot, i]
-                )
-            )
-    for copy in copies:
-        copy.start()
-    for copy in copies:
-        copy.wait()
-
-
-def fetch(n, width, dys, decoder, after):
-    count = 2 * len(dys)
-    return pl.pallas_call(
-        functools.partial(fetch_kernel, n, dys),
-        out_shape=pltpu.VMEM((count, decoder.shape[0], width), decoder.dtype),
-        in_specs=[HBM, VMEM],
-        out_specs=VMEM,
-        scratch_shapes=[pltpu.SemaphoreType.DMA((count, FETCHES))],
-        compiler_params=params(),
-        cost_estimate=cost(0, decoder.shape[0] * count * width * 2),
-        name="fetch",
-    )(in_hbm(decoder), in_vmem(after))
-
-
-def grad_kernel(n, slots, counts, final, with_prev, *refs):
+def grad_kernel(n, counts, here, then, final, *refs):
     refs = list(refs)
     errs = [[refs.pop(0) for _ in range(count)] for count in counts]
-    decoder_ref = refs.pop(0)
-    total = refs.pop(0)[...] if with_prev else None
-    for parts, slot in zip(errs, slots):
+    decoder_hbm = None if final else refs.pop(0)
+    if here:
+        total, columns_ref = None, refs[-2]
+    else:
+        columns_ref, total = refs.pop(0), refs.pop(0)[...]
+    loads, later = [], []
+    if not final:
+        out_ref, next_ref, sem = refs[0], refs[1], refs[-1]
+        wide = next_ref.shape[2]
+        for i, (dc, dy) in enumerate(here):
+            col = column(n, 0, 1, wide, dy, dc)
+            loads.append(loads_of(decoder_hbm, col, columns_ref.at[i], sem.at[len(then) + i]))
+        for i, (dc, dy) in enumerate(then):
+            later += loads_of(decoder_hbm, column(n, 0, 1, wide, dy, dc), next_ref.at[i], sem.at[i])
+        for copy in sum(loads, []) + later:
+            copy.start()
+    for i, parts in enumerate(errs):
+        if loads:
+            for copy in loads[i]:
+                copy.wait()
         err = parts[0][...] if len(parts) == 1 else jnp.concatenate([e[...] for e in parts], axis=0)
         part = lax.dot_general(
             err,
-            decoder_ref[slot],
+            columns_ref[i],
             (((1,), (1,)), ((), ())),
             preferred_element_type=jnp.float32,
         )
         total = part if total is None else total + part
     if not final:
-        refs[0][...] = total
+        out_ref[...] = total
+        for copy in later:
+            copy.wait()
         return
     ids_ref, loss_ref, out_ref, totals_ref = refs
     totals_ref[...] = total
@@ -271,23 +268,36 @@
                 out_ref[first // own + d] = acc[d * own : (d + 1) * own, :]
 
 
-def grad(n, rows, pieces, decoder, prev, final=None):
-    count, lat_dev, _ = decoder.shape
-    slots = tuple(dc * (count // 2) + dy % (count // 2) for (dc, dy), _ in pieces)
+def grad(n, rows, pieces, decoder, prev, then=(), final=None):
+    lat_dev = decoder.shape[0]
+    wide = pieces[0][1][0].shape[1]
     counts = tuple(len(e) for _, e in pieces)
-    args = [x for _, e in pieces for x in e] + [in_vmem(decoder)]
-    if prev is not None:
-        args.append(in_vmem(prev))
-    if final is not None:
+    here = tuple(at for at, _ in pieces) if prev is None else ()
+    args, specs = [x for _, e in pieces for x in e], []
+    specs = [VMEM] * len(args)
+    if final is None:
+        args.append(in_hbm(decoder))
+        specs.append(HBM)
+    for x in reversed(prev or ()):
+        args.append(in_vmem(x))
+        specs.append(VMEM)
+    totals = pltpu.VMEM((rows, lat_dev), jnp.float32)
+    if final is None:
+        out = [totals, pltpu.VMEM((len(then), lat_dev, wide), jnp.bfloat16)]
+        scratch = [pltpu.VMEM((len(here), lat_dev, wide), jnp.bfloat16)] if here else []
+        scratch.append(pltpu.SemaphoreType.DMA((len(then) + len(here), LOADS // 2)))
+    else:
         args += list(final)
-    totals = pltpu.VMEM((rows, lat_dev), jnp.float32)
-    size = pieces[0][1][0].shape[1] * len(pieces)
+        specs += [VMEM] * len(final)
+        out = jax.ShapeDtypeStruct((n, rows // n, LANES), jnp.float32)
+        scratch = [totals]
+    size = wide * len(pieces)
     return pl.pallas_call(
-        functools.partial(grad_kernel, n, slots, counts, final is not None, prev is not None),
-        out_shape=totals if final is None else jax.ShapeDtypeStruct((n, rows // n, LANES), jnp.float32),
-        in_specs=[VMEM] * len(args),
-        out_specs=VMEM,
-        scratch_shapes=[] if final is None else [totals],
+        functools.partial(grad_kernel, n, counts, here, then, final is not None),
+        out_shape=out,
+        in_specs=specs,
+        out_specs=VMEM if final is not None else [VMEM, VMEM],
+        scratch_shapes=scratch,
         compiler_params=params(),
         cost_estimate=cost(2 * rows * lat_dev * size, 4 * lat_dev * size),
         name="grad",
@@ -343,15 +353,11 @@
         return xs
 
     others = tuple((p, 1) for p in range(chunks))
-    *parts, dense, columns = decode(
-        n, chunks, sub, others, decoder, targets, (indices, codes), ((0, 0),)
-    )
+    *parts, dense = decode(n, chunks, sub, others, decoder, targets, (indices, codes))
     came = [swap(part, dc=1) for part in parts]
     summed, leaving, after = [], [], None
     for p in range(chunks):
-        (part,) = decode(
-            n, chunks, sub, ((p, 0),), decoder if p else columns, targets, dense=dense, after=after
-        )
+        (part,) = decode(n, chunks, sub, ((p, 0),), decoder, targets, dense=dense, after=after)
         total = part + came[p]
         blocks = [total[:, o * sub : (o + 1) * sub] for o in range(fy)]
         got = None
@@ -363,12 +369,9 @@
         leaving.append(after)
         summed.append((blocks[0], got))
 
-    wide = chunks * sub
-    half = fy // 2
-    near_columns = fetch(n, wide, tuple(range(half)), decoder, leaving[-1])
     sums, moved = [], []
     for p, (x, y) in enumerate(summed):
-        x = x + (hold(y, near_columns) if p == 0 else y)
+        x = x + (hold(y, leaving[-1]) if p == 0 else y)
         sums.append(lax.dynamic_slice_in_dim(x, z * group, group, 0))
         moved.append(
             [
@@ -385,12 +388,10 @@
 
     err = join(errs, 1)
     come = [swap(err, dz=j) for j in z_order(fz)]
-    far_columns = fetch(n, wide, tuple(range(half, fy)), decoder, err)
     own_part = swap(err, dy=1)
-    come = in_order(come[:-1], far_columns) + come[-1:]
-    own_part = hold(own_part, come[-2])
-    come[-1] = hold(come[-1], own_part)
-    near = [((0, 0), [err, join(come[:-1], 0), come[-1]])]
+    come = in_order(come[:-1] + [own_part] + come[-1:])
+    own_part = come.pop(-2)
+    near = [((0, 0), [err, join(come, 0)])]
     for b in bits(fy):
         last = [
             ((0, b | at[1]), in_order([own_part if e is err else swap(e, dy=b) for e in parts]))
@@ -398,18 +399,22 @@
         ]
         near += last
     near = near[: -len(last)]
-
-    def to_core(pieces):
-        sent = swap(join([e for _, parts in pieces for e in parts], 0), dc=1)
-        return [((1, at[1]), [sent[i * rows : (i + 1) * rows]]) for i, (at, _) in enumerate(pieces)]
-
-    far = to_core(near)
-    totals = grad(n, rows, near, near_columns, None)
-    totals = grad(n, rows, far, near_columns, totals)
-    last[-1][1][-1] = hold(last[-1][1][-1], totals)
-    far_last = to_core(last)
-    totals = grad(n, rows, last, far_columns, totals)
-    back = grad(n, rows, far_last, far_columns, totals, (indices, loss))
+    half = rows // 2
+
+    def halves(parts):
+        whole = join(parts, 0)
+        return [whole[:group], whole[group : group + half], whole[group + half :]]
+
+    far = [((1, at[1]), [swap(e, dc=1) for e in halves(parts)]) for at, parts in near]
+    far_last = [(1, at[1]) for at, _ in last]
+    sums = grad(n, rows, near, decoder, None, tuple(at for at, _ in far))
+    sums = grad(n, rows, far, decoder, sums, tuple(at for at, _ in last))
+    last[-1][1][-1] = hold(last[-1][1][-1], sums[0])
+    far_last = [
+        (at, [swap(join(parts, 0), dc=1)]) for at, (_, parts) in zip(far_last, last)
+    ]
+    sums = grad(n, rows, last, decoder, sums, tuple(at for at, _ in far_last))
+    back = grad(n, rows, far_last, decoder, sums, (), (indices, loss))
     pieces = near + far + last + far_last
     error = own_rows(n, [at for at, _ in pieces], own, width, [e[0][:group] for _, e in pieces])
 

time: 70.5 us -> 65.1 us (0.923)
  local copies, waits for them, and re-layouts: 3.8 us -> 0.19 us
  starting transfers between devices: 25.1 us -> 24.1 us
    unnamed x10 -> x4, local copies, waits for them, and re-layouts: 3.61 us -> 0.01 us
    ppermute x18 -> x19, starting transfers between devices: 21.4 us -> 20 us  [swap(): return lax.ppermute(x, 'lat', pairs(n, dz, dy, dc))]
    ppermute x18 -> x19, waiting for transfers between devices: 15.7 us -> 15.3 us  [swap(): return lax.ppermute(x, 'lat', pairs(n, dz, dy, dc))]
    pallas_call x6 -> x4, Pallas kernels: 8.2 us -> 8.23 us  [grad(): pl.pallas_call(functools.partial(grad_kernel, n, counts, here, then, fina...]
  transfers between devices with their start and end apart: 19 -> 20, of which waited for: 9 -> 9; matrix products, arithmetic and copies ran while one was open for 1% -> 1% of each run, Pallas kernels for 14% -> 18%
where the time goes in v9:
time: 65.1 us; the launch traced here: 64.8 us
  starting transfers between devices  24.1 us (37%)
  waiting for transfers between devices  21 us (32%)
  Pallas kernels  17.4 us (27%)
  other arithmetic  1.21 us (2%)
  between operations  0.88 us (1%)
    ppermute x19, starting transfers between devices, swap(): return lax.ppermute(x, 'lat', pairs(n, dz, dy, dc))  20 us
    ppermute x19, waiting for transfers between devices, swap(): return lax.ppermute(x, 'lat', pairs(n, dz, dy, dc))  15.3 us
    pallas_call x3, Pallas kernels, decode(): pl.pallas_call(functools.partial(decode_kernel, n, rows // n, chunks, par...  8.29 us
    pallas_call x4, Pallas kernels, grad(): pl.pallas_call(functools.partial(grad_kernel, n, counts, here, then, fina...  8.23 us
    all_to_all x1, waiting for transfers between devices, local(): back = jnp.sum(lax.all_to_all(back, 'lat', 0, 0, tiled=True), axis=0)  5.77 us
    all_to_all x1, starting transfers between devices, local(): back = jnp.sum(lax.all_to_all(back, 'lat', 0, 0, tiled=True), axis=0)  4.1 us
  transfers between devices with their start and end apart: 20, of which 9 were waited for; matrix products, arithmetic and copies ran while one was open for 1% of the time, Pallas kernels for 18%

profile of v9, /device:TPU:0, one launch (start us, length us, event | category | flops | bytes accessed | tf_op | source)
XLA Modules:
  0.0 64.8 jit_solution(5304196219040876674)
XLA Ops:
  0.6 4.4 %decode.3 = (f32[64,2048]{1,0:T(8,128)S(1)}, f32[64,2048]{1,0:T(8,128)S(1)}, bf16[64,512]{1,0:T(8,128)(2,1)S(1)}) custom-call(s32[64,64]{1,0:T(8,128)} %refs_3_.5, bf16[64,64]{1,0:T(8,128)(2,1)} %refs_1_.3, bf16[512,8192]{1,0:T(8,128)(2,1)} %refs_2_.9, bf16[4,8192]{1,0:T(4,128)(2,1)} %refs_2_.7), custom_call_target="tpu_custom_call" | custom-call | flops 268435456 | bytes 8388608 | tf_op jit(solution)/shard_map/decode/pallas_call | solution.py:193
  5.1 0.5 collective-permute-start
  5.6 0.1 collective-permute-start.2
  5.7 1.9 %decode.4 = f32[64,2048]{1,0:T(8,128)S(1)} custom-call(bf16[64,512]{1,0:T(8,128)(2,1)S(1)} %get-tuple-element.12.refs_0_, bf16[512,8192]{1,0:T(8,128)(2,1)} %refs_2_.9, bf16[4,8192]{1,0:T(4,128)(2,1)} %refs_2_.7), custom_call_target="tpu_custom_call" | custom-call | flops 134217728 | bytes 4194304 | tf_op jit(solution)/shard_map/decode/pallas_call | solution.py:193
  7.6 0.0 collective-permute-done
  7.6 0.1 add.52
  7.7 3.0 %collective-permute-start.1 = (f32[64,1024]{1,0:T(8,128)S(1)}, f32[64,1024]{1,0:T(8,128)S(1)}, u32[]{:S(2)}, u32[]{:S(2)}) collective-permute-start(f32[64,1024]{1,0:T(8,128)S(1)} %slice.31.refs_3_), channel_id=1, source_target_pairs={{0,2},{1,3},{2,0},{3,1},{4,6},{5,7},{6,4},{7,5},{8,10},{9,11},{10,... | collective-permute-start | bytes 786440 | tf_op jit(solution)/shard_map/ppermute | solution.py:343
  10.7 1.9 %decode.5 = f32[64,2048]{1,0:T(8,128)S(1)} custom-call(bf16[64,512]{1,0:T(8,128)(2,1)S(1)} %get-tuple-element.12.refs_0_, bf16[512,8192]{1,0:T(8,128)(2,1)} %refs_2_.9, bf16[4,8192]{1,0:T(4,128)(2,1)} %refs_2_.7, f32[64,1024]{1,0:T(8,128)S(1)} %slice.31.refs_3_), custom_call_target="tpu_custom_call" | custom-call | flops 134217728 | bytes 4194304 | tf_op jit(solution)/shard_map/decode/pallas_call | solution.py:193
  12.7 0.0 collective-permute-done.2
  12.7 0.1 add.53
  12.8 0.1 collective-permute-start.4
  12.9 5.0 %collective-permute-done.1.refs_0_ = f32[64,1024]{1,0:T(8,128)S(1)} collective-permute-done((f32[64,1024]{1,0:T(8,128)S(1)}, f32[64,1024]{1,0:T(8,128)S(1)}, u32[]{:S(2)}, u32[]{:S(2)}) %collective-permute-start.1) | collective-permute-done | bytes 262176 | tf_op jit(solution)/shard_map/ppermute | solution.py:343
  17.9 4.2 %collective-permute-start.3 = (f32[16,1024]{1,0:T(8,128)S(1)}, f32[16,1024]{1,0:T(8,128)S(1)}, u32[]{:S(2)}, u32[]{:S(2)}) collective-permute-start(f32[16,1024]{1,0:T(8,128)S(1)} %get-tuple-element.29), channel_id=1, source_target_pairs={{0,12},{1,13},{2,14},{3,15},{4,8},{5,9},{6,10},{7,11},{8,4},{9,5},... | collective-permute-start | bytes 196616 | tf_op jit(solution)/shard_map/ppermute | solution.py:343
  22.1 0.0 collective-permute-start.5
  22.1 0.6 collective-permute-start.6
  22.8 0.1 collective-permute-done.4
  23.0 3.9 %collective-permute-start.7 = (f32[16,1024]{1,0:T(8,128)S(1)}, f32[16,1024]{1,0:T(8,128)S(1)}, u32[]{:S(2)}, u32[]{:S(2)}) collective-permute-start(f32[16,1024]{1,0:T(8,128)S(1)} %get-tuple-element.28), channel_id=1, source_target_pairs={{0,12},{1,13},{2,14},{3,15},{4,8},{5,9},{6,10},{7,11},{8,4},{9,5},... | collective-permute-start | bytes 196616 | tf_op jit(solution)/shard_map/ppermute | solution.py:343
  26.9 0.0 collective-permute-start.8
  26.9 0.0 collective-permute-done.3.refs_0_
  26.9 0.6 collective-permute-start.9
  27.5 0.0 collective-permute-done.5.refs_0_
  27.5 0.8 %collective-permute-done.6.refs_0_ = f32[16,1024]{1,0:T(8,128)S(1)} collective-permute-done((f32[16,1024]{1,0:T(8,128)S(1)}, f32[16,1024]{1,0:T(8,128)S(1)}, u32[]{:S(2)}, u32[]{:S(2)}) %collective-permute-start.6) | collective-permute-done | bytes 65568 | tf_op jit(solution)/shard_map/ppermute | solution.py:343
  28.4 0.1 multiply_reduce_fusion.1
  28.5 1.3 %collective-permute-done.7.refs_0_ = f32[16,1024]{1,0:T(8,128)S(1)} collective-permute-done((f32[16,1024]{1,0:T(8,128)S(1)}, f32[16,1024]{1,0:T(8,128)S(1)}, u32[]{:S(2)}, u32[]{:S(2)}) %collective-permute-start.7) | collective-permute-done | bytes 65568 | tf_op jit(solution)/shard_map/ppermute | solution.py:343
  29.8 1.4 %collective-permute-done.8.refs_0_ = f32[16,1024]{1,0:T(8,128)S(1)} collective-permute-done((f32[16,1024]{1,0:T(8,128)S(1)}, f32[16,1024]{1,0:T(8,128)S(1)}, u32[]{:S(2)}, u32[]{:S(2)}) %collective-permute-start.8) | collective-permute-done | bytes 65568 | tf_op jit(solution)/shard_map/ppermute | solution.py:343
  31.2 1.2 %collective-permute-done.9.refs_0_ = f32[16,1024]{1,0:T(8,128)S(1)} collective-permute-done((f32[16,1024]{1,0:T(8,128)S(1)}, f32[16,1024]{1,0:T(8,128)S(1)}, u32[]{:S(2)}, u32[]{:S(2)}) %collective-permute-start.9) | collective-permute-done | bytes 65568 | tf_op jit(solution)/shard_map/ppermute | solution.py:343
  32.4 0.1 multiply_reduce_fusion
  32.6 1.7 %collective-permute-start.12 = (bf16[16,2048]{1,0:T(8,128)(2,1)S(1)}, bf16[16,2048]{1,0:T(8,128)(2,1)S(1)}, u32[]{:S(2)}, u32[]{:S(2)}) collective-permute-start(bf16[16,2048]{1,0:T(8,128)(2,1)S(1)} %pad_maximum_fusion.3.refs_0_), channel_id=1, source_target_pairs={{0,4},{1,5},{2,6},{3,7},{4,0},{5,1},{6,2},{7,3},{8,12},{9,13},{10,... | collective-permute-start | bytes 196616 | tf_op jit(solution)/shard_map/ppermute | solution.py:343
  34.3 1.4 %collective-permute-start.13 = (bf16[16,2048]{1,0:T(8,128)(2,1)S(1)}, bf16[16,2048]{1,0:T(8,128)(2,1)S(1)}, u32[]{:S(2)}, u32[]{:S(2)}) collective-permute-start(bf16[16,2048]{1,0:T(8,128)(2,1)S(1)} %pad_maximum_fusion.3.refs_0_), channel_id=1, source_target_pairs={{0,12},{1,13},{2,14},{3,15},{4,8},{5,9},{6,10},{7,11},{8,4},{9,5},... | collective-permute-start | bytes 196616 | tf_op jit(solution)/shard_map/ppermute | solution.py:343
  35.7 1.5 %collective-permute-start.11 = (bf16[16,2048]{1,0:T(8,128)(2,1)S(1)}, bf16[16,2048]{1,0:T(8,128)(2,1)S(1)}, u32[]{:S(2)}, u32[]{:S(2)}) collective-permute-start(bf16[16,2048]{1,0:T(8,128)(2,1)S(1)} %pad_maximum_fusion.3.refs_0_), channel_id=1, source_target_pairs={{0,2},{1,3},{2,0},{3,1},{4,6},{5,7},{6,4},{7,5},{8,10},{9,11},{10,... | collective-permute-start | bytes 196616 | tf_op jit(solution)/shard_map/ppermute | solution.py:343
  37.2 0.5 collective-permute-start.14
  37.7 0.0 collective-permute-done.12.refs_0_
  37.7 3.0 %collective-permute-done.13.refs_1_ = bf16[16,2048]{1,0:T(8,128)(2,1)S(1)} collective-permute-done((bf16[16,2048]{1,0:T(8,128)(2,1)S(1)}, bf16[16,2048]{1,0:T(8,128)(2,1)S(1)}, u32[]{:S(2)}, u32[]{:S(2)}) %collective-permute-start.13) | collective-permute-done | bytes 65568 | tf_op jit(solution)/shard_map/ppermute | solution.py:343
  40.7 0.0 collective-permute-done.11.refs_0_
  40.7 2.4 %collective-permute-done.14.refs_0_ = bf16[16,2048]{1,0:T(8,128)(2,1)S(1)} collective-permute-done((bf16[16,2048]{1,0:T(8,128)(2,1)S(1)}, bf16[16,2048]{1,0:T(8,128)(2,1)S(1)}, u32[]{:S(2)}, u32[]{:S(2)}) %collective-permute-start.14) | collective-permute-done | bytes 65568 | tf_op jit(solution)/shard_map/ppermute | solution.py:343
  43.1 0.6 collective-permute-start.15
  43.7 0.1 collective-permute-start.16
  43.8 0.5 collective-permute-start.10
  44.2 0.1 collective-permute-start.17
  44.3 2.4 %grad.4 = (f32[64,512]{1,0:T(8,128)S(1)}, bf16[1,512,2048]{2,1,0:T(8,128)(2,1)S(1)}) custom-call(bf16[16,2048]{1,0:T(8,128)(2,1)S(1)} %pad_maximum_fusion.3.refs_0_, bf16[48,2048]{1,0:T(8,128)(2,1)S(1)} %pad_maximum_fusion.1.refs_1_, bf16[512,8192]{1,0:T(8,128)(2,1)} %refs_2_.9), custom_call_target="tpu_custom_call" | custom-call | flops 134217728 | bytes 4194304 | tf_op jit(solution)/shard_map/grad/pallas_call | solution.py:295
  46.7 0.0 collective-permute-done.10.refs_0_.refs_1_
  46.7 0.0 collective-permute-done.17.refs_2_
  46.7 0.0 collective-permute-done.16.refs_1_
  46.7 2.2 %grad.5 = (f32[64,512]{1,0:T(8,128)S(1)}, bf16[1,512,2048]{2,1,0:T(8,128)(2,1)S(1)}) custom-call(bf16[16,2048]{1,0:T(8,128)(2,1)S(1)} %collective-permute-done.10.refs_0_.refs_1_, bf16[32,2048]{1,0:T(8,128)(2,1)S(1)} %collective-permute-done.16.refs_1_, bf16[16,2048]{1,0:T(8,128)(2,1)S(1)} %collective-permute-done.17.refs_2_, bf16[512,8192]{1,0:T(8,128)(2,1)} %refs_2_.9, ...), custom_call_target="tpu_custom_call" | custom-call | flops 134217728 | bytes 4194304 | tf_op jit(solution)/shard_map/grad/pallas_call | solution.py:295
  48.9 0.0 collective-permute-done.15.refs_0_
  49.0 0.5 collective-permute-start.18
  49.5 0.1 copy.19.refs_4_
  49.6 0.0 copy-start
  49.6 2.2 %grad.6 = (f32[64,512]{1,0:T(8,128)S(1)}, bf16[1,512,2048]{2,1,0:T(8,128)(2,1)S(1)}) custom-call(bf16[16,2048]{1,0:T(8,128)(2,1)S(1)} %hold.20.refs_1_.refs_2_.refs_0_, bf16[48,2048]{1,0:T(8,128)(2,1)S(1)} %hold.23.refs_1_, bf16[512,8192]{1,0:T(8,128)(2,1)} %refs_2_.9, bf16[1,512,2048]{2,1,0:T(8,128)(2,1)S(1)} %get-tuple-element.18.refs_3_, ...), custom_call_target="tpu_custom_call" | custom-call | flops 134217728 | bytes 4194304 | tf_op jit(solution)/shard_map/grad/pallas_call | solution.py:295
  51.8 0.0 collective-permute-done.18.refs_0_
  51.8 0.0 copy-done
  51.8 1.5 %grad.7 = f32[16,4,128]{2,1,0:T(4,128)} custom-call(bf16[64,2048]{1,0:T(8,128)(2,1)S(1)} %collective-permute-done.18.refs_0_, bf16[1,512,2048]{2,1,0:T(8,128)(2,1)S(1)} %get-tuple-element.19.refs_1_, f32[64,512]{1,0:T(8,128)S(1)} %get-tuple-element.20.refs_2_, s32[64,64]{1,0:T(8,128)S(1)} %copy-done, f32[16,1]{1,0:T(8,128)S(1)} %copy.19.refs_4_), custom_call_target="tpu_custom_call" | custom-call | flops 134217728 | bytes 4194304 | tf_op jit(solution)/shard_map/grad/pallas_call | solution.py:295
  53.3 4.1 %all-to-all-start = ((f32[16,4,128]{2,1,0:T(4,128)}), f32[16,4,128]{2,1,0:T(4,128)S(1)}, u32[]{:S(2)}, u32[]{:S(2)}) async-start(f32[16,4,128]{2,1,0:T(4,128)} %grad.7), calls=%async_computation | async-start | bytes 65536 | tf_op jit(solution)/shard_map/all_to_all | solution.py:421
  57.4 0.8 %own_rows.1 = bf16[4,8192]{1,0:T(4,128)(2,1)} custom-call(bf16[16,2048]{1,0:T(8,128)(2,1)S(1)} %pad_maximum_fusion.3.refs_0_, bf16[16,2048]{1,0:T(8,128)(2,1)S(1)} %collective-permute-done.10.refs_0_.refs_1_, bf16[16,2048]{1,0:T(8,128)(2,1)S(1)} %hold.20.refs_1_.refs_2_.refs_0_, bf16[16,2048]{1,0:T(8,128)(2,1)S(1)} %slice.34.refs_3_), custom_call_target="tpu_custom_call" | custom-call | tf_op jit(solution)/shard_map/own_rows/pallas_call | solution.py:321
  58.3 5.8 %all-to-all-done = f32[16,4,128]{2,1,0:T(4,128)S(1)} async-done(((f32[16,4,128]{2,1,0:T(4,128)}), f32[16,4,128]{2,1,0:T(4,128)S(1)}, u32[]{:S(2)}, u32[]{:S(2)}) %all-to-all-start) | async-done | bytes 32800 | tf_op jit(solution)/shard_map/all_to_all | solution.py:421
  64.1 0.0 copy-start.1
  64.1 0.7 %multiply_reduce_fusion.2 = f32[4]{0:T(128)} fusion(f32[4,128]{1,0:T(4,128)S(1)} %reduce_sum.29), kind=kLoop, calls=%fused_computation.10 | loop fusion | flops 4 | bytes 32 | tf_op jit(solution)/shard_map/div | solution.py:422
  64.8 0.0 copy-done.1
  (25 shorter events, 0.2 us)
Async XLA Ops:
  5.1 2.5 %collective-permute-start = (f32[64,2048]{1,0:T(8,128)S(1)}, f32[64,2048]{1,0:T(8,128)S(1)}, u32[]{:S(2)}, u32[]{:S(2)}) collective-permute-start(f32[64,2048]{1,0:T(8,128)S(1)} %get-tuple-element.13), channel_id=1, source_target_pairs={{0,1},{1,0},{2,3},{3,2},{4,5},{5,4},{6,7},{7,6},{8,9},{9,8},{10,11... | collective-permute-start | bytes 1572872 | tf_op jit(solution)/shard_map/ppermute | solution.py:343
  5.6 7.1 %collective-permute-start.2 = (f32[64,2048]{1,0:T(8,128)S(1)}, f32[64,2048]{1,0:T(8,128)S(1)}, u32[]{:S(2)}, u32[]{:S(2)}) collective-permute-start(f32[64,2048]{1,0:T(8,128)S(1)} %get-tuple-element.14), channel_id=1, source_target_pairs={{0,1},{1,0},{2,3},{3,2},{4,5},{5,4},{6,7},{7,6},{8,9},{9,8},{10,11... | collective-permute-start | bytes 1572872 | tf_op jit(solution)/shard_map/ppermute | solution.py:343
  7.7 10.1 %collective-permute-start.1 = (f32[64,1024]{1,0:T(8,128)S(1)}, f32[64,1024]{1,0:T(8,128)S(1)}, u32[]{:S(2)}, u32[]{:S(2)}) collective-permute-start(f32[64,1024]{1,0:T(8,128)S(1)} %slice.31.refs_3_), channel_id=1, source_target_pairs={{0,2},{1,3},{2,0},{3,1},{4,6},{5,7},{6,4},{7,5},{8,10},{9,11},{10,... | collective-permute-start | bytes 786440 | tf_op jit(solution)/shard_map/ppermute | solution.py:343
  12.8 10.1 %collective-permute-start.4 = (f32[64,1024]{1,0:T(8,128)S(1)}, f32[64,1024]{1,0:T(8,128)S(1)}, u32[]{:S(2)}, u32[]{:S(2)}) collective-permute-start(f32[64,1024]{1,0:T(8,128)S(1)} %slice.32.refs_1_), channel_id=1, source_target_pairs={{0,2},{1,3},{2,0},{3,1},{4,6},{5,7},{6,4},{7,5},{8,10},{9,11},{10,... | collective-permute-start | bytes 786440 | tf_op jit(solution)/shard_map/ppermute | solution.py:343
  17.9 9.0 %collective-permute-start.3 = (f32[16,1024]{1,0:T(8,128)S(1)}, f32[16,1024]{1,0:T(8,128)S(1)}, u32[]{:S(2)}, u32[]{:S(2)}) collective-permute-start(f32[16,1024]{1,0:T(8,128)S(1)} %get-tuple-element.29), channel_id=1, source_target_pairs={{0,12},{1,13},{2,14},{3,15},{4,8},{5,9},{6,10},{7,11},{8,4},{9,5},... | collective-permute-start | bytes 196616 | tf_op jit(solution)/shard_map/ppermute | solution.py:343
  22.1 5.4 %collective-permute-start.5 = (f32[16,1024]{1,0:T(8,128)S(1)}, f32[16,1024]{1,0:T(8,128)S(1)}, u32[]{:S(2)}, u32[]{:S(2)}) collective-permute-start(f32[16,1024]{1,0:T(8,128)S(1)} %get-tuple-element.31), channel_id=1, source_target_pairs={{0,4},{1,5},{2,6},{3,7},{4,0},{5,1},{6,2},{7,3},{8,12},{9,13},{10,... | collective-permute-start | bytes 196616 | tf_op jit(solution)/shard_map/ppermute | solution.py:343
  22.1 6.2 %collective-permute-start.6 = (f32[16,1024]{1,0:T(8,128)S(1)}, f32[16,1024]{1,0:T(8,128)S(1)}, u32[]{:S(2)}, u32[]{:S(2)}) collective-permute-start(f32[16,1024]{1,0:T(8,128)S(1)} %get-tuple-element.30), channel_id=1, source_target_pairs={{0,8},{1,9},{2,10},{3,11},{4,12},{5,13},{6,14},{7,15},{8,0},{9,1},... | collective-permute-start | bytes 196616 | tf_op jit(solution)/shard_map/ppermute | solution.py:343
  23.0 6.9 %collective-permute-start.7 = (f32[16,1024]{1,0:T(8,128)S(1)}, f32[16,1024]{1,0:T(8,128)S(1)}, u32[]{:S(2)}, u32[]{:S(2)}) collective-permute-start(f32[16,1024]{1,0:T(8,128)S(1)} %get-tuple-element.28), channel_id=1, source_target_pairs={{0,12},{1,13},{2,14},{3,15},{4,8},{5,9},{6,10},{7,11},{8,4},{9,5},... | collective-permute-start | bytes 196616 | tf_op jit(solution)/shard_map/ppermute | solution.py:343
  26.9 4.4 %collective-permute-start.8 = (f32[16,1024]{1,0:T(8,128)S(1)}, f32[16,1024]{1,0:T(8,128)S(1)}, u32[]{:S(2)}, u32[]{:S(2)}) collective-permute-start(f32[16,1024]{1,0:T(8,128)S(1)} %get-tuple-element.27), channel_id=1, source_target_pairs={{0,4},{1,5},{2,6},{3,7},{4,0},{5,1},{6,2},{7,3},{8,12},{9,13},{10,... | collective-permute-start | bytes 196616 | tf_op jit(solution)/shard_map/ppermute | solution.py:343
  26.9 5.5 %collective-permute-start.9 = (f32[16,1024]{1,0:T(8,128)S(1)}, f32[16,1024]{1,0:T(8,128)S(1)}, u32[]{:S(2)}, u32[]{:S(2)}) collective-permute-start(f32[16,1024]{1,0:T(8,128)S(1)} %get-tuple-element.26), channel_id=1, source_target_pairs={{0,8},{1,9},{2,10},{3,11},{4,12},{5,13},{6,14},{7,15},{8,0},{9,1},... | collective-permute-start | bytes 196616 | tf_op jit(solution)/shard_map/ppermute | solution.py:343
  32.6 5.1 %collective-permute-start.12 = (bf16[16,2048]{1,0:T(8,128)(2,1)S(1)}, bf16[16,2048]{1,0:T(8,128)(2,1)S(1)}, u32[]{:S(2)}, u32[]{:S(2)}) collective-permute-start(bf16[16,2048]{1,0:T(8,128)(2,1)S(1)} %pad_maximum_fusion.3.refs_0_), channel_id=1, source_target_pairs={{0,4},{1,5},{2,6},{3,7},{4,0},{5,1},{6,2},{7,3},{8,12},{9,13},{10,... | collective-permute-start | bytes 196616 | tf_op jit(solution)/shard_map/ppermute | solution.py:343
  34.3 6.4 %collective-permute-start.13 = (bf16[16,2048]{1,0:T(8,128)(2,1)S(1)}, bf16[16,2048]{1,0:T(8,128)(2,1)S(1)}, u32[]{:S(2)}, u32[]{:S(2)}) collective-permute-start(bf16[16,2048]{1,0:T(8,128)(2,1)S(1)} %pad_maximum_fusion.3.refs_0_), channel_id=1, source_target_pairs={{0,12},{1,13},{2,14},{3,15},{4,8},{5,9},{6,10},{7,11},{8,4},{9,5},... | collective-permute-start | bytes 196616 | tf_op jit(solution)/shard_map/ppermute | solution.py:343
  35.7 5.0 %collective-permute-start.11 = (bf16[16,2048]{1,0:T(8,128)(2,1)S(1)}, bf16[16,2048]{1,0:T(8,128)(2,1)S(1)}, u32[]{:S(2)}, u32[]{:S(2)}) collective-permute-start(bf16[16,2048]{1,0:T(8,128)(2,1)S(1)} %pad_maximum_fusion.3.refs_0_), channel_id=1, source_target_pairs={{0,2},{1,3},{2,0},{3,1},{4,6},{5,7},{6,4},{7,5},{8,10},{9,11},{10,... | collective-permute-start | bytes 196616 | tf_op jit(solution)/shard_map/ppermute | solution.py:343
  37.2 5.9 %collective-permute-start.14 = (bf16[16,2048]{1,0:T(8,128)(2,1)S(1)}, bf16[16,2048]{1,0:T(8,128)(2,1)S(1)}, u32[]{:S(2)}, u32[]{:S(2)}) collective-permute-start(bf16[16,2048]{1,0:T(8,128)(2,1)S(1)} %pad_maximum_fusion.3.refs_0_), channel_id=1, source_target_pairs={{0,8},{1,9},{2,10},{3,11},{4,12},{5,13},{6,14},{7,15},{8,0},{9,1},... | collective-permute-start | bytes 196616 | tf_op jit(solution)/shard_map/ppermute | solution.py:343
  43.1 5.8 %collective-permute-start.15 = (bf16[48,2048]{1,0:T(8,128)(2,1)S(1)}, bf16[48,2048]{1,0:T(8,128)(2,1)S(1)}, u32[]{:S(2)}, u32[]{:S(2)}) collective-permute-start(bf16[48,2048]{1,0:T(8,128)(2,1)S(1)} %pad_maximum_fusion.1.refs_1_), channel_id=1, source_target_pairs={{0,2},{1,3},{2,0},{3,1},{4,6},{5,7},{6,4},{7,5},{8,10},{9,11},{10,... | collective-permute-start | bytes 589832 | tf_op jit(solution)/shard_map/ppermute | solution.py:343
  43.7 3.0 %collective-permute-start.16 = (bf16[32,2048]{1,0:T(8,128)(2,1)S(1)}, bf16[32,2048]{1,0:T(8,128)(2,1)S(1)}, u32[]{:S(2)}, u32[]{:S(2)}) collective-permute-start(bf16[32,2048]{1,0:T(8,128)(2,1)S(1)} %pad_maximum_fusion.2), channel_id=1, source_target_pairs={{0,1},{1,0},{2,3},{3,2},{4,5},{5,4},{6,7},{7,6},{8,9},{9,8},{10,11... | collective-permute-start | bytes 393224 | tf_op jit(solution)/shard_map/ppermute | solution.py:343
  43.8 2.9 %collective-permute-start.10 = (bf16[16,2048]{1,0:T(8,128)(2,1)S(1)}, bf16[16,2048]{1,0:T(8,128)(2,1)S(1)}, u32[]{:S(2)}, u32[]{:S(2)}) collective-permute-start(bf16[16,2048]{1,0:T(8,128)(2,1)S(1)} %pad_maximum_fusion.3.refs_0_), channel_id=1, source_target_pairs={{0,1},{1,0},{2,3},{3,2},{4,5},{5,4},{6,7},{7,6},{8,9},{9,8},{10,11... | collective-permute-start | bytes 196616 | tf_op jit(solution)/shard_map/ppermute | solution.py:343
  44.2 2.5 %collective-permute-start.17 = (bf16[16,2048]{1,0:T(8,128)(2,1)S(1)}, bf16[16,2048]{1,0:T(8,128)(2,1)S(1)}, u32[]{:S(2)}, u32[]{:S(2)}) collective-permute-start(bf16[16,2048]{1,0:T(8,128)(2,1)S(1)} %hold.21), channel_id=1, source_target_pairs={{0,1},{1,0},{2,3},{3,2},{4,5},{5,4},{6,7},{7,6},{8,9},{9,8},{10,11... | collective-permute-start | bytes 196616 | tf_op jit(solution)/shard_map/ppermute | solution.py:343
  49.0 2.8 %collective-permute-start.18 = (bf16[64,2048]{1,0:T(8,128)(2,1)S(1)}, bf16[64,2048]{1,0:T(8,128)(2,1)S(1)}, u32[]{:S(2)}, u32[]{:S(2)}) collective-permute-start(bf16[64,2048]{1,0:T(8,128)(2,1)S(1)} %pad_maximum_fusion), channel_id=1, source_target_pairs={{0,1},{1,0},{2,3},{3,2},{4,5},{5,4},{6,7},{7,6},{8,9},{9,8},{10,11... | collective-permute-start | bytes 786440 | tf_op jit(solution)/shard_map/ppermute | solution.py:343
  49.6 2.2 %copy-start = (s32[64,64]{1,0:T(8,128)S(1)}, s32[64,64]{1,0:T(8,128)}, u32[]{:S(2)}) copy-start(s32[64,64]{1,0:T(8,128)} %refs_3_.5) | copy-start | bytes 49156
  53.3 10.7 %all-to-all-start = ((f32[16,4,128]{2,1,0:T(4,128)}), f32[16,4,128]{2,1,0:T(4,128)S(1)}, u32[]{:S(2)}, u32[]{:S(2)}) async-start(f32[16,4,128]{2,1,0:T(4,128)} %grad.7), calls=%async_computation | async-start | bytes 65536 | tf_op jit(solution)/shard_map/all_to_all | solution.py:421
  64.1 0.7 %copy-start.1 = (f32[4,128]{1,0:T(4,128)}, f32[4,128]{1,0:T(4,128)S(1)}, u32[]{:S(2)}) copy-start(f32[4,128]{1,0:T(4,128)S(1)} %reduce_sum.29) | copy-start | bytes 6148

commit v10 on v9

--- a/solution.py
+++ b/solution.py
@@ -11,7 +11,7 @@
 ROW_STEP = 16
 LANES = 128
 SUBLANES = 8
-LOADS = 8
+LOADS = 4
 VMEM = pl.BlockSpec(memory_space=pltpu.VMEM)
 HBM = pl.BlockSpec(memory_space=pltpu.HBM)
 
@@ -120,12 +120,7 @@
     rows, lat_dev = dense_ref.shape
     sub = outs[0].shape[1] // fy
     cols = [column(n, p, chunks, sub, o, dc) for p, dc in parts for o in range(fy)]
-    if first:
-        _, _, c = place(n, me)
-        slab = pl.multiple_of((c ^ 1) * buf.shape[2], buf.shape[2])
-        loads = [loads_of(decoder_hbm, slab, buf.at[0], sem.at[0])]
-    else:
-        loads = [loads_of(decoder_hbm, col, buf.at[i], sem.at[i]) for i, col in enumerate(cols)]
+    loads = [loads_of(decoder_hbm, col, buf.at[i], sem.at[i]) for i, col in enumerate(cols)]
     for copies in loads:
         for copy in copies:
             copy.start()
@@ -146,21 +141,15 @@
             return carry
 
         lax.fori_loop(0, rows // ROW_STEP, body, 0)
-        for copy in loads[0]:
-            copy.wait()
     per = SUBLANES // own
     tile = pl.ds(pl.multiple_of(me // per * SUBLANES, SUBLANES), SUBLANES)
     mine = lax.broadcasted_iota(jnp.int32, (SUBLANES, sub), 0) // own == me % per
     for i, col in enumerate(cols):
-        if first:
-            columns = buf[0, :, pl.ds(pl.multiple_of(col - slab, sub), sub)]
-        else:
-            for copy in loads[i]:
-                copy.wait()
-            columns = buf[i]
+        for copy in loads[i]:
+            copy.wait()
         out_ref = outs[i // fy]
         here = slice(i % fy * sub, (i % fy + 1) * sub)
-        out_ref[:, here] = jnp.dot(dense_ref[...], columns, preferred_element_type=jnp.float32)
+        out_ref[:, here] = jnp.dot(dense_ref[...], buf[i], preferred_element_type=jnp.float32)
         target = targets_ref[:, pl.ds(col, sub)].astype(jnp.float32)
         target = jnp.concatenate([target] * per, axis=0)
         out_ref[tile, here] -= jnp.where(mine, target, 0.0)
@@ -173,10 +162,9 @@
     lat_dev = decoder.shape[0]
     out = [pltpu.VMEM((rows, fy * sub), jnp.float32)] * len(parts)
     count = len(parts) * fy
-    blocks = (1, lat_dev, count * sub) if first else (count, lat_dev, sub)
     scratch = [
-        pltpu.VMEM(blocks, jnp.bfloat16),
-        pltpu.SemaphoreType.DMA((blocks[0], LOADS if first else 2)),
+        pltpu.VMEM((count, lat_dev, sub), jnp.bfloat16),
+        pltpu.SemaphoreType.DMA((count, 1)),
         pltpu.VMEM(targets.shape, targets.dtype),
         pltpu.SemaphoreType.DMA((3,)),
     ]
@@ -202,41 +190,49 @@
     )(*args)
 
 
-def grad_kernel(n, counts, here, then, final, *refs):
+def fetch_kernel(n, places, decoder_hbm, _, *refs):
+    outs, token_ref, sem = refs[:-2], refs[-2], refs[-1]
+    copies = []
+    for i, (dc, dy) in enumerate(places):
+        col = column(n, 0, 1, outs[i].shape[1], dy, dc)
+        copies += loads_of(decoder_hbm, col, outs[i], sem.at[i])
+    for copy in copies:
+        copy.start()
+    token_ref[...] = jnp.zeros_like(token_ref)
+    for copy in copies:
+        copy.wait()
+
+
+def fetch(n, width, places, decoder, after):
+    block = pltpu.VMEM((decoder.shape[0], width), decoder.dtype)
+    return pl.pallas_call(
+        functools.partial(fetch_kernel, n, places),
+        out_shape=[block] * len(places) + [pltpu.VMEM((SUBLANES, LANES), jnp.float32)],
+        in_specs=[HBM, VMEM],
+        out_specs=[VMEM] * (1 + len(places)),
+        scratch_shapes=[pltpu.SemaphoreType.DMA((len(places), LOADS))],
+        compiler_params=params(),
+        cost_estimate=cost(0, decoder.shape[0] * len(places) * width * 2),
+        name="fetch",
+    )(in_hbm(decoder), in_vmem(after))
+
+
+def grad_kernel(n, counts, with_prev, final, *refs):
     refs = list(refs)
     errs = [[refs.pop(0) for _ in range(count)] for count in counts]
-    decoder_hbm = None if final else refs.pop(0)
-    if here:
-        total, columns_ref = None, refs[-2]
-    else:
-        columns_ref, total = refs.pop(0), refs.pop(0)[...]
-    loads, later = [], []
-    if not final:
-        out_ref, next_ref, sem = refs[0], refs[1], refs[-1]
-        wide = next_ref.shape[2]
-        for i, (dc, dy) in enumerate(here):
-            col = column(n, 0, 1, wide, dy, dc)
-            loads.append(loads_of(decoder_hbm, col, columns_ref.at[i], sem.at[len(then) + i]))
-        for i, (dc, dy) in enumerate(then):
-            later += loads_of(decoder_hbm, column(n, 0, 1, wide, dy, dc), next_ref.at[i], sem.at[i])
-        for copy in sum(loads, []) + later:
-            copy.start()
-    for i, parts in enumerate(errs):
-        if loads:
-            for copy in loads[i]:
-                copy.wait()
+    columns = [refs.pop(0) for _ in counts]
+    total = refs.pop(0)[...] if with_prev else None
+    for parts, columns_ref in zip(errs, columns):
         err = parts[0][...] if len(parts) == 1 else jnp.concatenate([e[...] for e in parts], axis=0)
         part = lax.dot_general(
             err,
-            columns_ref[i],
+            columns_ref[...],
             (((1,), (1,)), ((), ())),
             preferred_element_type=jnp.float32,
         )
         total = part if total is None else total + part
     if not final:
-        out_ref[...] = total
-        for copy in later:
-            copy.wait()
+        refs[0][...] = total
         return
     ids_ref, loss_ref, out_ref, totals_ref = refs
     totals_ref[...] = total
@@ -268,36 +264,22 @@
                 out_ref[first // own + d] = acc[d * own : (d + 1) * own, :]
 
 
-def grad(n, rows, pieces, decoder, prev, then=(), final=None):
-    lat_dev = decoder.shape[0]
-    wide = pieces[0][1][0].shape[1]
+def grad(n, rows, pieces, columns, prev, final=None):
+    lat_dev, wide = columns[pieces[0][0]].shape
     counts = tuple(len(e) for _, e in pieces)
-    here = tuple(at for at, _ in pieces) if prev is None else ()
-    args, specs = [x for _, e in pieces for x in e], []
-    specs = [VMEM] * len(args)
-    if final is None:
-        args.append(in_hbm(decoder))
-        specs.append(HBM)
-    for x in reversed(prev or ()):
-        args.append(in_vmem(x))
-        specs.append(VMEM)
+    args = [x for _, e in pieces for x in e] + [in_vmem(columns[at]) for at, _ in pieces]
+    if prev is not None:
+        args.append(in_vmem(prev))
+    if final is not None:
+        args += list(final)
     totals = pltpu.VMEM((rows, lat_dev), jnp.float32)
-    if final is None:
-        out = [totals, pltpu.VMEM((len(then), lat_dev, wide), jnp.bfloat16)]
-        scratch = [pltpu.VMEM((len(here), lat_dev, wide), jnp.bfloat16)] if here else []
-        scratch.append(pltpu.SemaphoreType.DMA((len(then) + len(here), LOADS // 2)))
-    else:
-        args += list(final)
-        specs += [VMEM] * len(final)
-        out = jax.ShapeDtypeStruct((n, rows // n, LANES), jnp.float32)
-        scratch = [totals]
     size = wide * len(pieces)
     return pl.pallas_call(
-        functools.partial(grad_kernel, n, counts, here, then, final is not None),
-        out_shape=out,
-        in_specs=specs,
-        out_specs=VMEM if final is not None else [VMEM, VMEM],
-        scratch_shapes=scratch,
+        functools.partial(grad_kernel, n, counts, prev is not None, final is not None),
+        out_shape=totals if final is None else jax.ShapeDtypeStruct((n, rows // n, LANES), jnp.float32),
+        in_specs=[VMEM] * len(args),
+        out_specs=VMEM,
+        scratch_shapes=[] if final is None else [totals],
         compiler_params=params(),
         cost_estimate=cost(2 * rows * lat_dev * size, 4 * lat_dev * size),
         name="grad",
@@ -369,9 +351,12 @@
         leaving.append(after)
         summed.append((blocks[0], got))
 
+    places = tuple((dc, dy) for dy in range(fy) for dc in range(fc))
+    *columns, token = fetch(n, chunks * sub, places, decoder, leaving[-1])
+    columns = dict(zip(places, columns))
     sums, moved = [], []
     for p, (x, y) in enumerate(summed):
-        x = x + (hold(y, leaving[-1]) if p == 0 else y)
+        x = x + (hold(y, token) if p == 0 else y)
         sums.append(lax.dynamic_slice_in_dim(x, z * group, group, 0))
         moved.append(
             [
@@ -406,15 +391,12 @@
         return [whole[:group], whole[group : group + half], whole[group + half :]]
 
     far = [((1, at[1]), [swap(e, dc=1) for e in halves(parts)]) for at, parts in near]
-    far_last = [(1, at[1]) for at, _ in last]
-    sums = grad(n, rows, near, decoder, None, tuple(at for at, _ in far))
-    sums = grad(n, rows, far, decoder, sums, tuple(at for at, _ in last))
-    last[-1][1][-1] = hold(last[-1][1][-1], sums[0])
-    far_last = [
-        (at, [swap(join(parts, 0), dc=1)]) for at, (_, parts) in zip(far_last, last)
-    ]
-    sums = grad(n, rows, last, decoder, sums, tuple(at for at, _ in far_last))
-    back = grad(n, rows, far_last, decoder, sums, (), (indices, loss))
+    totals = grad(n, rows, near, columns, None)
+    totals = grad(n, rows, far, columns, totals)
+    last[-1][1][-1] = hold(last[-1][1][-1], totals)
+    far_last = [((1, at[1]), [swap(join(parts, 0), dc=1)]) for at, parts in last]
+    totals = grad(n, rows, last, columns, totals)
+    back = grad(n, rows, far_last, columns, totals, (indices, loss))
     pieces = near + far + last + far_last
     error = own_rows(n, [at for at, _ in pieces], own, width, [e[0][:group] for _, e in pieces])
 

time: 65.1 us -> 62.2 us (0.955)
  waiting for transfers between devices: 21 us -> 18.3 us
  Pallas kernels: 17.4 us -> 15.6 us
  starting transfers between devices: 24.1 us -> 25.6 us
    ppermute x19, waiting for transfers between devices: 15.3 us -> 12.5 us  [swap(): return lax.ppermute(x, 'lat', pairs(n, dz, dy, dc))]
    ppermute x19, starting transfers between devices: 20 us -> 21.2 us  [swap(): return lax.ppermute(x, 'lat', pairs(n, dz, dy, dc))]
    pallas_call x4 -> x5, Pallas kernels: 8.23 us -> 7.27 us  [the longest x4 3.74 us: grad(): pl.pallas_call(functools.partial(grad_kernel, n, counts, prev is not None...]
    pallas_call x3, Pallas kernels: 8.29 us -> 7.51 us  [decode(): pl.pallas_call(functools.partial(decode_kernel, n, rows // n, chunks, par...]
  transfers between devices with their start and end apart: 20 -> 20, of which waited for: 9 -> 11; matrix products, arithmetic and copies ran while one was open for 1% -> 1% of each run, Pallas kernels for 18% -> 17%
where the time goes in v10:
time: 62.2 us; the launch traced here: 61.9 us
  starting transfers between devices  25.6 us (41%)
  waiting for transfers between devices  18.3 us (29%)
  Pallas kernels  15.6 us (25%)
  other arithmetic  1.21 us (2%)
  between operations  0.86 us (1%)
    ppermute x19, starting transfers between devices, swap(): return lax.ppermute(x, 'lat', pairs(n, dz, dy, dc))  21.2 us
    ppermute x19, waiting for transfers between devices, swap(): return lax.ppermute(x, 'lat', pairs(n, dz, dy, dc))  12.5 us
    pallas_call x3, Pallas kernels, decode(): pl.pallas_call(functools.partial(decode_kernel, n, rows // n, chunks, par...  7.51 us
    all_to_all x1, waiting for transfers between devices, local(): back = jnp.sum(lax.all_to_all(back, 'lat', 0, 0, tiled=True), axis=0)  5.77 us
    all_to_all x1, starting transfers between devices, local(): back = jnp.sum(lax.all_to_all(back, 'lat', 0, 0, tiled=True), axis=0)  4.4 us
    pallas_call x4, Pallas kernels, grad(): pl.pallas_call(functools.partial(grad_kernel, n, counts, prev is not None...  3.74 us
    pallas_call x1, Pallas kernels, fetch(): pl.pallas_call(functools.partial(fetch_kernel, n, places), out_shape=[blo...  3.53 us
  transfers between devices with their start and end apart: 20, of which 11 were waited for; matrix products, arithmetic and copies ran while one was open for 1% of the time, Pallas kernels for 17%

profile of v10, /device:TPU:0, one launch (start us, length us, event | category | flops | bytes accessed | tf_op | source)
XLA Modules:
  0.0 61.9 jit_solution(13719628525748041248)
XLA Ops:
  0.6 3.7 %decode.3 = (f32[64,2048]{1,0:T(8,128)S(1)}, f32[64,2048]{1,0:T(8,128)S(1)}, bf16[64,512]{1,0:T(8,128)(2,1)S(1)}) custom-call(s32[64,64]{1,0:T(8,128)} %refs_3_.3, bf16[64,64]{1,0:T(8,128)(2,1)} %refs_1_.3, bf16[512,8192]{1,0:T(8,128)(2,1)} %decoder_hbm.1, bf16[4,8192]{1,0:T(4,128)(2,1)} %refs_2_.5), custom_call_target="tpu_custom_call" | custom-call | flops 268435456 | bytes 8388608 | tf_op jit(solution)/shard_map/decode/pallas_call | solution.py:181
  4.3 0.5 collective-permute-start
  4.8 0.1 collective-permute-start.2
  4.9 1.9 %decode.4 = f32[64,2048]{1,0:T(8,128)S(1)} custom-call(bf16[64,512]{1,0:T(8,128)(2,1)S(1)} %get-tuple-element.11.refs_0_, bf16[512,8192]{1,0:T(8,128)(2,1)} %decoder_hbm.1, bf16[4,8192]{1,0:T(4,128)(2,1)} %refs_2_.5), custom_call_target="tpu_custom_call" | custom-call | flops 134217728 | bytes 4194304 | tf_op jit(solution)/shard_map/decode/pallas_call | solution.py:181
  6.8 0.0 collective-permute-done
  6.8 0.1 add.52
  6.9 3.0 %collective-permute-start.1 = (f32[64,1024]{1,0:T(8,128)S(1)}, f32[64,1024]{1,0:T(8,128)S(1)}, u32[]{:S(2)}, u32[]{:S(2)}) collective-permute-start(f32[64,1024]{1,0:T(8,128)S(1)} %slice.31.refs_3_), channel_id=1, source_target_pairs={{0,2},{1,3},{2,0},{3,1},{4,6},{5,7},{6,4},{7,5},{8,10},{9,11},{10,... | collective-permute-start | bytes 786440 | tf_op jit(solution)/shard_map/ppermute | solution.py:325
  9.9 1.9 %decode.5 = f32[64,2048]{1,0:T(8,128)S(1)} custom-call(bf16[64,512]{1,0:T(8,128)(2,1)S(1)} %get-tuple-element.11.refs_0_, bf16[512,8192]{1,0:T(8,128)(2,1)} %decoder_hbm.1, bf16[4,8192]{1,0:T(4,128)(2,1)} %refs_2_.5, f32[64,1024]{1,0:T(8,128)S(1)} %slice.31.refs_3_), custom_call_target="tpu_custom_call" | custom-call | flops 134217728 | bytes 4194304 | tf_op jit(solution)/shard_map/decode/pallas_call | solution.py:181
  11.9 0.0 collective-permute-done.2
  11.9 0.1 add.53
  12.0 0.1 collective-permute-start.4
  12.1 3.5 %fetch.1 = (bf16[512,2048]{1,0:T(8,128)(2,1)S(1)}, bf16[512,2048]{1,0:T(8,128)(2,1)S(1)}, bf16[512,2048]{1,0:T(8,128)(2,1)S(1)}, bf16[512,2048]{1,0:T(8,128)(2,1)S(1)}, f32[8,128]{1,0:T(8,128)S(1)}) custom-call(bf16[512,8192]{1,0:T(8,128)(2,1)} %decoder_hbm.1, f32[64,1024]{1,0:T(8,128)S(1)} %slice.32._), custom_call_target="tpu_custom_call" | custom-call | bytes 8388608 | tf_op jit(solution)/shard_map/fetch/pallas_call | solution.py:208
  15.6 0.0 copy-start
  15.6 1.4 %collective-permute-done.1.refs_0_ = f32[64,1024]{1,0:T(8,128)S(1)} collective-permute-done((f32[64,1024]{1,0:T(8,128)S(1)}, f32[64,1024]{1,0:T(8,128)S(1)}, u32[]{:S(2)}, u32[]{:S(2)}) %collective-permute-start.1) | collective-permute-done | bytes 262176 | tf_op jit(solution)/shard_map/ppermute | solution.py:325
  17.1 4.2 %collective-permute-start.3 = (f32[16,1024]{1,0:T(8,128)S(1)}, f32[16,1024]{1,0:T(8,128)S(1)}, u32[]{:S(2)}, u32[]{:S(2)}) collective-permute-start(f32[16,1024]{1,0:T(8,128)S(1)} %get-tuple-element.27), channel_id=1, source_target_pairs={{0,12},{1,13},{2,14},{3,15},{4,8},{5,9},{6,10},{7,11},{8,4},{9,5},... | collective-permute-start | bytes 196616 | tf_op jit(solution)/shard_map/ppermute | solution.py:325
  21.3 0.0 collective-permute-start.6
  21.3 0.6 %collective-permute-start.5 = (f32[16,1024]{1,0:T(8,128)S(1)}, f32[16,1024]{1,0:T(8,128)S(1)}, u32[]{:S(2)}, u32[]{:S(2)}) collective-permute-start(f32[16,1024]{1,0:T(8,128)S(1)} %get-tuple-element.29), channel_id=1, source_target_pairs={{0,4},{1,5},{2,6},{3,7},{4,0},{5,1},{6,2},{7,3},{8,12},{9,13},{10,... | collective-permute-start | bytes 196616 | tf_op jit(solution)/shard_map/ppermute | solution.py:325
  22.0 0.1 collective-permute-done.4
  22.2 2.9 %collective-permute-start.9 = (f32[16,1024]{1,0:T(8,128)S(1)}, f32[16,1024]{1,0:T(8,128)S(1)}, u32[]{:S(2)}, u32[]{:S(2)}) collective-permute-start(f32[16,1024]{1,0:T(8,128)S(1)} %get-tuple-element.24), channel_id=1, source_target_pairs={{0,8},{1,9},{2,10},{3,11},{4,12},{5,13},{6,14},{7,15},{8,0},{9,1},... | collective-permute-start | bytes 196616 | tf_op jit(solution)/shard_map/ppermute | solution.py:325
  25.1 1.6 %collective-permute-start.8 = (f32[16,1024]{1,0:T(8,128)S(1)}, f32[16,1024]{1,0:T(8,128)S(1)}, u32[]{:S(2)}, u32[]{:S(2)}) collective-permute-start(f32[16,1024]{1,0:T(8,128)S(1)} %get-tuple-element.25), channel_id=1, source_target_pairs={{0,4},{1,5},{2,6},{3,7},{4,0},{5,1},{6,2},{7,3},{8,12},{9,13},{10,... | collective-permute-start | bytes 196616 | tf_op jit(solution)/shard_map/ppermute | solution.py:325
  26.6 0.0 collective-permute-done.3.refs_0_
  26.6 0.9 %collective-permute-start.7 = (f32[16,1024]{1,0:T(8,128)S(1)}, f32[16,1024]{1,0:T(8,128)S(1)}, u32[]{:S(2)}, u32[]{:S(2)}) collective-permute-start(f32[16,1024]{1,0:T(8,128)S(1)} %get-tuple-element.26), channel_id=1, source_target_pairs={{0,12},{1,13},{2,14},{3,15},{4,8},{5,9},{6,10},{7,11},{8,4},{9,5},... | collective-permute-start | bytes 196616 | tf_op jit(solution)/shard_map/ppermute | solution.py:325
  27.5 0.0 collective-permute-done.5.refs_0_
  27.5 0.2 collective-permute-done.6.refs_0_
  27.7 0.1 multiply_reduce_fusion.1
  27.8 4.9 %collective-permute-done.7.refs_0_ = f32[16,1024]{1,0:T(8,128)S(1)} collective-permute-done((f32[16,1024]{1,0:T(8,128)S(1)}, f32[16,1024]{1,0:T(8,128)S(1)}, u32[]{:S(2)}, u32[]{:S(2)}) %collective-permute-start.7) | collective-permute-done | bytes 65568 | tf_op jit(solution)/shard_map/ppermute | solution.py:325
  32.7 0.0 collective-permute-done.8.refs_0_
  32.7 0.0 copy-done
  32.7 0.0 collective-permute-done.9.refs_0_
  32.8 0.1 multiply_reduce_fusion
  32.9 1.0 %collective-permute-start.13 = (bf16[16,2048]{1,0:T(8,128)(2,1)S(1)}, bf16[16,2048]{1,0:T(8,128)(2,1)S(1)}, u32[]{:S(2)}, u32[]{:S(2)}) collective-permute-start(bf16[16,2048]{1,0:T(8,128)(2,1)S(1)} %pad_maximum_fusion.3.refs_0_), channel_id=1, source_target_pairs={{0,12},{1,13},{2,14},{3,15},{4,8},{5,9},{6,10},{7,11},{8,4},{9,5},... | collective-permute-start | bytes 196616 | tf_op jit(solution)/shard_map/ppermute | solution.py:325
  33.9 0.4 collective-permute-start.12
  34.3 1.5 %collective-permute-start.11 = (bf16[16,2048]{1,0:T(8,128)(2,1)S(1)}, bf16[16,2048]{1,0:T(8,128)(2,1)S(1)}, u32[]{:S(2)}, u32[]{:S(2)}) collective-permute-start(bf16[16,2048]{1,0:T(8,128)(2,1)S(1)} %pad_maximum_fusion.3.refs_0_), channel_id=1, source_target_pairs={{0,2},{1,3},{2,0},{3,1},{4,6},{5,7},{6,4},{7,5},{8,10},{9,11},{10,... | collective-permute-start | bytes 196616 | tf_op jit(solution)/shard_map/ppermute | solution.py:325
  35.8 3.0 %collective-permute-start.14 = (bf16[16,2048]{1,0:T(8,128)(2,1)S(1)}, bf16[16,2048]{1,0:T(8,128)(2,1)S(1)}, u32[]{:S(2)}, u32[]{:S(2)}) collective-permute-start(bf16[16,2048]{1,0:T(8,128)(2,1)S(1)} %pad_maximum_fusion.3.refs_0_), channel_id=1, source_target_pairs={{0,8},{1,9},{2,10},{3,11},{4,12},{5,13},{6,14},{7,15},{8,0},{9,1},... | collective-permute-start | bytes 196616 | tf_op jit(solution)/shard_map/ppermute | solution.py:325
  38.9 0.4 collective-permute-done.13.refs_1_
  39.2 0.0 collective-permute-done.12.refs_0_
  39.2 0.0 collective-permute-done.11.refs_0_
  39.2 1.9 %collective-permute-done.14.refs_0_ = bf16[16,2048]{1,0:T(8,128)(2,1)S(1)} collective-permute-done((bf16[16,2048]{1,0:T(8,128)(2,1)S(1)}, bf16[16,2048]{1,0:T(8,128)(2,1)S(1)}, u32[]{:S(2)}, u32[]{:S(2)}) %collective-permute-start.14) | collective-permute-done | bytes 65568 | tf_op jit(solution)/shard_map/ppermute | solution.py:325
  41.1 0.6 collective-permute-start.15
  41.7 0.1 collective-permute-start.16
  41.8 0.5 collective-permute-start.10
  42.3 0.1 collective-permute-start.17
  42.4 0.8 %grad.4.refs_4_ = f32[64,512]{1,0:T(8,128)S(1)} custom-call(bf16[16,2048]{1,0:T(8,128)(2,1)S(1)} %pad_maximum_fusion.3.refs_0_, bf16[48,2048]{1,0:T(8,128)(2,1)S(1)} %pad_maximum_fusion.1.refs_1_, bf16[512,2048]{1,0:T(8,128)(2,1)S(1)} %get-tuple-element.16.refs_2_), custom_call_target="tpu_custom_call" | custom-call | flops 134217728 | bytes 4194304 | tf_op jit(solution)/shard_map/grad/pallas_call | solution.py:277
  43.1 0.1 collective-permute-done.10.refs_0_.refs_1_
  43.2 0.3 collective-permute-done.17.refs_2_
  43.5 0.0 collective-permute-done.16.refs_1_
  43.5 0.8 %grad.5.refs_1_.refs_3_ = f32[64,512]{1,0:T(8,128)S(1)} custom-call(bf16[16,2048]{1,0:T(8,128)(2,1)S(1)} %collective-permute-done.10.refs_0_.refs_1_, bf16[32,2048]{1,0:T(8,128)(2,1)S(1)} %collective-permute-done.16.refs_1_, bf16[16,2048]{1,0:T(8,128)(2,1)S(1)} %collective-permute-done.17.refs_2_, bf16[512,2048]{1,0:T(8,128)(2,1)S(1)} %get-tuple-element.15.refs_3_, ...), custom_call_target="tpu_custom_call" | custom-call | flops 134217728 | bytes 4194304 | tf_op jit(solution)/shard_map/grad/pallas_call | solution.py:277
  44.3 0.0 copy-start.2
  44.3 2.6 %collective-permute-done.15.refs_0_ = bf16[48,2048]{1,0:T(8,128)(2,1)S(1)} collective-permute-done((bf16[48,2048]{1,0:T(8,128)(2,1)S(1)}, bf16[48,2048]{1,0:T(8,128)(2,1)S(1)}, u32[]{:S(2)}, u32[]{:S(2)}) %collective-permute-start.15) | collective-permute-done | bytes 196640 | tf_op jit(solution)/shard_map/ppermute | solution.py:325
  46.9 0.1 collective-permute-start.18
  47.0 0.1 copy.19.refs_4_
  47.1 0.0 copy-start.1
  47.1 0.8 %grad.6.refs_2_ = f32[64,512]{1,0:T(8,128)S(1)} custom-call(bf16[16,2048]{1,0:T(8,128)(2,1)S(1)} %hold.20.refs_1_.refs_2_.refs_0_, bf16[48,2048]{1,0:T(8,128)(2,1)S(1)} %hold.23.refs_1_, bf16[512,2048]{1,0:T(8,128)(2,1)S(1)} %get-tuple-element.18.refs_2_, f32[64,512]{1,0:T(8,128)S(1)} %grad.5.refs_1_.refs_3_), custom_call_target="tpu_custom_call" | custom-call | flops 134217728 | bytes 4194304 | tf_op jit(solution)/shard_map/grad/pallas_call | solution.py:277
  47.8 0.7 %collective-permute-done.18.refs_0_ = bf16[64,2048]{1,0:T(8,128)(2,1)S(1)} collective-permute-done((bf16[64,2048]{1,0:T(8,128)(2,1)S(1)}, bf16[64,2048]{1,0:T(8,128)(2,1)S(1)}, u32[]{:S(2)}, u32[]{:S(2)}) %collective-permute-start.18) | collective-permute-done | bytes 262176 | tf_op jit(solution)/shard_map/ppermute | solution.py:325
  48.5 0.0 copy-done.2
  48.5 0.2 copy-done.1
  48.7 1.5 %grad.7 = f32[16,4,128]{2,1,0:T(4,128)} custom-call(bf16[64,2048]{1,0:T(8,128)(2,1)S(1)} %collective-permute-done.18.refs_0_, bf16[512,2048]{1,0:T(8,128)(2,1)S(1)} %copy-done.1, f32[64,512]{1,0:T(8,128)S(1)} %grad.6.refs_2_, s32[64,64]{1,0:T(8,128)S(1)} %copy-done.2, f32[16,1]{1,0:T(8,128)S(1)} %copy.19.refs_4_), custom_call_target="tpu_custom_call" | custom-call | flops 134217728 | bytes 4194304 | tf_op jit(solution)/shard_map/grad/pallas_call | solution.py:277
  50.1 4.4 %all-to-all-start = ((f32[16,4,128]{2,1,0:T(4,128)}), f32[16,4,128]{2,1,0:T(4,128)S(1)}, u32[]{:S(2)}, u32[]{:S(2)}) async-start(f32[16,4,128]{2,1,0:T(4,128)} %grad.7), calls=%async_computation | async-start | bytes 65536 | tf_op jit(solution)/shard_map/all_to_all | solution.py:403
  54.6 0.8 %own_rows.1 = bf16[4,8192]{1,0:T(4,128)(2,1)} custom-call(bf16[16,2048]{1,0:T(8,128)(2,1)S(1)} %pad_maximum_fusion.3.refs_0_, bf16[16,2048]{1,0:T(8,128)(2,1)S(1)} %collective-permute-done.10.refs_0_.refs_1_, bf16[16,2048]{1,0:T(8,128)(2,1)S(1)} %hold.20.refs_1_.refs_2_.refs_0_, bf16[16,2048]{1,0:T(8,128)(2,1)S(1)} %slice.34.refs_3_), custom_call_target="tpu_custom_call" | custom-call | tf_op jit(solution)/shard_map/own_rows/pallas_call | solution.py:303
  55.4 5.8 %all-to-all-done = f32[16,4,128]{2,1,0:T(4,128)S(1)} async-done(((f32[16,4,128]{2,1,0:T(4,128)}), f32[16,4,128]{2,1,0:T(4,128)S(1)}, u32[]{:S(2)}, u32[]{:S(2)}) %all-to-all-start) | async-done | bytes 32800 | tf_op jit(solution)/shard_map/all_to_all | solution.py:403
  61.2 0.0 copy-start.3
  61.2 0.7 %multiply_reduce_fusion.2 = f32[4]{0:T(128)} fusion(f32[4,128]{1,0:T(4,128)S(1)} %reduce_sum.29), kind=kLoop, calls=%fused_computation.10 | loop fusion | flops 4 | bytes 32 | tf_op jit(solution)/shard_map/div | solution.py:404
  61.9 0.0 copy-done.3
  (25 shorter events, 0.2 us)
Async XLA Ops:
  4.3 2.5 %collective-permute-start = (f32[64,2048]{1,0:T(8,128)S(1)}, f32[64,2048]{1,0:T(8,128)S(1)}, u32[]{:S(2)}, u32[]{:S(2)}) collective-permute-start(f32[64,2048]{1,0:T(8,128)S(1)} %get-tuple-element.12), channel_id=1, source_target_pairs={{0,1},{1,0},{2,3},{3,2},{4,5},{5,4},{6,7},{7,6},{8,9},{9,8},{10,11... | collective-permute-start | bytes 1572872 | tf_op jit(solution)/shard_map/ppermute | solution.py:325
  4.8 7.1 %collective-permute-start.2 = (f32[64,2048]{1,0:T(8,128)S(1)}, f32[64,2048]{1,0:T(8,128)S(1)}, u32[]{:S(2)}, u32[]{:S(2)}) collective-permute-start(f32[64,2048]{1,0:T(8,128)S(1)} %get-tuple-element.13), channel_id=1, source_target_pairs={{0,1},{1,0},{2,3},{3,2},{4,5},{5,4},{6,7},{7,6},{8,9},{9,8},{10,11... | collective-permute-start | bytes 1572872 | tf_op jit(solution)/shard_map/ppermute | solution.py:325
  6.9 10.1 %collective-permute-start.1 = (f32[64,1024]{1,0:T(8,128)S(1)}, f32[64,1024]{1,0:T(8,128)S(1)}, u32[]{:S(2)}, u32[]{:S(2)}) collective-permute-start(f32[64,1024]{1,0:T(8,128)S(1)} %slice.31.refs_3_), channel_id=1, source_target_pairs={{0,2},{1,3},{2,0},{3,1},{4,6},{5,7},{6,4},{7,5},{8,10},{9,11},{10,... | collective-permute-start | bytes 786440 | tf_op jit(solution)/shard_map/ppermute | solution.py:325
  12.0 10.1 %collective-permute-start.4 = (f32[64,1024]{1,0:T(8,128)S(1)}, f32[64,1024]{1,0:T(8,128)S(1)}, u32[]{:S(2)}, u32[]{:S(2)}) collective-permute-start(f32[64,1024]{1,0:T(8,128)S(1)} %slice.32._), channel_id=1, source_target_pairs={{0,2},{1,3},{2,0},{3,1},{4,6},{5,7},{6,4},{7,5},{8,10},{9,11},{10,... | collective-permute-start | bytes 786440 | tf_op jit(solution)/shard_map/ppermute | solution.py:325
  15.6 17.1 %copy-start = (bf16[512,2048]{1,0:T(8,128)(2,1)}, bf16[512,2048]{1,0:T(8,128)(2,1)S(1)}, u32[]{:S(2)}) copy-start(bf16[512,2048]{1,0:T(8,128)(2,1)S(1)} %get-tuple-element.17.refs_1_) | copy-start | bytes 6291460
  17.1 9.5 %collective-permute-start.3 = (f32[16,1024]{1,0:T(8,128)S(1)}, f32[16,1024]{1,0:T(8,128)S(1)}, u32[]{:S(2)}, u32[]{:S(2)}) collective-permute-start(f32[16,1024]{1,0:T(8,128)S(1)} %get-tuple-element.27), channel_id=1, source_target_pairs={{0,12},{1,13},{2,14},{3,15},{4,8},{5,9},{6,10},{7,11},{8,4},{9,5},... | collective-permute-start | bytes 196616 | tf_op jit(solution)/shard_map/ppermute | solution.py:325
  21.3 6.4 %collective-permute-start.6 = (f32[16,1024]{1,0:T(8,128)S(1)}, f32[16,1024]{1,0:T(8,128)S(1)}, u32[]{:S(2)}, u32[]{:S(2)}) collective-permute-start(f32[16,1024]{1,0:T(8,128)S(1)} %get-tuple-element.28), channel_id=1, source_target_pairs={{0,8},{1,9},{2,10},{3,11},{4,12},{5,13},{6,14},{7,15},{8,0},{9,1},... | collective-permute-start | bytes 196616 | tf_op jit(solution)/shard_map/ppermute | solution.py:325
  21.3 6.2 %collective-permute-start.5 = (f32[16,1024]{1,0:T(8,128)S(1)}, f32[16,1024]{1,0:T(8,128)S(1)}, u32[]{:S(2)}, u32[]{:S(2)}) collective-permute-start(f32[16,1024]{1,0:T(8,128)S(1)} %get-tuple-element.29), channel_id=1, source_target_pairs={{0,4},{1,5},{2,6},{3,7},{4,0},{5,1},{6,2},{7,3},{8,12},{9,13},{10,... | collective-permute-start | bytes 196616 | tf_op jit(solution)/shard_map/ppermute | solution.py:325
  22.2 10.6 %collective-permute-start.9 = (f32[16,1024]{1,0:T(8,128)S(1)}, f32[16,1024]{1,0:T(8,128)S(1)}, u32[]{:S(2)}, u32[]{:S(2)}) collective-permute-start(f32[16,1024]{1,0:T(8,128)S(1)} %get-tuple-element.24), channel_id=1, source_target_pairs={{0,8},{1,9},{2,10},{3,11},{4,12},{5,13},{6,14},{7,15},{8,0},{9,1},... | collective-permute-start | bytes 196616 | tf_op jit(solution)/shard_map/ppermute | solution.py:325
  25.1 7.7 %collective-permute-start.8 = (f32[16,1024]{1,0:T(8,128)S(1)}, f32[16,1024]{1,0:T(8,128)S(1)}, u32[]{:S(2)}, u32[]{:S(2)}) collective-permute-start(f32[16,1024]{1,0:T(8,128)S(1)} %get-tuple-element.25), channel_id=1, source_target_pairs={{0,4},{1,5},{2,6},{3,7},{4,0},{5,1},{6,2},{7,3},{8,12},{9,13},{10,... | collective-permute-start | bytes 196616 | tf_op jit(solution)/shard_map/ppermute | solution.py:325
  26.6 6.1 %collective-permute-start.7 = (f32[16,1024]{1,0:T(8,128)S(1)}, f32[16,1024]{1,0:T(8,128)S(1)}, u32[]{:S(2)}, u32[]{:S(2)}) collective-permute-start(f32[16,1024]{1,0:T(8,128)S(1)} %get-tuple-element.26), channel_id=1, source_target_pairs={{0,12},{1,13},{2,14},{3,15},{4,8},{5,9},{6,10},{7,11},{8,4},{9,5},... | collective-permute-start | bytes 196616 | tf_op jit(solution)/shard_map/ppermute | solution.py:325
  32.9 6.3 %collective-permute-start.13 = (bf16[16,2048]{1,0:T(8,128)(2,1)S(1)}, bf16[16,2048]{1,0:T(8,128)(2,1)S(1)}, u32[]{:S(2)}, u32[]{:S(2)}) collective-permute-start(bf16[16,2048]{1,0:T(8,128)(2,1)S(1)} %pad_maximum_fusion.3.refs_0_), channel_id=1, source_target_pairs={{0,12},{1,13},{2,14},{3,15},{4,8},{5,9},{6,10},{7,11},{8,4},{9,5},... | collective-permute-start | bytes 196616 | tf_op jit(solution)/shard_map/ppermute | solution.py:325
  33.9 5.3 %collective-permute-start.12 = (bf16[16,2048]{1,0:T(8,128)(2,1)S(1)}, bf16[16,2048]{1,0:T(8,128)(2,1)S(1)}, u32[]{:S(2)}, u32[]{:S(2)}) collective-permute-start(bf16[16,2048]{1,0:T(8,128)(2,1)S(1)} %pad_maximum_fusion.3.refs_0_), channel_id=1, source_target_pairs={{0,4},{1,5},{2,6},{3,7},{4,0},{5,1},{6,2},{7,3},{8,12},{9,13},{10,... | collective-permute-start | bytes 196616 | tf_op jit(solution)/shard_map/ppermute | solution.py:325
  34.3 4.9 %collective-permute-start.11 = (bf16[16,2048]{1,0:T(8,128)(2,1)S(1)}, bf16[16,2048]{1,0:T(8,128)(2,1)S(1)}, u32[]{:S(2)}, u32[]{:S(2)}) collective-permute-start(bf16[16,2048]{1,0:T(8,128)(2,1)S(1)} %pad_maximum_fusion.3.refs_0_), channel_id=1, source_target_pairs={{0,2},{1,3},{2,0},{3,1},{4,6},{5,7},{6,4},{7,5},{8,10},{9,11},{10,... | collective-permute-start | bytes 196616 | tf_op jit(solution)/shard_map/ppermute | solution.py:325
  35.8 5.3 %collective-permute-start.14 = (bf16[16,2048]{1,0:T(8,128)(2,1)S(1)}, bf16[16,2048]{1,0:T(8,128)(2,1)S(1)}, u32[]{:S(2)}, u32[]{:S(2)}) collective-permute-start(bf16[16,2048]{1,0:T(8,128)(2,1)S(1)} %pad_maximum_fusion.3.refs_0_), channel_id=1, source_target_pairs={{0,8},{1,9},{2,10},{3,11},{4,12},{5,13},{6,14},{7,15},{8,0},{9,1},... | collective-permute-start | bytes 196616 | tf_op jit(solution)/shard_map/ppermute | solution.py:325
  41.1 5.7 %collective-permute-start.15 = (bf16[48,2048]{1,0:T(8,128)(2,1)S(1)}, bf16[48,2048]{1,0:T(8,128)(2,1)S(1)}, u32[]{:S(2)}, u32[]{:S(2)}) collective-permute-start(bf16[48,2048]{1,0:T(8,128)(2,1)S(1)} %pad_maximum_fusion.1.refs_1_), channel_id=1, source_target_pairs={{0,2},{1,3},{2,0},{3,1},{4,6},{5,7},{6,4},{7,5},{8,10},{9,11},{10,... | collective-permute-start | bytes 589832 | tf_op jit(solution)/shard_map/ppermute | solution.py:325
  41.7 1.8 %collective-permute-start.16 = (bf16[32,2048]{1,0:T(8,128)(2,1)S(1)}, bf16[32,2048]{1,0:T(8,128)(2,1)S(1)}, u32[]{:S(2)}, u32[]{:S(2)}) collective-permute-start(bf16[32,2048]{1,0:T(8,128)(2,1)S(1)} %pad_maximum_fusion.2), channel_id=1, source_target_pairs={{0,1},{1,0},{2,3},{3,2},{4,5},{5,4},{6,7},{7,6},{8,9},{9,8},{10,11... | collective-permute-start | bytes 393224 | tf_op jit(solution)/shard_map/ppermute | solution.py:325
  41.8 1.4 %collective-permute-start.10 = (bf16[16,2048]{1,0:T(8,128)(2,1)S(1)}, bf16[16,2048]{1,0:T(8,128)(2,1)S(1)}, u32[]{:S(2)}, u32[]{:S(2)}) collective-permute-start(bf16[16,2048]{1,0:T(8,128)(2,1)S(1)} %pad_maximum_fusion.3.refs_0_), channel_id=1, source_target_pairs={{0,1},{1,0},{2,3},{3,2},{4,5},{5,4},{6,7},{7,6},{8,9},{9,8},{10,11... | collective-permute-start | bytes 196616 | tf_op jit(solution)/shard_map/ppermute | solution.py:325
  42.3 1.3 %collective-permute-start.17 = (bf16[16,2048]{1,0:T(8,128)(2,1)S(1)}, bf16[16,2048]{1,0:T(8,128)(2,1)S(1)}, u32[]{:S(2)}, u32[]{:S(2)}) collective-permute-start(bf16[16,2048]{1,0:T(8,128)(2,1)S(1)} %hold.21), channel_id=1, source_target_pairs={{0,1},{1,0},{2,3},{3,2},{4,5},{5,4},{6,7},{7,6},{8,9},{9,8},{10,11... | collective-permute-start | bytes 196616 | tf_op jit(solution)/shard_map/ppermute | solution.py:325
  44.3 4.2 %copy-start.2 = (s32[64,64]{1,0:T(8,128)S(1)}, s32[64,64]{1,0:T(8,128)}, u32[]{:S(2)}) copy-start(s32[64,64]{1,0:T(8,128)} %refs_3_.3) | copy-start | bytes 49156
  46.9 1.6 %collective-permute-start.18 = (bf16[64,2048]{1,0:T(8,128)(2,1)S(1)}, bf16[64,2048]{1,0:T(8,128)(2,1)S(1)}, u32[]{:S(2)}, u32[]{:S(2)}) collective-permute-start(bf16[64,2048]{1,0:T(8,128)(2,1)S(1)} %pad_maximum_fusion), channel_id=1, source_target_pairs={{0,1},{1,0},{2,3},{3,2},{4,5},{5,4},{6,7},{7,6},{8,9},{9,8},{10,11... | collective-permute-start | bytes 786440 | tf_op jit(solution)/shard_map/ppermute | solution.py:325
  47.1 1.6 %copy-start.1 = (bf16[512,2048]{1,0:T(8,128)(2,1)S(1)}, bf16[512,2048]{1,0:T(8,128)(2,1)}, u32[]{:S(2)}) copy-start(bf16[512,2048]{1,0:T(8,128)(2,1)} %copy-done) | copy-start | bytes 6291460
  50.1 11.0 %all-to-all-start = ((f32[16,4,128]{2,1,0:T(4,128)}), f32[16,4,128]{2,1,0:T(4,128)S(1)}, u32[]{:S(2)}, u32[]{:S(2)}) async-start(f32[16,4,128]{2,1,0:T(4,128)} %grad.7), calls=%async_computation | async-start | bytes 65536 | tf_op jit(solution)/shard_map/all_to_all | solution.py:403
  61.2 0.7 %copy-start.3 = (f32[4,128]{1,0:T(4,128)}, f32[4,128]{1,0:T(4,128)S(1)}, u32[]{:S(2)}) copy-start(f32[4,128]{1,0:T(4,128)S(1)} %reduce_sum.29) | copy-start | bytes 6148

commit v11 on v10

v11 whole, which is shorter than its diff:
```python
import functools

import jax
import jax.numpy as jnp
from jax import lax
from jax.experimental import pallas as pl
from jax.experimental.pallas import tpu as pltpu
from jax.sharding import PartitionSpec as P

CHUNKS = 2
ROW_STEP = 16
LANES = 128
SUBLANES = 8
LOADS = 4
VMEM = pl.BlockSpec(memory_space=pltpu.VMEM)
HBM = pl.BlockSpec(memory_space=pltpu.HBM)


def factors(n):
    assert n > 1 and n & (n - 1) == 0
    c = 2
    m = n // c
    y = 1
    while 4 * y * y <= m:
        y *= 2
    return m // y, y, c


def place(n, index):
    _, y, c = factors(n)
    return index // (y * c), (index // c) % y, index % c


def bits(size):
    return [1 << i for i in range(size.bit_length() - 1)]


def z_order(fz):
    return ([fz - 1] if fz > 1 else []) + list(range(1, fz - 1))


def pairs(n, dz, dy, dc):
    _, fy, fc = factors(n)
    out = []
    for i in range(n):
        z, y, c = place(n, i)
        out.append((i, ((z ^ dz) * fy + (y ^ dy)) * fc + (c ^ dc)))
    return out


def cost(flops, size):
    return pl.CostEstimate(flops=flops, bytes_accessed=size, transcendentals=0)


def params():
    return pltpu.CompilerParams(vmem_limit_bytes=24 * 1024 * 1024)


def in_hbm(x):
    return pltpu.with_memory_space_constraint(x, pltpu.HBM)


def in_vmem(x):
    return pltpu.with_memory_space_constraint(x, pltpu.VMEM)


def column(n, chunk, chunks, sub, dy, dc):
    _, fy, fc = factors(n)
    _, y, c = place(n, lax.axis_index("lat"))
    return pl.multiple_of((((c ^ dc) * fy + (y ^ dy)) * chunks + chunk) * sub, sub)


def hold(x, *after):
    def kernel(x_ref, *refs):
        refs[-1][...] = x_ref[...]

    return pl.pallas_call(
        kernel,
        out_shape=jax.ShapeDtypeStruct(x.shape, x.dtype),
        in_specs=[VMEM] * (1 + len(after)),
        out_specs=VMEM,
        input_output_aliases={0: 0},
        compiler_params=params(),
        name="hold",
    )(*[in_vmem(a) for a in (x, *after)])


def loads_of(decoder_hbm, col, buf, sem):
    count = sem.shape[0]
    step = buf.shape[0] // count
    return [
        pltpu.make_async_copy(
            decoder_hbm.at[pl.ds(i * step, step), pl.ds(col, buf.shape[1])],
            buf.at[pl.ds(i * step, step)],
            sem.at[i],
        )
        for i in range(count)
    ]


def add_targets(n, own, col, targets_ref, out_ref, here):
    me = lax.axis_index("lat")
    width = here.stop - here.start
    per = SUBLANES // own
    tile = pl.ds(pl.multiple_of(me // per * SUBLANES, SUBLANES), SUBLANES)
    mine = lax.broadcasted_iota(jnp.int32, (SUBLANES, width), 0) // own == me % per
    target = targets_ref[:, pl.ds(col, width)].astype(jnp.float32)
    target = jnp.concatenate([target] * per, axis=0)
    out_ref[tile, here] -= jnp.where(mine, target, 0.0)


def first_kernel(n, own, chunks, *refs):
    ids_hbm, codes_hbm, decoder_hbm, targets_hbm = refs[:4]
    outs = refs[4 : 4 + chunks]
    dense_ref, kept_ref, buf, sem, kept_sem, targets_ref, small, ids_ref, codes_ref = refs[4 + chunks :]
    _, fy, _ = factors(n)
    me = lax.axis_index("lat")
    smalls_in = [(ids_hbm, ids_ref), (codes_hbm, codes_ref), (targets_hbm, targets_ref)]
    smalls = [pltpu.make_async_copy(a, b, small.at[i]) for i, (a, b) in enumerate(smalls_in)]
    for copy in smalls:
        copy.start()
    rows, lat_dev = dense_ref.shape
    wide = buf.shape[2]
    sub = wide // chunks
    cols = [column(n, 0, 1, wide, o, 1) for o in range(fy)]
    loads = [loads_of(decoder_hbm, col, buf.at[i], sem.at[i]) for i, col in enumerate(cols)]
    later = []
    for o in range(fy):
        col = column(n, 0, chunks, sub, o, 0)
        later += loads_of(decoder_hbm, col, kept_ref.at[o], kept_sem.at[o])
    for copy in sum(loads, []) + later:
        copy.start()
    for copy in smalls:
        copy.wait()
    k_count = ids_ref.shape[1]
    lanes = lax.broadcasted_iota(jnp.int32, (ROW_STEP, lat_dev), 1) + me * lat_dev

    def body(g, carry):
        at = pl.ds(pl.multiple_of(g * ROW_STEP, ROW_STEP), ROW_STEP)
        ids = ids_ref[at, :]
        codes = codes_ref[at, :].astype(jnp.float32)
        acc = jnp.zeros((ROW_STEP, lat_dev), jnp.float32)
        for k in range(k_count):
            acc = jnp.where(ids[:, k : k + 1] == lanes, codes[:, k : k + 1], acc)
        dense_ref[at, :] = acc.astype(jnp.bfloat16)
        return carry

    lax.fori_loop(0, rows // ROW_STEP, body, 0)
    for o in range(fy):
        for copy in loads[o]:
            copy.wait()
        for p in range(chunks):
            here = slice(o * sub, (o + 1) * sub)
            outs[p][:, here] = jnp.dot(
                dense_ref[...], buf[o, :, p * sub : (p + 1) * sub], preferred_element_type=jnp.float32
            )
            add_targets(n, own, pl.multiple_of(cols[o] + p * sub, sub), targets_ref, outs[p], here)
    for copy in later:
        copy.wait()


def first_decode(n, chunks, sub, ids, codes, decoder, targets):
    _, fy, _ = factors(n)
    rows, lat_dev = ids.shape[0], decoder.shape[0]
    return pl.pallas_call(
        functools.partial(first_kernel, n, rows // n, chunks),
        out_shape=[pltpu.VMEM((rows, fy * sub), jnp.float32)] * chunks
        + [pltpu.VMEM((rows, lat_dev), jnp.bfloat16), pltpu.VMEM((fy, lat_dev, sub), jnp.bfloat16)],
        in_specs=[HBM] * 4,
        out_specs=[VMEM] * (chunks + 2),
        scratch_shapes=[
            pltpu.VMEM((fy, lat_dev, chunks * sub), jnp.bfloat16),
            pltpu.SemaphoreType.DMA((fy, LOADS)),
            pltpu.SemaphoreType.DMA((fy, LOADS)),
            pltpu.VMEM(targets.shape, targets.dtype),
            pltpu.SemaphoreType.DMA((3,)),
            pltpu.VMEM(ids.shape, ids.dtype),
            pltpu.VMEM(codes.shape, codes.dtype),
        ],
        compiler_params=params(),
        cost_estimate=cost(2 * rows * lat_dev * chunks * fy * sub, 4 * lat_dev * chunks * fy * sub),
        name="first_decode",
    )(*[in_hbm(x) for x in (ids, codes, decoder, targets)])


def decode_kernel(n, own, chunk, chunks, loaded, dense_ref, columns_ref, targets_hbm, *refs):
    _, fy, _ = factors(n)
    out_ref, targets_ref, small = refs[0 if loaded else 1 :][:3]
    copy_targets = pltpu.make_async_copy(targets_hbm, targets_ref, small)
    copy_targets.start()
    sub = out_ref.shape[1] // fy
    cols = [column(n, chunk, chunks, sub, o, 0) for o in range(fy)]
    loads, buf = [[]] * fy, columns_ref
    if not loaded:
        buf, sem = refs[4:]
        loads = [loads_of(columns_ref, col, buf.at[i], sem.at[i]) for i, col in enumerate(cols)]
        for copy in sum(loads, []):
            copy.start()
    for o, col in enumerate(cols):
        for copy in loads[o]:
            copy.wait()
        here = slice(o * sub, (o + 1) * sub)
        out_ref[:, here] = jnp.dot(dense_ref[...], buf[o], preferred_element_type=jnp.float32)
    copy_targets.wait()
    for o, col in enumerate(cols):
        add_targets(n, own, col, targets_ref, out_ref, slice(o * sub, (o + 1) * sub))


def decode(n, chunk, chunks, sub, dense, columns, targets, after=None):
    _, fy, _ = factors(n)
    loaded = columns.ndim == 3
    rows, lat_dev = dense.shape
    scratch = [pltpu.VMEM(targets.shape, targets.dtype), pltpu.SemaphoreType.DMA]
    if loaded:
        args, specs = [dense, in_vmem(columns), in_hbm(targets)], [VMEM, VMEM, HBM]
    else:
        args, specs = [dense, in_hbm(columns), in_hbm(targets), in_vmem(after)], [VMEM, HBM, HBM, VMEM]
        scratch += [
            pltpu.VMEM((fy, lat_dev, sub), jnp.bfloat16),
            pltpu.SemaphoreType.DMA((fy, LOADS)),
        ]
    return pl.pallas_call(
        functools.partial(decode_kernel, n, rows // n, chunk, chunks, loaded),
        out_shape=pltpu.VMEM((rows, fy * sub), jnp.float32),
        in_specs=specs,
        out_specs=VMEM,
        scratch_shapes=scratch,
        compiler_params=params(),
        cost_estimate=cost(2 * rows * lat_dev * fy * sub, 4 * lat_dev * fy * sub),
        name="decode",
    )(*args)


def fetch_kernel(n, places, decoder_hbm, ids_hbm, _, *refs):
    outs = refs[: len(places)]
    ids_ref, token_ref, sem, ids_sem = refs[len(places) :]
    copies = [pltpu.make_async_copy(ids_hbm, ids_ref, ids_sem)]
    for i, (dc, dy) in enumerate(places):
        col = column(n, 0, 1, outs[i].shape[1], dy, dc)
        copies += loads_of(decoder_hbm, col, outs[i], sem.at[i])
    for copy in copies:
        copy.start()
    token_ref[...] = jnp.zeros_like(token_ref)
    for copy in copies:
        copy.wait()


def fetch(n, width, places, decoder, ids, after):
    block = pltpu.VMEM((decoder.shape[0], width), decoder.dtype)
    return pl.pallas_call(
        functools.partial(fetch_kernel, n, places),
        out_shape=[block] * len(places)
        + [pltpu.VMEM(ids.shape, ids.dtype), pltpu.VMEM((SUBLANES, LANES), jnp.float32)],
        in_specs=[HBM, HBM, VMEM],
        out_specs=[VMEM] * (2 + len(places)),
        scratch_shapes=[pltpu.SemaphoreType.DMA((len(places), LOADS)), pltpu.SemaphoreType.DMA],
        compiler_params=params(),
        cost_estimate=cost(0, decoder.shape[0] * len(places) * width * 2),
        name="fetch",
    )(in_hbm(decoder), in_hbm(ids), in_vmem(after))


def grad_kernel(n, count, with_prev, final, *refs):
    refs = list(refs)
    errs = [refs.pop(0) for _ in range(count)]
    columns = [(refs.pop(0), refs.pop(0)) for _ in errs]
    prev_ref = refs.pop(0) if with_prev else None
    totals_ref, token_ref = (refs[-1], None) if final else refs
    for i, err in enumerate(errs):
        for core in range(2):
            part = lax.dot_general(
                err[...],
                columns[i][core][...],
                (((1,), (1,)), ((), ())),
                preferred_element_type=jnp.float32,
            )
            if i:
                part += totals_ref[core]
            elif with_prev:
                part += prev_ref[core]
            totals_ref[core] = part
    if not final:
        token_ref[...] = jnp.zeros_like(token_ref)
        return
    ids_ref, loss_ref, out_ref = refs[:3]
    rows, k_count = ids_ref.shape
    lat_dev = totals_ref.shape[2]
    own = out_ref.shape[1]
    fz, _, _ = factors(n)
    me = lax.axis_index("lat")
    z, _, _ = place(n, me)
    group = rows // fz
    places = lax.broadcasted_iota(jnp.int32, (ROW_STEP, LANES), 1)
    pad = jnp.zeros((ROW_STEP, LANES - k_count), jnp.int32)
    for q, j in enumerate([0] + z_order(fz)):
        for s in range(0, group, ROW_STEP):
            first = (z ^ j) * group + s
            rows_at = pl.ds(pl.multiple_of(first, ROW_STEP), ROW_STEP)
            ids = jnp.concatenate([ids_ref[rows_at, :], pad], axis=1)
            acc = jnp.zeros((ROW_STEP, LANES), jnp.float32)
            if q == 0:
                acc = jnp.where(places == k_count, loss_ref[s : s + ROW_STEP, :], acc)
            here = slice(q * group + s, q * group + s + ROW_STEP)
            for core in range(2):
                local_ids = ids - (me ^ core) * lat_dev
                held = jnp.where(places < k_count, local_ids // LANES, -1)
                inside = local_ids % LANES
                for t in range(lat_dev // LANES):
                    values = totals_ref[core, here, t * LANES : (t + 1) * LANES]
                    found = jnp.take_along_axis(values, inside, axis=1, mode="promise_in_bounds")
                    acc = jnp.where(held == t, found, acc)
            for d in range(ROW_STEP // own):
                out_ref[first // own + d] = acc[d * own : (d + 1) * own, :]


def grad(n, rows, pieces, columns, prev, final=None):
    lat_dev, wide = columns[pieces[0][0]][0].shape
    args = [e for _, e in pieces]
    args += [in_vmem(x) for at, _ in pieces for x in columns[at]]
    if prev is not None:
        args.append(in_vmem(prev))
    if final is not None:
        args += list(final)
    totals = pltpu.VMEM((2, rows, lat_dev), jnp.float32)
    size = 2 * wide * len(pieces)
    return pl.pallas_call(
        functools.partial(grad_kernel, n, len(pieces), prev is not None, final is not None),
        out_shape=[totals, pltpu.VMEM((SUBLANES, LANES), jnp.float32)]
        if final is None
        else jax.ShapeDtypeStruct((n, rows // n, LANES), jnp.float32),
        in_specs=[VMEM] * len(args),
        out_specs=[VMEM] * 2 if final is None else VMEM,
        scratch_shapes=[] if final is None else [totals],
        compiler_params=params(),
        cost_estimate=cost(2 * rows * lat_dev * size, 4 * lat_dev * size),
        name="grad",
    )(*args)


def own_kernel(n, places, *refs):
    parts, out_ref = refs[:-1], refs[-1]
    for part, (dc, dy) in zip(parts, places):
        width = part.shape[1]
        out_ref[:, pl.ds(column(n, 0, 1, width, dy, dc), width)] = part[...]


def own_rows(n, places, width, parts):
    return pl.pallas_call(
        functools.partial(own_kernel, n, places),
        out_shape=jax.ShapeDtypeStruct((parts[0].shape[0], width), jnp.bfloat16),
        in_specs=[VMEM] * len(parts),
        out_specs=VMEM,
        compiler_params=params(),
        name="own_rows",
    )(*parts)


def local(codes, indices, decoder, targets):
    width = decoder.shape[1]
    rows, k_count = codes.shape
    n = lax.axis_size("lat")
    own = rows // n
    fz, fy, fc = factors(n)
    group = rows // fz
    chunks = CHUNKS
    wide = width // (fc * fy)
    sub = wide // chunks
    z, y_at, core_at = place(n, lax.axis_index("lat"))

    def swap(x, dz=0, dy=0, dc=0):
        return lax.ppermute(x, "lat", pairs(n, dz, dy, dc))

    def join(xs, axis):
        return xs[0] if len(xs) == 1 else jnp.concatenate(xs, axis=axis)

    def in_order(xs, after=None):
        for i, x in enumerate(xs):
            if after is not None:
                xs[i] = hold(x, after)
            after = xs[i]
        return xs

    *parts, dense, columns = first_decode(n, chunks, sub, indices, codes, decoder, targets)
    came = [swap(part, dc=1) for part in parts]
    summed, leaving, after = [], [], None
    for p in range(chunks):
        part = decode(n, p, chunks, sub, dense, decoder if p else columns, targets, after)
        total = part + came[p]
        blocks = [total[:, o * sub : (o + 1) * sub] for o in range(fy)]
        got = None
        for b in reversed(bits(fy)):
            if got is not None:
                blocks = [blocks[o] + got[:, o * sub : (o + 1) * sub] for o in range(2 * b)]
            after = join(blocks[b:], 1)
            got = swap(after, dy=b)
        leaving.append(after)
        summed.append((blocks[0], got))

    places = tuple((dc, dy) for dc in range(fc) for dy in range(fy))
    *kept, ids, token = fetch(n, wide, places, decoder, indices, leaving[-1])

    sums, moved = [], []
    for p, (x, y) in enumerate(summed):
        if p == 0:
            y = hold(y, token)
            columns = [(kept[dy], swap(hold(kept[fy + dy], y), dc=1)) for dy in range(fy)]
        x = x + y
        sums.append(lax.dynamic_slice_in_dim(x, z * group, group, 0))
        moved.append(
            [
                swap(lax.dynamic_slice_in_dim(x, (z ^ j) * group, group, 0), dz=j)
                for j in z_order(fz)
            ]
        )
    errs, loss, after = [], 0.0, sums[-1]
    for p in range(chunks):
        diff = sum(in_order(moved[p], after), sums[p])
        loss = loss + jnp.sum(diff * diff, axis=1, keepdims=True)
        errs.append(diff.astype(jnp.bfloat16))
        after = errs[p]

    err = join(errs, 1)
    near = [(0, join([err] + [swap(err, dz=j) for j in z_order(fz)], 0))]
    for b in bits(fy):
        last = [(b | dy, swap(e, dy=b)) for dy, e in near]
        near += last
    pieces, near = near, near[: -len(last)]
    totals, token = grad(n, rows, near, columns, None)

    def rows_of(core):
        first = (y_at * fc + core) * own
        return [lax.dynamic_slice_in_dim(e, first, own, 0) for _, e in pieces]

    other = swap(hold(join(rows_of(1 - core_at), 0), token), dc=1)
    last[-1] = (last[-1][0], hold(last[-1][1], other))
    back = grad(n, rows, last, columns, totals, (ids, loss))
    own_places = tuple((dc, dy) for dc in range(fc) for dy, _ in pieces)
    error = own_rows(
        n, own_places, width, rows_of(core_at) + [other[i * own : (i + 1) * own] for i in range(fy)]
    )

    back = jnp.sum(lax.all_to_all(back, "lat", 0, 0, tiled=True), axis=0)
    return error, back[:, k_count] / width, back[:, :k_count]


def solution(mesh):
    in_specs = (P("groups", None), P("groups", None), P("lat", None), P(("groups", "lat"), None))
    out_specs = (P(("groups", "lat"), None), P(("groups", "lat")), P(("groups", "lat"), None))
    return jax.shard_map(local, mesh=mesh, in_specs=in_specs, out_specs=out_specs, check_vma=False)
```

time: 62.2 us -> 79.2 us (1.27)
  Pallas kernels: 15.6 us -> 27.5 us
  waiting for transfers between devices: 18.3 us -> 22 us
  local copies, waits for them, and re-layouts: 0.36 us -> 3.16 us
  starting transfers between devices: 25.6 us -> 24 us
    pallas_call x20 -> x17, Pallas kernels: 12.1 us -> 21.9 us  [the longest x2 6.68 us: grad(): pl.pallas_call(functools.partial(grad_kernel, n, len(pieces), prev is not...]
    ppermute x19 -> x17, waiting for transfers between devices: 12.5 us -> 16.1 us  [swap(): return lax.ppermute(x, 'lat', pairs(n, dz, dy, dc))]
    unnamed x8 -> x6, local copies, waits for them, and re-layouts: 0.18 us -> 2.92 us
    pallas_call x1, Pallas kernels: 3.53 us -> 5.66 us  [fetch(): pl.pallas_call(functools.partial(fetch_kernel, n, places), out_shape=[blo...]
    ppermute x19 -> x17, starting transfers between devices: 21.2 us -> 19.1 us  [swap(): return lax.ppermute(x, 'lat', pairs(n, dz, dy, dc))]
  transfers between devices with their start and end apart: 20 -> 18, of which waited for: 11 -> 10; matrix products, arithmetic and copies ran while one was open for 1% -> 1% of each run, Pallas kernels for 17% -> 23%
where the time goes in v11:
time: 79.2 us; the launch traced here: 78.8 us
  Pallas kernels  27.5 us (35%)
  starting transfers between devices  24 us (30%)
  waiting for transfers between devices  22 us (28%)
  local copies, waits for them, and re-layouts  3.16 us (4%)
  other arithmetic  1.21 us (2%)
  between operations  0.9 us (1%)
    ppermute x17, starting transfers between devices, swap(): return lax.ppermute(x, 'lat', pairs(n, dz, dy, dc))  19.1 us
    ppermute x17, waiting for transfers between devices, swap(): return lax.ppermute(x, 'lat', pairs(n, dz, dy, dc))  16.1 us
    pallas_call x2, Pallas kernels, grad(): pl.pallas_call(functools.partial(grad_kernel, n, len(pieces), prev is not...  6.68 us
    pallas_call x11, Pallas kernels, hold(): pl.pallas_call(kernel, out_shape=jax.ShapeDtypeStruct(x.shape, x.dtype),...  6.28 us
    all_to_all x1, waiting for transfers between devices, local(): back = jnp.sum(lax.all_to_all(back, 'lat', 0, 0, tiled=True), axis=0)  5.95 us
    pallas_call x1, Pallas kernels, fetch(): pl.pallas_call(functools.partial(fetch_kernel, n, places), out_shape=[blo...  5.66 us
    pallas_call x1, Pallas kernels, first_decode(): pl.pallas_call(functools.partial(first_kernel, n, rows // n, chunks), out...  5.43 us
    all_to_all x1, starting transfers between devices, local(): back = jnp.sum(lax.all_to_all(back, 'lat', 0, 0, tiled=True), axis=0)  4.97 us
  transfers between devices with their start and end apart: 18, of which 10 were waited for; matrix products, arithmetic and copies ran while one was open for 1% of the time, Pallas kernels for 23%

profile of v11, /device:TPU:0, one launch (start us, length us, event | category | flops | bytes accessed | tf_op | source)
XLA Modules:
  0.0 78.8 jit_solution(6144018074563808867)
XLA Ops:
  0.6 5.4 %first_decode.1 = (f32[64,2048]{1,0:T(8,128)S(1)}, f32[64,2048]{1,0:T(8,128)S(1)}, bf16[64,512]{1,0:T(8,128)(2,1)S(1)}, bf16[2,512,1024]{2,1,0:T(8,128)(2,1)S(1)}) custom-call(s32[64,64]{1,0:T(8,128)} %ids_hbm.1, bf16[64,64]{1,0:T(8,128)(2,1)} %refs_1_.1, bf16[512,8192]{1,0:T(8,128)(2,1)} %decoder_hbm.1, bf16[4,8192]{1,0:T(4,128)(2,1)} %targets_hbm.3), custom_call_target="tpu_custom_call" | custom-call | flops 268435456 | bytes 8388608 | tf_op jit(solution)/shard_map/first_decode/pallas_call | solution.py:165
  6.1 0.5 collective-permute-start
  6.6 0.1 collective-permute-start.2
  6.7 0.9 %decode.2 = f32[64,2048]{1,0:T(8,128)S(1)} custom-call(bf16[64,512]{1,0:T(8,128)(2,1)S(1)} %get-tuple-element.15.dense_ref, bf16[2,512,1024]{2,1,0:T(8,128)(2,1)S(1)} %get-tuple-element.16.columns_ref, bf16[4,8192]{1,0:T(4,128)(2,1)} %targets_hbm.3), custom_call_target="tpu_custom_call" | custom-call | flops 134217728 | bytes 4194304 | tf_op jit(solution)/shard_map/decode/pallas_call | solution.py:222
  7.5 0.6 collective-permute-done
  8.1 0.1 add.74
  8.2 3.0 %collective-permute-start.1 = (f32[64,1024]{1,0:T(8,128)S(1)}, f32[64,1024]{1,0:T(8,128)S(1)}, u32[]{:S(2)}, u32[]{:S(2)}) collective-permute-start(f32[64,1024]{1,0:T(8,128)S(1)} %slice.33.refs_0_), channel_id=1, source_target_pairs={{0,2},{1,3},{2,0},{3,1},{4,6},{5,7},{6,4},{7,5},{8,10},{9,11},{10,... | collective-permute-start | bytes 786440 | tf_op jit(solution)/shard_map/ppermute | solution.py:371
  11.2 1.9 %decode.3 = f32[64,2048]{1,0:T(8,128)S(1)} custom-call(bf16[64,512]{1,0:T(8,128)(2,1)S(1)} %get-tuple-element.15.dense_ref, bf16[512,8192]{1,0:T(8,128)(2,1)} %decoder_hbm.1, bf16[4,8192]{1,0:T(4,128)(2,1)} %targets_hbm.3, f32[64,1024]{1,0:T(8,128)S(1)} %slice.33.refs_0_), custom_call_target="tpu_custom_call" | custom-call | flops 134217728 | bytes 4194304 | tf_op jit(solution)/shard_map/decode/pallas_call | solution.py:222
  13.1 0.0 collective-permute-done.2
  13.1 0.1 add.75
  13.2 5.7 %fetch.1 = (bf16[512,2048]{1,0:T(8,128)(2,1)S(1)}, bf16[512,2048]{1,0:T(8,128)(2,1)S(1)}, bf16[512,2048]{1,0:T(8,128)(2,1)}, bf16[512,2048]{1,0:T(8,128)(2,1)}, ...) custom-call(bf16[512,8192]{1,0:T(8,128)(2,1)} %decoder_hbm.1, s32[64,64]{1,0:T(8,128)} %ids_hbm.1, f32[64,1024]{1,0:T(8,128)S(1)} %slice.34._), custom_call_target="tpu_custom_call" | custom-call | bytes 8388608 | tf_op jit(solution)/shard_map/fetch/pallas_call | solution.py:250
  18.9 0.0 copy-start
  18.9 1.3 %copy-done = bf16[512,2048]{1,0:T(8,128)(2,1)} copy-done((bf16[512,2048]{1,0:T(8,128)(2,1)}, bf16[512,2048]{1,0:T(8,128)(2,1)S(1)}, u32[]{:S(2)}) %copy-start) | copy-done | bytes 2097176
  20.2 0.1 collective-permute-start.4
  20.3 0.0 collective-permute-done.1.x_ref
  20.3 3.1 %hold.18 = bf16[512,2048]{1,0:T(8,128)(2,1)} custom-call(bf16[512,2048]{1,0:T(8,128)(2,1)} %get-tuple-element.21.x_ref, f32[64,1024]{1,0:T(8,128)S(1)} %hold.11.refs_0_), custom_call_target="tpu_custom_call", output_to_operand_aliasing={{}: (0, {})} | custom-call | tf_op jit(solution)/shard_map/hold/pallas_call | solution.py:77
  23.4 0.0 collective-permute-start.14
  23.5 4.1 %collective-permute-start.3 = (f32[16,1024]{1,0:T(8,128)S(1)}, f32[16,1024]{1,0:T(8,128)S(1)}, u32[]{:S(2)}, u32[]{:S(2)}) collective-permute-start(f32[16,1024]{1,0:T(8,128)S(1)} %get-tuple-element.39), channel_id=1, source_target_pairs={{0,12},{1,13},{2,14},{3,15},{4,8},{5,9},{6,10},{7,11},{8,4},{9,5},... | collective-permute-start | bytes 196616 | tf_op jit(solution)/shard_map/ppermute | solution.py:371
  27.6 0.0 collective-permute-start.5
  27.6 0.6 collective-permute-start.6
  28.3 3.0 %hold.21 = bf16[512,2048]{1,0:T(8,128)(2,1)} custom-call(bf16[512,2048]{1,0:T(8,128)(2,1)} %get-tuple-element.24.x_ref, f32[64,1024]{1,0:T(8,128)S(1)} %hold.11.refs_0_), custom_call_target="tpu_custom_call", output_to_operand_aliasing={{}: (0, {})} | custom-call | tf_op jit(solution)/shard_map/hold/pallas_call | solution.py:77
  31.3 0.0 collective-permute-done.4
  31.3 0.0 collective-permute-start.16
  31.4 0.0 collective-permute-done.3.x_ref
  31.4 3.8 %collective-permute-start.7 = (f32[16,1024]{1,0:T(8,128)S(1)}, f32[16,1024]{1,0:T(8,128)S(1)}, u32[]{:S(2)}, u32[]{:S(2)}) collective-permute-start(f32[16,1024]{1,0:T(8,128)S(1)} %get-tuple-element.38), channel_id=1, source_target_pairs={{0,12},{1,13},{2,14},{3,15},{4,8},{5,9},{6,10},{7,11},{8,4},{9,5},... | collective-permute-start | bytes 196616 | tf_op jit(solution)/shard_map/ppermute | solution.py:371
  35.2 0.0 collective-permute-done.5.x_ref
  35.2 0.1 collective-permute-start.8
  35.3 0.0 collective-permute-done.6.x_ref
  35.3 0.7 collective-permute-start.9
  36.0 0.1 multiply_reduce_fusion.1
  36.2 2.1 %collective-permute-done.7.x_ref = f32[16,1024]{1,0:T(8,128)S(1)} collective-permute-done((f32[16,1024]{1,0:T(8,128)S(1)}, f32[16,1024]{1,0:T(8,128)S(1)}, u32[]{:S(2)}, u32[]{:S(2)}) %collective-permute-start.7) | collective-permute-done | bytes 65568 | tf_op jit(solution)/shard_map/ppermute | solution.py:371
  38.3 2.5 %collective-permute-done.8.x_ref = f32[16,1024]{1,0:T(8,128)S(1)} collective-permute-done((f32[16,1024]{1,0:T(8,128)S(1)}, f32[16,1024]{1,0:T(8,128)S(1)}, u32[]{:S(2)}, u32[]{:S(2)}) %collective-permute-start.8) | collective-permute-done | bytes 65568 | tf_op jit(solution)/shard_map/ppermute | solution.py:371
  40.8 0.4 collective-permute-done.9.x_ref
  41.3 0.1 multiply_reduce_fusion
  41.4 2.1 %collective-permute-start.10 = (bf16[16,2048]{1,0:T(8,128)(2,1)S(1)}, bf16[16,2048]{1,0:T(8,128)(2,1)S(1)}, u32[]{:S(2)}, u32[]{:S(2)}) collective-permute-start(bf16[16,2048]{1,0:T(8,128)(2,1)S(1)} %pad_maximum_fusion.1), channel_id=1, source_target_pairs={{0,12},{1,13},{2,14},{3,15},{4,8},{5,9},{6,10},{7,11},{8,4},{9,5},... | collective-permute-start | bytes 196616 | tf_op jit(solution)/shard_map/ppermute | solution.py:371
  43.5 0.7 collective-permute-start.11
  44.2 1.7 %collective-permute-start.12 = (bf16[16,2048]{1,0:T(8,128)(2,1)S(1)}, bf16[16,2048]{1,0:T(8,128)(2,1)S(1)}, u32[]{:S(2)}, u32[]{:S(2)}) collective-permute-start(bf16[16,2048]{1,0:T(8,128)(2,1)S(1)} %pad_maximum_fusion.1), channel_id=1, source_target_pairs={{0,8},{1,9},{2,10},{3,11},{4,12},{5,13},{6,14},{7,15},{8,0},{9,1},... | collective-permute-start | bytes 196616 | tf_op jit(solution)/shard_map/ppermute | solution.py:371
  45.9 1.8 %collective-permute-done.10 = bf16[16,2048]{1,0:T(8,128)(2,1)S(1)} collective-permute-done((bf16[16,2048]{1,0:T(8,128)(2,1)S(1)}, bf16[16,2048]{1,0:T(8,128)(2,1)S(1)}, u32[]{:S(2)}, u32[]{:S(2)}) %collective-permute-start.10) | collective-permute-done | bytes 65568 | tf_op jit(solution)/shard_map/ppermute | solution.py:371
  47.7 1.3 %collective-permute-done.11 = bf16[16,2048]{1,0:T(8,128)(2,1)S(1)} collective-permute-done((bf16[16,2048]{1,0:T(8,128)(2,1)S(1)}, bf16[16,2048]{1,0:T(8,128)(2,1)S(1)}, u32[]{:S(2)}, u32[]{:S(2)}) %collective-permute-start.11) | collective-permute-done | bytes 65568 | tf_op jit(solution)/shard_map/ppermute | solution.py:371
  49.0 1.4 %collective-permute-done.12 = bf16[16,2048]{1,0:T(8,128)(2,1)S(1)} collective-permute-done((bf16[16,2048]{1,0:T(8,128)(2,1)S(1)}, bf16[16,2048]{1,0:T(8,128)(2,1)S(1)}, u32[]{:S(2)}, u32[]{:S(2)}) %collective-permute-start.12) | collective-permute-done | bytes 65568 | tf_op jit(solution)/shard_map/ppermute | solution.py:371
  50.4 1.6 %collective-permute-start.13 = (bf16[64,2048]{1,0:T(8,128)(2,1)S(1)}, bf16[64,2048]{1,0:T(8,128)(2,1)S(1)}, u32[]{:S(2)}, u32[]{:S(2)}) collective-permute-start(bf16[64,2048]{1,0:T(8,128)(2,1)S(1)} %pad_maximum_fusion.refs_0_), channel_id=1, source_target_pairs={{0,2},{1,3},{2,0},{3,1},{4,6},{5,7},{6,4},{7,5},{8,10},{9,11},{10,... | collective-permute-start | bytes 786440 | tf_op jit(solution)/shard_map/ppermute | solution.py:371
  52.0 4.8 %collective-permute-done.13.x_ref = bf16[64,2048]{1,0:T(8,128)(2,1)S(1)} collective-permute-done((bf16[64,2048]{1,0:T(8,128)(2,1)S(1)}, bf16[64,2048]{1,0:T(8,128)(2,1)S(1)}, u32[]{:S(2)}, u32[]{:S(2)}) %collective-permute-start.13) | collective-permute-done | bytes 262176 | tf_op jit(solution)/shard_map/ppermute | solution.py:371
  56.9 0.0 collective-permute-done.14.refs_2_
  56.9 0.0 copy-start.1
  56.9 1.6 %copy-done.1 = bf16[512,2048]{1,0:T(8,128)(2,1)S(1)} copy-done((bf16[512,2048]{1,0:T(8,128)(2,1)S(1)}, bf16[512,2048]{1,0:T(8,128)(2,1)}, u32[]{:S(2)}) %copy-start.1) | copy-done | bytes 2097176
  58.5 3.0 %grad.2 = (f32[2,64,512]{2,1,0:T(8,128)S(1)}, f32[8,128]{1,0:T(8,128)S(1)}) custom-call(bf16[64,2048]{1,0:T(8,128)(2,1)S(1)} %pad_maximum_fusion.refs_0_, bf16[512,2048]{1,0:T(8,128)(2,1)S(1)} %copy-done.1, bf16[512,2048]{1,0:T(8,128)(2,1)} %collective-permute-done.14.refs_2_), custom_call_target="tpu_custom_call" | custom-call | flops 268435456 | bytes 8388608 | tf_op jit(solution)/shard_map/grad/pallas_call | solution.py:326
  61.5 0.1 collective-permute-start.15
  61.6 0.1 copy.18.refs_5_
  61.6 1.1 %collective-permute-done.15.refs_0_ = bf16[8,2048]{1,0:T(8,128)(2,1)S(1)} collective-permute-done((bf16[8,2048]{1,0:T(8,128)(2,1)S(1)}, bf16[8,2048]{1,0:T(8,128)(2,1)S(1)}, u32[]{:S(2)}, u32[]{:S(2)}) %collective-permute-start.15) | collective-permute-done | bytes 32800 | tf_op jit(solution)/shard_map/ppermute | solution.py:371
  62.8 0.0 collective-permute-done.16.refs_2_
  62.8 3.7 %grad.3 = f32[16,4,128]{2,1,0:T(4,128)} custom-call(bf16[64,2048]{1,0:T(8,128)(2,1)S(1)} %hold.20.refs_0_, bf16[512,2048]{1,0:T(8,128)(2,1)S(1)} %get-tuple-element.23.refs_1_, bf16[512,2048]{1,0:T(8,128)(2,1)} %collective-permute-done.16.refs_2_, f32[2,64,512]{2,1,0:T(8,128)S(1)} %get-tuple-element.25.refs_3_, s32[64,64]{1,0:T(8,128)S(1)} %get-tuple-element.26.refs_4_, ...), custom_call_target="tpu_custom_call" | custom-call | flops 268435456 | bytes 8388608 | tf_op jit(solution)/shard_map/grad/pallas_call | solution.py:326
  66.5 5.0 %all-to-all-start = ((f32[16,4,128]{2,1,0:T(4,128)}), f32[16,4,128]{2,1,0:T(4,128)S(1)}, u32[]{:S(2)}, u32[]{:S(2)}) async-start(f32[16,4,128]{2,1,0:T(4,128)} %grad.3), calls=%async_computation | async-start | bytes 65536 | tf_op jit(solution)/shard_map/all_to_all | solution.py:442
  71.5 0.7 own_rows.1
  72.1 6.0 %all-to-all-done = f32[16,4,128]{2,1,0:T(4,128)S(1)} async-done(((f32[16,4,128]{2,1,0:T(4,128)}), f32[16,4,128]{2,1,0:T(4,128)S(1)}, u32[]{:S(2)}, u32[]{:S(2)}) %all-to-all-start) | async-done | bytes 32800 | tf_op jit(solution)/shard_map/all_to_all | solution.py:442
  78.1 0.0 copy-start.2
  78.1 0.7 multiply_reduce_fusion.2
  78.8 0.0 copy-done.2
  (23 shorter events, 0.4 us)
Async XLA Ops:
  6.1 2.1 %collective-permute-start = (f32[64,2048]{1,0:T(8,128)S(1)}, f32[64,2048]{1,0:T(8,128)S(1)}, u32[]{:S(2)}, u32[]{:S(2)}) collective-permute-start(f32[64,2048]{1,0:T(8,128)S(1)} %get-tuple-element.17), channel_id=1, source_target_pairs={{0,1},{1,0},{2,3},{3,2},{4,5},{5,4},{6,7},{7,6},{8,9},{9,8},{10,11... | collective-permute-start | bytes 1572872 | tf_op jit(solution)/shard_map/ppermute | solution.py:371
  6.6 6.5 %collective-permute-start.2 = (f32[64,2048]{1,0:T(8,128)S(1)}, f32[64,2048]{1,0:T(8,128)S(1)}, u32[]{:S(2)}, u32[]{:S(2)}) collective-permute-start(f32[64,2048]{1,0:T(8,128)S(1)} %get-tuple-element.18), channel_id=1, source_target_pairs={{0,1},{1,0},{2,3},{3,2},{4,5},{5,4},{6,7},{7,6},{8,9},{9,8},{10,11... | collective-permute-start | bytes 1572872 | tf_op jit(solution)/shard_map/ppermute | solution.py:371
  8.2 12.1 %collective-permute-start.1 = (f32[64,1024]{1,0:T(8,128)S(1)}, f32[64,1024]{1,0:T(8,128)S(1)}, u32[]{:S(2)}, u32[]{:S(2)}) collective-permute-start(f32[64,1024]{1,0:T(8,128)S(1)} %slice.33.refs_0_), channel_id=1, source_target_pairs={{0,2},{1,3},{2,0},{3,1},{4,6},{5,7},{6,4},{7,5},{8,10},{9,11},{10,... | collective-permute-start | bytes 786440 | tf_op jit(solution)/shard_map/ppermute | solution.py:371
  18.9 1.3 %copy-start = (bf16[512,2048]{1,0:T(8,128)(2,1)}, bf16[512,2048]{1,0:T(8,128)(2,1)S(1)}, u32[]{:S(2)}) copy-start(bf16[512,2048]{1,0:T(8,128)(2,1)S(1)} %get-tuple-element.20.refs_1_) | copy-start | bytes 6291460
  20.2 11.1 %collective-permute-start.4 = (f32[64,1024]{1,0:T(8,128)S(1)}, f32[64,1024]{1,0:T(8,128)S(1)}, u32[]{:S(2)}, u32[]{:S(2)}) collective-permute-start(f32[64,1024]{1,0:T(8,128)S(1)} %slice.34._), channel_id=1, source_target_pairs={{0,2},{1,3},{2,0},{3,1},{4,6},{5,7},{6,4},{7,5},{8,10},{9,11},{10,... | collective-permute-start | bytes 786440 | tf_op jit(solution)/shard_map/ppermute | solution.py:371
  23.4 33.4 %collective-permute-start.14 = (bf16[512,2048]{1,0:T(8,128)(2,1)}, bf16[512,2048]{1,0:T(8,128)(2,1)}, u32[]{:S(2)}, u32[]{:S(2)}) collective-permute-start(bf16[512,2048]{1,0:T(8,128)(2,1)} %hold.18), channel_id=1, source_target_pairs={{0,1},{1,0},{2,3},{3,2},{4,5},{5,4},{6,7},{7,6},{8,9},{9,8},{10,11... | collective-permute-start | bytes 6291464 | tf_op jit(solution)/shard_map/ppermute | solution.py:371
  23.5 7.9 %collective-permute-start.3 = (f32[16,1024]{1,0:T(8,128)S(1)}, f32[16,1024]{1,0:T(8,128)S(1)}, u32[]{:S(2)}, u32[]{:S(2)}) collective-permute-start(f32[16,1024]{1,0:T(8,128)S(1)} %get-tuple-element.39), channel_id=1, source_target_pairs={{0,12},{1,13},{2,14},{3,15},{4,8},{5,9},{6,10},{7,11},{8,4},{9,5},... | collective-permute-start | bytes 196616 | tf_op jit(solution)/shard_map/ppermute | solution.py:371
  27.6 7.6 %collective-permute-start.5 = (f32[16,1024]{1,0:T(8,128)S(1)}, f32[16,1024]{1,0:T(8,128)S(1)}, u32[]{:S(2)}, u32[]{:S(2)}) collective-permute-start(f32[16,1024]{1,0:T(8,128)S(1)} %get-tuple-element.41), channel_id=1, source_target_pairs={{0,4},{1,5},{2,6},{3,7},{4,0},{5,1},{6,2},{7,3},{8,12},{9,13},{10,... | collective-permute-start | bytes 196616 | tf_op jit(solution)/shard_map/ppermute | solution.py:371
  27.6 7.7 %collective-permute-start.6 = (f32[16,1024]{1,0:T(8,128)S(1)}, f32[16,1024]{1,0:T(8,128)S(1)}, u32[]{:S(2)}, u32[]{:S(2)}) collective-permute-start(f32[16,1024]{1,0:T(8,128)S(1)} %get-tuple-element.40), channel_id=1, source_target_pairs={{0,8},{1,9},{2,10},{3,11},{4,12},{5,13},{6,14},{7,15},{8,0},{9,1},... | collective-permute-start | bytes 196616 | tf_op jit(solution)/shard_map/ppermute | solution.py:371
  31.3 31.5 %collective-permute-start.16 = (bf16[512,2048]{1,0:T(8,128)(2,1)}, bf16[512,2048]{1,0:T(8,128)(2,1)}, u32[]{:S(2)}, u32[]{:S(2)}) collective-permute-start(bf16[512,2048]{1,0:T(8,128)(2,1)} %hold.21), channel_id=1, source_target_pairs={{0,1},{1,0},{2,3},{3,2},{4,5},{5,4},{6,7},{7,6},{8,9},{9,8},{10,11... | collective-permute-start | bytes 6291464 | tf_op jit(solution)/shard_map/ppermute | solution.py:371
  31.4 6.9 %collective-permute-start.7 = (f32[16,1024]{1,0:T(8,128)S(1)}, f32[16,1024]{1,0:T(8,128)S(1)}, u32[]{:S(2)}, u32[]{:S(2)}) collective-permute-start(f32[16,1024]{1,0:T(8,128)S(1)} %get-tuple-element.38), channel_id=1, source_target_pairs={{0,12},{1,13},{2,14},{3,15},{4,8},{5,9},{6,10},{7,11},{8,4},{9,5},... | collective-permute-start | bytes 196616 | tf_op jit(solution)/shard_map/ppermute | solution.py:371
  35.2 5.6 %collective-permute-start.8 = (f32[16,1024]{1,0:T(8,128)S(1)}, f32[16,1024]{1,0:T(8,128)S(1)}, u32[]{:S(2)}, u32[]{:S(2)}) collective-permute-start(f32[16,1024]{1,0:T(8,128)S(1)} %get-tuple-element.37), channel_id=1, source_target_pairs={{0,4},{1,5},{2,6},{3,7},{4,0},{5,1},{6,2},{7,3},{8,12},{9,13},{10,... | collective-permute-start | bytes 196616 | tf_op jit(solution)/shard_map/ppermute | solution.py:371
  35.3 5.9 %collective-permute-start.9 = (f32[16,1024]{1,0:T(8,128)S(1)}, f32[16,1024]{1,0:T(8,128)S(1)}, u32[]{:S(2)}, u32[]{:S(2)}) collective-permute-start(f32[16,1024]{1,0:T(8,128)S(1)} %get-tuple-element.36), channel_id=1, source_target_pairs={{0,8},{1,9},{2,10},{3,11},{4,12},{5,13},{6,14},{7,15},{8,0},{9,1},... | collective-permute-start | bytes 196616 | tf_op jit(solution)/shard_map/ppermute | solution.py:371
  41.4 6.3 %collective-permute-start.10 = (bf16[16,2048]{1,0:T(8,128)(2,1)S(1)}, bf16[16,2048]{1,0:T(8,128)(2,1)S(1)}, u32[]{:S(2)}, u32[]{:S(2)}) collective-permute-start(bf16[16,2048]{1,0:T(8,128)(2,1)S(1)} %pad_maximum_fusion.1), channel_id=1, source_target_pairs={{0,12},{1,13},{2,14},{3,15},{4,8},{5,9},{6,10},{7,11},{8,4},{9,5},... | collective-permute-start | bytes 196616 | tf_op jit(solution)/shard_map/ppermute | solution.py:371
  43.5 5.4 %collective-permute-start.11 = (bf16[16,2048]{1,0:T(8,128)(2,1)S(1)}, bf16[16,2048]{1,0:T(8,128)(2,1)S(1)}, u32[]{:S(2)}, u32[]{:S(2)}) collective-permute-start(bf16[16,2048]{1,0:T(8,128)(2,1)S(1)} %pad_maximum_fusion.1), channel_id=1, source_target_pairs={{0,4},{1,5},{2,6},{3,7},{4,0},{5,1},{6,2},{7,3},{8,12},{9,13},{10,... | collective-permute-start | bytes 196616 | tf_op jit(solution)/shard_map/ppermute | solution.py:371
  44.2 6.2 %collective-permute-start.12 = (bf16[16,2048]{1,0:T(8,128)(2,1)S(1)}, bf16[16,2048]{1,0:T(8,128)(2,1)S(1)}, u32[]{:S(2)}, u32[]{:S(2)}) collective-permute-start(bf16[16,2048]{1,0:T(8,128)(2,1)S(1)} %pad_maximum_fusion.1), channel_id=1, source_target_pairs={{0,8},{1,9},{2,10},{3,11},{4,12},{5,13},{6,14},{7,15},{8,0},{9,1},... | collective-permute-start | bytes 196616 | tf_op jit(solution)/shard_map/ppermute | solution.py:371
  50.4 6.4 %collective-permute-start.13 = (bf16[64,2048]{1,0:T(8,128)(2,1)S(1)}, bf16[64,2048]{1,0:T(8,128)(2,1)S(1)}, u32[]{:S(2)}, u32[]{:S(2)}) collective-permute-start(bf16[64,2048]{1,0:T(8,128)(2,1)S(1)} %pad_maximum_fusion.refs_0_), channel_id=1, source_target_pairs={{0,2},{1,3},{2,0},{3,1},{4,6},{5,7},{6,4},{7,5},{8,10},{9,11},{10,... | collective-permute-start | bytes 786440 | tf_op jit(solution)/shard_map/ppermute | solution.py:371
  56.9 1.6 %copy-start.1 = (bf16[512,2048]{1,0:T(8,128)(2,1)S(1)}, bf16[512,2048]{1,0:T(8,128)(2,1)}, u32[]{:S(2)}) copy-start(bf16[512,2048]{1,0:T(8,128)(2,1)} %copy-done) | copy-start | bytes 6291460
  61.5 1.3 %collective-permute-start.15 = (bf16[8,2048]{1,0:T(8,128)(2,1)S(1)}, bf16[8,2048]{1,0:T(8,128)(2,1)S(1)}, u32[]{:S(2)}, u32[]{:S(2)}) collective-permute-start(bf16[8,2048]{1,0:T(8,128)(2,1)S(1)} %hold.19), channel_id=1, source_target_pairs={{0,1},{1,0},{2,3},{3,2},{4,5},{5,4},{6,7},{7,6},{8,9},{9,8},{10,11... | collective-permute-start | bytes 98312 | tf_op jit(solution)/shard_map/ppermute | solution.py:371
  66.5 11.6 %all-to-all-start = ((f32[16,4,128]{2,1,0:T(4,128)}), f32[16,4,128]{2,1,0:T(4,128)S(1)}, u32[]{:S(2)}, u32[]{:S(2)}) async-start(f32[16,4,128]{2,1,0:T(4,128)} %grad.3), calls=%async_computation | async-start | bytes 65536 | tf_op jit(solution)/shard_map/all_to_all | solution.py:442
  78.1 0.7 copy-start.2

commit v12 on v10

--- a/solution.py
+++ b/solution.py
@@ -71,8 +71,11 @@
 
 
 def hold(x, *after):
+    def kernel(x_ref, *refs):
+        refs[-1][...] = x_ref[...]
+
     return pl.pallas_call(
-        lambda *refs: None,
+        kernel,
         out_shape=jax.ShapeDtypeStruct(x.shape, x.dtype),
         in_specs=[VMEM] * (1 + len(after)),
         out_specs=VMEM,
@@ -128,16 +131,19 @@
         copy.wait()
     if first:
         k_count = ids_ref.shape[1]
-        lanes = lax.broadcasted_iota(jnp.int32, (ROW_STEP, lat_dev), 1) + me * lat_dev
+        assert lat_dev <= 512
+        half = lat_dev // 2
+        lanes = (lax.broadcasted_iota(jnp.int32, (ROW_STEP, lat_dev), 1) - half).astype(jnp.bfloat16)
 
         def body(g, carry):
             at = pl.ds(pl.multiple_of(g * ROW_STEP, ROW_STEP), ROW_STEP)
-            ids = ids_ref[at, :]
-            codes = codes_ref[at, :].astype(jnp.float32)
-            acc = jnp.zeros((ROW_STEP, lat_dev), jnp.float32)
+            ids = ids_ref[at, :] - (me * lat_dev + half)
+            ids = jnp.where((ids >= -half) & (ids < half), ids, half + 44).astype(jnp.bfloat16)
+            codes = codes_ref[at, :]
+            acc = jnp.zeros((ROW_STEP, lat_dev), jnp.bfloat16)
             for k in range(k_count):
                 acc = jnp.where(ids[:, k : k + 1] == lanes, codes[:, k : k + 1], acc)
-            dense_ref[at, :] = acc.astype(jnp.bfloat16)
+            dense_ref[at, :] = acc
             return carry
 
         lax.fori_loop(0, rows // ROW_STEP, body, 0)
@@ -190,9 +196,10 @@
     )(*args)
 
 
-def fetch_kernel(n, places, decoder_hbm, _, *refs):
-    outs, token_ref, sem = refs[:-2], refs[-2], refs[-1]
-    copies = []
+def fetch_kernel(n, places, decoder_hbm, ids_hbm, _, *refs):
+    outs = refs[: len(places)]
+    ids_ref, token_ref, sem, ids_sem = refs[len(places) :]
+    copies = [pltpu.make_async_copy(ids_hbm, ids_ref, ids_sem)]
     for i, (dc, dy) in enumerate(places):
         col = column(n, 0, 1, outs[i].shape[1], dy, dc)
         copies += loads_of(decoder_hbm, col, outs[i], sem.at[i])
@@ -203,18 +210,19 @@
         copy.wait()
 
 
-def fetch(n, width, places, decoder, after):
+def fetch(n, width, places, decoder, ids, after):
     block = pltpu.VMEM((decoder.shape[0], width), decoder.dtype)
     return pl.pallas_call(
         functools.partial(fetch_kernel, n, places),
-        out_shape=[block] * len(places) + [pltpu.VMEM((SUBLANES, LANES), jnp.float32)],
-        in_specs=[HBM, VMEM],
-        out_specs=[VMEM] * (1 + len(places)),
-        scratch_shapes=[pltpu.SemaphoreType.DMA((len(places), LOADS))],
+        out_shape=[block] * len(places)
+        + [pltpu.VMEM(ids.shape, ids.dtype), pltpu.VMEM((SUBLANES, LANES), jnp.float32)],
+        in_specs=[HBM, HBM, VMEM],
+        out_specs=[VMEM] * (2 + len(places)),
+        scratch_shapes=[pltpu.SemaphoreType.DMA((len(places), LOADS)), pltpu.SemaphoreType.DMA],
         compiler_params=params(),
         cost_estimate=cost(0, decoder.shape[0] * len(places) * width * 2),
         name="fetch",
-    )(in_hbm(decoder), in_vmem(after))
+    )(in_hbm(decoder), in_hbm(ids), in_vmem(after))
 
 
 def grad_kernel(n, counts, with_prev, final, *refs):
@@ -352,7 +360,7 @@
         summed.append((blocks[0], got))
 
     places = tuple((dc, dy) for dy in range(fy) for dc in range(fc))
-    *columns, token = fetch(n, chunks * sub, places, decoder, leaving[-1])
+    *columns, ids, token = fetch(n, chunks * sub, places, decoder, indices, leaving[-1])
     columns = dict(zip(places, columns))
     sums, moved = [], []
     for p, (x, y) in enumerate(summed):
@@ -372,16 +380,9 @@
         after = errs[p]
 
     err = join(errs, 1)
-    come = [swap(err, dz=j) for j in z_order(fz)]
-    own_part = swap(err, dy=1)
-    come = in_order(come[:-1] + [own_part] + come[-1:])
-    own_part = come.pop(-2)
-    near = [((0, 0), [err, join(come, 0)])]
+    near = [((0, 0), [join([err] + [swap(err, dz=j) for j in z_order(fz)], 0)])]
     for b in bits(fy):
-        last = [
-            ((0, b | at[1]), in_order([own_part if e is err else swap(e, dy=b) for e in parts]))
-            for at, parts in near
-        ]
+        last = [((0, b | at[1]), [swap(e, dy=b) for e in parts]) for at, parts in near]
         near += last
     near = near[: -len(last)]
     half = rows // 2
@@ -396,7 +397,7 @@
     last[-1][1][-1] = hold(last[-1][1][-1], totals)
     far_last = [((1, at[1]), [swap(join(parts, 0), dc=1)]) for at, parts in last]
     totals = grad(n, rows, last, columns, totals)
-    back = grad(n, rows, far_last, columns, totals, (indices, loss))
+    back = grad(n, rows, far_last, columns, totals, (in_vmem(ids), loss))
     pieces = near + far + last + far_last
     error = own_rows(n, [at for at, _ in pieces], own, width, [e[0][:group] for _, e in pieces])
 

time: 62.2 us -> 63.3 us (1.018)
    all_to_all x1, starting transfers between devices: 4.4 us -> 5.25 us  [local(): back = jnp.sum(lax.all_to_all(back, 'lat', 0, 0, tiled=True), axis=0)]
    ppermute x19 -> x18, waiting for transfers between devices: 12.5 us -> 13 us  [swap(): return lax.ppermute(x, 'lat', pairs(n, dz, dy, dc))]
    ppermute x19 -> x18, starting transfers between devices: 21.2 us -> 20.7 us  [swap(): return lax.ppermute(x, 'lat', pairs(n, dz, dy, dc))]
  transfers between devices with their start and end apart: 20 -> 19, of which waited for: 11 -> 12; matrix products, arithmetic and copies ran while one was open for 1% -> 1% of each run, Pallas kernels for 17% -> 17%
where the time goes in v12:
time: 63.3 us; the launch traced here: 63 us
  starting transfers between devices  26 us (41%)
  waiting for transfers between devices  18.8 us (30%)
  Pallas kernels  15.8 us (25%)
  other arithmetic  1.2 us (2%)
  between operations  0.9 us (1%)
    ppermute x18, starting transfers between devices, swap(): return lax.ppermute(x, 'lat', pairs(n, dz, dy, dc))  20.7 us
    ppermute x18, waiting for transfers between devices, swap(): return lax.ppermute(x, 'lat', pairs(n, dz, dy, dc))  13 us
    pallas_call x3, Pallas kernels, decode(): pl.pallas_call(functools.partial(decode_kernel, n, rows // n, chunks, par...  7.51 us
    all_to_all x1, waiting for transfers between devices, local(): back = jnp.sum(lax.all_to_all(back, 'lat', 0, 0, tiled=True), axis=0)  5.75 us
    all_to_all x1, starting transfers between devices, local(): back = jnp.sum(lax.all_to_all(back, 'lat', 0, 0, tiled=True), axis=0)  5.25 us
    pallas_call x4, Pallas kernels, grad(): pl.pallas_call(functools.partial(grad_kernel, n, counts, prev is not None...  3.74 us
    pallas_call x1, Pallas kernels, fetch(): pl.pallas_call(functools.partial(fetch_kernel, n, places), out_shape=[blo...  3.54 us
  transfers between devices with their start and end apart: 19, of which 12 were waited for; matrix products, arithmetic and copies ran while one was open for 1% of the time, Pallas kernels for 17%

profile of v12, /device:TPU:0, one launch (start us, length us, event | category | flops | bytes accessed | tf_op | source)
XLA Modules:
  0.0 63.0 jit_solution(10909932624063472482)
XLA Ops:
  0.6 3.7 %decode.3 = (f32[64,2048]{1,0:T(8,128)S(1)}, f32[64,2048]{1,0:T(8,128)S(1)}, bf16[64,512]{1,0:T(8,128)(2,1)S(1)}) custom-call(s32[64,64]{1,0:T(8,128)} %ids_hbm.1, bf16[64,64]{1,0:T(8,128)(2,1)} %refs_1_.3, bf16[512,8192]{1,0:T(8,128)(2,1)} %decoder_hbm.1, bf16[4,8192]{1,0:T(4,128)(2,1)} %refs_2_.5), custom_call_target="tpu_custom_call" | custom-call | flops 268435456 | bytes 8388608 | tf_op jit(solution)/shard_map/decode/pallas_call | solution.py:187
  4.3 0.5 collective-permute-start
  4.8 0.1 collective-permute-start.2
  4.9 1.9 %decode.4 = f32[64,2048]{1,0:T(8,128)S(1)} custom-call(bf16[64,512]{1,0:T(8,128)(2,1)S(1)} %get-tuple-element.12.refs_0_, bf16[512,8192]{1,0:T(8,128)(2,1)} %decoder_hbm.1, bf16[4,8192]{1,0:T(4,128)(2,1)} %refs_2_.5), custom_call_target="tpu_custom_call" | custom-call | flops 134217728 | bytes 4194304 | tf_op jit(solution)/shard_map/decode/pallas_call | solution.py:187
  6.8 0.0 collective-permute-done
  6.8 0.1 add.52
  6.9 3.0 %collective-permute-start.1 = (f32[64,1024]{1,0:T(8,128)S(1)}, f32[64,1024]{1,0:T(8,128)S(1)}, u32[]{:S(2)}, u32[]{:S(2)}) collective-permute-start(f32[64,1024]{1,0:T(8,128)S(1)} %slice.35.refs_3_), channel_id=1, source_target_pairs={{0,2},{1,3},{2,0},{3,1},{4,6},{5,7},{6,4},{7,5},{8,10},{9,11},{10,... | collective-permute-start | bytes 786440 | tf_op jit(solution)/shard_map/ppermute | solution.py:333
  9.9 1.9 %decode.5 = f32[64,2048]{1,0:T(8,128)S(1)} custom-call(bf16[64,512]{1,0:T(8,128)(2,1)S(1)} %get-tuple-element.12.refs_0_, bf16[512,8192]{1,0:T(8,128)(2,1)} %decoder_hbm.1, bf16[4,8192]{1,0:T(4,128)(2,1)} %refs_2_.5, f32[64,1024]{1,0:T(8,128)S(1)} %slice.35.refs_3_), custom_call_target="tpu_custom_call" | custom-call | flops 134217728 | bytes 4194304 | tf_op jit(solution)/shard_map/decode/pallas_call | solution.py:187
  11.9 0.0 collective-permute-done.2
  11.9 0.1 add.53
  12.0 0.1 collective-permute-start.4
  12.1 3.5 %fetch.1 = (bf16[512,2048]{1,0:T(8,128)(2,1)S(1)}, bf16[512,2048]{1,0:T(8,128)(2,1)S(1)}, bf16[512,2048]{1,0:T(8,128)(2,1)S(1)}, bf16[512,2048]{1,0:T(8,128)(2,1...) custom-call(bf16[512,8192]{1,0:T(8,128)(2,1)} %decoder_hbm.1, s32[64,64]{1,0:T(8,128)} %ids_hbm.1, f32[64,1024]{1,0:T(8,128)S(1)} %slice.36._), custom_call_target="tpu_custom_call" | custom-call | bytes 8388608 | tf_op jit(solution)/shard_map/fetch/pallas_call | solution.py:215
  15.7 0.0 copy-start
  15.7 1.4 %collective-permute-done.1.x_ref = f32[64,1024]{1,0:T(8,128)S(1)} collective-permute-done((f32[64,1024]{1,0:T(8,128)S(1)}, f32[64,1024]{1,0:T(8,128)S(1)}, u32[]{:S(2)}, u32[]{:S(2)}) %collective-permute-start.1) | collective-permute-done | bytes 262176 | tf_op jit(solution)/shard_map/ppermute | solution.py:333
  17.2 4.2 %collective-permute-start.3 = (f32[16,1024]{1,0:T(8,128)S(1)}, f32[16,1024]{1,0:T(8,128)S(1)}, u32[]{:S(2)}, u32[]{:S(2)}) collective-permute-start(f32[16,1024]{1,0:T(8,128)S(1)} %get-tuple-element.29), channel_id=1, source_target_pairs={{0,12},{1,13},{2,14},{3,15},{4,8},{5,9},{6,10},{7,11},{8,4},{9,5},... | collective-permute-start | bytes 196616 | tf_op jit(solution)/shard_map/ppermute | solution.py:333
  21.4 0.0 collective-permute-start.6
  21.4 0.6 %collective-permute-start.5 = (f32[16,1024]{1,0:T(8,128)S(1)}, f32[16,1024]{1,0:T(8,128)S(1)}, u32[]{:S(2)}, u32[]{:S(2)}) collective-permute-start(f32[16,1024]{1,0:T(8,128)S(1)} %get-tuple-element.31), channel_id=1, source_target_pairs={{0,4},{1,5},{2,6},{3,7},{4,0},{5,1},{6,2},{7,3},{8,12},{9,13},{10,... | collective-permute-start | bytes 196616 | tf_op jit(solution)/shard_map/ppermute | solution.py:333
  22.0 0.1 collective-permute-done.4
  22.2 2.9 %collective-permute-start.9 = (f32[16,1024]{1,0:T(8,128)S(1)}, f32[16,1024]{1,0:T(8,128)S(1)}, u32[]{:S(2)}, u32[]{:S(2)}) collective-permute-start(f32[16,1024]{1,0:T(8,128)S(1)} %get-tuple-element.26), channel_id=1, source_target_pairs={{0,8},{1,9},{2,10},{3,11},{4,12},{5,13},{6,14},{7,15},{8,0},{9,1},... | collective-permute-start | bytes 196616 | tf_op jit(solution)/shard_map/ppermute | solution.py:333
  25.1 1.6 %collective-permute-start.8 = (f32[16,1024]{1,0:T(8,128)S(1)}, f32[16,1024]{1,0:T(8,128)S(1)}, u32[]{:S(2)}, u32[]{:S(2)}) collective-permute-start(f32[16,1024]{1,0:T(8,128)S(1)} %get-tuple-element.27), channel_id=1, source_target_pairs={{0,4},{1,5},{2,6},{3,7},{4,0},{5,1},{6,2},{7,3},{8,12},{9,13},{10,... | collective-permute-start | bytes 196616 | tf_op jit(solution)/shard_map/ppermute | solution.py:333
  26.6 0.0 collective-permute-done.3.x_ref
  26.7 0.9 %collective-permute-start.7 = (f32[16,1024]{1,0:T(8,128)S(1)}, f32[16,1024]{1,0:T(8,128)S(1)}, u32[]{:S(2)}, u32[]{:S(2)}) collective-permute-start(f32[16,1024]{1,0:T(8,128)S(1)} %get-tuple-element.28), channel_id=1, source_target_pairs={{0,12},{1,13},{2,14},{3,15},{4,8},{5,9},{6,10},{7,11},{8,4},{9,5},... | collective-permute-start | bytes 196616 | tf_op jit(solution)/shard_map/ppermute | solution.py:333
  27.6 0.0 collective-permute-done.5.x_ref
  27.6 0.1 collective-permute-done.6.x_ref
  27.8 0.1 multiply_reduce_fusion.1
  27.9 4.8 %collective-permute-done.7.x_ref = f32[16,1024]{1,0:T(8,128)S(1)} collective-permute-done((f32[16,1024]{1,0:T(8,128)S(1)}, f32[16,1024]{1,0:T(8,128)S(1)}, u32[]{:S(2)}, u32[]{:S(2)}) %collective-permute-start.7) | collective-permute-done | bytes 65568 | tf_op jit(solution)/shard_map/ppermute | solution.py:333
  32.7 0.0 collective-permute-done.8.x_ref
  32.8 0.0 copy-done
  32.8 0.0 collective-permute-done.9.x_ref
  32.8 0.1 multiply_reduce_fusion
  32.9 0.9 %collective-permute-start.13 = (bf16[16,2048]{1,0:T(8,128)(2,1)S(1)}, bf16[16,2048]{1,0:T(8,128)(2,1)S(1)}, u32[]{:S(2)}, u32[]{:S(2)}) collective-permute-start(bf16[16,2048]{1,0:T(8,128)(2,1)S(1)} %pad_maximum_fusion.2.refs_0_), channel_id=1, source_target_pairs={{0,8},{1,9},{2,10},{3,11},{4,12},{5,13},{6,14},{7,15},{8,0},{9,1},... | collective-permute-start | bytes 196616 | tf_op jit(solution)/shard_map/ppermute | solution.py:333
  33.8 0.8 %collective-permute-start.12 = (bf16[16,2048]{1,0:T(8,128)(2,1)S(1)}, bf16[16,2048]{1,0:T(8,128)(2,1)S(1)}, u32[]{:S(2)}, u32[]{:S(2)}) collective-permute-start(bf16[16,2048]{1,0:T(8,128)(2,1)S(1)} %pad_maximum_fusion.2.refs_0_), channel_id=1, source_target_pairs={{0,4},{1,5},{2,6},{3,7},{4,0},{5,1},{6,2},{7,3},{8,12},{9,13},{10,... | collective-permute-start | bytes 196616 | tf_op jit(solution)/shard_map/ppermute | solution.py:333
  34.6 2.8 %collective-permute-start.11 = (bf16[16,2048]{1,0:T(8,128)(2,1)S(1)}, bf16[16,2048]{1,0:T(8,128)(2,1)S(1)}, u32[]{:S(2)}, u32[]{:S(2)}) collective-permute-start(bf16[16,2048]{1,0:T(8,128)(2,1)S(1)} %pad_maximum_fusion.2.refs_0_), channel_id=1, source_target_pairs={{0,12},{1,13},{2,14},{3,15},{4,8},{5,9},{6,10},{7,11},{8,4},{9,5},... | collective-permute-start | bytes 196616 | tf_op jit(solution)/shard_map/ppermute | solution.py:333
  37.4 0.8 %collective-permute-done.13 = bf16[16,2048]{1,0:T(8,128)(2,1)S(1)} collective-permute-done((bf16[16,2048]{1,0:T(8,128)(2,1)S(1)}, bf16[16,2048]{1,0:T(8,128)(2,1)S(1)}, u32[]{:S(2)}, u32[]{:S(2)}) %collective-permute-start.13) | collective-permute-done | bytes 65568 | tf_op jit(solution)/shard_map/ppermute | solution.py:333
  38.2 0.6 collective-permute-done.12
  38.8 1.8 %collective-permute-done.11 = bf16[16,2048]{1,0:T(8,128)(2,1)S(1)} collective-permute-done((bf16[16,2048]{1,0:T(8,128)(2,1)S(1)}, bf16[16,2048]{1,0:T(8,128)(2,1)S(1)}, u32[]{:S(2)}, u32[]{:S(2)}) %collective-permute-start.11) | collective-permute-done | bytes 65568 | tf_op jit(solution)/shard_map/ppermute | solution.py:333
  40.7 1.6 %collective-permute-start.14 = (bf16[64,2048]{1,0:T(8,128)(2,1)S(1)}, bf16[64,2048]{1,0:T(8,128)(2,1)S(1)}, u32[]{:S(2)}, u32[]{:S(2)}) collective-permute-start(bf16[64,2048]{1,0:T(8,128)(2,1)S(1)} %pad_maximum_fusion.refs_0_), channel_id=1, source_target_pairs={{0,2},{1,3},{2,0},{3,1},{4,6},{5,7},{6,4},{7,5},{8,10},{9,11},{10,... | collective-permute-start | bytes 786440 | tf_op jit(solution)/shard_map/ppermute | solution.py:333
  42.3 0.1 collective-permute-start.15
  42.4 0.5 collective-permute-start.10
  42.8 0.1 collective-permute-start.16
  42.9 0.8 %grad.4.refs_4_ = f32[64,512]{1,0:T(8,128)S(1)} custom-call(bf16[64,2048]{1,0:T(8,128)(2,1)S(1)} %pad_maximum_fusion.refs_0_, bf16[512,2048]{1,0:T(8,128)(2,1)S(1)} %get-tuple-element.17.refs_1_), custom_call_target="tpu_custom_call" | custom-call | flops 134217728 | bytes 4194304 | tf_op jit(solution)/shard_map/grad/pallas_call | solution.py:285
  43.7 0.1 collective-permute-done.10.refs_0_.refs_1_
  43.8 0.3 collective-permute-done.16.refs_2_
  44.1 0.0 collective-permute-done.15.refs_1_
  44.1 0.8 %grad.5.refs_0_.refs_2_ = f32[64,512]{1,0:T(8,128)S(1)} custom-call(bf16[16,2048]{1,0:T(8,128)(2,1)S(1)} %collective-permute-done.10.refs_0_.refs_1_, bf16[32,2048]{1,0:T(8,128)(2,1)S(1)} %collective-permute-done.15.refs_1_, bf16[16,2048]{1,0:T(8,128)(2,1)S(1)} %collective-permute-done.16.refs_2_, bf16[512,2048]{1,0:T(8,128)(2,1)S(1)} %get-tuple-element.16.refs_3_, ...), custom_call_target="tpu_custom_call" | custom-call | flops 134217728 | bytes 4194304 | tf_op jit(solution)/shard_map/grad/pallas_call | solution.py:285
  44.9 2.2 %collective-permute-done.14.x_ref = bf16[64,2048]{1,0:T(8,128)(2,1)S(1)} collective-permute-done((bf16[64,2048]{1,0:T(8,128)(2,1)S(1)}, bf16[64,2048]{1,0:T(8,128)(2,1)S(1)}, u32[]{:S(2)}, u32[]{:S(2)}) %collective-permute-start.14) | collective-permute-done | bytes 262176 | tf_op jit(solution)/shard_map/ppermute | solution.py:333
  47.1 0.1 collective-permute-start.17
  47.2 0.1 copy.15.refs_4_
  47.3 0.0 copy-start.1
  47.3 0.8 %grad.6.refs_2_ = f32[64,512]{1,0:T(8,128)S(1)} custom-call(bf16[64,2048]{1,0:T(8,128)(2,1)S(1)} %hold.15.refs_0_, bf16[512,2048]{1,0:T(8,128)(2,1)S(1)} %get-tuple-element.19.refs_1_, f32[64,512]{1,0:T(8,128)S(1)} %grad.5.refs_0_.refs_2_), custom_call_target="tpu_custom_call" | custom-call | flops 134217728 | bytes 4194304 | tf_op jit(solution)/shard_map/grad/pallas_call | solution.py:285
  48.1 0.7 %collective-permute-done.17.refs_0_ = bf16[64,2048]{1,0:T(8,128)(2,1)S(1)} collective-permute-done((bf16[64,2048]{1,0:T(8,128)(2,1)S(1)}, bf16[64,2048]{1,0:T(8,128)(2,1)S(1)}, u32[]{:S(2)}, u32[]{:S(2)}) %collective-permute-start.17) | collective-permute-done | bytes 262176 | tf_op jit(solution)/shard_map/ppermute | solution.py:333
  48.7 0.2 copy-done.1
  48.9 1.5 %grad.7 = f32[16,4,128]{2,1,0:T(4,128)} custom-call(bf16[64,2048]{1,0:T(8,128)(2,1)S(1)} %collective-permute-done.17.refs_0_, bf16[512,2048]{1,0:T(8,128)(2,1)S(1)} %copy-done.1, f32[64,512]{1,0:T(8,128)S(1)} %grad.6.refs_2_, s32[64,64]{1,0:T(8,128)S(1)} %get-tuple-element.20.refs_3_, f32[16,1]{1,0:T(8,128)S(1)} %copy.15.refs_4_), custom_call_target="tpu_custom_call" | custom-call | flops 134217728 | bytes 4194304 | tf_op jit(solution)/shard_map/grad/pallas_call | solution.py:285
  50.4 5.2 %all-to-all-start = ((f32[16,4,128]{2,1,0:T(4,128)}), f32[16,4,128]{2,1,0:T(4,128)S(1)}, u32[]{:S(2)}, u32[]{:S(2)}) async-start(f32[16,4,128]{2,1,0:T(4,128)} %grad.7), calls=%async_computation | async-start | bytes 65536 | tf_op jit(solution)/shard_map/all_to_all | solution.py:404
  55.7 0.9 %own_rows.1 = bf16[4,8192]{1,0:T(4,128)(2,1)} custom-call(bf16[16,2048]{1,0:T(8,128)(2,1)S(1)} %pad_maximum_fusion.2.refs_0_, bf16[16,2048]{1,0:T(8,128)(2,1)S(1)} %collective-permute-done.10.refs_0_.refs_1_, bf16[16,2048]{1,0:T(8,128)(2,1)S(1)} %slice.38.refs_2_, bf16[16,2048]{1,0:T(8,128)(2,1)S(1)} %slice.39.refs_3_), custom_call_target="tpu_custom_call" | custom-call | tf_op jit(solution)/shard_map/own_rows/pallas_call | solution.py:311
  56.5 5.8 %all-to-all-done = f32[16,4,128]{2,1,0:T(4,128)S(1)} async-done(((f32[16,4,128]{2,1,0:T(4,128)}), f32[16,4,128]{2,1,0:T(4,128)S(1)}, u32[]{:S(2)}, u32[]{:S(2)}) %all-to-all-start) | async-done | bytes 32800 | tf_op jit(solution)/shard_map/all_to_all | solution.py:404
  62.3 0.0 copy-start.2
  62.3 0.7 %multiply_reduce_fusion.2 = f32[4]{0:T(128)} fusion(f32[4,128]{1,0:T(4,128)S(1)} %reduce_sum.29), kind=kLoop, calls=%fused_computation.9 | loop fusion | flops 4 | bytes 32 | tf_op jit(solution)/shard_map/div | solution.py:405
  63.0 0.0 copy-done.2
  (21 shorter events, 0.4 us)
Async XLA Ops:
  4.3 2.5 %collective-permute-start = (f32[64,2048]{1,0:T(8,128)S(1)}, f32[64,2048]{1,0:T(8,128)S(1)}, u32[]{:S(2)}, u32[]{:S(2)}) collective-permute-start(f32[64,2048]{1,0:T(8,128)S(1)} %get-tuple-element.13), channel_id=1, source_target_pairs={{0,1},{1,0},{2,3},{3,2},{4,5},{5,4},{6,7},{7,6},{8,9},{9,8},{10,11... | collective-permute-start | bytes 1572872 | tf_op jit(solution)/shard_map/ppermute | solution.py:333
  4.8 7.1 %collective-permute-start.2 = (f32[64,2048]{1,0:T(8,128)S(1)}, f32[64,2048]{1,0:T(8,128)S(1)}, u32[]{:S(2)}, u32[]{:S(2)}) collective-permute-start(f32[64,2048]{1,0:T(8,128)S(1)} %get-tuple-element.14), channel_id=1, source_target_pairs={{0,1},{1,0},{2,3},{3,2},{4,5},{5,4},{6,7},{7,6},{8,9},{9,8},{10,11... | collective-permute-start | bytes 1572872 | tf_op jit(solution)/shard_map/ppermute | solution.py:333
  6.9 10.1 %collective-permute-start.1 = (f32[64,1024]{1,0:T(8,128)S(1)}, f32[64,1024]{1,0:T(8,128)S(1)}, u32[]{:S(2)}, u32[]{:S(2)}) collective-permute-start(f32[64,1024]{1,0:T(8,128)S(1)} %slice.35.refs_3_), channel_id=1, source_target_pairs={{0,2},{1,3},{2,0},{3,1},{4,6},{5,7},{6,4},{7,5},{8,10},{9,11},{10,... | collective-permute-start | bytes 786440 | tf_op jit(solution)/shard_map/ppermute | solution.py:333
  12.0 10.1 %collective-permute-start.4 = (f32[64,1024]{1,0:T(8,128)S(1)}, f32[64,1024]{1,0:T(8,128)S(1)}, u32[]{:S(2)}, u32[]{:S(2)}) collective-permute-start(f32[64,1024]{1,0:T(8,128)S(1)} %slice.36._), channel_id=1, source_target_pairs={{0,2},{1,3},{2,0},{3,1},{4,6},{5,7},{6,4},{7,5},{8,10},{9,11},{10,... | collective-permute-start | bytes 786440 | tf_op jit(solution)/shard_map/ppermute | solution.py:333
  15.7 17.1 %copy-start = (bf16[512,2048]{1,0:T(8,128)(2,1)}, bf16[512,2048]{1,0:T(8,128)(2,1)S(1)}, u32[]{:S(2)}) copy-start(bf16[512,2048]{1,0:T(8,128)(2,1)S(1)} %get-tuple-element.18.refs_1_) | copy-start | bytes 6291460
  17.2 9.5 %collective-permute-start.3 = (f32[16,1024]{1,0:T(8,128)S(1)}, f32[16,1024]{1,0:T(8,128)S(1)}, u32[]{:S(2)}, u32[]{:S(2)}) collective-permute-start(f32[16,1024]{1,0:T(8,128)S(1)} %get-tuple-element.29), channel_id=1, source_target_pairs={{0,12},{1,13},{2,14},{3,15},{4,8},{5,9},{6,10},{7,11},{8,4},{9,5},... | collective-permute-start | bytes 196616 | tf_op jit(solution)/shard_map/ppermute | solution.py:333
  21.4 6.4 %collective-permute-start.6 = (f32[16,1024]{1,0:T(8,128)S(1)}, f32[16,1024]{1,0:T(8,128)S(1)}, u32[]{:S(2)}, u32[]{:S(2)}) collective-permute-start(f32[16,1024]{1,0:T(8,128)S(1)} %get-tuple-element.30), channel_id=1, source_target_pairs={{0,8},{1,9},{2,10},{3,11},{4,12},{5,13},{6,14},{7,15},{8,0},{9,1},... | collective-permute-start | bytes 196616 | tf_op jit(solution)/shard_map/ppermute | solution.py:333
  21.4 6.2 %collective-permute-start.5 = (f32[16,1024]{1,0:T(8,128)S(1)}, f32[16,1024]{1,0:T(8,128)S(1)}, u32[]{:S(2)}, u32[]{:S(2)}) collective-permute-start(f32[16,1024]{1,0:T(8,128)S(1)} %get-tuple-element.31), channel_id=1, source_target_pairs={{0,4},{1,5},{2,6},{3,7},{4,0},{5,1},{6,2},{7,3},{8,12},{9,13},{10,... | collective-permute-start | bytes 196616 | tf_op jit(solution)/shard_map/ppermute | solution.py:333
  22.2 10.6 %collective-permute-start.9 = (f32[16,1024]{1,0:T(8,128)S(1)}, f32[16,1024]{1,0:T(8,128)S(1)}, u32[]{:S(2)}, u32[]{:S(2)}) collective-permute-start(f32[16,1024]{1,0:T(8,128)S(1)} %get-tuple-element.26), channel_id=1, source_target_pairs={{0,8},{1,9},{2,10},{3,11},{4,12},{5,13},{6,14},{7,15},{8,0},{9,1},... | collective-permute-start | bytes 196616 | tf_op jit(solution)/shard_map/ppermute | solution.py:333
  25.1 7.7 %collective-permute-start.8 = (f32[16,1024]{1,0:T(8,128)S(1)}, f32[16,1024]{1,0:T(8,128)S(1)}, u32[]{:S(2)}, u32[]{:S(2)}) collective-permute-start(f32[16,1024]{1,0:T(8,128)S(1)} %get-tuple-element.27), channel_id=1, source_target_pairs={{0,4},{1,5},{2,6},{3,7},{4,0},{5,1},{6,2},{7,3},{8,12},{9,13},{10,... | collective-permute-start | bytes 196616 | tf_op jit(solution)/shard_map/ppermute | solution.py:333
  26.7 6.1 %collective-permute-start.7 = (f32[16,1024]{1,0:T(8,128)S(1)}, f32[16,1024]{1,0:T(8,128)S(1)}, u32[]{:S(2)}, u32[]{:S(2)}) collective-permute-start(f32[16,1024]{1,0:T(8,128)S(1)} %get-tuple-element.28), channel_id=1, source_target_pairs={{0,12},{1,13},{2,14},{3,15},{4,8},{5,9},{6,10},{7,11},{8,4},{9,5},... | collective-permute-start | bytes 196616 | tf_op jit(solution)/shard_map/ppermute | solution.py:333
  32.9 5.3 %collective-permute-start.13 = (bf16[16,2048]{1,0:T(8,128)(2,1)S(1)}, bf16[16,2048]{1,0:T(8,128)(2,1)S(1)}, u32[]{:S(2)}, u32[]{:S(2)}) collective-permute-start(bf16[16,2048]{1,0:T(8,128)(2,1)S(1)} %pad_maximum_fusion.2.refs_0_), channel_id=1, source_target_pairs={{0,8},{1,9},{2,10},{3,11},{4,12},{5,13},{6,14},{7,15},{8,0},{9,1},... | collective-permute-start | bytes 196616 | tf_op jit(solution)/shard_map/ppermute | solution.py:333
  33.8 5.0 %collective-permute-start.12 = (bf16[16,2048]{1,0:T(8,128)(2,1)S(1)}, bf16[16,2048]{1,0:T(8,128)(2,1)S(1)}, u32[]{:S(2)}, u32[]{:S(2)}) collective-permute-start(bf16[16,2048]{1,0:T(8,128)(2,1)S(1)} %pad_maximum_fusion.2.refs_0_), channel_id=1, source_target_pairs={{0,4},{1,5},{2,6},{3,7},{4,0},{5,1},{6,2},{7,3},{8,12},{9,13},{10,... | collective-permute-start | bytes 196616 | tf_op jit(solution)/shard_map/ppermute | solution.py:333
  34.6 6.1 %collective-permute-start.11 = (bf16[16,2048]{1,0:T(8,128)(2,1)S(1)}, bf16[16,2048]{1,0:T(8,128)(2,1)S(1)}, u32[]{:S(2)}, u32[]{:S(2)}) collective-permute-start(bf16[16,2048]{1,0:T(8,128)(2,1)S(1)} %pad_maximum_fusion.2.refs_0_), channel_id=1, source_target_pairs={{0,12},{1,13},{2,14},{3,15},{4,8},{5,9},{6,10},{7,11},{8,4},{9,5},... | collective-permute-start | bytes 196616 | tf_op jit(solution)/shard_map/ppermute | solution.py:333
  40.7 6.4 %collective-permute-start.14 = (bf16[64,2048]{1,0:T(8,128)(2,1)S(1)}, bf16[64,2048]{1,0:T(8,128)(2,1)S(1)}, u32[]{:S(2)}, u32[]{:S(2)}) collective-permute-start(bf16[64,2048]{1,0:T(8,128)(2,1)S(1)} %pad_maximum_fusion.refs_0_), channel_id=1, source_target_pairs={{0,2},{1,3},{2,0},{3,1},{4,6},{5,7},{6,4},{7,5},{8,10},{9,11},{10,... | collective-permute-start | bytes 786440 | tf_op jit(solution)/shard_map/ppermute | solution.py:333
  42.3 1.8 %collective-permute-start.15 = (bf16[32,2048]{1,0:T(8,128)(2,1)S(1)}, bf16[32,2048]{1,0:T(8,128)(2,1)S(1)}, u32[]{:S(2)}, u32[]{:S(2)}) collective-permute-start(bf16[32,2048]{1,0:T(8,128)(2,1)S(1)} %pad_maximum_fusion.1), channel_id=1, source_target_pairs={{0,1},{1,0},{2,3},{3,2},{4,5},{5,4},{6,7},{7,6},{8,9},{9,8},{10,11... | collective-permute-start | bytes 393224 | tf_op jit(solution)/shard_map/ppermute | solution.py:333
  42.4 1.4 %collective-permute-start.10 = (bf16[16,2048]{1,0:T(8,128)(2,1)S(1)}, bf16[16,2048]{1,0:T(8,128)(2,1)S(1)}, u32[]{:S(2)}, u32[]{:S(2)}) collective-permute-start(bf16[16,2048]{1,0:T(8,128)(2,1)S(1)} %pad_maximum_fusion.2.refs_0_), channel_id=1, source_target_pairs={{0,1},{1,0},{2,3},{3,2},{4,5},{5,4},{6,7},{7,6},{8,9},{9,8},{10,11... | collective-permute-start | bytes 196616 | tf_op jit(solution)/shard_map/ppermute | solution.py:333
  42.8 1.3 %collective-permute-start.16 = (bf16[16,2048]{1,0:T(8,128)(2,1)S(1)}, bf16[16,2048]{1,0:T(8,128)(2,1)S(1)}, u32[]{:S(2)}, u32[]{:S(2)}) collective-permute-start(bf16[16,2048]{1,0:T(8,128)(2,1)S(1)} %collective-permute-done.13), channel_id=1, source_target_pairs={{0,1},{1,0},{2,3},{3,2},{4,5},{5,4},{6,7},{7,6},{8,9},{9,8},{10,11... | collective-permute-start | bytes 196616 | tf_op jit(solution)/shard_map/ppermute | solution.py:333
  47.1 1.6 %collective-permute-start.17 = (bf16[64,2048]{1,0:T(8,128)(2,1)S(1)}, bf16[64,2048]{1,0:T(8,128)(2,1)S(1)}, u32[]{:S(2)}, u32[]{:S(2)}) collective-permute-start(bf16[64,2048]{1,0:T(8,128)(2,1)S(1)} %hold.15.refs_0_), channel_id=1, source_target_pairs={{0,1},{1,0},{2,3},{3,2},{4,5},{5,4},{6,7},{7,6},{8,9},{9,8},{10,11... | collective-permute-start | bytes 786440 | tf_op jit(solution)/shard_map/ppermute | solution.py:333
  47.3 1.6 %copy-start.1 = (bf16[512,2048]{1,0:T(8,128)(2,1)S(1)}, bf16[512,2048]{1,0:T(8,128)(2,1)}, u32[]{:S(2)}) copy-start(bf16[512,2048]{1,0:T(8,128)(2,1)} %copy-done) | copy-start | bytes 6291460
  50.4 11.9 %all-to-all-start = ((f32[16,4,128]{2,1,0:T(4,128)}), f32[16,4,128]{2,1,0:T(4,128)S(1)}, u32[]{:S(2)}, u32[]{:S(2)}) async-start(f32[16,4,128]{2,1,0:T(4,128)} %grad.7), calls=%async_computation | async-start | bytes 65536 | tf_op jit(solution)/shard_map/all_to_all | solution.py:404
  62.3 0.7 %copy-start.2 = (f32[4,128]{1,0:T(4,128)}, f32[4,128]{1,0:T(4,128)S(1)}, u32[]{:S(2)}) copy-start(f32[4,128]{1,0:T(4,128)S(1)} %reduce_sum.29) | copy-start | bytes 6148

commit v13 on v12

--- a/solution.py
+++ b/solution.py
@@ -284,7 +284,7 @@
     size = wide * len(pieces)
     return pl.pallas_call(
         functools.partial(grad_kernel, n, counts, prev is not None, final is not None),
-        out_shape=totals if final is None else jax.ShapeDtypeStruct((n, rows // n, LANES), jnp.float32),
+        out_shape=totals if final is None else pltpu.VMEM((n, rows // n, LANES), jnp.float32),
         in_specs=[VMEM] * len(args),
         out_specs=VMEM,
         scratch_shapes=[] if final is None else [totals],
@@ -380,9 +380,10 @@
         after = errs[p]
 
     err = join(errs, 1)
-    near = [((0, 0), [join([err] + [swap(err, dz=j) for j in z_order(fz)], 0)])]
+    come = [swap(err, dz=j) for j in z_order(fz)]
+    near = [((0, 0), [join([err] + come[:-1], 0), come[-1]])]
     for b in bits(fy):
-        last = [((0, b | at[1]), [swap(e, dy=b) for e in parts]) for at, parts in near]
+        last = [((0, b | at[1]), in_order([swap(e, dy=b) for e in parts])) for at, parts in near]
         near += last
     near = near[: -len(last)]
     half = rows // 2

time: 63.3 us -> 61.9 us (0.978)
  starting transfers between devices: 26 us -> 25.2 us
  waiting for transfers between devices: 18.8 us -> 18.1 us
    all_to_all x1, starting transfers between devices: 5.25 us -> 4.5 us  [local(): back = jnp.sum(lax.all_to_all(back, 'lat', 0, 0, tiled=True), axis=0)]
    ppermute x18 -> x19, waiting for transfers between devices: 13 us -> 12.4 us  [swap(): return lax.ppermute(x, 'lat', pairs(n, dz, dy, dc))]
    ppermute x18 -> x19, starting transfers between devices: 20.7 us -> 20.7 us  [swap(): return lax.ppermute(x, 'lat', pairs(n, dz, dy, dc))]
  transfers between devices with their start and end apart: 19 -> 20, of which waited for: 12 -> 9; matrix products, arithmetic and copies ran while one was open for 1% -> 1% of each run, Pallas kernels for 17% -> 17%
where the time goes in v13:
time: 61.9 us; the launch traced here: 61.6 us
  starting transfers between devices  25.2 us (41%)
  waiting for transfers between devices  18.1 us (29%)
  Pallas kernels  15.8 us (26%)
  other arithmetic  1.22 us (2%)
  between operations  0.94 us (2%)
    ppermute x19, starting transfers between devices, swap(): return lax.ppermute(x, 'lat', pairs(n, dz, dy, dc))  20.7 us
    ppermute x19, waiting for transfers between devices, swap(): return lax.ppermute(x, 'lat', pairs(n, dz, dy, dc))  12.4 us
    pallas_call x3, Pallas kernels, decode(): pl.pallas_call(functools.partial(decode_kernel, n, rows // n, chunks, par...  7.51 us
    all_to_all x1, waiting for transfers between devices, local(): back = jnp.sum(lax.all_to_all(back, 'lat', 0, 0, tiled=True), axis=0)  5.75 us
    all_to_all x1, starting transfers between devices, local(): back = jnp.sum(lax.all_to_all(back, 'lat', 0, 0, tiled=True), axis=0)  4.5 us
    pallas_call x4, Pallas kernels, grad(): pl.pallas_call(functools.partial(grad_kernel, n, counts, prev is not None...  3.76 us
    pallas_call x1, Pallas kernels, fetch(): pl.pallas_call(functools.partial(fetch_kernel, n, places), out_shape=[blo...  3.54 us
  transfers between devices with their start and end apart: 20, of which 9 were waited for; matrix products, arithmetic and copies ran while one was open for 1% of the time, Pallas kernels for 17%

profile of v13, /device:TPU:0, one launch (start us, length us, event | category | flops | bytes accessed | tf_op | source)
XLA Modules:
  0.0 61.6 jit_solution(11987862388894096524)
XLA Ops:
  0.6 3.7 %decode.3 = (f32[64,2048]{1,0:T(8,128)S(1)}, f32[64,2048]{1,0:T(8,128)S(1)}, bf16[64,512]{1,0:T(8,128)(2,1)S(1)}) custom-call(s32[64,64]{1,0:T(8,128)} %ids_hbm.1, bf16[64,64]{1,0:T(8,128)(2,1)} %refs_1_.3, bf16[512,8192]{1,0:T(8,128)(2,1)} %decoder_hbm.1, bf16[4,8192]{1,0:T(4,128)(2,1)} %refs_2_.5), custom_call_target="tpu_custom_call" | custom-call | flops 268435456 | bytes 8388608 | tf_op jit(solution)/shard_map/decode/pallas_call | solution.py:187
  4.3 0.5 collective-permute-start
  4.8 0.1 collective-permute-start.2
  4.9 1.9 %decode.4 = f32[64,2048]{1,0:T(8,128)S(1)} custom-call(bf16[64,512]{1,0:T(8,128)(2,1)S(1)} %get-tuple-element.12.refs_0_, bf16[512,8192]{1,0:T(8,128)(2,1)} %decoder_hbm.1, bf16[4,8192]{1,0:T(4,128)(2,1)} %refs_2_.5), custom_call_target="tpu_custom_call" | custom-call | flops 134217728 | bytes 4194304 | tf_op jit(solution)/shard_map/decode/pallas_call | solution.py:187
  6.8 0.0 collective-permute-done
  6.8 0.1 add.52
  6.9 3.0 %collective-permute-start.1 = (f32[64,1024]{1,0:T(8,128)S(1)}, f32[64,1024]{1,0:T(8,128)S(1)}, u32[]{:S(2)}, u32[]{:S(2)}) collective-permute-start(f32[64,1024]{1,0:T(8,128)S(1)} %slice.35.refs_3_), channel_id=1, source_target_pairs={{0,2},{1,3},{2,0},{3,1},{4,6},{5,7},{6,4},{7,5},{8,10},{9,11},{10,... | collective-permute-start | bytes 786440 | tf_op jit(solution)/shard_map/ppermute | solution.py:333
  9.9 1.9 %decode.5 = f32[64,2048]{1,0:T(8,128)S(1)} custom-call(bf16[64,512]{1,0:T(8,128)(2,1)S(1)} %get-tuple-element.12.refs_0_, bf16[512,8192]{1,0:T(8,128)(2,1)} %decoder_hbm.1, bf16[4,8192]{1,0:T(4,128)(2,1)} %refs_2_.5, f32[64,1024]{1,0:T(8,128)S(1)} %slice.35.refs_3_), custom_call_target="tpu_custom_call" | custom-call | flops 134217728 | bytes 4194304 | tf_op jit(solution)/shard_map/decode/pallas_call | solution.py:187
  11.9 0.0 collective-permute-done.2
  11.9 0.1 add.53
  12.0 0.1 collective-permute-start.4
  12.1 3.5 %fetch.1 = (bf16[512,2048]{1,0:T(8,128)(2,1)S(1)}, bf16[512,2048]{1,0:T(8,128)(2,1)S(1)}, bf16[512,2048]{1,0:T(8,128)(2,1)S(1)}, bf16[512,2048]{1,0:T(8,128)(2,1...) custom-call(bf16[512,8192]{1,0:T(8,128)(2,1)} %decoder_hbm.1, s32[64,64]{1,0:T(8,128)} %ids_hbm.1, f32[64,1024]{1,0:T(8,128)S(1)} %slice.36._), custom_call_target="tpu_custom_call" | custom-call | bytes 8388608 | tf_op jit(solution)/shard_map/fetch/pallas_call | solution.py:215
  15.7 0.0 copy-start
  15.7 1.4 %collective-permute-done.1.x_ref = f32[64,1024]{1,0:T(8,128)S(1)} collective-permute-done((f32[64,1024]{1,0:T(8,128)S(1)}, f32[64,1024]{1,0:T(8,128)S(1)}, u32[]{:S(2)}, u32[]{:S(2)}) %collective-permute-start.1) | collective-permute-done | bytes 262176 | tf_op jit(solution)/shard_map/ppermute | solution.py:333
  17.2 4.2 %collective-permute-start.3 = (f32[16,1024]{1,0:T(8,128)S(1)}, f32[16,1024]{1,0:T(8,128)S(1)}, u32[]{:S(2)}, u32[]{:S(2)}) collective-permute-start(f32[16,1024]{1,0:T(8,128)S(1)} %get-tuple-element.29), channel_id=1, source_target_pairs={{0,12},{1,13},{2,14},{3,15},{4,8},{5,9},{6,10},{7,11},{8,4},{9,5},... | collective-permute-start | bytes 196616 | tf_op jit(solution)/shard_map/ppermute | solution.py:333
  21.4 0.0 collective-permute-start.6
  21.4 0.6 %collective-permute-start.5 = (f32[16,1024]{1,0:T(8,128)S(1)}, f32[16,1024]{1,0:T(8,128)S(1)}, u32[]{:S(2)}, u32[]{:S(2)}) collective-permute-start(f32[16,1024]{1,0:T(8,128)S(1)} %get-tuple-element.31), channel_id=1, source_target_pairs={{0,4},{1,5},{2,6},{3,7},{4,0},{5,1},{6,2},{7,3},{8,12},{9,13},{10,... | collective-permute-start | bytes 196616 | tf_op jit(solution)/shard_map/ppermute | solution.py:333
  22.0 0.1 collective-permute-done.4
  22.2 2.9 %collective-permute-start.9 = (f32[16,1024]{1,0:T(8,128)S(1)}, f32[16,1024]{1,0:T(8,128)S(1)}, u32[]{:S(2)}, u32[]{:S(2)}) collective-permute-start(f32[16,1024]{1,0:T(8,128)S(1)} %get-tuple-element.26), channel_id=1, source_target_pairs={{0,8},{1,9},{2,10},{3,11},{4,12},{5,13},{6,14},{7,15},{8,0},{9,1},... | collective-permute-start | bytes 196616 | tf_op jit(solution)/shard_map/ppermute | solution.py:333
  25.1 1.6 %collective-permute-start.8 = (f32[16,1024]{1,0:T(8,128)S(1)}, f32[16,1024]{1,0:T(8,128)S(1)}, u32[]{:S(2)}, u32[]{:S(2)}) collective-permute-start(f32[16,1024]{1,0:T(8,128)S(1)} %get-tuple-element.27), channel_id=1, source_target_pairs={{0,4},{1,5},{2,6},{3,7},{4,0},{5,1},{6,2},{7,3},{8,12},{9,13},{10,... | collective-permute-start | bytes 196616 | tf_op jit(solution)/shard_map/ppermute | solution.py:333
  26.6 0.0 collective-permute-done.3.x_ref
  26.7 0.9 %collective-permute-start.7 = (f32[16,1024]{1,0:T(8,128)S(1)}, f32[16,1024]{1,0:T(8,128)S(1)}, u32[]{:S(2)}, u32[]{:S(2)}) collective-permute-start(f32[16,1024]{1,0:T(8,128)S(1)} %get-tuple-element.28), channel_id=1, source_target_pairs={{0,12},{1,13},{2,14},{3,15},{4,8},{5,9},{6,10},{7,11},{8,4},{9,5},... | collective-permute-start | bytes 196616 | tf_op jit(solution)/shard_map/ppermute | solution.py:333
  27.6 0.0 collective-permute-done.5.x_ref
  27.6 0.1 collective-permute-done.6.x_ref
  27.8 0.1 multiply_reduce_fusion.1
  27.9 4.8 %collective-permute-done.7.x_ref = f32[16,1024]{1,0:T(8,128)S(1)} collective-permute-done((f32[16,1024]{1,0:T(8,128)S(1)}, f32[16,1024]{1,0:T(8,128)S(1)}, u32[]{:S(2)}, u32[]{:S(2)}) %collective-permute-start.7) | collective-permute-done | bytes 65568 | tf_op jit(solution)/shard_map/ppermute | solution.py:333
  32.7 0.0 collective-permute-done.8.x_ref
  32.8 0.0 copy-done
  32.8 0.0 collective-permute-done.9.x_ref
  32.8 0.1 multiply_reduce_fusion
  32.9 0.1 collective-permute-start.12
  33.0 2.2 %collective-permute-start.11 = (bf16[16,2048]{1,0:T(8,128)(2,1)S(1)}, bf16[16,2048]{1,0:T(8,128)(2,1)S(1)}, u32[]{:S(2)}, u32[]{:S(2)}) collective-permute-start(bf16[16,2048]{1,0:T(8,128)(2,1)S(1)} %pad_maximum_fusion.3.refs_0_), channel_id=1, source_target_pairs={{0,12},{1,13},{2,14},{3,15},{4,8},{5,9},{6,10},{7,11},{8,4},{9,5},... | collective-permute-start | bytes 196616 | tf_op jit(solution)/shard_map/ppermute | solution.py:333
  35.2 1.2 %collective-permute-start.14 = (bf16[16,2048]{1,0:T(8,128)(2,1)S(1)}, bf16[16,2048]{1,0:T(8,128)(2,1)S(1)}, u32[]{:S(2)}, u32[]{:S(2)}) collective-permute-start(bf16[16,2048]{1,0:T(8,128)(2,1)S(1)} %pad_maximum_fusion.3.refs_0_), channel_id=1, source_target_pairs={{0,8},{1,9},{2,10},{3,11},{4,12},{5,13},{6,14},{7,15},{8,0},{9,1},... | collective-permute-start | bytes 196616 | tf_op jit(solution)/shard_map/ppermute | solution.py:333
  36.5 1.4 %collective-permute-done.12 = bf16[16,2048]{1,0:T(8,128)(2,1)S(1)} collective-permute-done((bf16[16,2048]{1,0:T(8,128)(2,1)S(1)}, bf16[16,2048]{1,0:T(8,128)(2,1)S(1)}, u32[]{:S(2)}, u32[]{:S(2)}) %collective-permute-start.12) | collective-permute-done | bytes 65568 | tf_op jit(solution)/shard_map/ppermute | solution.py:333
  37.9 1.4 %collective-permute-done.11 = bf16[16,2048]{1,0:T(8,128)(2,1)S(1)} collective-permute-done((bf16[16,2048]{1,0:T(8,128)(2,1)S(1)}, bf16[16,2048]{1,0:T(8,128)(2,1)S(1)}, u32[]{:S(2)}, u32[]{:S(2)}) %collective-permute-start.11) | collective-permute-done | bytes 65568 | tf_op jit(solution)/shard_map/ppermute | solution.py:333
  39.3 1.6 %collective-permute-start.13 = (bf16[48,2048]{1,0:T(8,128)(2,1)S(1)}, bf16[48,2048]{1,0:T(8,128)(2,1)S(1)}, u32[]{:S(2)}, u32[]{:S(2)}) collective-permute-start(bf16[48,2048]{1,0:T(8,128)(2,1)S(1)} %pad_maximum_fusion.1.refs_0_), channel_id=1, source_target_pairs={{0,2},{1,3},{2,0},{3,1},{4,6},{5,7},{6,4},{7,5},{8,10},{9,11},{10,... | collective-permute-start | bytes 589832 | tf_op jit(solution)/shard_map/ppermute | solution.py:333
  40.9 0.1 collective-permute-start.16
  40.9 0.5 collective-permute-start.10
  41.4 0.0 collective-permute-done.14.refs_1_
  41.4 0.1 collective-permute-start.17
  41.5 0.8 %collective-permute-start.15 = (bf16[16,2048]{1,0:T(8,128)(2,1)S(1)}, bf16[16,2048]{1,0:T(8,128)(2,1)S(1)}, u32[]{:S(2)}, u32[]{:S(2)}) collective-permute-start(bf16[16,2048]{1,0:T(8,128)(2,1)S(1)} %collective-permute-done.14.refs_1_), channel_id=1, source_target_pairs={{0,2},{1,3},{2,0},{3,1},{4,6},{5,7},{6,4},{7,5},{8,10},{9,11},{10,... | collective-permute-start | bytes 196616 | tf_op jit(solution)/shard_map/ppermute | solution.py:333
  42.4 0.8 %grad.4.refs_4_ = f32[64,512]{1,0:T(8,128)S(1)} custom-call(bf16[48,2048]{1,0:T(8,128)(2,1)S(1)} %pad_maximum_fusion.1.refs_0_, bf16[16,2048]{1,0:T(8,128)(2,1)S(1)} %collective-permute-done.14.refs_1_, bf16[512,2048]{1,0:T(8,128)(2,1)S(1)} %get-tuple-element.17.refs_2_), custom_call_target="tpu_custom_call" | custom-call | flops 134217728 | bytes 4194304 | tf_op jit(solution)/shard_map/grad/pallas_call | solution.py:285
  43.1 0.0 collective-permute-done.10.refs_0_.refs_1_
  43.1 0.0 collective-permute-done.17.refs_2_
  43.1 0.0 collective-permute-done.16.refs_1_
  43.2 0.8 %grad.5.refs_0_.refs_3_ = f32[64,512]{1,0:T(8,128)S(1)} custom-call(bf16[16,2048]{1,0:T(8,128)(2,1)S(1)} %collective-permute-done.10.refs_0_.refs_1_, bf16[32,2048]{1,0:T(8,128)(2,1)S(1)} %collective-permute-done.16.refs_1_, bf16[16,2048]{1,0:T(8,128)(2,1)S(1)} %collective-permute-done.17.refs_2_, bf16[512,2048]{1,0:T(8,128)(2,1)S(1)} %get-tuple-element.16.refs_3_, ...), custom_call_target="tpu_custom_call" | custom-call | flops 134217728 | bytes 4194304 | tf_op jit(solution)/shard_map/grad/pallas_call | solution.py:285
  43.9 2.5 %collective-permute-done.15.x_ref = bf16[16,2048]{1,0:T(8,128)(2,1)S(1)} collective-permute-done((bf16[16,2048]{1,0:T(8,128)(2,1)S(1)}, bf16[16,2048]{1,0:T(8,128)(2,1)S(1)}, u32[]{:S(2)}, u32[]{:S(2)}) %collective-permute-start.15) | collective-permute-done | bytes 65568 | tf_op jit(solution)/shard_map/ppermute | solution.py:333
  46.4 0.0 collective-permute-done.13.refs_0_
  46.5 0.1 collective-permute-start.18
  46.6 0.1 copy.16.refs_4_
  46.6 0.0 copy-start.1
  46.6 0.8 %grad.6.refs_2_ = f32[64,512]{1,0:T(8,128)S(1)} custom-call(bf16[48,2048]{1,0:T(8,128)(2,1)S(1)} %collective-permute-done.13.refs_0_, bf16[16,2048]{1,0:T(8,128)(2,1)S(1)} %hold.17.refs_1_, bf16[512,2048]{1,0:T(8,128)(2,1)S(1)} %get-tuple-element.19.refs_2_, f32[64,512]{1,0:T(8,128)S(1)} %grad.5.refs_0_.refs_3_), custom_call_target="tpu_custom_call" | custom-call | flops 134217728 | bytes 4194304 | tf_op jit(solution)/shard_map/grad/pallas_call | solution.py:285
  47.4 0.7 %collective-permute-done.18.refs_0_ = bf16[64,2048]{1,0:T(8,128)(2,1)S(1)} collective-permute-done((bf16[64,2048]{1,0:T(8,128)(2,1)S(1)}, bf16[64,2048]{1,0:T(8,128)(2,1)S(1)}, u32[]{:S(2)}, u32[]{:S(2)}) %collective-permute-start.18) | collective-permute-done | bytes 262176 | tf_op jit(solution)/shard_map/ppermute | solution.py:333
  48.1 0.2 copy-done.1
  48.2 1.5 %grad.7 = f32[16,4,128]{2,1,0:T(4,128)} custom-call(bf16[64,2048]{1,0:T(8,128)(2,1)S(1)} %collective-permute-done.18.refs_0_, bf16[512,2048]{1,0:T(8,128)(2,1)S(1)} %copy-done.1, f32[64,512]{1,0:T(8,128)S(1)} %grad.6.refs_2_, s32[64,64]{1,0:T(8,128)S(1)} %get-tuple-element.20.refs_3_, f32[16,1]{1,0:T(8,128)S(1)} %copy.16.refs_4_), custom_call_target="tpu_custom_call" | custom-call | flops 134217728 | bytes 4194304 | tf_op jit(solution)/shard_map/grad/pallas_call | solution.py:285
  49.7 4.5 %all-to-all-start = ((f32[16,4,128]{2,1,0:T(4,128)}), f32[16,4,128]{2,1,0:T(4,128)S(1)}, u32[]{:S(2)}, u32[]{:S(2)}) async-start(f32[16,4,128]{2,1,0:T(4,128)} %grad.7), calls=%async_computation | async-start | bytes 65536 | tf_op jit(solution)/shard_map/all_to_all | solution.py:405
  54.3 0.9 %own_rows.1 = bf16[4,8192]{1,0:T(4,128)(2,1)} custom-call(bf16[16,2048]{1,0:T(8,128)(2,1)S(1)} %pad_maximum_fusion.3.refs_0_, bf16[16,2048]{1,0:T(8,128)(2,1)S(1)} %collective-permute-done.10.refs_0_.refs_1_, bf16[16,2048]{1,0:T(8,128)(2,1)S(1)} %slice.38.refs_2_, bf16[16,2048]{1,0:T(8,128)(2,1)S(1)} %slice.39.refs_3_), custom_call_target="tpu_custom_call" | custom-call | tf_op jit(solution)/shard_map/own_rows/pallas_call | solution.py:311
  55.1 5.7 %all-to-all-done = f32[16,4,128]{2,1,0:T(4,128)S(1)} async-done(((f32[16,4,128]{2,1,0:T(4,128)}), f32[16,4,128]{2,1,0:T(4,128)S(1)}, u32[]{:S(2)}, u32[]{:S(2)}) %all-to-all-start) | async-done | bytes 32800 | tf_op jit(solution)/shard_map/all_to_all | solution.py:405
  60.9 0.0 copy-start.2
  60.9 0.7 %multiply_reduce_fusion.2 = f32[4]{0:T(128)} fusion(f32[4,128]{1,0:T(4,128)S(1)} %reduce_sum.29), kind=kLoop, calls=%fused_computation.10 | loop fusion | flops 4 | bytes 32 | tf_op jit(solution)/shard_map/div | solution.py:406
  61.6 0.0 copy-done.2
  (23 shorter events, 0.4 us)
Async XLA Ops:
  4.3 2.5 %collective-permute-start = (f32[64,2048]{1,0:T(8,128)S(1)}, f32[64,2048]{1,0:T(8,128)S(1)}, u32[]{:S(2)}, u32[]{:S(2)}) collective-permute-start(f32[64,2048]{1,0:T(8,128)S(1)} %get-tuple-element.13), channel_id=1, source_target_pairs={{0,1},{1,0},{2,3},{3,2},{4,5},{5,4},{6,7},{7,6},{8,9},{9,8},{10,11... | collective-permute-start | bytes 1572872 | tf_op jit(solution)/shard_map/ppermute | solution.py:333
  4.8 7.1 %collective-permute-start.2 = (f32[64,2048]{1,0:T(8,128)S(1)}, f32[64,2048]{1,0:T(8,128)S(1)}, u32[]{:S(2)}, u32[]{:S(2)}) collective-permute-start(f32[64,2048]{1,0:T(8,128)S(1)} %get-tuple-element.14), channel_id=1, source_target_pairs={{0,1},{1,0},{2,3},{3,2},{4,5},{5,4},{6,7},{7,6},{8,9},{9,8},{10,11... | collective-permute-start | bytes 1572872 | tf_op jit(solution)/shard_map/ppermute | solution.py:333
  6.9 10.1 %collective-permute-start.1 = (f32[64,1024]{1,0:T(8,128)S(1)}, f32[64,1024]{1,0:T(8,128)S(1)}, u32[]{:S(2)}, u32[]{:S(2)}) collective-permute-start(f32[64,1024]{1,0:T(8,128)S(1)} %slice.35.refs_3_), channel_id=1, source_target_pairs={{0,2},{1,3},{2,0},{3,1},{4,6},{5,7},{6,4},{7,5},{8,10},{9,11},{10,... | collective-permute-start | bytes 786440 | tf_op jit(solution)/shard_map/ppermute | solution.py:333
  12.0 10.1 %collective-permute-start.4 = (f32[64,1024]{1,0:T(8,128)S(1)}, f32[64,1024]{1,0:T(8,128)S(1)}, u32[]{:S(2)}, u32[]{:S(2)}) collective-permute-start(f32[64,1024]{1,0:T(8,128)S(1)} %slice.36._), channel_id=1, source_target_pairs={{0,2},{1,3},{2,0},{3,1},{4,6},{5,7},{6,4},{7,5},{8,10},{9,11},{10,... | collective-permute-start | bytes 786440 | tf_op jit(solution)/shard_map/ppermute | solution.py:333
  15.7 17.1 %copy-start = (bf16[512,2048]{1,0:T(8,128)(2,1)}, bf16[512,2048]{1,0:T(8,128)(2,1)S(1)}, u32[]{:S(2)}) copy-start(bf16[512,2048]{1,0:T(8,128)(2,1)S(1)} %get-tuple-element.18.refs_1_) | copy-start | bytes 6291460
  17.2 9.5 %collective-permute-start.3 = (f32[16,1024]{1,0:T(8,128)S(1)}, f32[16,1024]{1,0:T(8,128)S(1)}, u32[]{:S(2)}, u32[]{:S(2)}) collective-permute-start(f32[16,1024]{1,0:T(8,128)S(1)} %get-tuple-element.29), channel_id=1, source_target_pairs={{0,12},{1,13},{2,14},{3,15},{4,8},{5,9},{6,10},{7,11},{8,4},{9,5},... | collective-permute-start | bytes 196616 | tf_op jit(solution)/shard_map/ppermute | solution.py:333
  21.4 6.4 %collective-permute-start.6 = (f32[16,1024]{1,0:T(8,128)S(1)}, f32[16,1024]{1,0:T(8,128)S(1)}, u32[]{:S(2)}, u32[]{:S(2)}) collective-permute-start(f32[16,1024]{1,0:T(8,128)S(1)} %get-tuple-element.30), channel_id=1, source_target_pairs={{0,8},{1,9},{2,10},{3,11},{4,12},{5,13},{6,14},{7,15},{8,0},{9,1},... | collective-permute-start | bytes 196616 | tf_op jit(solution)/shard_map/ppermute | solution.py:333
  21.4 6.2 %collective-permute-start.5 = (f32[16,1024]{1,0:T(8,128)S(1)}, f32[16,1024]{1,0:T(8,128)S(1)}, u32[]{:S(2)}, u32[]{:S(2)}) collective-permute-start(f32[16,1024]{1,0:T(8,128)S(1)} %get-tuple-element.31), channel_id=1, source_target_pairs={{0,4},{1,5},{2,6},{3,7},{4,0},{5,1},{6,2},{7,3},{8,12},{9,13},{10,... | collective-permute-start | bytes 196616 | tf_op jit(solution)/shard_map/ppermute | solution.py:333
  22.2 10.6 %collective-permute-start.9 = (f32[16,1024]{1,0:T(8,128)S(1)}, f32[16,1024]{1,0:T(8,128)S(1)}, u32[]{:S(2)}, u32[]{:S(2)}) collective-permute-start(f32[16,1024]{1,0:T(8,128)S(1)} %get-tuple-element.26), channel_id=1, source_target_pairs={{0,8},{1,9},{2,10},{3,11},{4,12},{5,13},{6,14},{7,15},{8,0},{9,1},... | collective-permute-start | bytes 196616 | tf_op jit(solution)/shard_map/ppermute | solution.py:333
  25.1 7.7 %collective-permute-start.8 = (f32[16,1024]{1,0:T(8,128)S(1)}, f32[16,1024]{1,0:T(8,128)S(1)}, u32[]{:S(2)}, u32[]{:S(2)}) collective-permute-start(f32[16,1024]{1,0:T(8,128)S(1)} %get-tuple-element.27), channel_id=1, source_target_pairs={{0,4},{1,5},{2,6},{3,7},{4,0},{5,1},{6,2},{7,3},{8,12},{9,13},{10,... | collective-permute-start | bytes 196616 | tf_op jit(solution)/shard_map/ppermute | solution.py:333
  26.7 6.1 %collective-permute-start.7 = (f32[16,1024]{1,0:T(8,128)S(1)}, f32[16,1024]{1,0:T(8,128)S(1)}, u32[]{:S(2)}, u32[]{:S(2)}) collective-permute-start(f32[16,1024]{1,0:T(8,128)S(1)} %get-tuple-element.28), channel_id=1, source_target_pairs={{0,12},{1,13},{2,14},{3,15},{4,8},{5,9},{6,10},{7,11},{8,4},{9,5},... | collective-permute-start | bytes 196616 | tf_op jit(solution)/shard_map/ppermute | solution.py:333
  32.9 5.0 %collective-permute-start.12 = (bf16[16,2048]{1,0:T(8,128)(2,1)S(1)}, bf16[16,2048]{1,0:T(8,128)(2,1)S(1)}, u32[]{:S(2)}, u32[]{:S(2)}) collective-permute-start(bf16[16,2048]{1,0:T(8,128)(2,1)S(1)} %pad_maximum_fusion.3.refs_0_), channel_id=1, source_target_pairs={{0,4},{1,5},{2,6},{3,7},{4,0},{5,1},{6,2},{7,3},{8,12},{9,13},{10,... | collective-permute-start | bytes 196616 | tf_op jit(solution)/shard_map/ppermute | solution.py:333
  33.0 6.2 %collective-permute-start.11 = (bf16[16,2048]{1,0:T(8,128)(2,1)S(1)}, bf16[16,2048]{1,0:T(8,128)(2,1)S(1)}, u32[]{:S(2)}, u32[]{:S(2)}) collective-permute-start(bf16[16,2048]{1,0:T(8,128)(2,1)S(1)} %pad_maximum_fusion.3.refs_0_), channel_id=1, source_target_pairs={{0,12},{1,13},{2,14},{3,15},{4,8},{5,9},{6,10},{7,11},{8,4},{9,5},... | collective-permute-start | bytes 196616 | tf_op jit(solution)/shard_map/ppermute | solution.py:333
  35.2 6.2 %collective-permute-start.14 = (bf16[16,2048]{1,0:T(8,128)(2,1)S(1)}, bf16[16,2048]{1,0:T(8,128)(2,1)S(1)}, u32[]{:S(2)}, u32[]{:S(2)}) collective-permute-start(bf16[16,2048]{1,0:T(8,128)(2,1)S(1)} %pad_maximum_fusion.3.refs_0_), channel_id=1, source_target_pairs={{0,8},{1,9},{2,10},{3,11},{4,12},{5,13},{6,14},{7,15},{8,0},{9,1},... | collective-permute-start | bytes 196616 | tf_op jit(solution)/shard_map/ppermute | solution.py:333
  39.3 7.1 %collective-permute-start.13 = (bf16[48,2048]{1,0:T(8,128)(2,1)S(1)}, bf16[48,2048]{1,0:T(8,128)(2,1)S(1)}, u32[]{:S(2)}, u32[]{:S(2)}) collective-permute-start(bf16[48,2048]{1,0:T(8,128)(2,1)S(1)} %pad_maximum_fusion.1.refs_0_), channel_id=1, source_target_pairs={{0,2},{1,3},{2,0},{3,1},{4,6},{5,7},{6,4},{7,5},{8,10},{9,11},{10,... | collective-permute-start | bytes 589832 | tf_op jit(solution)/shard_map/ppermute | solution.py:333
  40.9 2.3 %collective-permute-start.16 = (bf16[32,2048]{1,0:T(8,128)(2,1)S(1)}, bf16[32,2048]{1,0:T(8,128)(2,1)S(1)}, u32[]{:S(2)}, u32[]{:S(2)}) collective-permute-start(bf16[32,2048]{1,0:T(8,128)(2,1)S(1)} %pad_maximum_fusion.2), channel_id=1, source_target_pairs={{0,1},{1,0},{2,3},{3,2},{4,5},{5,4},{6,7},{7,6},{8,9},{9,8},{10,11... | collective-permute-start | bytes 393224 | tf_op jit(solution)/shard_map/ppermute | solution.py:333
  40.9 2.2 %collective-permute-start.10 = (bf16[16,2048]{1,0:T(8,128)(2,1)S(1)}, bf16[16,2048]{1,0:T(8,128)(2,1)S(1)}, u32[]{:S(2)}, u32[]{:S(2)}) collective-permute-start(bf16[16,2048]{1,0:T(8,128)(2,1)S(1)} %pad_maximum_fusion.3.refs_0_), channel_id=1, source_target_pairs={{0,1},{1,0},{2,3},{3,2},{4,5},{5,4},{6,7},{7,6},{8,9},{9,8},{10,11... | collective-permute-start | bytes 196616 | tf_op jit(solution)/shard_map/ppermute | solution.py:333
  41.4 1.7 %collective-permute-start.17 = (bf16[16,2048]{1,0:T(8,128)(2,1)S(1)}, bf16[16,2048]{1,0:T(8,128)(2,1)S(1)}, u32[]{:S(2)}, u32[]{:S(2)}) collective-permute-start(bf16[16,2048]{1,0:T(8,128)(2,1)S(1)} %collective-permute-done.14.refs_1_), channel_id=1, source_target_pairs={{0,1},{1,0},{2,3},{3,2},{4,5},{5,4},{6,7},{7,6},{8,9},{9,8},{10,11... | collective-permute-start | bytes 196616 | tf_op jit(solution)/shard_map/ppermute | solution.py:333
  41.5 4.9 %collective-permute-start.15 = (bf16[16,2048]{1,0:T(8,128)(2,1)S(1)}, bf16[16,2048]{1,0:T(8,128)(2,1)S(1)}, u32[]{:S(2)}, u32[]{:S(2)}) collective-permute-start(bf16[16,2048]{1,0:T(8,128)(2,1)S(1)} %collective-permute-done.14.refs_1_), channel_id=1, source_target_pairs={{0,2},{1,3},{2,0},{3,1},{4,6},{5,7},{6,4},{7,5},{8,10},{9,11},{10,... | collective-permute-start | bytes 196616 | tf_op jit(solution)/shard_map/ppermute | solution.py:333
  46.5 1.6 %collective-permute-start.18 = (bf16[64,2048]{1,0:T(8,128)(2,1)S(1)}, bf16[64,2048]{1,0:T(8,128)(2,1)S(1)}, u32[]{:S(2)}, u32[]{:S(2)}) collective-permute-start(bf16[64,2048]{1,0:T(8,128)(2,1)S(1)} %pad_maximum_fusion), channel_id=1, source_target_pairs={{0,1},{1,0},{2,3},{3,2},{4,5},{5,4},{6,7},{7,6},{8,9},{9,8},{10,11... | collective-permute-start | bytes 786440 | tf_op jit(solution)/shard_map/ppermute | solution.py:333
  46.6 1.6 %copy-start.1 = (bf16[512,2048]{1,0:T(8,128)(2,1)S(1)}, bf16[512,2048]{1,0:T(8,128)(2,1)}, u32[]{:S(2)}) copy-start(bf16[512,2048]{1,0:T(8,128)(2,1)} %copy-done) | copy-start | bytes 6291460
  49.7 11.1 %all-to-all-start = ((f32[16,4,128]{2,1,0:T(4,128)}), f32[16,4,128]{2,1,0:T(4,128)S(1)}, u32[]{:S(2)}, u32[]{:S(2)}) async-start(f32[16,4,128]{2,1,0:T(4,128)} %grad.7), calls=%async_computation | async-start | bytes 65536 | tf_op jit(solution)/shard_map/all_to_all | solution.py:405
  60.9 0.7 %copy-start.2 = (f32[4,128]{1,0:T(4,128)}, f32[4,128]{1,0:T(4,128)S(1)}, u32[]{:S(2)}) copy-start(f32[4,128]{1,0:T(4,128)S(1)} %reduce_sum.29) | copy-start | bytes 6148

commit v14 on v13

--- a/solution.py
+++ b/solution.py
@@ -386,18 +386,15 @@
         last = [((0, b | at[1]), in_order([swap(e, dy=b) for e in parts])) for at, parts in near]
         near += last
     near = near[: -len(last)]
-    half = rows // 2
-
-    def halves(parts):
-        whole = join(parts, 0)
-        return [whole[:group], whole[group : group + half], whole[group + half :]]
-
-    far = [((1, at[1]), [swap(e, dc=1) for e in halves(parts)]) for at, parts in near]
     totals = grad(n, rows, near, columns, None)
-    totals = grad(n, rows, far, columns, totals)
     last[-1][1][-1] = hold(last[-1][1][-1], totals)
-    far_last = [((1, at[1]), [swap(join(parts, 0), dc=1)]) for at, parts in last]
-    totals = grad(n, rows, last, columns, totals)
+
+    def to_core(pieces):
+        return [((1, at[1]), [swap(join(parts, 0), dc=1)]) for at, parts in pieces]
+
+    far = [(at, [hold(e, last[-1][1][-1])]) for at, (e,) in to_core(near)]
+    far_last = to_core(last)
+    totals = grad(n, rows, far + last, columns, totals)
     back = grad(n, rows, far_last, columns, totals, (in_vmem(ids), loss))
     pieces = near + far + last + far_last
     error = own_rows(n, [at for at, _ in pieces], own, width, [e[0][:group] for _, e in pieces])

time: 61.9 us -> 65.5 us (1.058)
  local copies, waits for them, and re-layouts: 0.36 us -> 4.72 us
  waiting for transfers between devices: 18.1 us -> 15.4 us
  starting transfers between devices: 25.2 us -> 26.4 us
  other arithmetic: 1.22 us -> 1.95 us
    unnamed x6 -> x14, local copies, waits for them, and re-layouts: 0.17 us -> 4.52 us
    ppermute x19 -> x17, waiting for transfers between devices: 12.4 us -> 9.7 us  [swap(): return lax.ppermute(x, 'lat', pairs(n, dz, dy, dc))]
    concatenate x4, other arithmetic: 0.05 us -> 0.78 us  [join(): return xs[0] if len(xs) == 1 else jnp.concatenate(xs, axis=axis)]
    ppermute x19 -> x17, starting transfers between devices: 20.7 us -> 21.3 us  [swap(): return lax.ppermute(x, 'lat', pairs(n, dz, dy, dc))]
    pallas_call x4 -> x3, Pallas kernels: 3.76 us -> 3.62 us  [grad(): pl.pallas_call(functools.partial(grad_kernel, n, counts, prev is not None...]
  transfers between devices with their start and end apart: 20 -> 18, of which waited for: 9 -> 7; matrix products, arithmetic and copies ran while one was open for 1% -> 2% of each run, Pallas kernels for 17% -> 16%
where the time goes in v14:
time: 65.5 us; the launch traced here: 65.2 us
  starting transfers between devices  26.4 us (40%)
  Pallas kernels  15.7 us (24%)
  waiting for transfers between devices  15.4 us (24%)
  local copies, waits for them, and re-layouts  4.72 us (7%)
  other arithmetic  1.95 us (3%)
  between operations  0.97 us (1%)
    ppermute x17, starting transfers between devices, swap(): return lax.ppermute(x, 'lat', pairs(n, dz, dy, dc))  21.3 us
    ppermute x17, waiting for transfers between devices, swap(): return lax.ppermute(x, 'lat', pairs(n, dz, dy, dc))  9.7 us
    pallas_call x3, Pallas kernels, decode(): pl.pallas_call(functools.partial(decode_kernel, n, rows // n, chunks, par...  7.51 us
    all_to_all x1, waiting for transfers between devices, local(): back = jnp.sum(lax.all_to_all(back, 'lat', 0, 0, tiled=True), axis=0)  5.74 us
    all_to_all x1, starting transfers between devices, local(): back = jnp.sum(lax.all_to_all(back, 'lat', 0, 0, tiled=True), axis=0)  5.12 us
    unnamed x14, local copies, waits for them, and re-layouts  4.52 us
    pallas_call x3, Pallas kernels, grad(): pl.pallas_call(functools.partial(grad_kernel, n, counts, prev is not None...  3.62 us
    pallas_call x1, Pallas kernels, fetch(): pl.pallas_call(functools.partial(fetch_kernel, n, places), out_shape=[blo...  3.54 us
  transfers between devices with their start and end apart: 18, of which 7 were waited for; matrix products, arithmetic and copies ran while one was open for 2% of the time, Pallas kernels for 16%

profile of v14, /device:TPU:0, one launch (start us, length us, event | category | flops | bytes accessed | tf_op | source)
XLA Modules:
  0.0 65.2 jit_solution(17372176686038025805)
XLA Ops:
  0.6 3.7 %decode.3 = (f32[64,2048]{1,0:T(8,128)S(1)}, f32[64,2048]{1,0:T(8,128)S(1)}, bf16[64,512]{1,0:T(8,128)(2,1)S(1)}) custom-call(s32[64,64]{1,0:T(8,128)} %ids_hbm.1, bf16[64,64]{1,0:T(8,128)(2,1)} %refs_1_.3, bf16[512,8192]{1,0:T(8,128)(2,1)} %decoder_hbm.1, bf16[4,8192]{1,0:T(4,128)(2,1)} %refs_2_.5), custom_call_target="tpu_custom_call" | custom-call | flops 268435456 | bytes 8388608 | tf_op jit(solution)/shard_map/decode/pallas_call | solution.py:187
  4.3 0.5 collective-permute-start
  4.8 0.1 collective-permute-start.2
  4.9 1.9 %decode.4 = f32[64,2048]{1,0:T(8,128)S(1)} custom-call(bf16[64,512]{1,0:T(8,128)(2,1)S(1)} %get-tuple-element.12.refs_0_, bf16[512,8192]{1,0:T(8,128)(2,1)} %decoder_hbm.1, bf16[4,8192]{1,0:T(4,128)(2,1)} %refs_2_.5), custom_call_target="tpu_custom_call" | custom-call | flops 134217728 | bytes 4194304 | tf_op jit(solution)/shard_map/decode/pallas_call | solution.py:187
  6.8 0.0 collective-permute-done
  6.8 0.1 add.52
  6.9 0.0 copy-start.4
  6.9 3.0 %collective-permute-start.1 = (f32[64,1024]{1,0:T(8,128)S(1)}, f32[64,1024]{1,0:T(8,128)S(1)}, u32[]{:S(2)}, u32[]{:S(2)}) collective-permute-start(f32[64,1024]{1,0:T(8,128)S(1)} %slice.37.refs_3_), channel_id=1, source_target_pairs={{0,2},{1,3},{2,0},{3,1},{4,6},{5,7},{6,4},{7,5},{8,10},{9,11},{10,... | collective-permute-start | bytes 786440 | tf_op jit(solution)/shard_map/ppermute | solution.py:333
  10.0 1.9 %decode.5 = f32[64,2048]{1,0:T(8,128)S(1)} custom-call(bf16[64,512]{1,0:T(8,128)(2,1)S(1)} %get-tuple-element.12.refs_0_, bf16[512,8192]{1,0:T(8,128)(2,1)} %decoder_hbm.1, bf16[4,8192]{1,0:T(4,128)(2,1)} %refs_2_.5, f32[64,1024]{1,0:T(8,128)S(1)} %slice.37.refs_3_), custom_call_target="tpu_custom_call" | custom-call | flops 134217728 | bytes 4194304 | tf_op jit(solution)/shard_map/decode/pallas_call | solution.py:187
  11.9 0.0 copy-done.4
  11.9 0.0 collective-permute-done.2
  11.9 0.1 add.53
  12.0 0.0 copy-start.5
  12.0 0.2 collective-permute-start.4
  12.2 3.5 %fetch.1 = (bf16[512,2048]{1,0:T(8,128)(2,1)S(1)}, bf16[512,2048]{1,0:T(8,128)(2,1)S(1)}, bf16[512,2048]{1,0:T(8,128)(2,1)S(1)}, bf16[512,2048]{1,0:T(8,128)(2,1...) custom-call(bf16[512,8192]{1,0:T(8,128)(2,1)} %decoder_hbm.1, s32[64,64]{1,0:T(8,128)} %ids_hbm.1, f32[64,1024]{1,0:T(8,128)S(1)} %slice.38._), custom_call_target="tpu_custom_call" | custom-call | bytes 8388608 | tf_op jit(solution)/shard_map/fetch/pallas_call | solution.py:215
  15.7 0.0 copy-start
  15.7 1.3 %copy-done = bf16[512,2048]{1,0:T(8,128)(2,1)} copy-done((bf16[512,2048]{1,0:T(8,128)(2,1)}, bf16[512,2048]{1,0:T(8,128)(2,1)S(1)}, u32[]{:S(2)}) %copy-start) | copy-done | bytes 2097176
  17.1 0.0 collective-permute-done.1.x_ref
  17.1 0.0 copy-done.5
  17.2 4.2 %collective-permute-start.3 = (f32[16,1024]{1,0:T(8,128)S(1)}, f32[16,1024]{1,0:T(8,128)S(1)}, u32[]{:S(2)}, u32[]{:S(2)}) collective-permute-start(f32[16,1024]{1,0:T(8,128)S(1)} %get-tuple-element.29), channel_id=1, source_target_pairs={{0,12},{1,13},{2,14},{3,15},{4,8},{5,9},{6,10},{7,11},{8,4},{9,5},... | collective-permute-start | bytes 196616 | tf_op jit(solution)/shard_map/ppermute | solution.py:333
  21.4 0.0 collective-permute-start.6
  21.4 0.6 collective-permute-start.5
  22.0 0.1 collective-permute-done.4
  22.2 2.9 %collective-permute-start.9 = (f32[16,1024]{1,0:T(8,128)S(1)}, f32[16,1024]{1,0:T(8,128)S(1)}, u32[]{:S(2)}, u32[]{:S(2)}) collective-permute-start(f32[16,1024]{1,0:T(8,128)S(1)} %get-tuple-element.26), channel_id=1, source_target_pairs={{0,8},{1,9},{2,10},{3,11},{4,12},{5,13},{6,14},{7,15},{8,0},{9,1},... | collective-permute-start | bytes 196616 | tf_op jit(solution)/shard_map/ppermute | solution.py:333
  25.1 1.6 %collective-permute-start.8 = (f32[16,1024]{1,0:T(8,128)S(1)}, f32[16,1024]{1,0:T(8,128)S(1)}, u32[]{:S(2)}, u32[]{:S(2)}) collective-permute-start(f32[16,1024]{1,0:T(8,128)S(1)} %get-tuple-element.27), channel_id=1, source_target_pairs={{0,4},{1,5},{2,6},{3,7},{4,0},{5,1},{6,2},{7,3},{8,12},{9,13},{10,... | collective-permute-start | bytes 196616 | tf_op jit(solution)/shard_map/ppermute | solution.py:333
  26.7 0.0 collective-permute-done.3.x_ref
  26.7 1.5 %collective-permute-start.7 = (f32[16,1024]{1,0:T(8,128)S(1)}, f32[16,1024]{1,0:T(8,128)S(1)}, u32[]{:S(2)}, u32[]{:S(2)}) collective-permute-start(f32[16,1024]{1,0:T(8,128)S(1)} %get-tuple-element.28), channel_id=1, source_target_pairs={{0,12},{1,13},{2,14},{3,15},{4,8},{5,9},{6,10},{7,11},{8,4},{9,5},... | collective-permute-start | bytes 196616 | tf_op jit(solution)/shard_map/ppermute | solution.py:333
  28.2 0.0 collective-permute-done.5.x_ref
  28.2 0.0 collective-permute-done.6.x_ref
  28.2 0.1 multiply_reduce_fusion.1
  28.4 4.4 %collective-permute-done.7.x_ref = f32[16,1024]{1,0:T(8,128)S(1)} collective-permute-done((f32[16,1024]{1,0:T(8,128)S(1)}, f32[16,1024]{1,0:T(8,128)S(1)}, u32[]{:S(2)}, u32[]{:S(2)}) %collective-permute-start.7) | collective-permute-done | bytes 65568 | tf_op jit(solution)/shard_map/ppermute | solution.py:333
  32.7 0.0 collective-permute-done.8.x_ref
  32.8 0.0 copy-done.2
  32.8 0.0 collective-permute-done.9.x_ref
  32.8 0.1 multiply_reduce_fusion
  32.9 0.1 collective-permute-start.11
  33.0 2.7 %collective-permute-start.10 = (bf16[16,2048]{1,0:T(8,128)(2,1)S(1)}, bf16[16,2048]{1,0:T(8,128)(2,1)S(1)}, u32[]{:S(2)}, u32[]{:S(2)}) collective-permute-start(bf16[16,2048]{1,0:T(8,128)(2,1)S(1)} %pad_maximum_fusion.3.refs_0_), channel_id=1, source_target_pairs={{0,12},{1,13},{2,14},{3,15},{4,8},{5,9},{6,10},{7,11},{8,4},{9,5},... | collective-permute-start | bytes 196616 | tf_op jit(solution)/shard_map/ppermute | solution.py:333
  35.8 0.7 %collective-permute-start.12 = (bf16[16,2048]{1,0:T(8,128)(2,1)S(1)}, bf16[16,2048]{1,0:T(8,128)(2,1)S(1)}, u32[]{:S(2)}, u32[]{:S(2)}) collective-permute-start(bf16[16,2048]{1,0:T(8,128)(2,1)S(1)} %pad_maximum_fusion.3.refs_0_), channel_id=1, source_target_pairs={{0,8},{1,9},{2,10},{3,11},{4,12},{5,13},{6,14},{7,15},{8,0},{9,1},... | collective-permute-start | bytes 196616 | tf_op jit(solution)/shard_map/ppermute | solution.py:333
  36.5 0.8 %collective-permute-done.11 = bf16[16,2048]{1,0:T(8,128)(2,1)S(1)} collective-permute-done((bf16[16,2048]{1,0:T(8,128)(2,1)S(1)}, bf16[16,2048]{1,0:T(8,128)(2,1)S(1)}, u32[]{:S(2)}, u32[]{:S(2)}) %collective-permute-start.11) | collective-permute-done | bytes 65568 | tf_op jit(solution)/shard_map/ppermute | solution.py:333
  37.3 2.0 %collective-permute-done.10 = bf16[16,2048]{1,0:T(8,128)(2,1)S(1)} collective-permute-done((bf16[16,2048]{1,0:T(8,128)(2,1)S(1)}, bf16[16,2048]{1,0:T(8,128)(2,1)S(1)}, u32[]{:S(2)}, u32[]{:S(2)}) %collective-permute-start.10) | collective-permute-done | bytes 65568 | tf_op jit(solution)/shard_map/ppermute | solution.py:333
  39.3 1.6 %collective-permute-start.15 = (bf16[48,2048]{1,0:T(8,128)(2,1)S(1)}, bf16[48,2048]{1,0:T(8,128)(2,1)S(1)}, u32[]{:S(2)}, u32[]{:S(2)}) collective-permute-start(bf16[48,2048]{1,0:T(8,128)(2,1)S(1)} %pad_maximum_fusion.2.refs_0_), channel_id=1, source_target_pairs={{0,2},{1,3},{2,0},{3,1},{4,6},{5,7},{6,4},{7,5},{8,10},{9,11},{10,... | collective-permute-start | bytes 589832 | tf_op jit(solution)/shard_map/ppermute | solution.py:333
  40.9 0.2 collective-permute-done.12.refs_1_
  41.0 1.5 %collective-permute-start.14 = (bf16[16,2048]{1,0:T(8,128)(2,1)S(1)}, bf16[16,2048]{1,0:T(8,128)(2,1)S(1)}, u32[]{:S(2)}, u32[]{:S(2)}) collective-permute-start(bf16[16,2048]{1,0:T(8,128)(2,1)S(1)} %collective-permute-done.12.refs_1_), channel_id=1, source_target_pairs={{0,2},{1,3},{2,0},{3,1},{4,6},{5,7},{6,4},{7,5},{8,10},{9,11},{10,... | collective-permute-start | bytes 196616 | tf_op jit(solution)/shard_map/ppermute | solution.py:333
  42.6 0.1 collective-permute-start.13
  42.7 0.8 %grad.3.refs_0_.refs_5_ = f32[64,512]{1,0:T(8,128)S(1)} custom-call(bf16[48,2048]{1,0:T(8,128)(2,1)S(1)} %pad_maximum_fusion.2.refs_0_, bf16[16,2048]{1,0:T(8,128)(2,1)S(1)} %collective-permute-done.12.refs_1_, bf16[512,2048]{1,0:T(8,128)(2,1)S(1)} %get-tuple-element.16.refs_2_), custom_call_target="tpu_custom_call" | custom-call | flops 134217728 | bytes 4194304 | tf_op jit(solution)/shard_map/grad/pallas_call | solution.py:285
  43.4 2.3 %collective-permute-done.14.x_ref = bf16[16,2048]{1,0:T(8,128)(2,1)S(1)} collective-permute-done((bf16[16,2048]{1,0:T(8,128)(2,1)S(1)}, bf16[16,2048]{1,0:T(8,128)(2,1)S(1)}, u32[]{:S(2)}, u32[]{:S(2)}) %collective-permute-start.14) | collective-permute-done | bytes 65568 | tf_op jit(solution)/shard_map/ppermute | solution.py:333
  45.7 0.0 collective-permute-done.15.refs_0_.refs_1_
  45.8 0.7 %pad_maximum_fusion.1 = bf16[64,2048]{1,0:T(8,128)(2,1)} fusion(bf16[16,2048]{1,0:T(8,128)(2,1)S(1)} %hold.18.refs_0_.refs_2_, bf16[48,2048]{1,0:T(8,128)(2,1)S(1)} %collective-permute-done.15.refs_0_.refs_1_), kind=kLoop, calls=%fused_computation.3 | loop fusion | flops 524288 | bytes 524288 | tf_op jit(solution)/shard_map/concatenate | solution.py:336
  46.5 0.0 collective-permute-start.16
  46.5 0.1 copy.17.refs_4_
  46.6 0.0 collective-permute-done.13.x_ref
  46.6 0.0 copy-start.1
  46.6 1.6 %copy-done.1 = bf16[512,2048]{1,0:T(8,128)(2,1)S(1)} copy-done((bf16[512,2048]{1,0:T(8,128)(2,1)S(1)}, bf16[512,2048]{1,0:T(8,128)(2,1)}, u32[]{:S(2)}) %copy-start.1) | copy-done | bytes 2097176
  48.2 0.0 copy-start.3
  48.2 1.6 %copy-done.3 = bf16[512,2048]{1,0:T(8,128)(2,1)S(1)} copy-done((bf16[512,2048]{1,0:T(8,128)(2,1)S(1)}, bf16[512,2048]{1,0:T(8,128)(2,1)}, u32[]{:S(2)}) %copy-start.3) | copy-done | bytes 2097176
  49.8 1.4 %grad.4.refs_2_ = f32[64,512]{1,0:T(8,128)S(1)} custom-call(bf16[64,2048]{1,0:T(8,128)(2,1)S(1)} %hold.19.refs_0_, bf16[48,2048]{1,0:T(8,128)(2,1)S(1)} %collective-permute-done.15.refs_0_.refs_1_, bf16[16,2048]{1,0:T(8,128)(2,1)S(1)} %hold.18.refs_0_.refs_2_, bf16[512,2048]{1,0:T(8,128)(2,1)S(1)} %copy-done.1, bf16[512,2048]{1,0:T(8,128)(2,1)S(1)} %copy-done.3, ...), custom_call_target="tpu_custom_call" | custom-call | flops 268435456 | bytes 8388608 | tf_op jit(solution)/shard_map/grad/pallas_call | solution.py:285
  51.2 0.0 collective-permute-done.16.refs_0_
  51.2 1.5 %grad.5 = f32[16,4,128]{2,1,0:T(4,128)} custom-call(bf16[64,2048]{1,0:T(8,128)(2,1)S(1)} %collective-permute-done.16.refs_0_, bf16[512,2048]{1,0:T(8,128)(2,1)S(1)} %get-tuple-element.17.refs_1_, f32[64,512]{1,0:T(8,128)S(1)} %grad.4.refs_2_, s32[64,64]{1,0:T(8,128)S(1)} %get-tuple-element.20.refs_3_, f32[16,1]{1,0:T(8,128)S(1)} %copy.17.refs_4_), custom_call_target="tpu_custom_call" | custom-call | flops 134217728 | bytes 4194304 | tf_op jit(solution)/shard_map/grad/pallas_call | solution.py:285
  52.7 5.1 %all-to-all-start = ((f32[16,4,128]{2,1,0:T(4,128)}), f32[16,4,128]{2,1,0:T(4,128)S(1)}, u32[]{:S(2)}, u32[]{:S(2)}) async-start(f32[16,4,128]{2,1,0:T(4,128)} %grad.5), calls=%async_computation | async-start | bytes 65536 | tf_op jit(solution)/shard_map/all_to_all | solution.py:402
  57.9 0.9 %own_rows.1 = bf16[4,8192]{1,0:T(4,128)(2,1)} custom-call(bf16[16,2048]{1,0:T(8,128)(2,1)S(1)} %pad_maximum_fusion.3.refs_0_, bf16[16,2048]{1,0:T(8,128)(2,1)S(1)} %slice.40.refs_1_, bf16[16,2048]{1,0:T(8,128)(2,1)S(1)} %slice.41.refs_2_, bf16[16,2048]{1,0:T(8,128)(2,1)S(1)} %slice.42.refs_3_), custom_call_target="tpu_custom_call" | custom-call | tf_op jit(solution)/shard_map/own_rows/pallas_call | solution.py:311
  58.7 5.7 %all-to-all-done = f32[16,4,128]{2,1,0:T(4,128)S(1)} async-done(((f32[16,4,128]{2,1,0:T(4,128)}), f32[16,4,128]{2,1,0:T(4,128)S(1)}, u32[]{:S(2)}, u32[]{:S(2)}) %all-to-all-start) | async-done | bytes 32800 | tf_op jit(solution)/shard_map/all_to_all | solution.py:402
  64.5 0.0 copy-start.6
  64.5 0.7 %multiply_reduce_fusion.2 = f32[4]{0:T(128)} fusion(f32[4,128]{1,0:T(4,128)S(1)} %reduce_sum.29), kind=kLoop, calls=%fused_computation.10 | loop fusion | flops 4 | bytes 32 | tf_op jit(solution)/shard_map/div | solution.py:403
  65.2 0.0 copy-done.6
  (25 shorter events, 0.4 us)
Async XLA Ops:
  4.3 2.5 %collective-permute-start = (f32[64,2048]{1,0:T(8,128)S(1)}, f32[64,2048]{1,0:T(8,128)S(1)}, u32[]{:S(2)}, u32[]{:S(2)}) collective-permute-start(f32[64,2048]{1,0:T(8,128)S(1)} %get-tuple-element.13), channel_id=1, source_target_pairs={{0,1},{1,0},{2,3},{3,2},{4,5},{5,4},{6,7},{7,6},{8,9},{9,8},{10,11... | collective-permute-start | bytes 1572872 | tf_op jit(solution)/shard_map/ppermute | solution.py:333
  4.8 7.1 %collective-permute-start.2 = (f32[64,2048]{1,0:T(8,128)S(1)}, f32[64,2048]{1,0:T(8,128)S(1)}, u32[]{:S(2)}, u32[]{:S(2)}) collective-permute-start(f32[64,2048]{1,0:T(8,128)S(1)} %get-tuple-element.14), channel_id=1, source_target_pairs={{0,1},{1,0},{2,3},{3,2},{4,5},{5,4},{6,7},{7,6},{8,9},{9,8},{10,11... | collective-permute-start | bytes 1572872 | tf_op jit(solution)/shard_map/ppermute | solution.py:333
  6.9 5.0 %copy-start.4 = (f32[64,2048]{1,0:T(8,128)}, f32[64,2048]{1,0:T(8,128)S(1)}, u32[]{:S(2)}) copy-start(f32[64,2048]{1,0:T(8,128)S(1)} %add.52) | copy-start | bytes 1572868
  6.9 10.1 %collective-permute-start.1 = (f32[64,1024]{1,0:T(8,128)S(1)}, f32[64,1024]{1,0:T(8,128)S(1)}, u32[]{:S(2)}, u32[]{:S(2)}) collective-permute-start(f32[64,1024]{1,0:T(8,128)S(1)} %slice.37.refs_3_), channel_id=1, source_target_pairs={{0,2},{1,3},{2,0},{3,1},{4,6},{5,7},{6,4},{7,5},{8,10},{9,11},{10,... | collective-permute-start | bytes 786440 | tf_op jit(solution)/shard_map/ppermute | solution.py:333
  12.0 5.1 %copy-start.5 = (f32[64,2048]{1,0:T(8,128)S(1)}, f32[64,2048]{1,0:T(8,128)}, u32[]{:S(2)}) copy-start(f32[64,2048]{1,0:T(8,128)} %copy-done.4) | copy-start | bytes 1572868
  12.0 10.1 %collective-permute-start.4 = (f32[64,1024]{1,0:T(8,128)S(1)}, f32[64,1024]{1,0:T(8,128)S(1)}, u32[]{:S(2)}, u32[]{:S(2)}) collective-permute-start(f32[64,1024]{1,0:T(8,128)S(1)} %slice.38._), channel_id=1, source_target_pairs={{0,2},{1,3},{2,0},{3,1},{4,6},{5,7},{6,4},{7,5},{8,10},{9,11},{10,... | collective-permute-start | bytes 786440 | tf_op jit(solution)/shard_map/ppermute | solution.py:333
  15.7 1.3 %copy-start = (bf16[512,2048]{1,0:T(8,128)(2,1)}, bf16[512,2048]{1,0:T(8,128)(2,1)S(1)}, u32[]{:S(2)}) copy-start(bf16[512,2048]{1,0:T(8,128)(2,1)S(1)} %get-tuple-element.18.refs_3_) | copy-start | bytes 6291460
  17.1 15.7 %copy-start.2 = (bf16[512,2048]{1,0:T(8,128)(2,1)}, bf16[512,2048]{1,0:T(8,128)(2,1)S(1)}, u32[]{:S(2)}) copy-start(bf16[512,2048]{1,0:T(8,128)(2,1)S(1)} %get-tuple-element.19.refs_4_) | copy-start | bytes 6291460
  17.2 9.5 %collective-permute-start.3 = (f32[16,1024]{1,0:T(8,128)S(1)}, f32[16,1024]{1,0:T(8,128)S(1)}, u32[]{:S(2)}, u32[]{:S(2)}) collective-permute-start(f32[16,1024]{1,0:T(8,128)S(1)} %get-tuple-element.29), channel_id=1, source_target_pairs={{0,12},{1,13},{2,14},{3,15},{4,8},{5,9},{6,10},{7,11},{8,4},{9,5},... | collective-permute-start | bytes 196616 | tf_op jit(solution)/shard_map/ppermute | solution.py:333
  21.4 6.8 %collective-permute-start.6 = (f32[16,1024]{1,0:T(8,128)S(1)}, f32[16,1024]{1,0:T(8,128)S(1)}, u32[]{:S(2)}, u32[]{:S(2)}) collective-permute-start(f32[16,1024]{1,0:T(8,128)S(1)} %get-tuple-element.30), channel_id=1, source_target_pairs={{0,8},{1,9},{2,10},{3,11},{4,12},{5,13},{6,14},{7,15},{8,0},{9,1},... | collective-permute-start | bytes 196616 | tf_op jit(solution)/shard_map/ppermute | solution.py:333
  21.4 6.8 %collective-permute-start.5 = (f32[16,1024]{1,0:T(8,128)S(1)}, f32[16,1024]{1,0:T(8,128)S(1)}, u32[]{:S(2)}, u32[]{:S(2)}) collective-permute-start(f32[16,1024]{1,0:T(8,128)S(1)} %get-tuple-element.31), channel_id=1, source_target_pairs={{0,4},{1,5},{2,6},{3,7},{4,0},{5,1},{6,2},{7,3},{8,12},{9,13},{10,... | collective-permute-start | bytes 196616 | tf_op jit(solution)/shard_map/ppermute | solution.py:333
  22.2 10.6 %collective-permute-start.9 = (f32[16,1024]{1,0:T(8,128)S(1)}, f32[16,1024]{1,0:T(8,128)S(1)}, u32[]{:S(2)}, u32[]{:S(2)}) collective-permute-start(f32[16,1024]{1,0:T(8,128)S(1)} %get-tuple-element.26), channel_id=1, source_target_pairs={{0,8},{1,9},{2,10},{3,11},{4,12},{5,13},{6,14},{7,15},{8,0},{9,1},... | collective-permute-start | bytes 196616 | tf_op jit(solution)/shard_map/ppermute | solution.py:333
  25.1 7.7 %collective-permute-start.8 = (f32[16,1024]{1,0:T(8,128)S(1)}, f32[16,1024]{1,0:T(8,128)S(1)}, u32[]{:S(2)}, u32[]{:S(2)}) collective-permute-start(f32[16,1024]{1,0:T(8,128)S(1)} %get-tuple-element.27), channel_id=1, source_target_pairs={{0,4},{1,5},{2,6},{3,7},{4,0},{5,1},{6,2},{7,3},{8,12},{9,13},{10,... | collective-permute-start | bytes 196616 | tf_op jit(solution)/shard_map/ppermute | solution.py:333
  26.7 6.1 %collective-permute-start.7 = (f32[16,1024]{1,0:T(8,128)S(1)}, f32[16,1024]{1,0:T(8,128)S(1)}, u32[]{:S(2)}, u32[]{:S(2)}) collective-permute-start(f32[16,1024]{1,0:T(8,128)S(1)} %get-tuple-element.28), channel_id=1, source_target_pairs={{0,12},{1,13},{2,14},{3,15},{4,8},{5,9},{6,10},{7,11},{8,4},{9,5},... | collective-permute-start | bytes 196616 | tf_op jit(solution)/shard_map/ppermute | solution.py:333
  32.9 4.3 %collective-permute-start.11 = (bf16[16,2048]{1,0:T(8,128)(2,1)S(1)}, bf16[16,2048]{1,0:T(8,128)(2,1)S(1)}, u32[]{:S(2)}, u32[]{:S(2)}) collective-permute-start(bf16[16,2048]{1,0:T(8,128)(2,1)S(1)} %pad_maximum_fusion.3.refs_0_), channel_id=1, source_target_pairs={{0,4},{1,5},{2,6},{3,7},{4,0},{5,1},{6,2},{7,3},{8,12},{9,13},{10,... | collective-permute-start | bytes 196616 | tf_op jit(solution)/shard_map/ppermute | solution.py:333
  33.0 6.2 %collective-permute-start.10 = (bf16[16,2048]{1,0:T(8,128)(2,1)S(1)}, bf16[16,2048]{1,0:T(8,128)(2,1)S(1)}, u32[]{:S(2)}, u32[]{:S(2)}) collective-permute-start(bf16[16,2048]{1,0:T(8,128)(2,1)S(1)} %pad_maximum_fusion.3.refs_0_), channel_id=1, source_target_pairs={{0,12},{1,13},{2,14},{3,15},{4,8},{5,9},{6,10},{7,11},{8,4},{9,5},... | collective-permute-start | bytes 196616 | tf_op jit(solution)/shard_map/ppermute | solution.py:333
  35.8 5.3 %collective-permute-start.12 = (bf16[16,2048]{1,0:T(8,128)(2,1)S(1)}, bf16[16,2048]{1,0:T(8,128)(2,1)S(1)}, u32[]{:S(2)}, u32[]{:S(2)}) collective-permute-start(bf16[16,2048]{1,0:T(8,128)(2,1)S(1)} %pad_maximum_fusion.3.refs_0_), channel_id=1, source_target_pairs={{0,8},{1,9},{2,10},{3,11},{4,12},{5,13},{6,14},{7,15},{8,0},{9,1},... | collective-permute-start | bytes 196616 | tf_op jit(solution)/shard_map/ppermute | solution.py:333
  39.3 6.4 %collective-permute-start.15 = (bf16[48,2048]{1,0:T(8,128)(2,1)S(1)}, bf16[48,2048]{1,0:T(8,128)(2,1)S(1)}, u32[]{:S(2)}, u32[]{:S(2)}) collective-permute-start(bf16[48,2048]{1,0:T(8,128)(2,1)S(1)} %pad_maximum_fusion.2.refs_0_), channel_id=1, source_target_pairs={{0,2},{1,3},{2,0},{3,1},{4,6},{5,7},{6,4},{7,5},{8,10},{9,11},{10,... | collective-permute-start | bytes 589832 | tf_op jit(solution)/shard_map/ppermute | solution.py:333
  41.0 4.7 %collective-permute-start.14 = (bf16[16,2048]{1,0:T(8,128)(2,1)S(1)}, bf16[16,2048]{1,0:T(8,128)(2,1)S(1)}, u32[]{:S(2)}, u32[]{:S(2)}) collective-permute-start(bf16[16,2048]{1,0:T(8,128)(2,1)S(1)} %collective-permute-done.12.refs_1_), channel_id=1, source_target_pairs={{0,2},{1,3},{2,0},{3,1},{4,6},{5,7},{6,4},{7,5},{8,10},{9,11},{10,... | collective-permute-start | bytes 196616 | tf_op jit(solution)/shard_map/ppermute | solution.py:333
  42.6 4.0 %collective-permute-start.13 = (bf16[64,2048]{1,0:T(8,128)(2,1)S(1)}, bf16[64,2048]{1,0:T(8,128)(2,1)S(1)}, u32[]{:S(2)}, u32[]{:S(2)}) collective-permute-start(bf16[64,2048]{1,0:T(8,128)(2,1)S(1)} %pad_maximum_fusion), channel_id=1, source_target_pairs={{0,1},{1,0},{2,3},{3,2},{4,5},{5,4},{6,7},{7,6},{8,9},{9,8},{10,11... | collective-permute-start | bytes 786440 | tf_op jit(solution)/shard_map/ppermute | solution.py:333
  46.5 4.7 %collective-permute-start.16 = (bf16[64,2048]{1,0:T(8,128)(2,1)}, bf16[64,2048]{1,0:T(8,128)(2,1)S(1)}, u32[]{:S(2)}, u32[]{:S(2)}) collective-permute-start(bf16[64,2048]{1,0:T(8,128)(2,1)} %pad_maximum_fusion.1), channel_id=1, source_target_pairs={{0,1},{1,0},{2,3},{3,2},{4,5},{5,4},{6,7},{7,6},{8,9},{9,8},{10,11... | collective-permute-start | bytes 786440 | tf_op jit(solution)/shard_map/ppermute | solution.py:333
  46.6 1.6 %copy-start.1 = (bf16[512,2048]{1,0:T(8,128)(2,1)S(1)}, bf16[512,2048]{1,0:T(8,128)(2,1)}, u32[]{:S(2)}) copy-start(bf16[512,2048]{1,0:T(8,128)(2,1)} %copy-done) | copy-start | bytes 6291460
  48.2 1.6 %copy-start.3 = (bf16[512,2048]{1,0:T(8,128)(2,1)S(1)}, bf16[512,2048]{1,0:T(8,128)(2,1)}, u32[]{:S(2)}) copy-start(bf16[512,2048]{1,0:T(8,128)(2,1)} %copy-done.2) | copy-start | bytes 6291460
  52.7 11.8 %all-to-all-start = ((f32[16,4,128]{2,1,0:T(4,128)}), f32[16,4,128]{2,1,0:T(4,128)S(1)}, u32[]{:S(2)}, u32[]{:S(2)}) async-start(f32[16,4,128]{2,1,0:T(4,128)} %grad.5), calls=%async_computation | async-start | bytes 65536 | tf_op jit(solution)/shard_map/all_to_all | solution.py:402
  64.5 0.7 %copy-start.6 = (f32[4,128]{1,0:T(4,128)}, f32[4,128]{1,0:T(4,128)S(1)}, u32[]{:S(2)}) copy-start(f32[4,128]{1,0:T(4,128)S(1)} %reduce_sum.29) | copy-start | bytes 6148

commit v15 on v14

--- a/solution.py
+++ b/solution.py
@@ -53,7 +53,7 @@
 
 
 def params():
-    return pltpu.CompilerParams(vmem_limit_bytes=24 * 1024 * 1024)
+    return pltpu.CompilerParams(vmem_limit_bytes=12 * 1024 * 1024)
 
 
 def in_hbm(x):
@@ -394,7 +394,8 @@
 
     far = [(at, [hold(e, last[-1][1][-1])]) for at, (e,) in to_core(near)]
     far_last = to_core(last)
-    totals = grad(n, rows, far + last, columns, totals)
+    totals = grad(n, rows, far, columns, totals)
+    totals = grad(n, rows, last, columns, totals)
     back = grad(n, rows, far_last, columns, totals, (in_vmem(ids), loss))
     pieces = near + far + last + far_last
     error = own_rows(n, [at for at, _ in pieces], own, width, [e[0][:group] for _, e in pieces])

time: 65.5 us -> 63.5 us (0.969)
  local copies, waits for them, and re-layouts: 4.72 us -> 1.87 us
  waiting for transfers between devices: 15.4 us -> 17.3 us
  starting transfers between devices: 26.4 us -> 25.3 us
    unnamed x14, local copies, waits for them, and re-layouts: 4.52 us -> 1.67 us
    ppermute x17, waiting for transfers between devices: 9.7 us -> 11.6 us  [swap(): return lax.ppermute(x, 'lat', pairs(n, dz, dy, dc))]
    pallas_call x3 -> x4, Pallas kernels: 3.62 us -> 3.74 us  [grad(): pl.pallas_call(functools.partial(grad_kernel, n, counts, prev is not None...]
  transfers between devices with their start and end apart: 18 -> 18, of which waited for: 7 -> 8; matrix products, arithmetic and copies ran while one was open for 2% -> 2% of each run, Pallas kernels for 16% -> 17%
where the time goes in v15:
time: 63.5 us; the launch traced here: 63.2 us
  starting transfers between devices  25.3 us (40%)
  waiting for transfers between devices  17.3 us (27%)
  Pallas kernels  15.8 us (25%)
  other arithmetic  1.95 us (3%)
  local copies, waits for them, and re-layouts  1.87 us (3%)
  between operations  0.97 us (2%)
    ppermute x17, starting transfers between devices, swap(): return lax.ppermute(x, 'lat', pairs(n, dz, dy, dc))  20.7 us
    ppermute x17, waiting for transfers between devices, swap(): return lax.ppermute(x, 'lat', pairs(n, dz, dy, dc))  11.6 us
    pallas_call x3, Pallas kernels, decode(): pl.pallas_call(functools.partial(decode_kernel, n, rows // n, chunks, par...  7.51 us
    all_to_all x1, waiting for transfers between devices, local(): back = jnp.sum(lax.all_to_all(back, 'lat', 0, 0, tiled=True), axis=0)  5.74 us
    all_to_all x1, starting transfers between devices, local(): back = jnp.sum(lax.all_to_all(back, 'lat', 0, 0, tiled=True), axis=0)  4.52 us
    pallas_call x4, Pallas kernels, grad(): pl.pallas_call(functools.partial(grad_kernel, n, counts, prev is not None...  3.74 us
    pallas_call x1, Pallas kernels, fetch(): pl.pallas_call(functools.partial(fetch_kernel, n, places), out_shape=[blo...  3.54 us
    unnamed x14, local copies, waits for them, and re-layouts  1.67 us
  transfers between devices with their start and end apart: 18, of which 8 were waited for; matrix products, arithmetic and copies ran while one was open for 2% of the time, Pallas kernels for 17%

profile of v15, /device:TPU:0, one launch (start us, length us, event | category | flops | bytes accessed | tf_op | source)
XLA Modules:
  0.0 63.2 jit_solution(9281780927223538640)
XLA Ops:
  0.6 3.7 %decode.3 = (f32[64,2048]{1,0:T(8,128)S(1)}, f32[64,2048]{1,0:T(8,128)S(1)}, bf16[64,512]{1,0:T(8,128)(2,1)S(1)}) custom-call(s32[64,64]{1,0:T(8,128)} %ids_hbm.1, bf16[64,64]{1,0:T(8,128)(2,1)} %refs_1_.3, bf16[512,8192]{1,0:T(8,128)(2,1)} %decoder_hbm.1, bf16[4,8192]{1,0:T(4,128)(2,1)} %refs_2_.5), custom_call_target="tpu_custom_call" | custom-call | flops 268435456 | bytes 8388608 | tf_op jit(solution)/shard_map/decode/pallas_call | solution.py:187
  4.3 0.5 collective-permute-start
  4.8 0.1 collective-permute-start.2
  4.9 1.9 %decode.4 = f32[64,2048]{1,0:T(8,128)S(1)} custom-call(bf16[64,512]{1,0:T(8,128)(2,1)S(1)} %get-tuple-element.12.refs_0_, bf16[512,8192]{1,0:T(8,128)(2,1)} %decoder_hbm.1, bf16[4,8192]{1,0:T(4,128)(2,1)} %refs_2_.5), custom_call_target="tpu_custom_call" | custom-call | flops 134217728 | bytes 4194304 | tf_op jit(solution)/shard_map/decode/pallas_call | solution.py:187
  6.8 0.0 collective-permute-done
  6.8 0.1 add.52
  6.9 0.0 copy-start.4
  6.9 3.0 %collective-permute-start.1 = (f32[64,1024]{1,0:T(8,128)S(1)}, f32[64,1024]{1,0:T(8,128)S(1)}, u32[]{:S(2)}, u32[]{:S(2)}) collective-permute-start(f32[64,1024]{1,0:T(8,128)S(1)} %slice.37.refs_3_), channel_id=1, source_target_pairs={{0,2},{1,3},{2,0},{3,1},{4,6},{5,7},{6,4},{7,5},{8,10},{9,11},{10,... | collective-permute-start | bytes 786440 | tf_op jit(solution)/shard_map/ppermute | solution.py:333
  10.0 1.9 %decode.5 = f32[64,2048]{1,0:T(8,128)S(1)} custom-call(bf16[64,512]{1,0:T(8,128)(2,1)S(1)} %get-tuple-element.12.refs_0_, bf16[512,8192]{1,0:T(8,128)(2,1)} %decoder_hbm.1, bf16[4,8192]{1,0:T(4,128)(2,1)} %refs_2_.5, f32[64,1024]{1,0:T(8,128)S(1)} %slice.37.refs_3_), custom_call_target="tpu_custom_call" | custom-call | flops 134217728 | bytes 4194304 | tf_op jit(solution)/shard_map/decode/pallas_call | solution.py:187
  11.9 0.0 copy-done.4
  11.9 0.0 collective-permute-done.2
  11.9 0.1 add.53
  12.0 0.0 copy-start.5
  12.0 0.2 collective-permute-start.4
  12.2 3.5 %fetch.1 = (bf16[512,2048]{1,0:T(8,128)(2,1)S(1)}, bf16[512,2048]{1,0:T(8,128)(2,1)S(1)}, bf16[512,2048]{1,0:T(8,128)(2,1)S(1)}, bf16[512,2048]{1,0:T(8,128)(2,1...) custom-call(bf16[512,8192]{1,0:T(8,128)(2,1)} %decoder_hbm.1, s32[64,64]{1,0:T(8,128)} %ids_hbm.1, f32[64,1024]{1,0:T(8,128)S(1)} %slice.38._), custom_call_target="tpu_custom_call" | custom-call | bytes 8388608 | tf_op jit(solution)/shard_map/fetch/pallas_call | solution.py:215
  15.7 0.0 copy-start
  15.7 0.0 copy-start.2
  15.7 1.3 %collective-permute-done.1.x_ref = f32[64,1024]{1,0:T(8,128)S(1)} collective-permute-done((f32[64,1024]{1,0:T(8,128)S(1)}, f32[64,1024]{1,0:T(8,128)S(1)}, u32[]{:S(2)}, u32[]{:S(2)}) %collective-permute-start.1) | collective-permute-done | bytes 262176 | tf_op jit(solution)/shard_map/ppermute | solution.py:333
  17.1 0.0 copy-done.5
  17.2 4.2 %collective-permute-start.3 = (f32[16,1024]{1,0:T(8,128)S(1)}, f32[16,1024]{1,0:T(8,128)S(1)}, u32[]{:S(2)}, u32[]{:S(2)}) collective-permute-start(f32[16,1024]{1,0:T(8,128)S(1)} %get-tuple-element.29), channel_id=1, source_target_pairs={{0,12},{1,13},{2,14},{3,15},{4,8},{5,9},{6,10},{7,11},{8,4},{9,5},... | collective-permute-start | bytes 196616 | tf_op jit(solution)/shard_map/ppermute | solution.py:333
  21.4 0.0 collective-permute-start.6
  21.4 0.6 %collective-permute-start.5 = (f32[16,1024]{1,0:T(8,128)S(1)}, f32[16,1024]{1,0:T(8,128)S(1)}, u32[]{:S(2)}, u32[]{:S(2)}) collective-permute-start(f32[16,1024]{1,0:T(8,128)S(1)} %get-tuple-element.31), channel_id=1, source_target_pairs={{0,4},{1,5},{2,6},{3,7},{4,0},{5,1},{6,2},{7,3},{8,12},{9,13},{10,... | collective-permute-start | bytes 196616 | tf_op jit(solution)/shard_map/ppermute | solution.py:333
  22.0 0.1 collective-permute-done.4
  22.2 2.9 %collective-permute-start.9 = (f32[16,1024]{1,0:T(8,128)S(1)}, f32[16,1024]{1,0:T(8,128)S(1)}, u32[]{:S(2)}, u32[]{:S(2)}) collective-permute-start(f32[16,1024]{1,0:T(8,128)S(1)} %get-tuple-element.26), channel_id=1, source_target_pairs={{0,8},{1,9},{2,10},{3,11},{4,12},{5,13},{6,14},{7,15},{8,0},{9,1},... | collective-permute-start | bytes 196616 | tf_op jit(solution)/shard_map/ppermute | solution.py:333
  25.1 1.6 %collective-permute-start.8 = (f32[16,1024]{1,0:T(8,128)S(1)}, f32[16,1024]{1,0:T(8,128)S(1)}, u32[]{:S(2)}, u32[]{:S(2)}) collective-permute-start(f32[16,1024]{1,0:T(8,128)S(1)} %get-tuple-element.27), channel_id=1, source_target_pairs={{0,4},{1,5},{2,6},{3,7},{4,0},{5,1},{6,2},{7,3},{8,12},{9,13},{10,... | collective-permute-start | bytes 196616 | tf_op jit(solution)/shard_map/ppermute | solution.py:333
  26.7 0.0 collective-permute-done.3.x_ref
  26.7 0.9 %collective-permute-start.7 = (f32[16,1024]{1,0:T(8,128)S(1)}, f32[16,1024]{1,0:T(8,128)S(1)}, u32[]{:S(2)}, u32[]{:S(2)}) collective-permute-start(f32[16,1024]{1,0:T(8,128)S(1)} %get-tuple-element.28), channel_id=1, source_target_pairs={{0,12},{1,13},{2,14},{3,15},{4,8},{5,9},{6,10},{7,11},{8,4},{9,5},... | collective-permute-start | bytes 196616 | tf_op jit(solution)/shard_map/ppermute | solution.py:333
  27.6 0.0 collective-permute-done.5.x_ref
  27.6 0.1 collective-permute-done.6.x_ref
  27.8 0.1 multiply_reduce_fusion.1
  27.9 4.8 %collective-permute-done.7.x_ref = f32[16,1024]{1,0:T(8,128)S(1)} collective-permute-done((f32[16,1024]{1,0:T(8,128)S(1)}, f32[16,1024]{1,0:T(8,128)S(1)}, u32[]{:S(2)}, u32[]{:S(2)}) %collective-permute-start.7) | collective-permute-done | bytes 65568 | tf_op jit(solution)/shard_map/ppermute | solution.py:333
  32.7 0.0 collective-permute-done.8.x_ref
  32.8 0.0 copy-done
  32.8 0.0 copy-done.2
  32.8 0.0 collective-permute-done.9.x_ref
  32.8 0.1 multiply_reduce_fusion
  33.0 0.1 collective-permute-start.11
  33.0 2.2 %collective-permute-start.10 = (bf16[16,2048]{1,0:T(8,128)(2,1)S(1)}, bf16[16,2048]{1,0:T(8,128)(2,1)S(1)}, u32[]{:S(2)}, u32[]{:S(2)}) collective-permute-start(bf16[16,2048]{1,0:T(8,128)(2,1)S(1)} %pad_maximum_fusion.3.refs_0_), channel_id=1, source_target_pairs={{0,12},{1,13},{2,14},{3,15},{4,8},{5,9},{6,10},{7,11},{8,4},{9,5},... | collective-permute-start | bytes 196616 | tf_op jit(solution)/shard_map/ppermute | solution.py:333
  35.3 1.2 %collective-permute-start.12 = (bf16[16,2048]{1,0:T(8,128)(2,1)S(1)}, bf16[16,2048]{1,0:T(8,128)(2,1)S(1)}, u32[]{:S(2)}, u32[]{:S(2)}) collective-permute-start(bf16[16,2048]{1,0:T(8,128)(2,1)S(1)} %pad_maximum_fusion.3.refs_0_), channel_id=1, source_target_pairs={{0,8},{1,9},{2,10},{3,11},{4,12},{5,13},{6,14},{7,15},{8,0},{9,1},... | collective-permute-start | bytes 196616 | tf_op jit(solution)/shard_map/ppermute | solution.py:333
  36.5 1.4 %collective-permute-done.11 = bf16[16,2048]{1,0:T(8,128)(2,1)S(1)} collective-permute-done((bf16[16,2048]{1,0:T(8,128)(2,1)S(1)}, bf16[16,2048]{1,0:T(8,128)(2,1)S(1)}, u32[]{:S(2)}, u32[]{:S(2)}) %collective-permute-start.11) | collective-permute-done | bytes 65568 | tf_op jit(solution)/shard_map/ppermute | solution.py:333
  37.9 1.3 %collective-permute-done.10 = bf16[16,2048]{1,0:T(8,128)(2,1)S(1)} collective-permute-done((bf16[16,2048]{1,0:T(8,128)(2,1)S(1)}, bf16[16,2048]{1,0:T(8,128)(2,1)S(1)}, u32[]{:S(2)}, u32[]{:S(2)}) %collective-permute-start.10) | collective-permute-done | bytes 65568 | tf_op jit(solution)/shard_map/ppermute | solution.py:333
  39.3 1.6 %collective-permute-start.15 = (bf16[48,2048]{1,0:T(8,128)(2,1)S(1)}, bf16[48,2048]{1,0:T(8,128)(2,1)S(1)}, u32[]{:S(2)}, u32[]{:S(2)}) collective-permute-start(bf16[48,2048]{1,0:T(8,128)(2,1)S(1)} %pad_maximum_fusion.2.refs_0_), channel_id=1, source_target_pairs={{0,2},{1,3},{2,0},{3,1},{4,6},{5,7},{6,4},{7,5},{8,10},{9,11},{10,... | collective-permute-start | bytes 589832 | tf_op jit(solution)/shard_map/ppermute | solution.py:333
  40.9 0.0 collective-permute-done.12.refs_1_
  40.9 1.5 %collective-permute-start.14 = (bf16[16,2048]{1,0:T(8,128)(2,1)S(1)}, bf16[16,2048]{1,0:T(8,128)(2,1)S(1)}, u32[]{:S(2)}, u32[]{:S(2)}) collective-permute-start(bf16[16,2048]{1,0:T(8,128)(2,1)S(1)} %collective-permute-done.12.refs_1_), channel_id=1, source_target_pairs={{0,2},{1,3},{2,0},{3,1},{4,6},{5,7},{6,4},{7,5},{8,10},{9,11},{10,... | collective-permute-start | bytes 196616 | tf_op jit(solution)/shard_map/ppermute | solution.py:333
  42.4 0.1 collective-permute-start.13
  42.5 0.8 %grad.4.refs_0_.refs_2_ = f32[64,512]{1,0:T(8,128)S(1)} custom-call(bf16[48,2048]{1,0:T(8,128)(2,1)S(1)} %pad_maximum_fusion.2.refs_0_, bf16[16,2048]{1,0:T(8,128)(2,1)S(1)} %collective-permute-done.12.refs_1_, bf16[512,2048]{1,0:T(8,128)(2,1)S(1)} %get-tuple-element.16.refs_2_), custom_call_target="tpu_custom_call" | custom-call | flops 134217728 | bytes 4194304 | tf_op jit(solution)/shard_map/grad/pallas_call | solution.py:285
  43.2 2.5 %collective-permute-done.14.x_ref = bf16[16,2048]{1,0:T(8,128)(2,1)S(1)} collective-permute-done((bf16[16,2048]{1,0:T(8,128)(2,1)S(1)}, bf16[16,2048]{1,0:T(8,128)(2,1)S(1)}, u32[]{:S(2)}, u32[]{:S(2)}) %collective-permute-start.14) | collective-permute-done | bytes 65568 | tf_op jit(solution)/shard_map/ppermute | solution.py:333
  45.7 0.0 collective-permute-done.15.refs_0_
  45.8 0.7 %pad_maximum_fusion.1 = bf16[64,2048]{1,0:T(8,128)(2,1)} fusion(bf16[16,2048]{1,0:T(8,128)(2,1)S(1)} %hold.18.refs_0_.refs_1_, bf16[48,2048]{1,0:T(8,128)(2,1)S(1)} %collective-permute-done.15.refs_0_), kind=kLoop, calls=%fused_computation.3 | loop fusion | flops 524288 | bytes 524288 | tf_op jit(solution)/shard_map/concatenate | solution.py:336
  46.5 0.0 collective-permute-start.16
  46.5 0.1 copy.17.refs_4_
  46.6 0.0 collective-permute-done.13.x_ref
  46.6 0.0 copy-start.1
  46.7 1.6 %copy-done.1 = bf16[512,2048]{1,0:T(8,128)(2,1)S(1)} copy-done((bf16[512,2048]{1,0:T(8,128)(2,1)S(1)}, bf16[512,2048]{1,0:T(8,128)(2,1)}, u32[]{:S(2)}) %copy-start.1) | copy-done | bytes 2097176
  48.2 0.8 %grad.5.refs_3_ = f32[64,512]{1,0:T(8,128)S(1)} custom-call(bf16[64,2048]{1,0:T(8,128)(2,1)S(1)} %hold.19.refs_0_, bf16[512,2048]{1,0:T(8,128)(2,1)S(1)} %copy-done.1, f32[64,512]{1,0:T(8,128)S(1)} %grad.4.refs_0_.refs_2_), custom_call_target="tpu_custom_call" | custom-call | flops 134217728 | bytes 4194304 | tf_op jit(solution)/shard_map/grad/pallas_call | solution.py:285
  49.0 0.8 %grad.6.refs_2_ = f32[64,512]{1,0:T(8,128)S(1)} custom-call(bf16[48,2048]{1,0:T(8,128)(2,1)S(1)} %collective-permute-done.15.refs_0_, bf16[16,2048]{1,0:T(8,128)(2,1)S(1)} %hold.18.refs_0_.refs_1_, bf16[512,2048]{1,0:T(8,128)(2,1)S(1)} %get-tuple-element.18.refs_2_, f32[64,512]{1,0:T(8,128)S(1)} %grad.5.refs_3_), custom_call_target="tpu_custom_call" | custom-call | flops 134217728 | bytes 4194304 | tf_op jit(solution)/shard_map/grad/pallas_call | solution.py:285
  49.7 0.0 collective-permute-done.16.refs_0_
  49.8 0.1 copy-done.3
  49.8 1.5 %grad.7 = f32[16,4,128]{2,1,0:T(4,128)} custom-call(bf16[64,2048]{1,0:T(8,128)(2,1)S(1)} %collective-permute-done.16.refs_0_, bf16[512,2048]{1,0:T(8,128)(2,1)S(1)} %copy-done.3, f32[64,512]{1,0:T(8,128)S(1)} %grad.6.refs_2_, s32[64,64]{1,0:T(8,128)S(1)} %get-tuple-element.20.refs_3_, f32[16,1]{1,0:T(8,128)S(1)} %copy.17.refs_4_), custom_call_target="tpu_custom_call" | custom-call | flops 134217728 | bytes 4194304 | tf_op jit(solution)/shard_map/grad/pallas_call | solution.py:285
  51.3 4.5 %all-to-all-start = ((f32[16,4,128]{2,1,0:T(4,128)}), f32[16,4,128]{2,1,0:T(4,128)S(1)}, u32[]{:S(2)}, u32[]{:S(2)}) async-start(f32[16,4,128]{2,1,0:T(4,128)} %grad.7), calls=%async_computation | async-start | bytes 65536 | tf_op jit(solution)/shard_map/all_to_all | solution.py:403
  55.9 0.8 %own_rows.1 = bf16[4,8192]{1,0:T(4,128)(2,1)} custom-call(bf16[16,2048]{1,0:T(8,128)(2,1)S(1)} %pad_maximum_fusion.3.refs_0_, bf16[16,2048]{1,0:T(8,128)(2,1)S(1)} %slice.40.refs_1_, bf16[16,2048]{1,0:T(8,128)(2,1)S(1)} %slice.41.refs_2_, bf16[16,2048]{1,0:T(8,128)(2,1)S(1)} %slice.42.refs_3_), custom_call_target="tpu_custom_call" | custom-call | tf_op jit(solution)/shard_map/own_rows/pallas_call | solution.py:311
  56.7 5.7 %all-to-all-done = f32[16,4,128]{2,1,0:T(4,128)S(1)} async-done(((f32[16,4,128]{2,1,0:T(4,128)}), f32[16,4,128]{2,1,0:T(4,128)S(1)}, u32[]{:S(2)}, u32[]{:S(2)}) %all-to-all-start) | async-done | bytes 32800 | tf_op jit(solution)/shard_map/all_to_all | solution.py:403
  62.5 0.7 %multiply_reduce_fusion.2 = f32[4]{0:T(128)} fusion(f32[4,128]{1,0:T(4,128)S(1)} %reduce_sum.29), kind=kLoop, calls=%fused_computation.10 | loop fusion | flops 4 | bytes 32 | tf_op jit(solution)/shard_map/div | solution.py:404
  63.2 0.0 copy-done.6
  (26 shorter events, 0.4 us)
Async XLA Ops:
  4.3 2.5 %collective-permute-start = (f32[64,2048]{1,0:T(8,128)S(1)}, f32[64,2048]{1,0:T(8,128)S(1)}, u32[]{:S(2)}, u32[]{:S(2)}) collective-permute-start(f32[64,2048]{1,0:T(8,128)S(1)} %get-tuple-element.13), channel_id=1, source_target_pairs={{0,1},{1,0},{2,3},{3,2},{4,5},{5,4},{6,7},{7,6},{8,9},{9,8},{10,11... | collective-permute-start | bytes 1572872 | tf_op jit(solution)/shard_map/ppermute | solution.py:333
  4.8 7.1 %collective-permute-start.2 = (f32[64,2048]{1,0:T(8,128)S(1)}, f32[64,2048]{1,0:T(8,128)S(1)}, u32[]{:S(2)}, u32[]{:S(2)}) collective-permute-start(f32[64,2048]{1,0:T(8,128)S(1)} %get-tuple-element.14), channel_id=1, source_target_pairs={{0,1},{1,0},{2,3},{3,2},{4,5},{5,4},{6,7},{7,6},{8,9},{9,8},{10,11... | collective-permute-start | bytes 1572872 | tf_op jit(solution)/shard_map/ppermute | solution.py:333
  6.9 5.0 %copy-start.4 = (f32[64,2048]{1,0:T(8,128)}, f32[64,2048]{1,0:T(8,128)S(1)}, u32[]{:S(2)}) copy-start(f32[64,2048]{1,0:T(8,128)S(1)} %add.52) | copy-start | bytes 1572868
  6.9 10.1 %collective-permute-start.1 = (f32[64,1024]{1,0:T(8,128)S(1)}, f32[64,1024]{1,0:T(8,128)S(1)}, u32[]{:S(2)}, u32[]{:S(2)}) collective-permute-start(f32[64,1024]{1,0:T(8,128)S(1)} %slice.37.refs_3_), channel_id=1, source_target_pairs={{0,2},{1,3},{2,0},{3,1},{4,6},{5,7},{6,4},{7,5},{8,10},{9,11},{10,... | collective-permute-start | bytes 786440 | tf_op jit(solution)/shard_map/ppermute | solution.py:333
  12.0 5.1 %copy-start.5 = (f32[64,2048]{1,0:T(8,128)S(1)}, f32[64,2048]{1,0:T(8,128)}, u32[]{:S(2)}) copy-start(f32[64,2048]{1,0:T(8,128)} %copy-done.4) | copy-start | bytes 1572868
  12.0 10.1 %collective-permute-start.4 = (f32[64,1024]{1,0:T(8,128)S(1)}, f32[64,1024]{1,0:T(8,128)S(1)}, u32[]{:S(2)}, u32[]{:S(2)}) collective-permute-start(f32[64,1024]{1,0:T(8,128)S(1)} %slice.38._), channel_id=1, source_target_pairs={{0,2},{1,3},{2,0},{3,1},{4,6},{5,7},{6,4},{7,5},{8,10},{9,11},{10,... | collective-permute-start | bytes 786440 | tf_op jit(solution)/shard_map/ppermute | solution.py:333
  15.7 17.0 %copy-start = (bf16[512,2048]{1,0:T(8,128)(2,1)}, bf16[512,2048]{1,0:T(8,128)(2,1)S(1)}, u32[]{:S(2)}) copy-start(bf16[512,2048]{1,0:T(8,128)(2,1)S(1)} %get-tuple-element.19.refs_1_) | copy-start | bytes 6291460
  15.7 17.0 %copy-start.2 = (bf16[512,2048]{1,0:T(8,128)(2,1)}, bf16[512,2048]{1,0:T(8,128)(2,1)S(1)}, u32[]{:S(2)}) copy-start(bf16[512,2048]{1,0:T(8,128)(2,1)S(1)} %get-tuple-element.17.refs_1_) | copy-start | bytes 6291460
  17.2 9.5 %collective-permute-start.3 = (f32[16,1024]{1,0:T(8,128)S(1)}, f32[16,1024]{1,0:T(8,128)S(1)}, u32[]{:S(2)}, u32[]{:S(2)}) collective-permute-start(f32[16,1024]{1,0:T(8,128)S(1)} %get-tuple-element.29), channel_id=1, source_target_pairs={{0,12},{1,13},{2,14},{3,15},{4,8},{5,9},{6,10},{7,11},{8,4},{9,5},... | collective-permute-start | bytes 196616 | tf_op jit(solution)/shard_map/ppermute | solution.py:333
  21.4 6.4 %collective-permute-start.6 = (f32[16,1024]{1,0:T(8,128)S(1)}, f32[16,1024]{1,0:T(8,128)S(1)}, u32[]{:S(2)}, u32[]{:S(2)}) collective-permute-start(f32[16,1024]{1,0:T(8,128)S(1)} %get-tuple-element.30), channel_id=1, source_target_pairs={{0,8},{1,9},{2,10},{3,11},{4,12},{5,13},{6,14},{7,15},{8,0},{9,1},... | collective-permute-start | bytes 196616 | tf_op jit(solution)/shard_map/ppermute | solution.py:333
  21.4 6.2 %collective-permute-start.5 = (f32[16,1024]{1,0:T(8,128)S(1)}, f32[16,1024]{1,0:T(8,128)S(1)}, u32[]{:S(2)}, u32[]{:S(2)}) collective-permute-start(f32[16,1024]{1,0:T(8,128)S(1)} %get-tuple-element.31), channel_id=1, source_target_pairs={{0,4},{1,5},{2,6},{3,7},{4,0},{5,1},{6,2},{7,3},{8,12},{9,13},{10,... | collective-permute-start | bytes 196616 | tf_op jit(solution)/shard_map/ppermute | solution.py:333
  22.2 10.6 %collective-permute-start.9 = (f32[16,1024]{1,0:T(8,128)S(1)}, f32[16,1024]{1,0:T(8,128)S(1)}, u32[]{:S(2)}, u32[]{:S(2)}) collective-permute-start(f32[16,1024]{1,0:T(8,128)S(1)} %get-tuple-element.26), channel_id=1, source_target_pairs={{0,8},{1,9},{2,10},{3,11},{4,12},{5,13},{6,14},{7,15},{8,0},{9,1},... | collective-permute-start | bytes 196616 | tf_op jit(solution)/shard_map/ppermute | solution.py:333
  25.1 7.7 %collective-permute-start.8 = (f32[16,1024]{1,0:T(8,128)S(1)}, f32[16,1024]{1,0:T(8,128)S(1)}, u32[]{:S(2)}, u32[]{:S(2)}) collective-permute-start(f32[16,1024]{1,0:T(8,128)S(1)} %get-tuple-element.27), channel_id=1, source_target_pairs={{0,4},{1,5},{2,6},{3,7},{4,0},{5,1},{6,2},{7,3},{8,12},{9,13},{10,... | collective-permute-start | bytes 196616 | tf_op jit(solution)/shard_map/ppermute | solution.py:333
  26.7 6.1 %collective-permute-start.7 = (f32[16,1024]{1,0:T(8,128)S(1)}, f32[16,1024]{1,0:T(8,128)S(1)}, u32[]{:S(2)}, u32[]{:S(2)}) collective-permute-start(f32[16,1024]{1,0:T(8,128)S(1)} %get-tuple-element.28), channel_id=1, source_target_pairs={{0,12},{1,13},{2,14},{3,15},{4,8},{5,9},{6,10},{7,11},{8,4},{9,5},... | collective-permute-start | bytes 196616 | tf_op jit(solution)/shard_map/ppermute | solution.py:333
  33.0 5.0 %collective-permute-start.11 = (bf16[16,2048]{1,0:T(8,128)(2,1)S(1)}, bf16[16,2048]{1,0:T(8,128)(2,1)S(1)}, u32[]{:S(2)}, u32[]{:S(2)}) collective-permute-start(bf16[16,2048]{1,0:T(8,128)(2,1)S(1)} %pad_maximum_fusion.3.refs_0_), channel_id=1, source_target_pairs={{0,4},{1,5},{2,6},{3,7},{4,0},{5,1},{6,2},{7,3},{8,12},{9,13},{10,... | collective-permute-start | bytes 196616 | tf_op jit(solution)/shard_map/ppermute | solution.py:333
  33.0 6.2 %collective-permute-start.10 = (bf16[16,2048]{1,0:T(8,128)(2,1)S(1)}, bf16[16,2048]{1,0:T(8,128)(2,1)S(1)}, u32[]{:S(2)}, u32[]{:S(2)}) collective-permute-start(bf16[16,2048]{1,0:T(8,128)(2,1)S(1)} %pad_maximum_fusion.3.refs_0_), channel_id=1, source_target_pairs={{0,12},{1,13},{2,14},{3,15},{4,8},{5,9},{6,10},{7,11},{8,4},{9,5},... | collective-permute-start | bytes 196616 | tf_op jit(solution)/shard_map/ppermute | solution.py:333
  35.3 5.6 %collective-permute-start.12 = (bf16[16,2048]{1,0:T(8,128)(2,1)S(1)}, bf16[16,2048]{1,0:T(8,128)(2,1)S(1)}, u32[]{:S(2)}, u32[]{:S(2)}) collective-permute-start(bf16[16,2048]{1,0:T(8,128)(2,1)S(1)} %pad_maximum_fusion.3.refs_0_), channel_id=1, source_target_pairs={{0,8},{1,9},{2,10},{3,11},{4,12},{5,13},{6,14},{7,15},{8,0},{9,1},... | collective-permute-start | bytes 196616 | tf_op jit(solution)/shard_map/ppermute | solution.py:333
  39.3 6.4 %collective-permute-start.15 = (bf16[48,2048]{1,0:T(8,128)(2,1)S(1)}, bf16[48,2048]{1,0:T(8,128)(2,1)S(1)}, u32[]{:S(2)}, u32[]{:S(2)}) collective-permute-start(bf16[48,2048]{1,0:T(8,128)(2,1)S(1)} %pad_maximum_fusion.2.refs_0_), channel_id=1, source_target_pairs={{0,2},{1,3},{2,0},{3,1},{4,6},{5,7},{6,4},{7,5},{8,10},{9,11},{10,... | collective-permute-start | bytes 589832 | tf_op jit(solution)/shard_map/ppermute | solution.py:333
  40.9 4.8 %collective-permute-start.14 = (bf16[16,2048]{1,0:T(8,128)(2,1)S(1)}, bf16[16,2048]{1,0:T(8,128)(2,1)S(1)}, u32[]{:S(2)}, u32[]{:S(2)}) collective-permute-start(bf16[16,2048]{1,0:T(8,128)(2,1)S(1)} %collective-permute-done.12.refs_1_), channel_id=1, source_target_pairs={{0,2},{1,3},{2,0},{3,1},{4,6},{5,7},{6,4},{7,5},{8,10},{9,11},{10,... | collective-permute-start | bytes 196616 | tf_op jit(solution)/shard_map/ppermute | solution.py:333
  42.4 4.2 %collective-permute-start.13 = (bf16[64,2048]{1,0:T(8,128)(2,1)S(1)}, bf16[64,2048]{1,0:T(8,128)(2,1)S(1)}, u32[]{:S(2)}, u32[]{:S(2)}) collective-permute-start(bf16[64,2048]{1,0:T(8,128)(2,1)S(1)} %pad_maximum_fusion), channel_id=1, source_target_pairs={{0,1},{1,0},{2,3},{3,2},{4,5},{5,4},{6,7},{7,6},{8,9},{9,8},{10,11... | collective-permute-start | bytes 786440 | tf_op jit(solution)/shard_map/ppermute | solution.py:333
  46.5 3.2 %collective-permute-start.16 = (bf16[64,2048]{1,0:T(8,128)(2,1)}, bf16[64,2048]{1,0:T(8,128)(2,1)S(1)}, u32[]{:S(2)}, u32[]{:S(2)}) collective-permute-start(bf16[64,2048]{1,0:T(8,128)(2,1)} %pad_maximum_fusion.1), channel_id=1, source_target_pairs={{0,1},{1,0},{2,3},{3,2},{4,5},{5,4},{6,7},{7,6},{8,9},{9,8},{10,11... | collective-permute-start | bytes 786440 | tf_op jit(solution)/shard_map/ppermute | solution.py:333
  46.6 1.6 %copy-start.1 = (bf16[512,2048]{1,0:T(8,128)(2,1)S(1)}, bf16[512,2048]{1,0:T(8,128)(2,1)}, u32[]{:S(2)}) copy-start(bf16[512,2048]{1,0:T(8,128)(2,1)} %copy-done) | copy-start | bytes 6291460
  48.2 1.6 %copy-start.3 = (bf16[512,2048]{1,0:T(8,128)(2,1)S(1)}, bf16[512,2048]{1,0:T(8,128)(2,1)}, u32[]{:S(2)}) copy-start(bf16[512,2048]{1,0:T(8,128)(2,1)} %copy-done.2) | copy-start | bytes 6291460
  51.3 11.2 %all-to-all-start = ((f32[16,4,128]{2,1,0:T(4,128)}), f32[16,4,128]{2,1,0:T(4,128)S(1)}, u32[]{:S(2)}, u32[]{:S(2)}) async-start(f32[16,4,128]{2,1,0:T(4,128)} %grad.7), calls=%async_computation | async-start | bytes 65536 | tf_op jit(solution)/shard_map/all_to_all | solution.py:403
  62.5 0.7 %copy-start.6 = (f32[4,128]{1,0:T(4,128)}, f32[4,128]{1,0:T(4,128)S(1)}, u32[]{:S(2)}) copy-start(f32[4,128]{1,0:T(4,128)S(1)} %reduce_sum.29) | copy-start | bytes 6148

commit v16 on v15

--- a/solution.py
+++ b/solution.py
@@ -389,13 +389,10 @@
     totals = grad(n, rows, near, columns, None)
     last[-1][1][-1] = hold(last[-1][1][-1], totals)
 
-    def to_core(pieces):
-        return [((1, at[1]), [swap(join(parts, 0), dc=1)]) for at, parts in pieces]
-
-    far = [(at, [hold(e, last[-1][1][-1])]) for at, (e,) in to_core(near)]
-    far_last = to_core(last)
+    far = [((1, at[1]), [hold(swap(join(e, 0), dc=1), last[-1][1][-1])]) for at, e in near]
+    far_last = [((1, at[1]), [swap(e, dc=1) for e in parts]) for at, parts in last]
+    totals = grad(n, rows, last, columns, totals)
     totals = grad(n, rows, far, columns, totals)
-    totals = grad(n, rows, last, columns, totals)
     back = grad(n, rows, far_last, columns, totals, (in_vmem(ids), loss))
     pieces = near + far + last + far_last
     error = own_rows(n, [at for at, _ in pieces], own, width, [e[0][:group] for _, e in pieces])

time: 63.5 us -> 63.9 us (level)
  other arithmetic: 1.95 us -> 1.2 us
  local copies, waits for them, and re-layouts: 1.87 us -> 2.57 us
    concatenate x4 -> x3, other arithmetic: 0.78 us -> 0.04 us  [join(): return xs[0] if len(xs) == 1 else jnp.concatenate(xs, axis=axis)]
    unnamed x14, local copies, waits for them, and re-layouts: 1.67 us -> 2.37 us
    ppermute x17 -> x18, starting transfers between devices: 20.7 us -> 21.3 us  [swap(): return lax.ppermute(x, 'lat', pairs(n, dz, dy, dc))]
    ppermute x17 -> x18, waiting for transfers between devices: 11.6 us -> 11.6 us  [swap(): return lax.ppermute(x, 'lat', pairs(n, dz, dy, dc))]
  transfers between devices with their start and end apart: 18 -> 19, of which waited for: 8 -> 8; matrix products, arithmetic and copies ran while one was open for 2% -> 1% of each run, Pallas kernels for 17% -> 17%
where the time goes in v16:
time: 63.9 us; the launch traced here: 63.6 us
  starting transfers between devices  25.7 us (40%)
  waiting for transfers between devices  17.3 us (27%)
  Pallas kernels  15.8 us (25%)
  local copies, waits for them, and re-layouts  2.57 us (4%)
  other arithmetic  1.2 us (2%)
  between operations  1 us (2%)
    ppermute x18, starting transfers between devices, swap(): return lax.ppermute(x, 'lat', pairs(n, dz, dy, dc))  21.3 us
    ppermute x18, waiting for transfers between devices, swap(): return lax.ppermute(x, 'lat', pairs(n, dz, dy, dc))  11.6 us
    pallas_call x3, Pallas kernels, decode(): pl.pallas_call(functools.partial(decode_kernel, n, rows // n, chunks, par...  7.51 us
    all_to_all x1, waiting for transfers between devices, local(): back = jnp.sum(lax.all_to_all(back, 'lat', 0, 0, tiled=True), axis=0)  5.74 us
    all_to_all x1, starting transfers between devices, local(): back = jnp.sum(lax.all_to_all(back, 'lat', 0, 0, tiled=True), axis=0)  4.41 us
    pallas_call x4, Pallas kernels, grad(): pl.pallas_call(functools.partial(grad_kernel, n, counts, prev is not None...  3.74 us
    pallas_call x1, Pallas kernels, fetch(): pl.pallas_call(functools.partial(fetch_kernel, n, places), out_shape=[blo...  3.54 us
    unnamed x14, local copies, waits for them, and re-layouts  2.37 us
  transfers between devices with their start and end apart: 19, of which 8 were waited for; matrix products, arithmetic and copies ran while one was open for 1% of the time, Pallas kernels for 17%

profile of v16, /device:TPU:0, one launch (start us, length us, event | category | flops | bytes accessed | tf_op | source)
XLA Modules:
  0.0 63.6 jit_solution(16812717410731976710)
XLA Ops:
  0.6 3.7 %decode.3 = (f32[64,2048]{1,0:T(8,128)S(1)}, f32[64,2048]{1,0:T(8,128)S(1)}, bf16[64,512]{1,0:T(8,128)(2,1)S(1)}) custom-call(s32[64,64]{1,0:T(8,128)} %ids_hbm.1, bf16[64,64]{1,0:T(8,128)(2,1)} %refs_1_.3, bf16[512,8192]{1,0:T(8,128)(2,1)} %decoder_hbm.1, bf16[4,8192]{1,0:T(4,128)(2,1)} %refs_2_.5), custom_call_target="tpu_custom_call" | custom-call | flops 268435456 | bytes 8388608 | tf_op jit(solution)/shard_map/decode/pallas_call | solution.py:187
  4.3 0.5 collective-permute-start
  4.8 0.1 collective-permute-start.2
  4.9 1.9 %decode.4 = f32[64,2048]{1,0:T(8,128)S(1)} custom-call(bf16[64,512]{1,0:T(8,128)(2,1)S(1)} %get-tuple-element.12.refs_0_, bf16[512,8192]{1,0:T(8,128)(2,1)} %decoder_hbm.1, bf16[4,8192]{1,0:T(4,128)(2,1)} %refs_2_.5), custom_call_target="tpu_custom_call" | custom-call | flops 134217728 | bytes 4194304 | tf_op jit(solution)/shard_map/decode/pallas_call | solution.py:187
  6.8 0.0 collective-permute-done
  6.8 0.1 add.52
  6.9 0.0 copy-start.4
  6.9 3.0 %collective-permute-start.1 = (f32[64,1024]{1,0:T(8,128)S(1)}, f32[64,1024]{1,0:T(8,128)S(1)}, u32[]{:S(2)}, u32[]{:S(2)}) collective-permute-start(f32[64,1024]{1,0:T(8,128)S(1)} %slice.37.refs_3_), channel_id=1, source_target_pairs={{0,2},{1,3},{2,0},{3,1},{4,6},{5,7},{6,4},{7,5},{8,10},{9,11},{10,... | collective-permute-start | bytes 786440 | tf_op jit(solution)/shard_map/ppermute | solution.py:333
  10.0 1.9 %decode.5 = f32[64,2048]{1,0:T(8,128)S(1)} custom-call(bf16[64,512]{1,0:T(8,128)(2,1)S(1)} %get-tuple-element.12.refs_0_, bf16[512,8192]{1,0:T(8,128)(2,1)} %decoder_hbm.1, bf16[4,8192]{1,0:T(4,128)(2,1)} %refs_2_.5, f32[64,1024]{1,0:T(8,128)S(1)} %slice.37.refs_3_), custom_call_target="tpu_custom_call" | custom-call | flops 134217728 | bytes 4194304 | tf_op jit(solution)/shard_map/decode/pallas_call | solution.py:187
  11.9 0.0 copy-done.4
  11.9 0.0 collective-permute-done.2
  11.9 0.1 add.53
  12.0 0.0 copy-start.5
  12.0 0.2 collective-permute-start.4
  12.2 3.5 %fetch.1 = (bf16[512,2048]{1,0:T(8,128)(2,1)S(1)}, bf16[512,2048]{1,0:T(8,128)(2,1)S(1)}, bf16[512,2048]{1,0:T(8,128)(2,1)S(1)}, bf16[512,2048]{1,0:T(8,128)(2,1...) custom-call(bf16[512,8192]{1,0:T(8,128)(2,1)} %decoder_hbm.1, s32[64,64]{1,0:T(8,128)} %ids_hbm.1, f32[64,1024]{1,0:T(8,128)S(1)} %slice.38._), custom_call_target="tpu_custom_call" | custom-call | bytes 8388608 | tf_op jit(solution)/shard_map/fetch/pallas_call | solution.py:215
  15.7 0.0 copy-start
  15.7 0.0 copy-start.2
  15.7 1.3 %collective-permute-done.1.x_ref = f32[64,1024]{1,0:T(8,128)S(1)} collective-permute-done((f32[64,1024]{1,0:T(8,128)S(1)}, f32[64,1024]{1,0:T(8,128)S(1)}, u32[]{:S(2)}, u32[]{:S(2)}) %collective-permute-start.1) | collective-permute-done | bytes 262176 | tf_op jit(solution)/shard_map/ppermute | solution.py:333
  17.1 0.0 copy-done.5
  17.2 4.2 %collective-permute-start.3 = (f32[16,1024]{1,0:T(8,128)S(1)}, f32[16,1024]{1,0:T(8,128)S(1)}, u32[]{:S(2)}, u32[]{:S(2)}) collective-permute-start(f32[16,1024]{1,0:T(8,128)S(1)} %get-tuple-element.29), channel_id=1, source_target_pairs={{0,12},{1,13},{2,14},{3,15},{4,8},{5,9},{6,10},{7,11},{8,4},{9,5},... | collective-permute-start | bytes 196616 | tf_op jit(solution)/shard_map/ppermute | solution.py:333
  21.4 0.0 collective-permute-start.6
  21.4 0.6 %collective-permute-start.5 = (f32[16,1024]{1,0:T(8,128)S(1)}, f32[16,1024]{1,0:T(8,128)S(1)}, u32[]{:S(2)}, u32[]{:S(2)}) collective-permute-start(f32[16,1024]{1,0:T(8,128)S(1)} %get-tuple-element.31), channel_id=1, source_target_pairs={{0,4},{1,5},{2,6},{3,7},{4,0},{5,1},{6,2},{7,3},{8,12},{9,13},{10,... | collective-permute-start | bytes 196616 | tf_op jit(solution)/shard_map/ppermute | solution.py:333
  22.0 0.1 collective-permute-done.4
  22.2 2.9 %collective-permute-start.9 = (f32[16,1024]{1,0:T(8,128)S(1)}, f32[16,1024]{1,0:T(8,128)S(1)}, u32[]{:S(2)}, u32[]{:S(2)}) collective-permute-start(f32[16,1024]{1,0:T(8,128)S(1)} %get-tuple-element.26), channel_id=1, source_target_pairs={{0,8},{1,9},{2,10},{3,11},{4,12},{5,13},{6,14},{7,15},{8,0},{9,1},... | collective-permute-start | bytes 196616 | tf_op jit(solution)/shard_map/ppermute | solution.py:333
  25.1 1.6 %collective-permute-start.8 = (f32[16,1024]{1,0:T(8,128)S(1)}, f32[16,1024]{1,0:T(8,128)S(1)}, u32[]{:S(2)}, u32[]{:S(2)}) collective-permute-start(f32[16,1024]{1,0:T(8,128)S(1)} %get-tuple-element.27), channel_id=1, source_target_pairs={{0,4},{1,5},{2,6},{3,7},{4,0},{5,1},{6,2},{7,3},{8,12},{9,13},{10,... | collective-permute-start | bytes 196616 | tf_op jit(solution)/shard_map/ppermute | solution.py:333
  26.7 0.0 collective-permute-done.3.x_ref
  26.7 0.9 %collective-permute-start.7 = (f32[16,1024]{1,0:T(8,128)S(1)}, f32[16,1024]{1,0:T(8,128)S(1)}, u32[]{:S(2)}, u32[]{:S(2)}) collective-permute-start(f32[16,1024]{1,0:T(8,128)S(1)} %get-tuple-element.28), channel_id=1, source_target_pairs={{0,12},{1,13},{2,14},{3,15},{4,8},{5,9},{6,10},{7,11},{8,4},{9,5},... | collective-permute-start | bytes 196616 | tf_op jit(solution)/shard_map/ppermute | solution.py:333
  27.6 0.0 collective-permute-done.5.x_ref
  27.6 0.1 collective-permute-done.6.x_ref
  27.8 0.1 multiply_reduce_fusion.1
  27.9 4.8 %collective-permute-done.7.x_ref = f32[16,1024]{1,0:T(8,128)S(1)} collective-permute-done((f32[16,1024]{1,0:T(8,128)S(1)}, f32[16,1024]{1,0:T(8,128)S(1)}, u32[]{:S(2)}, u32[]{:S(2)}) %collective-permute-start.7) | collective-permute-done | bytes 65568 | tf_op jit(solution)/shard_map/ppermute | solution.py:333
  32.7 0.0 collective-permute-done.8.x_ref
  32.8 0.0 copy-done
  32.8 0.0 copy-done.2
  32.8 0.0 collective-permute-done.9.x_ref
  32.8 0.1 multiply_reduce_fusion
  33.0 0.1 collective-permute-start.11
  33.0 2.2 %collective-permute-start.10 = (bf16[16,2048]{1,0:T(8,128)(2,1)S(1)}, bf16[16,2048]{1,0:T(8,128)(2,1)S(1)}, u32[]{:S(2)}, u32[]{:S(2)}) collective-permute-start(bf16[16,2048]{1,0:T(8,128)(2,1)S(1)} %pad_maximum_fusion.2.refs_0_), channel_id=1, source_target_pairs={{0,12},{1,13},{2,14},{3,15},{4,8},{5,9},{6,10},{7,11},{8,4},{9,5},... | collective-permute-start | bytes 196616 | tf_op jit(solution)/shard_map/ppermute | solution.py:333
  35.3 1.2 %collective-permute-start.12 = (bf16[16,2048]{1,0:T(8,128)(2,1)S(1)}, bf16[16,2048]{1,0:T(8,128)(2,1)S(1)}, u32[]{:S(2)}, u32[]{:S(2)}) collective-permute-start(bf16[16,2048]{1,0:T(8,128)(2,1)S(1)} %pad_maximum_fusion.2.refs_0_), channel_id=1, source_target_pairs={{0,8},{1,9},{2,10},{3,11},{4,12},{5,13},{6,14},{7,15},{8,0},{9,1},... | collective-permute-start | bytes 196616 | tf_op jit(solution)/shard_map/ppermute | solution.py:333
  36.5 1.4 %collective-permute-done.11 = bf16[16,2048]{1,0:T(8,128)(2,1)S(1)} collective-permute-done((bf16[16,2048]{1,0:T(8,128)(2,1)S(1)}, bf16[16,2048]{1,0:T(8,128)(2,1)S(1)}, u32[]{:S(2)}, u32[]{:S(2)}) %collective-permute-start.11) | collective-permute-done | bytes 65568 | tf_op jit(solution)/shard_map/ppermute | solution.py:333
  37.9 1.3 %collective-permute-done.10 = bf16[16,2048]{1,0:T(8,128)(2,1)S(1)} collective-permute-done((bf16[16,2048]{1,0:T(8,128)(2,1)S(1)}, bf16[16,2048]{1,0:T(8,128)(2,1)S(1)}, u32[]{:S(2)}, u32[]{:S(2)}) %collective-permute-start.10) | collective-permute-done | bytes 65568 | tf_op jit(solution)/shard_map/ppermute | solution.py:333
  39.3 1.6 %collective-permute-start.15 = (bf16[48,2048]{1,0:T(8,128)(2,1)S(1)}, bf16[48,2048]{1,0:T(8,128)(2,1)S(1)}, u32[]{:S(2)}, u32[]{:S(2)}) collective-permute-start(bf16[48,2048]{1,0:T(8,128)(2,1)S(1)} %pad_maximum_fusion.1.refs_0_), channel_id=1, source_target_pairs={{0,2},{1,3},{2,0},{3,1},{4,6},{5,7},{6,4},{7,5},{8,10},{9,11},{10,... | collective-permute-start | bytes 589832 | tf_op jit(solution)/shard_map/ppermute | solution.py:333
  40.9 0.0 collective-permute-done.12.refs_1_
  40.9 1.5 %collective-permute-start.14 = (bf16[16,2048]{1,0:T(8,128)(2,1)S(1)}, bf16[16,2048]{1,0:T(8,128)(2,1)S(1)}, u32[]{:S(2)}, u32[]{:S(2)}) collective-permute-start(bf16[16,2048]{1,0:T(8,128)(2,1)S(1)} %collective-permute-done.12.refs_1_), channel_id=1, source_target_pairs={{0,2},{1,3},{2,0},{3,1},{4,6},{5,7},{6,4},{7,5},{8,10},{9,11},{10,... | collective-permute-start | bytes 196616 | tf_op jit(solution)/shard_map/ppermute | solution.py:333
  42.4 0.1 collective-permute-start.13
  42.5 0.8 %grad.4.refs_0_.refs_3_ = f32[64,512]{1,0:T(8,128)S(1)} custom-call(bf16[48,2048]{1,0:T(8,128)(2,1)S(1)} %pad_maximum_fusion.1.refs_0_, bf16[16,2048]{1,0:T(8,128)(2,1)S(1)} %collective-permute-done.12.refs_1_, bf16[512,2048]{1,0:T(8,128)(2,1)S(1)} %get-tuple-element.16.refs_2_), custom_call_target="tpu_custom_call" | custom-call | flops 134217728 | bytes 4194304 | tf_op jit(solution)/shard_map/grad/pallas_call | solution.py:285
  43.2 2.5 %collective-permute-done.14.x_ref = bf16[16,2048]{1,0:T(8,128)(2,1)S(1)} collective-permute-done((bf16[16,2048]{1,0:T(8,128)(2,1)S(1)}, bf16[16,2048]{1,0:T(8,128)(2,1)S(1)}, u32[]{:S(2)}, u32[]{:S(2)}) %collective-permute-start.14) | collective-permute-done | bytes 65568 | tf_op jit(solution)/shard_map/ppermute | solution.py:333
  45.7 0.0 collective-permute-done.15.refs_0_
  45.8 0.1 collective-permute-start.17
  45.8 0.5 collective-permute-start.16
  46.3 0.1 copy.17.refs_5_
  46.4 1.6 %copy-done.1 = bf16[512,2048]{1,0:T(8,128)(2,1)S(1)} copy-done((bf16[512,2048]{1,0:T(8,128)(2,1)S(1)}, bf16[512,2048]{1,0:T(8,128)(2,1)}, u32[]{:S(2)}) %copy-start.1) | copy-done | bytes 2097176
  48.0 0.8 %grad.5.refs_2_ = f32[64,512]{1,0:T(8,128)S(1)} custom-call(bf16[48,2048]{1,0:T(8,128)(2,1)S(1)} %collective-permute-done.15.refs_0_, bf16[16,2048]{1,0:T(8,128)(2,1)S(1)} %hold.18.refs_0_.refs_1_, bf16[512,2048]{1,0:T(8,128)(2,1)S(1)} %copy-done.1, f32[64,512]{1,0:T(8,128)S(1)} %grad.4.refs_0_.refs_3_), custom_call_target="tpu_custom_call" | custom-call | flops 134217728 | bytes 4194304 | tf_op jit(solution)/shard_map/grad/pallas_call | solution.py:285
  48.8 0.0 collective-permute-done.13.x_ref
  48.8 0.8 %grad.6.refs_3_ = f32[64,512]{1,0:T(8,128)S(1)} custom-call(bf16[64,2048]{1,0:T(8,128)(2,1)S(1)} %hold.19.refs_0_, bf16[512,2048]{1,0:T(8,128)(2,1)S(1)} %get-tuple-element.18.refs_1_, f32[64,512]{1,0:T(8,128)S(1)} %grad.5.refs_2_), custom_call_target="tpu_custom_call" | custom-call | flops 134217728 | bytes 4194304 | tf_op jit(solution)/shard_map/grad/pallas_call | solution.py:285
  49.6 0.0 collective-permute-done.17.refs_1_
  49.6 0.0 collective-permute-done.16.refs_0_
  49.6 0.8 %copy-done.3 = bf16[512,2048]{1,0:T(8,128)(2,1)S(1)} copy-done((bf16[512,2048]{1,0:T(8,128)(2,1)S(1)}, bf16[512,2048]{1,0:T(8,128)(2,1)}, u32[]{:S(2)}) %copy-start.3) | copy-done | bytes 2097176
  50.4 1.5 %grad.7 = f32[16,4,128]{2,1,0:T(4,128)} custom-call(bf16[48,2048]{1,0:T(8,128)(2,1)S(1)} %collective-permute-done.16.refs_0_, bf16[16,2048]{1,0:T(8,128)(2,1)S(1)} %collective-permute-done.17.refs_1_, bf16[512,2048]{1,0:T(8,128)(2,1)S(1)} %copy-done.3, f32[64,512]{1,0:T(8,128)S(1)} %grad.6.refs_3_, s32[64,64]{1,0:T(8,128)S(1)} %get-tuple-element.20.refs_4_, ...), custom_call_target="tpu_custom_call" | custom-call | flops 134217728 | bytes 4194304 | tf_op jit(solution)/shard_map/grad/pallas_call | solution.py:285
  51.8 4.4 %all-to-all-start = ((f32[16,4,128]{2,1,0:T(4,128)}), f32[16,4,128]{2,1,0:T(4,128)S(1)}, u32[]{:S(2)}, u32[]{:S(2)}) async-start(f32[16,4,128]{2,1,0:T(4,128)} %grad.7), calls=%async_computation | async-start | bytes 65536 | tf_op jit(solution)/shard_map/all_to_all | solution.py:400
  56.3 0.8 %own_rows.1 = bf16[4,8192]{1,0:T(4,128)(2,1)} custom-call(bf16[16,2048]{1,0:T(8,128)(2,1)S(1)} %pad_maximum_fusion.2.refs_0_, bf16[16,2048]{1,0:T(8,128)(2,1)S(1)} %slice.40.refs_1_, bf16[16,2048]{1,0:T(8,128)(2,1)S(1)} %slice.41.refs_2_, bf16[16,2048]{1,0:T(8,128)(2,1)S(1)} %slice.42.refs_3_), custom_call_target="tpu_custom_call" | custom-call | tf_op jit(solution)/shard_map/own_rows/pallas_call | solution.py:311
  57.1 5.7 %all-to-all-done = f32[16,4,128]{2,1,0:T(4,128)S(1)} async-done(((f32[16,4,128]{2,1,0:T(4,128)}), f32[16,4,128]{2,1,0:T(4,128)S(1)}, u32[]{:S(2)}, u32[]{:S(2)}) %all-to-all-start) | async-done | bytes 32800 | tf_op jit(solution)/shard_map/all_to_all | solution.py:400
  62.9 0.7 %multiply_reduce_fusion.2 = f32[4]{0:T(128)} fusion(f32[4,128]{1,0:T(4,128)S(1)} %reduce_sum.29), kind=kLoop, calls=%fused_computation.9 | loop fusion | flops 4 | bytes 32 | tf_op jit(solution)/shard_map/div | solution.py:401
  63.6 0.0 copy-done.6
  (27 shorter events, 0.4 us)
Async XLA Ops:
  4.3 2.5 %collective-permute-start = (f32[64,2048]{1,0:T(8,128)S(1)}, f32[64,2048]{1,0:T(8,128)S(1)}, u32[]{:S(2)}, u32[]{:S(2)}) collective-permute-start(f32[64,2048]{1,0:T(8,128)S(1)} %get-tuple-element.13), channel_id=1, source_target_pairs={{0,1},{1,0},{2,3},{3,2},{4,5},{5,4},{6,7},{7,6},{8,9},{9,8},{10,11... | collective-permute-start | bytes 1572872 | tf_op jit(solution)/shard_map/ppermute | solution.py:333
  4.8 7.1 %collective-permute-start.2 = (f32[64,2048]{1,0:T(8,128)S(1)}, f32[64,2048]{1,0:T(8,128)S(1)}, u32[]{:S(2)}, u32[]{:S(2)}) collective-permute-start(f32[64,2048]{1,0:T(8,128)S(1)} %get-tuple-element.14), channel_id=1, source_target_pairs={{0,1},{1,0},{2,3},{3,2},{4,5},{5,4},{6,7},{7,6},{8,9},{9,8},{10,11... | collective-permute-start | bytes 1572872 | tf_op jit(solution)/shard_map/ppermute | solution.py:333
  6.9 5.0 %copy-start.4 = (f32[64,2048]{1,0:T(8,128)}, f32[64,2048]{1,0:T(8,128)S(1)}, u32[]{:S(2)}) copy-start(f32[64,2048]{1,0:T(8,128)S(1)} %add.52) | copy-start | bytes 1572868
  6.9 10.1 %collective-permute-start.1 = (f32[64,1024]{1,0:T(8,128)S(1)}, f32[64,1024]{1,0:T(8,128)S(1)}, u32[]{:S(2)}, u32[]{:S(2)}) collective-permute-start(f32[64,1024]{1,0:T(8,128)S(1)} %slice.37.refs_3_), channel_id=1, source_target_pairs={{0,2},{1,3},{2,0},{3,1},{4,6},{5,7},{6,4},{7,5},{8,10},{9,11},{10,... | collective-permute-start | bytes 786440 | tf_op jit(solution)/shard_map/ppermute | solution.py:333
  12.0 5.1 %copy-start.5 = (f32[64,2048]{1,0:T(8,128)S(1)}, f32[64,2048]{1,0:T(8,128)}, u32[]{:S(2)}) copy-start(f32[64,2048]{1,0:T(8,128)} %copy-done.4) | copy-start | bytes 1572868
  12.0 10.1 %collective-permute-start.4 = (f32[64,1024]{1,0:T(8,128)S(1)}, f32[64,1024]{1,0:T(8,128)S(1)}, u32[]{:S(2)}, u32[]{:S(2)}) collective-permute-start(f32[64,1024]{1,0:T(8,128)S(1)} %slice.38._), channel_id=1, source_target_pairs={{0,2},{1,3},{2,0},{3,1},{4,6},{5,7},{6,4},{7,5},{8,10},{9,11},{10,... | collective-permute-start | bytes 786440 | tf_op jit(solution)/shard_map/ppermute | solution.py:333
  15.7 17.0 %copy-start = (bf16[512,2048]{1,0:T(8,128)(2,1)}, bf16[512,2048]{1,0:T(8,128)(2,1)S(1)}, u32[]{:S(2)}) copy-start(bf16[512,2048]{1,0:T(8,128)(2,1)S(1)} %get-tuple-element.19.refs_2_) | copy-start | bytes 6291460
  15.7 17.0 %copy-start.2 = (bf16[512,2048]{1,0:T(8,128)(2,1)}, bf16[512,2048]{1,0:T(8,128)(2,1)S(1)}, u32[]{:S(2)}) copy-start(bf16[512,2048]{1,0:T(8,128)(2,1)S(1)} %get-tuple-element.17.refs_2_) | copy-start | bytes 6291460
  17.2 9.5 %collective-permute-start.3 = (f32[16,1024]{1,0:T(8,128)S(1)}, f32[16,1024]{1,0:T(8,128)S(1)}, u32[]{:S(2)}, u32[]{:S(2)}) collective-permute-start(f32[16,1024]{1,0:T(8,128)S(1)} %get-tuple-element.29), channel_id=1, source_target_pairs={{0,12},{1,13},{2,14},{3,15},{4,8},{5,9},{6,10},{7,11},{8,4},{9,5},... | collective-permute-start | bytes 196616 | tf_op jit(solution)/shard_map/ppermute | solution.py:333
  21.4 6.4 %collective-permute-start.6 = (f32[16,1024]{1,0:T(8,128)S(1)}, f32[16,1024]{1,0:T(8,128)S(1)}, u32[]{:S(2)}, u32[]{:S(2)}) collective-permute-start(f32[16,1024]{1,0:T(8,128)S(1)} %get-tuple-element.30), channel_id=1, source_target_pairs={{0,8},{1,9},{2,10},{3,11},{4,12},{5,13},{6,14},{7,15},{8,0},{9,1},... | collective-permute-start | bytes 196616 | tf_op jit(solution)/shard_map/ppermute | solution.py:333
  21.4 6.2 %collective-permute-start.5 = (f32[16,1024]{1,0:T(8,128)S(1)}, f32[16,1024]{1,0:T(8,128)S(1)}, u32[]{:S(2)}, u32[]{:S(2)}) collective-permute-start(f32[16,1024]{1,0:T(8,128)S(1)} %get-tuple-element.31), channel_id=1, source_target_pairs={{0,4},{1,5},{2,6},{3,7},{4,0},{5,1},{6,2},{7,3},{8,12},{9,13},{10,... | collective-permute-start | bytes 196616 | tf_op jit(solution)/shard_map/ppermute | solution.py:333
  22.2 10.6 %collective-permute-start.9 = (f32[16,1024]{1,0:T(8,128)S(1)}, f32[16,1024]{1,0:T(8,128)S(1)}, u32[]{:S(2)}, u32[]{:S(2)}) collective-permute-start(f32[16,1024]{1,0:T(8,128)S(1)} %get-tuple-element.26), channel_id=1, source_target_pairs={{0,8},{1,9},{2,10},{3,11},{4,12},{5,13},{6,14},{7,15},{8,0},{9,1},... | collective-permute-start | bytes 196616 | tf_op jit(solution)/shard_map/ppermute | solution.py:333
  25.1 7.7 %collective-permute-start.8 = (f32[16,1024]{1,0:T(8,128)S(1)}, f32[16,1024]{1,0:T(8,128)S(1)}, u32[]{:S(2)}, u32[]{:S(2)}) collective-permute-start(f32[16,1024]{1,0:T(8,128)S(1)} %get-tuple-element.27), channel_id=1, source_target_pairs={{0,4},{1,5},{2,6},{3,7},{4,0},{5,1},{6,2},{7,3},{8,12},{9,13},{10,... | collective-permute-start | bytes 196616 | tf_op jit(solution)/shard_map/ppermute | solution.py:333
  26.7 6.1 %collective-permute-start.7 = (f32[16,1024]{1,0:T(8,128)S(1)}, f32[16,1024]{1,0:T(8,128)S(1)}, u32[]{:S(2)}, u32[]{:S(2)}) collective-permute-start(f32[16,1024]{1,0:T(8,128)S(1)} %get-tuple-element.28), channel_id=1, source_target_pairs={{0,12},{1,13},{2,14},{3,15},{4,8},{5,9},{6,10},{7,11},{8,4},{9,5},... | collective-permute-start | bytes 196616 | tf_op jit(solution)/shard_map/ppermute | solution.py:333
  33.0 5.0 %collective-permute-start.11 = (bf16[16,2048]{1,0:T(8,128)(2,1)S(1)}, bf16[16,2048]{1,0:T(8,128)(2,1)S(1)}, u32[]{:S(2)}, u32[]{:S(2)}) collective-permute-start(bf16[16,2048]{1,0:T(8,128)(2,1)S(1)} %pad_maximum_fusion.2.refs_0_), channel_id=1, source_target_pairs={{0,4},{1,5},{2,6},{3,7},{4,0},{5,1},{6,2},{7,3},{8,12},{9,13},{10,... | collective-permute-start | bytes 196616 | tf_op jit(solution)/shard_map/ppermute | solution.py:333
  33.0 6.2 %collective-permute-start.10 = (bf16[16,2048]{1,0:T(8,128)(2,1)S(1)}, bf16[16,2048]{1,0:T(8,128)(2,1)S(1)}, u32[]{:S(2)}, u32[]{:S(2)}) collective-permute-start(bf16[16,2048]{1,0:T(8,128)(2,1)S(1)} %pad_maximum_fusion.2.refs_0_), channel_id=1, source_target_pairs={{0,12},{1,13},{2,14},{3,15},{4,8},{5,9},{6,10},{7,11},{8,4},{9,5},... | collective-permute-start | bytes 196616 | tf_op jit(solution)/shard_map/ppermute | solution.py:333
  35.3 5.6 %collective-permute-start.12 = (bf16[16,2048]{1,0:T(8,128)(2,1)S(1)}, bf16[16,2048]{1,0:T(8,128)(2,1)S(1)}, u32[]{:S(2)}, u32[]{:S(2)}) collective-permute-start(bf16[16,2048]{1,0:T(8,128)(2,1)S(1)} %pad_maximum_fusion.2.refs_0_), channel_id=1, source_target_pairs={{0,8},{1,9},{2,10},{3,11},{4,12},{5,13},{6,14},{7,15},{8,0},{9,1},... | collective-permute-start | bytes 196616 | tf_op jit(solution)/shard_map/ppermute | solution.py:333
  39.3 6.4 %collective-permute-start.15 = (bf16[48,2048]{1,0:T(8,128)(2,1)S(1)}, bf16[48,2048]{1,0:T(8,128)(2,1)S(1)}, u32[]{:S(2)}, u32[]{:S(2)}) collective-permute-start(bf16[48,2048]{1,0:T(8,128)(2,1)S(1)} %pad_maximum_fusion.1.refs_0_), channel_id=1, source_target_pairs={{0,2},{1,3},{2,0},{3,1},{4,6},{5,7},{6,4},{7,5},{8,10},{9,11},{10,... | collective-permute-start | bytes 589832 | tf_op jit(solution)/shard_map/ppermute | solution.py:333
  40.9 4.8 %collective-permute-start.14 = (bf16[16,2048]{1,0:T(8,128)(2,1)S(1)}, bf16[16,2048]{1,0:T(8,128)(2,1)S(1)}, u32[]{:S(2)}, u32[]{:S(2)}) collective-permute-start(bf16[16,2048]{1,0:T(8,128)(2,1)S(1)} %collective-permute-done.12.refs_1_), channel_id=1, source_target_pairs={{0,2},{1,3},{2,0},{3,1},{4,6},{5,7},{6,4},{7,5},{8,10},{9,11},{10,... | collective-permute-start | bytes 196616 | tf_op jit(solution)/shard_map/ppermute | solution.py:333
  42.4 6.4 %collective-permute-start.13 = (bf16[64,2048]{1,0:T(8,128)(2,1)S(1)}, bf16[64,2048]{1,0:T(8,128)(2,1)S(1)}, u32[]{:S(2)}, u32[]{:S(2)}) collective-permute-start(bf16[64,2048]{1,0:T(8,128)(2,1)S(1)} %pad_maximum_fusion), channel_id=1, source_target_pairs={{0,1},{1,0},{2,3},{3,2},{4,5},{5,4},{6,7},{7,6},{8,9},{9,8},{10,11... | collective-permute-start | bytes 786440 | tf_op jit(solution)/shard_map/ppermute | solution.py:333
  45.8 3.8 %collective-permute-start.17 = (bf16[16,2048]{1,0:T(8,128)(2,1)S(1)}, bf16[16,2048]{1,0:T(8,128)(2,1)S(1)}, u32[]{:S(2)}, u32[]{:S(2)}) collective-permute-start(bf16[16,2048]{1,0:T(8,128)(2,1)S(1)} %hold.18.refs_0_.refs_1_), channel_id=1, source_target_pairs={{0,1},{1,0},{2,3},{3,2},{4,5},{5,4},{6,7},{7,6},{8,9},{9,8},{10,11... | collective-permute-start | bytes 196616 | tf_op jit(solution)/shard_map/ppermute | solution.py:333
  45.8 3.8 %collective-permute-start.16 = (bf16[48,2048]{1,0:T(8,128)(2,1)S(1)}, bf16[48,2048]{1,0:T(8,128)(2,1)S(1)}, u32[]{:S(2)}, u32[]{:S(2)}) collective-permute-start(bf16[48,2048]{1,0:T(8,128)(2,1)S(1)} %collective-permute-done.15.refs_0_), channel_id=1, source_target_pairs={{0,1},{1,0},{2,3},{3,2},{4,5},{5,4},{6,7},{7,6},{8,9},{9,8},{10,11... | collective-permute-start | bytes 589832 | tf_op jit(solution)/shard_map/ppermute | solution.py:333
  46.4 1.6 %copy-start.1 = (bf16[512,2048]{1,0:T(8,128)(2,1)S(1)}, bf16[512,2048]{1,0:T(8,128)(2,1)}, u32[]{:S(2)}) copy-start(bf16[512,2048]{1,0:T(8,128)(2,1)} %copy-done) | copy-start | bytes 6291460
  48.8 1.6 %copy-start.3 = (bf16[512,2048]{1,0:T(8,128)(2,1)S(1)}, bf16[512,2048]{1,0:T(8,128)(2,1)}, u32[]{:S(2)}) copy-start(bf16[512,2048]{1,0:T(8,128)(2,1)} %copy-done.2) | copy-start | bytes 6291460
  51.8 11.0 %all-to-all-start = ((f32[16,4,128]{2,1,0:T(4,128)}), f32[16,4,128]{2,1,0:T(4,128)S(1)}, u32[]{:S(2)}, u32[]{:S(2)}) async-start(f32[16,4,128]{2,1,0:T(4,128)} %grad.7), calls=%async_computation | async-start | bytes 65536 | tf_op jit(solution)/shard_map/all_to_all | solution.py:400
  62.9 0.7 %copy-start.6 = (f32[4,128]{1,0:T(4,128)}, f32[4,128]{1,0:T(4,128)S(1)}, u32[]{:S(2)}) copy-start(f32[4,128]{1,0:T(4,128)S(1)} %reduce_sum.29) | copy-start | bytes 6148

commit v17 on v16

--- a/solution.py
+++ b/solution.py
@@ -359,7 +359,7 @@
         leaving.append(after)
         summed.append((blocks[0], got))
 
-    places = tuple((dc, dy) for dy in range(fy) for dc in range(fc))
+    places = tuple((dc, dy) for dy in range(fy // 2) for dc in range(fc))
     *columns, ids, token = fetch(n, chunks * sub, places, decoder, indices, leaving[-1])
     columns = dict(zip(places, columns))
     sums, moved = [], []
@@ -387,7 +387,10 @@
         near += last
     near = near[: -len(last)]
     totals = grad(n, rows, near, columns, None)
-    last[-1][1][-1] = hold(last[-1][1][-1], totals)
+    places = tuple((dc, dy) for dy in range(fy // 2, fy) for dc in range(fc))
+    *more, _, token = fetch(n, chunks * sub, places, decoder, indices, come[-1])
+    columns.update(zip(places, more))
+    last[-1][1][-1] = hold(last[-1][1][-1], totals, token)
 
     far = [((1, at[1]), [hold(swap(join(e, 0), dc=1), last[-1][1][-1])]) for at, e in near]
     far_last = [((1, at[1]), [swap(e, dc=1) for e in parts]) for at, parts in last]

time: 63.9 us -> 68.6 us (1.074)
  local copies, waits for them, and re-layouts: 2.57 us -> 5.18 us
  waiting for transfers between devices: 17.3 us -> 19.2 us
  Pallas kernels: 15.8 us -> 17.4 us
  starting transfers between devices: 25.7 us -> 24.3 us
    unnamed x14, local copies, waits for them, and re-layouts: 2.37 us -> 4.98 us
    ppermute x18, waiting for transfers between devices: 11.6 us -> 13.5 us  [swap(): return lax.ppermute(x, 'lat', pairs(n, dz, dy, dc))]
    pallas_call x1 -> x2, Pallas kernels: 3.54 us -> 5.13 us  [fetch(): pl.pallas_call(functools.partial(fetch_kernel, n, places), out_shape=[blo...]
    all_to_all x1, starting transfers between devices: 4.41 us -> 3.48 us  [local(): back = jnp.sum(lax.all_to_all(back, 'lat', 0, 0, tiled=True), axis=0)]
  transfers between devices with their start and end apart: 19 -> 19, of which waited for: 8 -> 7; matrix products, arithmetic and copies ran while one was open for 1% -> 1% of each run, Pallas kernels for 17% -> 18%
where the time goes in v17:
time: 68.6 us; the launch traced here: 68.2 us
  starting transfers between devices  24.3 us (35%)
  waiting for transfers between devices  19.2 us (28%)
  Pallas kernels  17.4 us (25%)
  local copies, waits for them, and re-layouts  5.18 us (8%)
  other arithmetic  1.21 us (2%)
  between operations  1.01 us (1%)
    ppermute x18, starting transfers between devices, swap(): return lax.ppermute(x, 'lat', pairs(n, dz, dy, dc))  20.8 us
    ppermute x18, waiting for transfers between devices, swap(): return lax.ppermute(x, 'lat', pairs(n, dz, dy, dc))  13.5 us
    pallas_call x3, Pallas kernels, decode(): pl.pallas_call(functools.partial(decode_kernel, n, rows // n, chunks, par...  7.51 us
    all_to_all x1, waiting for transfers between devices, local(): back = jnp.sum(lax.all_to_all(back, 'lat', 0, 0, tiled=True), axis=0)  5.7 us
    pallas_call x2, Pallas kernels, fetch(): pl.pallas_call(functools.partial(fetch_kernel, n, places), out_shape=[blo...  5.13 us
    unnamed x14, local copies, waits for them, and re-layouts  4.98 us
    pallas_call x4, Pallas kernels, grad(): pl.pallas_call(functools.partial(grad_kernel, n, counts, prev is not None...  3.73 us
    all_to_all x1, starting transfers between devices, local(): back = jnp.sum(lax.all_to_all(back, 'lat', 0, 0, tiled=True), axis=0)  3.48 us
  transfers between devices with their start and end apart: 19, of which 7 were waited for; matrix products, arithmetic and copies ran while one was open for 1% of the time, Pallas kernels for 18%

profile of v17, /device:TPU:0, one launch (start us, length us, event | category | flops | bytes accessed | tf_op | source)
XLA Modules:
  0.0 68.2 jit_solution(2914593563014780135)
XLA Ops:
  0.6 3.7 %decode.3 = (f32[64,2048]{1,0:T(8,128)S(1)}, f32[64,2048]{1,0:T(8,128)S(1)}, bf16[64,512]{1,0:T(8,128)(2,1)S(1)}) custom-call(s32[64,64]{1,0:T(8,128)} %ids_hbm.3, bf16[64,64]{1,0:T(8,128)(2,1)} %refs_1_.3, bf16[512,8192]{1,0:T(8,128)(2,1)} %decoder_hbm.3, bf16[4,8192]{1,0:T(4,128)(2,1)} %refs_2_.5), custom_call_target="tpu_custom_call" | custom-call | flops 268435456 | bytes 8388608 | tf_op jit(solution)/shard_map/decode/pallas_call | solution.py:187
  4.3 0.5 collective-permute-start
  4.8 0.1 collective-permute-start.2
  4.9 1.9 %decode.4 = f32[64,2048]{1,0:T(8,128)S(1)} custom-call(bf16[64,512]{1,0:T(8,128)(2,1)S(1)} %get-tuple-element.13.refs_0_, bf16[512,8192]{1,0:T(8,128)(2,1)} %decoder_hbm.3, bf16[4,8192]{1,0:T(4,128)(2,1)} %refs_2_.5), custom_call_target="tpu_custom_call" | custom-call | flops 134217728 | bytes 4194304 | tf_op jit(solution)/shard_map/decode/pallas_call | solution.py:187
  6.8 0.0 collective-permute-done
  6.8 0.1 add.52
  6.9 0.0 copy-start.4
  6.9 3.0 %collective-permute-start.1 = (f32[64,1024]{1,0:T(8,128)S(1)}, f32[64,1024]{1,0:T(8,128)S(1)}, u32[]{:S(2)}, u32[]{:S(2)}) collective-permute-start(f32[64,1024]{1,0:T(8,128)S(1)} %slice.37.refs_3_), channel_id=1, source_target_pairs={{0,2},{1,3},{2,0},{3,1},{4,6},{5,7},{6,4},{7,5},{8,10},{9,11},{10,... | collective-permute-start | bytes 786440 | tf_op jit(solution)/shard_map/ppermute | solution.py:333
  10.0 1.9 %decode.5 = f32[64,2048]{1,0:T(8,128)S(1)} custom-call(bf16[64,512]{1,0:T(8,128)(2,1)S(1)} %get-tuple-element.13.refs_0_, bf16[512,8192]{1,0:T(8,128)(2,1)} %decoder_hbm.3, bf16[4,8192]{1,0:T(4,128)(2,1)} %refs_2_.5, f32[64,1024]{1,0:T(8,128)S(1)} %slice.37.refs_3_), custom_call_target="tpu_custom_call" | custom-call | flops 134217728 | bytes 4194304 | tf_op jit(solution)/shard_map/decode/pallas_call | solution.py:187
  11.9 0.0 copy-done.4
  11.9 0.0 collective-permute-done.2
  11.9 0.1 add.53
  12.0 0.0 copy-start.5
  12.0 0.2 collective-permute-start.4
  12.2 2.2 %fetch.2 = (bf16[512,2048]{1,0:T(8,128)(2,1)S(1)}, bf16[512,2048]{1,0:T(8,128)(2,1)S(1)}, s32[64,64]{1,0:T(8,128)S(1)}, f32[8,128]{1,0:T(8,128)S(1)}) custom-call(bf16[512,8192]{1,0:T(8,128)(2,1)} %decoder_hbm.3, s32[64,64]{1,0:T(8,128)} %ids_hbm.3, f32[64,1024]{1,0:T(8,128)S(1)} %slice.38._), custom_call_target="tpu_custom_call" | custom-call | bytes 4194304 | tf_op jit(solution)/shard_map/fetch/pallas_call | solution.py:215
  14.4 2.6 %collective-permute-done.1.x_ref = f32[64,1024]{1,0:T(8,128)S(1)} collective-permute-done((f32[64,1024]{1,0:T(8,128)S(1)}, f32[64,1024]{1,0:T(8,128)S(1)}, u32[]{:S(2)}, u32[]{:S(2)}) %collective-permute-start.1) | collective-permute-done | bytes 262176 | tf_op jit(solution)/shard_map/ppermute | solution.py:333
  17.1 0.0 copy-done.5
  17.2 3.2 %collective-permute-start.6 = (f32[16,1024]{1,0:T(8,128)S(1)}, f32[16,1024]{1,0:T(8,128)S(1)}, u32[]{:S(2)}, u32[]{:S(2)}) collective-permute-start(f32[16,1024]{1,0:T(8,128)S(1)} %get-tuple-element.32), channel_id=1, source_target_pairs={{0,8},{1,9},{2,10},{3,11},{4,12},{5,13},{6,14},{7,15},{8,0},{9,1},... | collective-permute-start | bytes 196616 | tf_op jit(solution)/shard_map/ppermute | solution.py:333
  20.4 1.6 %collective-permute-start.5 = (f32[16,1024]{1,0:T(8,128)S(1)}, f32[16,1024]{1,0:T(8,128)S(1)}, u32[]{:S(2)}, u32[]{:S(2)}) collective-permute-start(f32[16,1024]{1,0:T(8,128)S(1)} %get-tuple-element.33), channel_id=1, source_target_pairs={{0,4},{1,5},{2,6},{3,7},{4,0},{5,1},{6,2},{7,3},{8,12},{9,13},{10,... | collective-permute-start | bytes 196616 | tf_op jit(solution)/shard_map/ppermute | solution.py:333
  22.0 0.0 collective-permute-start.3
  22.0 0.2 collective-permute-done.4
  22.2 2.9 %collective-permute-start.9 = (f32[16,1024]{1,0:T(8,128)S(1)}, f32[16,1024]{1,0:T(8,128)S(1)}, u32[]{:S(2)}, u32[]{:S(2)}) collective-permute-start(f32[16,1024]{1,0:T(8,128)S(1)} %get-tuple-element.28), channel_id=1, source_target_pairs={{0,8},{1,9},{2,10},{3,11},{4,12},{5,13},{6,14},{7,15},{8,0},{9,1},... | collective-permute-start | bytes 196616 | tf_op jit(solution)/shard_map/ppermute | solution.py:333
  25.1 1.6 %collective-permute-start.8 = (f32[16,1024]{1,0:T(8,128)S(1)}, f32[16,1024]{1,0:T(8,128)S(1)}, u32[]{:S(2)}, u32[]{:S(2)}) collective-permute-start(f32[16,1024]{1,0:T(8,128)S(1)} %get-tuple-element.29), channel_id=1, source_target_pairs={{0,4},{1,5},{2,6},{3,7},{4,0},{5,1},{6,2},{7,3},{8,12},{9,13},{10,... | collective-permute-start | bytes 196616 | tf_op jit(solution)/shard_map/ppermute | solution.py:333
  26.7 1.7 %collective-permute-done.3.x_ref = f32[16,1024]{1,0:T(8,128)S(1)} collective-permute-done((f32[16,1024]{1,0:T(8,128)S(1)}, f32[16,1024]{1,0:T(8,128)S(1)}, u32[]{:S(2)}, u32[]{:S(2)}) %collective-permute-start.3) | collective-permute-done | bytes 65568 | tf_op jit(solution)/shard_map/ppermute | solution.py:333
  28.4 0.4 collective-permute-start.7
  28.8 0.0 collective-permute-done.5.x_ref
  28.9 0.0 collective-permute-done.6.x_ref
  28.9 0.1 multiply_reduce_fusion.1
  29.0 6.2 %collective-permute-done.7.x_ref = f32[16,1024]{1,0:T(8,128)S(1)} collective-permute-done((f32[16,1024]{1,0:T(8,128)S(1)}, f32[16,1024]{1,0:T(8,128)S(1)}, u32[]{:S(2)}, u32[]{:S(2)}) %collective-permute-start.7) | collective-permute-done | bytes 65568 | tf_op jit(solution)/shard_map/ppermute | solution.py:333
  35.3 0.0 collective-permute-done.8.x_ref
  35.3 0.0 collective-permute-done.9.x_ref
  35.3 0.1 multiply_reduce_fusion
  35.4 0.1 collective-permute-start.11
  35.5 0.1 collective-permute-start.10
  35.6 3.4 %collective-permute-start.12 = (bf16[16,2048]{1,0:T(8,128)(2,1)S(1)}, bf16[16,2048]{1,0:T(8,128)(2,1)S(1)}, u32[]{:S(2)}, u32[]{:S(2)}) collective-permute-start(bf16[16,2048]{1,0:T(8,128)(2,1)S(1)} %pad_maximum_fusion.2.refs_0_), channel_id=1, source_target_pairs={{0,8},{1,9},{2,10},{3,11},{4,12},{5,13},{6,14},{7,15},{8,0},{9,1},... | collective-permute-start | bytes 196616 | tf_op jit(solution)/shard_map/ppermute | solution.py:333
  39.0 0.8 %collective-permute-done.11 = bf16[16,2048]{1,0:T(8,128)(2,1)S(1)} collective-permute-done((bf16[16,2048]{1,0:T(8,128)(2,1)S(1)}, bf16[16,2048]{1,0:T(8,128)(2,1)S(1)}, u32[]{:S(2)}, u32[]{:S(2)}) %collective-permute-start.11) | collective-permute-done | bytes 65568 | tf_op jit(solution)/shard_map/ppermute | solution.py:333
  39.8 2.0 %collective-permute-done.10 = bf16[16,2048]{1,0:T(8,128)(2,1)S(1)} collective-permute-done((bf16[16,2048]{1,0:T(8,128)(2,1)S(1)}, bf16[16,2048]{1,0:T(8,128)(2,1)S(1)}, u32[]{:S(2)}, u32[]{:S(2)}) %collective-permute-start.10) | collective-permute-done | bytes 65568 | tf_op jit(solution)/shard_map/ppermute | solution.py:333
  41.8 1.6 %collective-permute-start.15 = (bf16[48,2048]{1,0:T(8,128)(2,1)S(1)}, bf16[48,2048]{1,0:T(8,128)(2,1)S(1)}, u32[]{:S(2)}, u32[]{:S(2)}) collective-permute-start(bf16[48,2048]{1,0:T(8,128)(2,1)S(1)} %pad_maximum_fusion.1.refs_0_), channel_id=1, source_target_pairs={{0,2},{1,3},{2,0},{3,1},{4,6},{5,7},{6,4},{7,5},{8,10},{9,11},{10,... | collective-permute-start | bytes 589832 | tf_op jit(solution)/shard_map/ppermute | solution.py:333
  43.4 0.0 collective-permute-done.12.refs_1_._
  43.4 1.5 %collective-permute-start.14 = (bf16[16,2048]{1,0:T(8,128)(2,1)S(1)}, bf16[16,2048]{1,0:T(8,128)(2,1)S(1)}, u32[]{:S(2)}, u32[]{:S(2)}) collective-permute-start(bf16[16,2048]{1,0:T(8,128)(2,1)S(1)} %collective-permute-done.12.refs_1_._), channel_id=1, source_target_pairs={{0,2},{1,3},{2,0},{3,1},{4,6},{5,7},{6,4},{7,5},{8,10},{9,11},{10,... | collective-permute-start | bytes 196616 | tf_op jit(solution)/shard_map/ppermute | solution.py:333
  44.9 0.1 collective-permute-start.13
  45.0 2.9 %fetch.3 = (bf16[512,2048]{1,0:T(8,128)(2,1)S(1)}, bf16[512,2048]{1,0:T(8,128)(2,1)S(1)}, s32[64,64]{1,0:T(8,128)}, f32[8,128]{1,0:T(8,128)S(1)}) custom-call(bf16[512,8192]{1,0:T(8,128)(2,1)} %decoder_hbm.3, s32[64,64]{1,0:T(8,128)} %ids_hbm.3, bf16[16,2048]{1,0:T(8,128)(2,1)S(1)} %collective-permute-done.12.refs_1_._), custom_call_target="tpu_custom_call" | custom-call | bytes 4194304 | tf_op jit(solution)/shard_map/fetch/pallas_call | solution.py:215
  47.9 0.0 copy-start
  47.9 1.3 %copy-done = bf16[512,2048]{1,0:T(8,128)(2,1)} copy-done((bf16[512,2048]{1,0:T(8,128)(2,1)}, bf16[512,2048]{1,0:T(8,128)(2,1)S(1)}, u32[]{:S(2)}) %copy-start) | copy-done | bytes 2097176
  49.2 1.3 %copy-done.2 = bf16[512,2048]{1,0:T(8,128)(2,1)} copy-done((bf16[512,2048]{1,0:T(8,128)(2,1)}, bf16[512,2048]{1,0:T(8,128)(2,1)S(1)}, u32[]{:S(2)}) %copy-start.2) | copy-done | bytes 2097176
  50.5 0.7 %grad.4.refs_0_.refs_3_ = f32[64,512]{1,0:T(8,128)S(1)} custom-call(bf16[48,2048]{1,0:T(8,128)(2,1)S(1)} %pad_maximum_fusion.1.refs_0_, bf16[16,2048]{1,0:T(8,128)(2,1)S(1)} %collective-permute-done.12.refs_1_._, bf16[512,2048]{1,0:T(8,128)(2,1)S(1)} %get-tuple-element.17.refs_2_), custom_call_target="tpu_custom_call" | custom-call | flops 134217728 | bytes 4194304 | tf_op jit(solution)/shard_map/grad/pallas_call | solution.py:285
  51.2 0.0 collective-permute-done.14.x_ref
  51.2 0.0 collective-permute-done.15.refs_0_
  51.3 0.5 collective-permute-start.17
  51.8 0.1 collective-permute-start.16
  51.9 0.1 copy.17.refs_5_
  52.0 1.6 %copy-done.1 = bf16[512,2048]{1,0:T(8,128)(2,1)S(1)} copy-done((bf16[512,2048]{1,0:T(8,128)(2,1)S(1)}, bf16[512,2048]{1,0:T(8,128)(2,1)}, u32[]{:S(2)}) %copy-start.1) | copy-done | bytes 2097176
  53.6 0.8 %grad.5.refs_2_ = f32[64,512]{1,0:T(8,128)S(1)} custom-call(bf16[48,2048]{1,0:T(8,128)(2,1)S(1)} %collective-permute-done.15.refs_0_, bf16[16,2048]{1,0:T(8,128)(2,1)S(1)} %hold.18.refs_0_.refs_1_, bf16[512,2048]{1,0:T(8,128)(2,1)S(1)} %copy-done.1, f32[64,512]{1,0:T(8,128)S(1)} %grad.4.refs_0_.refs_3_), custom_call_target="tpu_custom_call" | custom-call | flops 134217728 | bytes 4194304 | tf_op jit(solution)/shard_map/grad/pallas_call | solution.py:285
  54.4 0.0 copy-start.3
  54.4 0.0 collective-permute-done.13.x_ref
  54.4 0.8 %grad.6.refs_3_ = f32[64,512]{1,0:T(8,128)S(1)} custom-call(bf16[64,2048]{1,0:T(8,128)(2,1)S(1)} %hold.19.refs_0_, bf16[512,2048]{1,0:T(8,128)(2,1)S(1)} %get-tuple-element.20.refs_1_, f32[64,512]{1,0:T(8,128)S(1)} %grad.5.refs_2_), custom_call_target="tpu_custom_call" | custom-call | flops 134217728 | bytes 4194304 | tf_op jit(solution)/shard_map/grad/pallas_call | solution.py:285
  55.2 0.0 collective-permute-done.17.refs_1_
  55.2 0.0 collective-permute-done.16.refs_0_
  55.2 0.8 %copy-done.3 = bf16[512,2048]{1,0:T(8,128)(2,1)S(1)} copy-done((bf16[512,2048]{1,0:T(8,128)(2,1)S(1)}, bf16[512,2048]{1,0:T(8,128)(2,1)}, u32[]{:S(2)}) %copy-start.3) | copy-done | bytes 2097176
  56.0 1.5 %grad.7 = f32[16,4,128]{2,1,0:T(4,128)} custom-call(bf16[48,2048]{1,0:T(8,128)(2,1)S(1)} %collective-permute-done.16.refs_0_, bf16[16,2048]{1,0:T(8,128)(2,1)S(1)} %collective-permute-done.17.refs_1_, bf16[512,2048]{1,0:T(8,128)(2,1)S(1)} %copy-done.3, f32[64,512]{1,0:T(8,128)S(1)} %grad.6.refs_3_, s32[64,64]{1,0:T(8,128)S(1)} %get-tuple-element.22.refs_4_, ...), custom_call_target="tpu_custom_call" | custom-call | flops 134217728 | bytes 4194304 | tf_op jit(solution)/shard_map/grad/pallas_call | solution.py:285
  57.4 3.5 %all-to-all-start = ((f32[16,4,128]{2,1,0:T(4,128)}), f32[16,4,128]{2,1,0:T(4,128)S(1)}, u32[]{:S(2)}, u32[]{:S(2)}) async-start(f32[16,4,128]{2,1,0:T(4,128)} %grad.7), calls=%async_computation | async-start | bytes 65536 | tf_op jit(solution)/shard_map/all_to_all | solution.py:403
  61.0 0.9 %own_rows.1 = bf16[4,8192]{1,0:T(4,128)(2,1)} custom-call(bf16[16,2048]{1,0:T(8,128)(2,1)S(1)} %pad_maximum_fusion.2.refs_0_, bf16[16,2048]{1,0:T(8,128)(2,1)S(1)} %slice.40.refs_1_, bf16[16,2048]{1,0:T(8,128)(2,1)S(1)} %slice.41.refs_2_, bf16[16,2048]{1,0:T(8,128)(2,1)S(1)} %slice.42.refs_3_), custom_call_target="tpu_custom_call" | custom-call | tf_op jit(solution)/shard_map/own_rows/pallas_call | solution.py:311
  61.8 5.7 %all-to-all-done = f32[16,4,128]{2,1,0:T(4,128)S(1)} async-done(((f32[16,4,128]{2,1,0:T(4,128)}), f32[16,4,128]{2,1,0:T(4,128)S(1)}, u32[]{:S(2)}, u32[]{:S(2)}) %all-to-all-start) | async-done | bytes 32800 | tf_op jit(solution)/shard_map/all_to_all | solution.py:403
  67.5 0.7 %multiply_reduce_fusion.2 = f32[4]{0:T(128)} fusion(f32[4,128]{1,0:T(4,128)S(1)} %reduce_sum.29), kind=kLoop, calls=%fused_computation.9 | loop fusion | flops 4 | bytes 32 | tf_op jit(solution)/shard_map/div | solution.py:404
  (28 shorter events, 0.4 us)
Async XLA Ops:
  4.3 2.5 %collective-permute-start = (f32[64,2048]{1,0:T(8,128)S(1)}, f32[64,2048]{1,0:T(8,128)S(1)}, u32[]{:S(2)}, u32[]{:S(2)}) collective-permute-start(f32[64,2048]{1,0:T(8,128)S(1)} %get-tuple-element.14), channel_id=1, source_target_pairs={{0,1},{1,0},{2,3},{3,2},{4,5},{5,4},{6,7},{7,6},{8,9},{9,8},{10,11... | collective-permute-start | bytes 1572872 | tf_op jit(solution)/shard_map/ppermute | solution.py:333
  4.8 7.1 %collective-permute-start.2 = (f32[64,2048]{1,0:T(8,128)S(1)}, f32[64,2048]{1,0:T(8,128)S(1)}, u32[]{:S(2)}, u32[]{:S(2)}) collective-permute-start(f32[64,2048]{1,0:T(8,128)S(1)} %get-tuple-element.15), channel_id=1, source_target_pairs={{0,1},{1,0},{2,3},{3,2},{4,5},{5,4},{6,7},{7,6},{8,9},{9,8},{10,11... | collective-permute-start | bytes 1572872 | tf_op jit(solution)/shard_map/ppermute | solution.py:333
  6.9 5.0 %copy-start.4 = (f32[64,2048]{1,0:T(8,128)}, f32[64,2048]{1,0:T(8,128)S(1)}, u32[]{:S(2)}) copy-start(f32[64,2048]{1,0:T(8,128)S(1)} %add.52) | copy-start | bytes 1572868
  6.9 10.1 %collective-permute-start.1 = (f32[64,1024]{1,0:T(8,128)S(1)}, f32[64,1024]{1,0:T(8,128)S(1)}, u32[]{:S(2)}, u32[]{:S(2)}) collective-permute-start(f32[64,1024]{1,0:T(8,128)S(1)} %slice.37.refs_3_), channel_id=1, source_target_pairs={{0,2},{1,3},{2,0},{3,1},{4,6},{5,7},{6,4},{7,5},{8,10},{9,11},{10,... | collective-permute-start | bytes 786440 | tf_op jit(solution)/shard_map/ppermute | solution.py:333
  12.0 5.1 %copy-start.5 = (f32[64,2048]{1,0:T(8,128)S(1)}, f32[64,2048]{1,0:T(8,128)}, u32[]{:S(2)}) copy-start(f32[64,2048]{1,0:T(8,128)} %copy-done.4) | copy-start | bytes 1572868
  12.0 10.1 %collective-permute-start.4 = (f32[64,1024]{1,0:T(8,128)S(1)}, f32[64,1024]{1,0:T(8,128)S(1)}, u32[]{:S(2)}, u32[]{:S(2)}) collective-permute-start(f32[64,1024]{1,0:T(8,128)S(1)} %slice.38._), channel_id=1, source_target_pairs={{0,2},{1,3},{2,0},{3,1},{4,6},{5,7},{6,4},{7,5},{8,10},{9,11},{10,... | collective-permute-start | bytes 786440 | tf_op jit(solution)/shard_map/ppermute | solution.py:333
  17.2 11.7 %collective-permute-start.6 = (f32[16,1024]{1,0:T(8,128)S(1)}, f32[16,1024]{1,0:T(8,128)S(1)}, u32[]{:S(2)}, u32[]{:S(2)}) collective-permute-start(f32[16,1024]{1,0:T(8,128)S(1)} %get-tuple-element.32), channel_id=1, source_target_pairs={{0,8},{1,9},{2,10},{3,11},{4,12},{5,13},{6,14},{7,15},{8,0},{9,1},... | collective-permute-start | bytes 196616 | tf_op jit(solution)/shard_map/ppermute | solution.py:333
  20.4 8.5 %collective-permute-start.5 = (f32[16,1024]{1,0:T(8,128)S(1)}, f32[16,1024]{1,0:T(8,128)S(1)}, u32[]{:S(2)}, u32[]{:S(2)}) collective-permute-start(f32[16,1024]{1,0:T(8,128)S(1)} %get-tuple-element.33), channel_id=1, source_target_pairs={{0,4},{1,5},{2,6},{3,7},{4,0},{5,1},{6,2},{7,3},{8,12},{9,13},{10,... | collective-permute-start | bytes 196616 | tf_op jit(solution)/shard_map/ppermute | solution.py:333
  22.0 6.4 %collective-permute-start.3 = (f32[16,1024]{1,0:T(8,128)S(1)}, f32[16,1024]{1,0:T(8,128)S(1)}, u32[]{:S(2)}, u32[]{:S(2)}) collective-permute-start(f32[16,1024]{1,0:T(8,128)S(1)} %get-tuple-element.31), channel_id=1, source_target_pairs={{0,12},{1,13},{2,14},{3,15},{4,8},{5,9},{6,10},{7,11},{8,4},{9,5},... | collective-permute-start | bytes 196616 | tf_op jit(solution)/shard_map/ppermute | solution.py:333
  22.2 13.1 %collective-permute-start.9 = (f32[16,1024]{1,0:T(8,128)S(1)}, f32[16,1024]{1,0:T(8,128)S(1)}, u32[]{:S(2)}, u32[]{:S(2)}) collective-permute-start(f32[16,1024]{1,0:T(8,128)S(1)} %get-tuple-element.28), channel_id=1, source_target_pairs={{0,8},{1,9},{2,10},{3,11},{4,12},{5,13},{6,14},{7,15},{8,0},{9,1},... | collective-permute-start | bytes 196616 | tf_op jit(solution)/shard_map/ppermute | solution.py:333
  25.1 10.2 %collective-permute-start.8 = (f32[16,1024]{1,0:T(8,128)S(1)}, f32[16,1024]{1,0:T(8,128)S(1)}, u32[]{:S(2)}, u32[]{:S(2)}) collective-permute-start(f32[16,1024]{1,0:T(8,128)S(1)} %get-tuple-element.29), channel_id=1, source_target_pairs={{0,4},{1,5},{2,6},{3,7},{4,0},{5,1},{6,2},{7,3},{8,12},{9,13},{10,... | collective-permute-start | bytes 196616 | tf_op jit(solution)/shard_map/ppermute | solution.py:333
  28.4 6.9 %collective-permute-start.7 = (f32[16,1024]{1,0:T(8,128)S(1)}, f32[16,1024]{1,0:T(8,128)S(1)}, u32[]{:S(2)}, u32[]{:S(2)}) collective-permute-start(f32[16,1024]{1,0:T(8,128)S(1)} %get-tuple-element.30), channel_id=1, source_target_pairs={{0,12},{1,13},{2,14},{3,15},{4,8},{5,9},{6,10},{7,11},{8,4},{9,5},... | collective-permute-start | bytes 196616 | tf_op jit(solution)/shard_map/ppermute | solution.py:333
  35.4 4.3 %collective-permute-start.11 = (bf16[16,2048]{1,0:T(8,128)(2,1)S(1)}, bf16[16,2048]{1,0:T(8,128)(2,1)S(1)}, u32[]{:S(2)}, u32[]{:S(2)}) collective-permute-start(bf16[16,2048]{1,0:T(8,128)(2,1)S(1)} %pad_maximum_fusion.2.refs_0_), channel_id=1, source_target_pairs={{0,4},{1,5},{2,6},{3,7},{4,0},{5,1},{6,2},{7,3},{8,12},{9,13},{10,... | collective-permute-start | bytes 196616 | tf_op jit(solution)/shard_map/ppermute | solution.py:333
  35.5 6.2 %collective-permute-start.10 = (bf16[16,2048]{1,0:T(8,128)(2,1)S(1)}, bf16[16,2048]{1,0:T(8,128)(2,1)S(1)}, u32[]{:S(2)}, u32[]{:S(2)}) collective-permute-start(bf16[16,2048]{1,0:T(8,128)(2,1)S(1)} %pad_maximum_fusion.2.refs_0_), channel_id=1, source_target_pairs={{0,12},{1,13},{2,14},{3,15},{4,8},{5,9},{6,10},{7,11},{8,4},{9,5},... | collective-permute-start | bytes 196616 | tf_op jit(solution)/shard_map/ppermute | solution.py:333
  35.6 7.8 %collective-permute-start.12 = (bf16[16,2048]{1,0:T(8,128)(2,1)S(1)}, bf16[16,2048]{1,0:T(8,128)(2,1)S(1)}, u32[]{:S(2)}, u32[]{:S(2)}) collective-permute-start(bf16[16,2048]{1,0:T(8,128)(2,1)S(1)} %pad_maximum_fusion.2.refs_0_), channel_id=1, source_target_pairs={{0,8},{1,9},{2,10},{3,11},{4,12},{5,13},{6,14},{7,15},{8,0},{9,1},... | collective-permute-start | bytes 196616 | tf_op jit(solution)/shard_map/ppermute | solution.py:333
  41.8 9.5 %collective-permute-start.15 = (bf16[48,2048]{1,0:T(8,128)(2,1)S(1)}, bf16[48,2048]{1,0:T(8,128)(2,1)S(1)}, u32[]{:S(2)}, u32[]{:S(2)}) collective-permute-start(bf16[48,2048]{1,0:T(8,128)(2,1)S(1)} %pad_maximum_fusion.1.refs_0_), channel_id=1, source_target_pairs={{0,2},{1,3},{2,0},{3,1},{4,6},{5,7},{6,4},{7,5},{8,10},{9,11},{10,... | collective-permute-start | bytes 589832 | tf_op jit(solution)/shard_map/ppermute | solution.py:333
  43.4 7.9 %collective-permute-start.14 = (bf16[16,2048]{1,0:T(8,128)(2,1)S(1)}, bf16[16,2048]{1,0:T(8,128)(2,1)S(1)}, u32[]{:S(2)}, u32[]{:S(2)}) collective-permute-start(bf16[16,2048]{1,0:T(8,128)(2,1)S(1)} %collective-permute-done.12.refs_1_._), channel_id=1, source_target_pairs={{0,2},{1,3},{2,0},{3,1},{4,6},{5,7},{6,4},{7,5},{8,10},{9,11},{10,... | collective-permute-start | bytes 196616 | tf_op jit(solution)/shard_map/ppermute | solution.py:333
  44.9 9.5 %collective-permute-start.13 = (bf16[64,2048]{1,0:T(8,128)(2,1)S(1)}, bf16[64,2048]{1,0:T(8,128)(2,1)S(1)}, u32[]{:S(2)}, u32[]{:S(2)}) collective-permute-start(bf16[64,2048]{1,0:T(8,128)(2,1)S(1)} %pad_maximum_fusion), channel_id=1, source_target_pairs={{0,1},{1,0},{2,3},{3,2},{4,5},{5,4},{6,7},{7,6},{8,9},{9,8},{10,11... | collective-permute-start | bytes 786440 | tf_op jit(solution)/shard_map/ppermute | solution.py:333
  47.9 1.3 %copy-start = (bf16[512,2048]{1,0:T(8,128)(2,1)}, bf16[512,2048]{1,0:T(8,128)(2,1)S(1)}, u32[]{:S(2)}) copy-start(bf16[512,2048]{1,0:T(8,128)(2,1)S(1)} %get-tuple-element.21.refs_2_) | copy-start | bytes 6291460
  49.2 1.3 %copy-start.2 = (bf16[512,2048]{1,0:T(8,128)(2,1)}, bf16[512,2048]{1,0:T(8,128)(2,1)S(1)}, u32[]{:S(2)}) copy-start(bf16[512,2048]{1,0:T(8,128)(2,1)S(1)} %get-tuple-element.19.refs_2_) | copy-start | bytes 6291460
  51.3 3.9 %collective-permute-start.17 = (bf16[16,2048]{1,0:T(8,128)(2,1)S(1)}, bf16[16,2048]{1,0:T(8,128)(2,1)S(1)}, u32[]{:S(2)}, u32[]{:S(2)}) collective-permute-start(bf16[16,2048]{1,0:T(8,128)(2,1)S(1)} %hold.18.refs_0_.refs_1_), channel_id=1, source_target_pairs={{0,1},{1,0},{2,3},{3,2},{4,5},{5,4},{6,7},{7,6},{8,9},{9,8},{10,11... | collective-permute-start | bytes 196616 | tf_op jit(solution)/shard_map/ppermute | solution.py:333
  51.8 3.3 %collective-permute-start.16 = (bf16[48,2048]{1,0:T(8,128)(2,1)S(1)}, bf16[48,2048]{1,0:T(8,128)(2,1)S(1)}, u32[]{:S(2)}, u32[]{:S(2)}) collective-permute-start(bf16[48,2048]{1,0:T(8,128)(2,1)S(1)} %collective-permute-done.15.refs_0_), channel_id=1, source_target_pairs={{0,1},{1,0},{2,3},{3,2},{4,5},{5,4},{6,7},{7,6},{8,9},{9,8},{10,11... | collective-permute-start | bytes 589832 | tf_op jit(solution)/shard_map/ppermute | solution.py:333
  52.0 1.6 %copy-start.1 = (bf16[512,2048]{1,0:T(8,128)(2,1)S(1)}, bf16[512,2048]{1,0:T(8,128)(2,1)}, u32[]{:S(2)}) copy-start(bf16[512,2048]{1,0:T(8,128)(2,1)} %copy-done) | copy-start | bytes 6291460
  54.4 1.6 %copy-start.3 = (bf16[512,2048]{1,0:T(8,128)(2,1)S(1)}, bf16[512,2048]{1,0:T(8,128)(2,1)}, u32[]{:S(2)}) copy-start(bf16[512,2048]{1,0:T(8,128)(2,1)} %copy-done.2) | copy-start | bytes 6291460
  57.4 10.1 %all-to-all-start = ((f32[16,4,128]{2,1,0:T(4,128)}), f32[16,4,128]{2,1,0:T(4,128)S(1)}, u32[]{:S(2)}, u32[]{:S(2)}) async-start(f32[16,4,128]{2,1,0:T(4,128)} %grad.7), calls=%async_computation | async-start | bytes 65536 | tf_op jit(solution)/shard_map/all_to_all | solution.py:403
  67.5 0.7 %copy-start.6 = (f32[4,128]{1,0:T(4,128)}, f32[4,128]{1,0:T(4,128)S(1)}, u32[]{:S(2)}) copy-start(f32[4,128]{1,0:T(4,128)S(1)} %reduce_sum.29) | copy-start | bytes 6148

commit v18 on v13

--- a/solution.py
+++ b/solution.py
@@ -53,7 +53,7 @@
 
 
 def params():
-    return pltpu.CompilerParams(vmem_limit_bytes=24 * 1024 * 1024)
+    return pltpu.CompilerParams(vmem_limit_bytes=12 * 1024 * 1024)
 
 
 def in_hbm(x):

time: 61.9 us -> 61.9 us (level)
  no operation moved by 1% of the time
where the time goes in v18:
time: 61.9 us; the launch traced here: 61.6 us
  starting transfers between devices  25.2 us (41%)
  waiting for transfers between devices  18.1 us (29%)
  Pallas kernels  15.8 us (26%)
  other arithmetic  1.23 us (2%)
  between operations  0.94 us (2%)
    ppermute x19, starting transfers between devices, swap(): return lax.ppermute(x, 'lat', pairs(n, dz, dy, dc))  20.7 us
    ppermute x19, waiting for transfers between devices, swap(): return lax.ppermute(x, 'lat', pairs(n, dz, dy, dc))  12.4 us
    pallas_call x3, Pallas kernels, decode(): pl.pallas_call(functools.partial(decode_kernel, n, rows // n, chunks, par...  7.51 us
    all_to_all x1, waiting for transfers between devices, local(): back = jnp.sum(lax.all_to_all(back, 'lat', 0, 0, tiled=True), axis=0)  5.76 us
    all_to_all x1, starting transfers between devices, local(): back = jnp.sum(lax.all_to_all(back, 'lat', 0, 0, tiled=True), axis=0)  4.5 us
    pallas_call x4, Pallas kernels, grad(): pl.pallas_call(functools.partial(grad_kernel, n, counts, prev is not None...  3.76 us
    pallas_call x1, Pallas kernels, fetch(): pl.pallas_call(functools.partial(fetch_kernel, n, places), out_shape=[blo...  3.54 us
  transfers between devices with their start and end apart: 20, of which 9 were waited for; matrix products, arithmetic and copies ran while one was open for 1% of the time, Pallas kernels for 17%

profile of v18, /device:TPU:0, one launch (start us, length us, event | category | flops | bytes accessed | tf_op | source)
XLA Modules:
  0.0 61.6 jit_solution(4838197667594707812)
XLA Ops:
  0.6 3.7 %decode.3 = (f32[64,2048]{1,0:T(8,128)S(1)}, f32[64,2048]{1,0:T(8,128)S(1)}, bf16[64,512]{1,0:T(8,128)(2,1)S(1)}) custom-call(s32[64,64]{1,0:T(8,128)} %ids_hbm.1, bf16[64,64]{1,0:T(8,128)(2,1)} %refs_1_.3, bf16[512,8192]{1,0:T(8,128)(2,1)} %decoder_hbm.1, bf16[4,8192]{1,0:T(4,128)(2,1)} %refs_2_.5), custom_call_target="tpu_custom_call" | custom-call | flops 268435456 | bytes 8388608 | tf_op jit(solution)/shard_map/decode/pallas_call | solution.py:187
  4.3 0.5 collective-permute-start
  4.8 0.1 collective-permute-start.2
  4.9 1.9 %decode.4 = f32[64,2048]{1,0:T(8,128)S(1)} custom-call(bf16[64,512]{1,0:T(8,128)(2,1)S(1)} %get-tuple-element.12.refs_0_, bf16[512,8192]{1,0:T(8,128)(2,1)} %decoder_hbm.1, bf16[4,8192]{1,0:T(4,128)(2,1)} %refs_2_.5), custom_call_target="tpu_custom_call" | custom-call | flops 134217728 | bytes 4194304 | tf_op jit(solution)/shard_map/decode/pallas_call | solution.py:187
  6.8 0.0 collective-permute-done
  6.8 0.1 add.52
  6.9 3.0 %collective-permute-start.1 = (f32[64,1024]{1,0:T(8,128)S(1)}, f32[64,1024]{1,0:T(8,128)S(1)}, u32[]{:S(2)}, u32[]{:S(2)}) collective-permute-start(f32[64,1024]{1,0:T(8,128)S(1)} %slice.35.refs_3_), channel_id=1, source_target_pairs={{0,2},{1,3},{2,0},{3,1},{4,6},{5,7},{6,4},{7,5},{8,10},{9,11},{10,... | collective-permute-start | bytes 786440 | tf_op jit(solution)/shard_map/ppermute | solution.py:333
  10.0 1.9 %decode.5 = f32[64,2048]{1,0:T(8,128)S(1)} custom-call(bf16[64,512]{1,0:T(8,128)(2,1)S(1)} %get-tuple-element.12.refs_0_, bf16[512,8192]{1,0:T(8,128)(2,1)} %decoder_hbm.1, bf16[4,8192]{1,0:T(4,128)(2,1)} %refs_2_.5, f32[64,1024]{1,0:T(8,128)S(1)} %slice.35.refs_3_), custom_call_target="tpu_custom_call" | custom-call | flops 134217728 | bytes 4194304 | tf_op jit(solution)/shard_map/decode/pallas_call | solution.py:187
  11.9 0.0 collective-permute-done.2
  11.9 0.1 add.53
  12.0 0.1 collective-permute-start.4
  12.1 3.5 %fetch.1 = (bf16[512,2048]{1,0:T(8,128)(2,1)S(1)}, bf16[512,2048]{1,0:T(8,128)(2,1)S(1)}, bf16[512,2048]{1,0:T(8,128)(2,1)S(1)}, bf16[512,2048]{1,0:T(8,128)(2,1...) custom-call(bf16[512,8192]{1,0:T(8,128)(2,1)} %decoder_hbm.1, s32[64,64]{1,0:T(8,128)} %ids_hbm.1, f32[64,1024]{1,0:T(8,128)S(1)} %slice.36._), custom_call_target="tpu_custom_call" | custom-call | bytes 8388608 | tf_op jit(solution)/shard_map/fetch/pallas_call | solution.py:215
  15.7 0.0 copy-start
  15.7 1.4 %collective-permute-done.1.x_ref = f32[64,1024]{1,0:T(8,128)S(1)} collective-permute-done((f32[64,1024]{1,0:T(8,128)S(1)}, f32[64,1024]{1,0:T(8,128)S(1)}, u32[]{:S(2)}, u32[]{:S(2)}) %collective-permute-start.1) | collective-permute-done | bytes 262176 | tf_op jit(solution)/shard_map/ppermute | solution.py:333
  17.2 4.2 %collective-permute-start.3 = (f32[16,1024]{1,0:T(8,128)S(1)}, f32[16,1024]{1,0:T(8,128)S(1)}, u32[]{:S(2)}, u32[]{:S(2)}) collective-permute-start(f32[16,1024]{1,0:T(8,128)S(1)} %get-tuple-element.29), channel_id=1, source_target_pairs={{0,12},{1,13},{2,14},{3,15},{4,8},{5,9},{6,10},{7,11},{8,4},{9,5},... | collective-permute-start | bytes 196616 | tf_op jit(solution)/shard_map/ppermute | solution.py:333
  21.4 0.0 collective-permute-start.6
  21.4 0.6 %collective-permute-start.5 = (f32[16,1024]{1,0:T(8,128)S(1)}, f32[16,1024]{1,0:T(8,128)S(1)}, u32[]{:S(2)}, u32[]{:S(2)}) collective-permute-start(f32[16,1024]{1,0:T(8,128)S(1)} %get-tuple-element.31), channel_id=1, source_target_pairs={{0,4},{1,5},{2,6},{3,7},{4,0},{5,1},{6,2},{7,3},{8,12},{9,13},{10,... | collective-permute-start | bytes 196616 | tf_op jit(solution)/shard_map/ppermute | solution.py:333
  22.0 0.1 collective-permute-done.4
  22.2 2.9 %collective-permute-start.9 = (f32[16,1024]{1,0:T(8,128)S(1)}, f32[16,1024]{1,0:T(8,128)S(1)}, u32[]{:S(2)}, u32[]{:S(2)}) collective-permute-start(f32[16,1024]{1,0:T(8,128)S(1)} %get-tuple-element.26), channel_id=1, source_target_pairs={{0,8},{1,9},{2,10},{3,11},{4,12},{5,13},{6,14},{7,15},{8,0},{9,1},... | collective-permute-start | bytes 196616 | tf_op jit(solution)/shard_map/ppermute | solution.py:333
  25.1 1.6 %collective-permute-start.8 = (f32[16,1024]{1,0:T(8,128)S(1)}, f32[16,1024]{1,0:T(8,128)S(1)}, u32[]{:S(2)}, u32[]{:S(2)}) collective-permute-start(f32[16,1024]{1,0:T(8,128)S(1)} %get-tuple-element.27), channel_id=1, source_target_pairs={{0,4},{1,5},{2,6},{3,7},{4,0},{5,1},{6,2},{7,3},{8,12},{9,13},{10,... | collective-permute-start | bytes 196616 | tf_op jit(solution)/shard_map/ppermute | solution.py:333
  26.7 0.0 collective-permute-done.3.x_ref
  26.7 0.9 %collective-permute-start.7 = (f32[16,1024]{1,0:T(8,128)S(1)}, f32[16,1024]{1,0:T(8,128)S(1)}, u32[]{:S(2)}, u32[]{:S(2)}) collective-permute-start(f32[16,1024]{1,0:T(8,128)S(1)} %get-tuple-element.28), channel_id=1, source_target_pairs={{0,12},{1,13},{2,14},{3,15},{4,8},{5,9},{6,10},{7,11},{8,4},{9,5},... | collective-permute-start | bytes 196616 | tf_op jit(solution)/shard_map/ppermute | solution.py:333
  27.6 0.0 collective-permute-done.5.x_ref
  27.6 0.1 collective-permute-done.6.x_ref
  27.8 0.1 multiply_reduce_fusion.1
  27.9 4.8 %collective-permute-done.7.x_ref = f32[16,1024]{1,0:T(8,128)S(1)} collective-permute-done((f32[16,1024]{1,0:T(8,128)S(1)}, f32[16,1024]{1,0:T(8,128)S(1)}, u32[]{:S(2)}, u32[]{:S(2)}) %collective-permute-start.7) | collective-permute-done | bytes 65568 | tf_op jit(solution)/shard_map/ppermute | solution.py:333
  32.7 0.0 collective-permute-done.8.x_ref
  32.8 0.0 copy-done
  32.8 0.0 collective-permute-done.9.x_ref
  32.8 0.1 multiply_reduce_fusion
  32.9 0.1 collective-permute-start.12
  33.0 2.2 %collective-permute-start.11 = (bf16[16,2048]{1,0:T(8,128)(2,1)S(1)}, bf16[16,2048]{1,0:T(8,128)(2,1)S(1)}, u32[]{:S(2)}, u32[]{:S(2)}) collective-permute-start(bf16[16,2048]{1,0:T(8,128)(2,1)S(1)} %pad_maximum_fusion.3.refs_0_), channel_id=1, source_target_pairs={{0,12},{1,13},{2,14},{3,15},{4,8},{5,9},{6,10},{7,11},{8,4},{9,5},... | collective-permute-start | bytes 196616 | tf_op jit(solution)/shard_map/ppermute | solution.py:333
  35.3 1.2 %collective-permute-start.14 = (bf16[16,2048]{1,0:T(8,128)(2,1)S(1)}, bf16[16,2048]{1,0:T(8,128)(2,1)S(1)}, u32[]{:S(2)}, u32[]{:S(2)}) collective-permute-start(bf16[16,2048]{1,0:T(8,128)(2,1)S(1)} %pad_maximum_fusion.3.refs_0_), channel_id=1, source_target_pairs={{0,8},{1,9},{2,10},{3,11},{4,12},{5,13},{6,14},{7,15},{8,0},{9,1},... | collective-permute-start | bytes 196616 | tf_op jit(solution)/shard_map/ppermute | solution.py:333
  36.5 1.4 %collective-permute-done.12 = bf16[16,2048]{1,0:T(8,128)(2,1)S(1)} collective-permute-done((bf16[16,2048]{1,0:T(8,128)(2,1)S(1)}, bf16[16,2048]{1,0:T(8,128)(2,1)S(1)}, u32[]{:S(2)}, u32[]{:S(2)}) %collective-permute-start.12) | collective-permute-done | bytes 65568 | tf_op jit(solution)/shard_map/ppermute | solution.py:333
  37.9 1.4 %collective-permute-done.11 = bf16[16,2048]{1,0:T(8,128)(2,1)S(1)} collective-permute-done((bf16[16,2048]{1,0:T(8,128)(2,1)S(1)}, bf16[16,2048]{1,0:T(8,128)(2,1)S(1)}, u32[]{:S(2)}, u32[]{:S(2)}) %collective-permute-start.11) | collective-permute-done | bytes 65568 | tf_op jit(solution)/shard_map/ppermute | solution.py:333
  39.3 1.6 %collective-permute-start.13 = (bf16[48,2048]{1,0:T(8,128)(2,1)S(1)}, bf16[48,2048]{1,0:T(8,128)(2,1)S(1)}, u32[]{:S(2)}, u32[]{:S(2)}) collective-permute-start(bf16[48,2048]{1,0:T(8,128)(2,1)S(1)} %pad_maximum_fusion.1.refs_0_), channel_id=1, source_target_pairs={{0,2},{1,3},{2,0},{3,1},{4,6},{5,7},{6,4},{7,5},{8,10},{9,11},{10,... | collective-permute-start | bytes 589832 | tf_op jit(solution)/shard_map/ppermute | solution.py:333
  40.9 0.1 collective-permute-start.16
  41.0 0.5 collective-permute-start.10
  41.5 0.0 collective-permute-done.14.refs_1_
  41.5 0.1 collective-permute-start.17
  41.5 0.8 %collective-permute-start.15 = (bf16[16,2048]{1,0:T(8,128)(2,1)S(1)}, bf16[16,2048]{1,0:T(8,128)(2,1)S(1)}, u32[]{:S(2)}, u32[]{:S(2)}) collective-permute-start(bf16[16,2048]{1,0:T(8,128)(2,1)S(1)} %collective-permute-done.14.refs_1_), channel_id=1, source_target_pairs={{0,2},{1,3},{2,0},{3,1},{4,6},{5,7},{6,4},{7,5},{8,10},{9,11},{10,... | collective-permute-start | bytes 196616 | tf_op jit(solution)/shard_map/ppermute | solution.py:333
  42.4 0.8 %grad.4.refs_4_ = f32[64,512]{1,0:T(8,128)S(1)} custom-call(bf16[48,2048]{1,0:T(8,128)(2,1)S(1)} %pad_maximum_fusion.1.refs_0_, bf16[16,2048]{1,0:T(8,128)(2,1)S(1)} %collective-permute-done.14.refs_1_, bf16[512,2048]{1,0:T(8,128)(2,1)S(1)} %get-tuple-element.17.refs_2_), custom_call_target="tpu_custom_call" | custom-call | flops 134217728 | bytes 4194304 | tf_op jit(solution)/shard_map/grad/pallas_call | solution.py:285
  43.1 0.0 collective-permute-done.10.refs_0_.refs_1_
  43.1 0.0 collective-permute-done.17.refs_2_
  43.2 0.0 collective-permute-done.16.refs_1_
  43.2 0.8 %grad.5.refs_0_.refs_3_ = f32[64,512]{1,0:T(8,128)S(1)} custom-call(bf16[16,2048]{1,0:T(8,128)(2,1)S(1)} %collective-permute-done.10.refs_0_.refs_1_, bf16[32,2048]{1,0:T(8,128)(2,1)S(1)} %collective-permute-done.16.refs_1_, bf16[16,2048]{1,0:T(8,128)(2,1)S(1)} %collective-permute-done.17.refs_2_, bf16[512,2048]{1,0:T(8,128)(2,1)S(1)} %get-tuple-element.16.refs_3_, ...), custom_call_target="tpu_custom_call" | custom-call | flops 134217728 | bytes 4194304 | tf_op jit(solution)/shard_map/grad/pallas_call | solution.py:285
  43.9 2.5 %collective-permute-done.15.x_ref = bf16[16,2048]{1,0:T(8,128)(2,1)S(1)} collective-permute-done((bf16[16,2048]{1,0:T(8,128)(2,1)S(1)}, bf16[16,2048]{1,0:T(8,128)(2,1)S(1)}, u32[]{:S(2)}, u32[]{:S(2)}) %collective-permute-start.15) | collective-permute-done | bytes 65568 | tf_op jit(solution)/shard_map/ppermute | solution.py:333
  46.4 0.0 collective-permute-done.13.refs_0_
  46.5 0.1 collective-permute-start.18
  46.6 0.1 copy.16.refs_4_
  46.7 0.0 copy-start.1
  46.7 0.8 %grad.6.refs_2_ = f32[64,512]{1,0:T(8,128)S(1)} custom-call(bf16[48,2048]{1,0:T(8,128)(2,1)S(1)} %collective-permute-done.13.refs_0_, bf16[16,2048]{1,0:T(8,128)(2,1)S(1)} %hold.17.refs_1_, bf16[512,2048]{1,0:T(8,128)(2,1)S(1)} %get-tuple-element.19.refs_2_, f32[64,512]{1,0:T(8,128)S(1)} %grad.5.refs_0_.refs_3_), custom_call_target="tpu_custom_call" | custom-call | flops 134217728 | bytes 4194304 | tf_op jit(solution)/shard_map/grad/pallas_call | solution.py:285
  47.4 0.7 %collective-permute-done.18.refs_0_ = bf16[64,2048]{1,0:T(8,128)(2,1)S(1)} collective-permute-done((bf16[64,2048]{1,0:T(8,128)(2,1)S(1)}, bf16[64,2048]{1,0:T(8,128)(2,1)S(1)}, u32[]{:S(2)}, u32[]{:S(2)}) %collective-permute-start.18) | collective-permute-done | bytes 262176 | tf_op jit(solution)/shard_map/ppermute | solution.py:333
  48.1 0.2 copy-done.1
  48.2 1.5 %grad.7 = f32[16,4,128]{2,1,0:T(4,128)} custom-call(bf16[64,2048]{1,0:T(8,128)(2,1)S(1)} %collective-permute-done.18.refs_0_, bf16[512,2048]{1,0:T(8,128)(2,1)S(1)} %copy-done.1, f32[64,512]{1,0:T(8,128)S(1)} %grad.6.refs_2_, s32[64,64]{1,0:T(8,128)S(1)} %get-tuple-element.20.refs_3_, f32[16,1]{1,0:T(8,128)S(1)} %copy.16.refs_4_), custom_call_target="tpu_custom_call" | custom-call | flops 134217728 | bytes 4194304 | tf_op jit(solution)/shard_map/grad/pallas_call | solution.py:285
  49.7 4.5 %all-to-all-start = ((f32[16,4,128]{2,1,0:T(4,128)}), f32[16,4,128]{2,1,0:T(4,128)S(1)}, u32[]{:S(2)}, u32[]{:S(2)}) async-start(f32[16,4,128]{2,1,0:T(4,128)} %grad.7), calls=%async_computation | async-start | bytes 65536 | tf_op jit(solution)/shard_map/all_to_all | solution.py:405
  54.3 0.8 %own_rows.1 = bf16[4,8192]{1,0:T(4,128)(2,1)} custom-call(bf16[16,2048]{1,0:T(8,128)(2,1)S(1)} %pad_maximum_fusion.3.refs_0_, bf16[16,2048]{1,0:T(8,128)(2,1)S(1)} %collective-permute-done.10.refs_0_.refs_1_, bf16[16,2048]{1,0:T(8,128)(2,1)S(1)} %slice.38.refs_2_, bf16[16,2048]{1,0:T(8,128)(2,1)S(1)} %slice.39.refs_3_), custom_call_target="tpu_custom_call" | custom-call | tf_op jit(solution)/shard_map/own_rows/pallas_call | solution.py:311
  55.1 5.8 %all-to-all-done = f32[16,4,128]{2,1,0:T(4,128)S(1)} async-done(((f32[16,4,128]{2,1,0:T(4,128)}), f32[16,4,128]{2,1,0:T(4,128)S(1)}, u32[]{:S(2)}, u32[]{:S(2)}) %all-to-all-start) | async-done | bytes 32800 | tf_op jit(solution)/shard_map/all_to_all | solution.py:405
  60.9 0.0 copy-start.2
  60.9 0.7 %multiply_reduce_fusion.2 = f32[4]{0:T(128)} fusion(f32[4,128]{1,0:T(4,128)S(1)} %reduce_sum.29), kind=kLoop, calls=%fused_computation.10 | loop fusion | flops 4 | bytes 32 | tf_op jit(solution)/shard_map/div | solution.py:406
  61.6 0.0 copy-done.2
  (23 shorter events, 0.4 us)
Async XLA Ops:
  4.3 2.5 %collective-permute-start = (f32[64,2048]{1,0:T(8,128)S(1)}, f32[64,2048]{1,0:T(8,128)S(1)}, u32[]{:S(2)}, u32[]{:S(2)}) collective-permute-start(f32[64,2048]{1,0:T(8,128)S(1)} %get-tuple-element.13), channel_id=1, source_target_pairs={{0,1},{1,0},{2,3},{3,2},{4,5},{5,4},{6,7},{7,6},{8,9},{9,8},{10,11... | collective-permute-start | bytes 1572872 | tf_op jit(solution)/shard_map/ppermute | solution.py:333
  4.8 7.1 %collective-permute-start.2 = (f32[64,2048]{1,0:T(8,128)S(1)}, f32[64,2048]{1,0:T(8,128)S(1)}, u32[]{:S(2)}, u32[]{:S(2)}) collective-permute-start(f32[64,2048]{1,0:T(8,128)S(1)} %get-tuple-element.14), channel_id=1, source_target_pairs={{0,1},{1,0},{2,3},{3,2},{4,5},{5,4},{6,7},{7,6},{8,9},{9,8},{10,11... | collective-permute-start | bytes 1572872 | tf_op jit(solution)/shard_map/ppermute | solution.py:333
  6.9 10.1 %collective-permute-start.1 = (f32[64,1024]{1,0:T(8,128)S(1)}, f32[64,1024]{1,0:T(8,128)S(1)}, u32[]{:S(2)}, u32[]{:S(2)}) collective-permute-start(f32[64,1024]{1,0:T(8,128)S(1)} %slice.35.refs_3_), channel_id=1, source_target_pairs={{0,2},{1,3},{2,0},{3,1},{4,6},{5,7},{6,4},{7,5},{8,10},{9,11},{10,... | collective-permute-start | bytes 786440 | tf_op jit(solution)/shard_map/ppermute | solution.py:333
  12.0 10.1 %collective-permute-start.4 = (f32[64,1024]{1,0:T(8,128)S(1)}, f32[64,1024]{1,0:T(8,128)S(1)}, u32[]{:S(2)}, u32[]{:S(2)}) collective-permute-start(f32[64,1024]{1,0:T(8,128)S(1)} %slice.36._), channel_id=1, source_target_pairs={{0,2},{1,3},{2,0},{3,1},{4,6},{5,7},{6,4},{7,5},{8,10},{9,11},{10,... | collective-permute-start | bytes 786440 | tf_op jit(solution)/shard_map/ppermute | solution.py:333
  15.7 17.1 %copy-start = (bf16[512,2048]{1,0:T(8,128)(2,1)}, bf16[512,2048]{1,0:T(8,128)(2,1)S(1)}, u32[]{:S(2)}) copy-start(bf16[512,2048]{1,0:T(8,128)(2,1)S(1)} %get-tuple-element.18.refs_1_) | copy-start | bytes 6291460
  17.2 9.5 %collective-permute-start.3 = (f32[16,1024]{1,0:T(8,128)S(1)}, f32[16,1024]{1,0:T(8,128)S(1)}, u32[]{:S(2)}, u32[]{:S(2)}) collective-permute-start(f32[16,1024]{1,0:T(8,128)S(1)} %get-tuple-element.29), channel_id=1, source_target_pairs={{0,12},{1,13},{2,14},{3,15},{4,8},{5,9},{6,10},{7,11},{8,4},{9,5},... | collective-permute-start | bytes 196616 | tf_op jit(solution)/shard_map/ppermute | solution.py:333
  21.4 6.4 %collective-permute-start.6 = (f32[16,1024]{1,0:T(8,128)S(1)}, f32[16,1024]{1,0:T(8,128)S(1)}, u32[]{:S(2)}, u32[]{:S(2)}) collective-permute-start(f32[16,1024]{1,0:T(8,128)S(1)} %get-tuple-element.30), channel_id=1, source_target_pairs={{0,8},{1,9},{2,10},{3,11},{4,12},{5,13},{6,14},{7,15},{8,0},{9,1},... | collective-permute-start | bytes 196616 | tf_op jit(solution)/shard_map/ppermute | solution.py:333
  21.4 6.2 %collective-permute-start.5 = (f32[16,1024]{1,0:T(8,128)S(1)}, f32[16,1024]{1,0:T(8,128)S(1)}, u32[]{:S(2)}, u32[]{:S(2)}) collective-permute-start(f32[16,1024]{1,0:T(8,128)S(1)} %get-tuple-element.31), channel_id=1, source_target_pairs={{0,4},{1,5},{2,6},{3,7},{4,0},{5,1},{6,2},{7,3},{8,12},{9,13},{10,... | collective-permute-start | bytes 196616 | tf_op jit(solution)/shard_map/ppermute | solution.py:333
  22.2 10.6 %collective-permute-start.9 = (f32[16,1024]{1,0:T(8,128)S(1)}, f32[16,1024]{1,0:T(8,128)S(1)}, u32[]{:S(2)}, u32[]{:S(2)}) collective-permute-start(f32[16,1024]{1,0:T(8,128)S(1)} %get-tuple-element.26), channel_id=1, source_target_pairs={{0,8},{1,9},{2,10},{3,11},{4,12},{5,13},{6,14},{7,15},{8,0},{9,1},... | collective-permute-start | bytes 196616 | tf_op jit(solution)/shard_map/ppermute | solution.py:333
  25.1 7.7 %collective-permute-start.8 = (f32[16,1024]{1,0:T(8,128)S(1)}, f32[16,1024]{1,0:T(8,128)S(1)}, u32[]{:S(2)}, u32[]{:S(2)}) collective-permute-start(f32[16,1024]{1,0:T(8,128)S(1)} %get-tuple-element.27), channel_id=1, source_target_pairs={{0,4},{1,5},{2,6},{3,7},{4,0},{5,1},{6,2},{7,3},{8,12},{9,13},{10,... | collective-permute-start | bytes 196616 | tf_op jit(solution)/shard_map/ppermute | solution.py:333
  26.7 6.1 %collective-permute-start.7 = (f32[16,1024]{1,0:T(8,128)S(1)}, f32[16,1024]{1,0:T(8,128)S(1)}, u32[]{:S(2)}, u32[]{:S(2)}) collective-permute-start(f32[16,1024]{1,0:T(8,128)S(1)} %get-tuple-element.28), channel_id=1, source_target_pairs={{0,12},{1,13},{2,14},{3,15},{4,8},{5,9},{6,10},{7,11},{8,4},{9,5},... | collective-permute-start | bytes 196616 | tf_op jit(solution)/shard_map/ppermute | solution.py:333
  32.9 5.0 %collective-permute-start.12 = (bf16[16,2048]{1,0:T(8,128)(2,1)S(1)}, bf16[16,2048]{1,0:T(8,128)(2,1)S(1)}, u32[]{:S(2)}, u32[]{:S(2)}) collective-permute-start(bf16[16,2048]{1,0:T(8,128)(2,1)S(1)} %pad_maximum_fusion.3.refs_0_), channel_id=1, source_target_pairs={{0,4},{1,5},{2,6},{3,7},{4,0},{5,1},{6,2},{7,3},{8,12},{9,13},{10,... | collective-permute-start | bytes 196616 | tf_op jit(solution)/shard_map/ppermute | solution.py:333
  33.0 6.2 %collective-permute-start.11 = (bf16[16,2048]{1,0:T(8,128)(2,1)S(1)}, bf16[16,2048]{1,0:T(8,128)(2,1)S(1)}, u32[]{:S(2)}, u32[]{:S(2)}) collective-permute-start(bf16[16,2048]{1,0:T(8,128)(2,1)S(1)} %pad_maximum_fusion.3.refs_0_), channel_id=1, source_target_pairs={{0,12},{1,13},{2,14},{3,15},{4,8},{5,9},{6,10},{7,11},{8,4},{9,5},... | collective-permute-start | bytes 196616 | tf_op jit(solution)/shard_map/ppermute | solution.py:333
  35.3 6.2 %collective-permute-start.14 = (bf16[16,2048]{1,0:T(8,128)(2,1)S(1)}, bf16[16,2048]{1,0:T(8,128)(2,1)S(1)}, u32[]{:S(2)}, u32[]{:S(2)}) collective-permute-start(bf16[16,2048]{1,0:T(8,128)(2,1)S(1)} %pad_maximum_fusion.3.refs_0_), channel_id=1, source_target_pairs={{0,8},{1,9},{2,10},{3,11},{4,12},{5,13},{6,14},{7,15},{8,0},{9,1},... | collective-permute-start | bytes 196616 | tf_op jit(solution)/shard_map/ppermute | solution.py:333
  39.3 7.1 %collective-permute-start.13 = (bf16[48,2048]{1,0:T(8,128)(2,1)S(1)}, bf16[48,2048]{1,0:T(8,128)(2,1)S(1)}, u32[]{:S(2)}, u32[]{:S(2)}) collective-permute-start(bf16[48,2048]{1,0:T(8,128)(2,1)S(1)} %pad_maximum_fusion.1.refs_0_), channel_id=1, source_target_pairs={{0,2},{1,3},{2,0},{3,1},{4,6},{5,7},{6,4},{7,5},{8,10},{9,11},{10,... | collective-permute-start | bytes 589832 | tf_op jit(solution)/shard_map/ppermute | solution.py:333
  40.9 2.3 %collective-permute-start.16 = (bf16[32,2048]{1,0:T(8,128)(2,1)S(1)}, bf16[32,2048]{1,0:T(8,128)(2,1)S(1)}, u32[]{:S(2)}, u32[]{:S(2)}) collective-permute-start(bf16[32,2048]{1,0:T(8,128)(2,1)S(1)} %pad_maximum_fusion.2), channel_id=1, source_target_pairs={{0,1},{1,0},{2,3},{3,2},{4,5},{5,4},{6,7},{7,6},{8,9},{9,8},{10,11... | collective-permute-start | bytes 393224 | tf_op jit(solution)/shard_map/ppermute | solution.py:333
  41.0 2.2 %collective-permute-start.10 = (bf16[16,2048]{1,0:T(8,128)(2,1)S(1)}, bf16[16,2048]{1,0:T(8,128)(2,1)S(1)}, u32[]{:S(2)}, u32[]{:S(2)}) collective-permute-start(bf16[16,2048]{1,0:T(8,128)(2,1)S(1)} %pad_maximum_fusion.3.refs_0_), channel_id=1, source_target_pairs={{0,1},{1,0},{2,3},{3,2},{4,5},{5,4},{6,7},{7,6},{8,9},{9,8},{10,11... | collective-permute-start | bytes 196616 | tf_op jit(solution)/shard_map/ppermute | solution.py:333
  41.5 1.7 %collective-permute-start.17 = (bf16[16,2048]{1,0:T(8,128)(2,1)S(1)}, bf16[16,2048]{1,0:T(8,128)(2,1)S(1)}, u32[]{:S(2)}, u32[]{:S(2)}) collective-permute-start(bf16[16,2048]{1,0:T(8,128)(2,1)S(1)} %collective-permute-done.14.refs_1_), channel_id=1, source_target_pairs={{0,1},{1,0},{2,3},{3,2},{4,5},{5,4},{6,7},{7,6},{8,9},{9,8},{10,11... | collective-permute-start | bytes 196616 | tf_op jit(solution)/shard_map/ppermute | solution.py:333
  41.5 4.9 %collective-permute-start.15 = (bf16[16,2048]{1,0:T(8,128)(2,1)S(1)}, bf16[16,2048]{1,0:T(8,128)(2,1)S(1)}, u32[]{:S(2)}, u32[]{:S(2)}) collective-permute-start(bf16[16,2048]{1,0:T(8,128)(2,1)S(1)} %collective-permute-done.14.refs_1_), channel_id=1, source_target_pairs={{0,2},{1,3},{2,0},{3,1},{4,6},{5,7},{6,4},{7,5},{8,10},{9,11},{10,... | collective-permute-start | bytes 196616 | tf_op jit(solution)/shard_map/ppermute | solution.py:333
  46.5 1.6 %collective-permute-start.18 = (bf16[64,2048]{1,0:T(8,128)(2,1)S(1)}, bf16[64,2048]{1,0:T(8,128)(2,1)S(1)}, u32[]{:S(2)}, u32[]{:S(2)}) collective-permute-start(bf16[64,2048]{1,0:T(8,128)(2,1)S(1)} %pad_maximum_fusion), channel_id=1, source_target_pairs={{0,1},{1,0},{2,3},{3,2},{4,5},{5,4},{6,7},{7,6},{8,9},{9,8},{10,11... | collective-permute-start | bytes 786440 | tf_op jit(solution)/shard_map/ppermute | solution.py:333
  46.7 1.6 %copy-start.1 = (bf16[512,2048]{1,0:T(8,128)(2,1)S(1)}, bf16[512,2048]{1,0:T(8,128)(2,1)}, u32[]{:S(2)}) copy-start(bf16[512,2048]{1,0:T(8,128)(2,1)} %copy-done) | copy-start | bytes 6291460
  49.7 11.1 %all-to-all-start = ((f32[16,4,128]{2,1,0:T(4,128)}), f32[16,4,128]{2,1,0:T(4,128)S(1)}, u32[]{:S(2)}, u32[]{:S(2)}) async-start(f32[16,4,128]{2,1,0:T(4,128)} %grad.7), calls=%async_computation | async-start | bytes 65536 | tf_op jit(solution)/shard_map/all_to_all | solution.py:405
  60.9 0.7 %copy-start.2 = (f32[4,128]{1,0:T(4,128)}, f32[4,128]{1,0:T(4,128)S(1)}, u32[]{:S(2)}) copy-start(f32[4,128]{1,0:T(4,128)S(1)} %reduce_sum.29) | copy-start | bytes 6148
